TPU v7x, 32 devices: a whole 2x2x4 slice. The times are simulated.
32 devices in a mesh: dp: 8 (over y, x, core), mp: 4 (over z).
Axes of the slice: x: 2, y: 2, z: 4, core: 2. Of those that a mesh axis runs over, the one named last changes fastest.
Arguments:
- inputs: bfloat16 [6144, 512], P('dp'), may hold values from -6 to 6
- lengths: int32 [8], P('dp'), may hold values from 192 to 768, as said below
- filters: bfloat16 [768, 24], replicated, may hold values from -0.21875 to 0.21875
- first_gain: float32 [512], replicated, may hold values from 0.5 to 1.5
- stu_weight: bfloat16 [48, 512, 512], replicated, may hold values from -0.0390625 to 0.0390625
- ar_weight: bfloat16 [3, 512, 512], replicated, may hold values from -0.15625 to 0.15625
- second_gain: float32 [512], replicated, may hold values from 0.5 to 1.5
- gate_weight: bfloat16 [512, 2048], P(None, 'mp'), may hold values from -0.25 to 0.25
- up_weight: bfloat16 [512, 2048], P(None, 'mp'), may hold values from -0.25 to 0.25
- down_weight: bfloat16 [2048, 512], P('mp'), may hold values from -0.125 to 0.125
- cotangent: bfloat16 [6144, 512], P('dp'), may hold values from -6 to 6
Outputs:
- output: bfloat16 [6144, 512], P('dp')
- input_grad: float32 [6144, 512], P('dp')
- stu_grad: float32 [48, 512, 512], P('mp', 'dp')
- ar_grad: float32 [3, 512, 512], replicated
- first_gain_grad: float32 [512], replicated
- second_gain_grad: float32 [512], replicated
- gate_grad: float32 [512, 2048], P(None, 'mp')
- up_grad: float32 [512, 2048], P(None, 'mp')
- down_grad: float32 [2048, 512], P('mp')
Inputs may be any that keep to these rules, and one draw needn't show every extreme that they name: `lengths`: one sequence in every draw has all 768 positions valid.
All inputs are finite; a program needn't handle non-finite values.
Results may differ from a plain program's by a relative error of at most 0.017.
Values may be sent and summed in bfloat16 or wider, within the bound.
No kernel may reach another device: no remote copies, remote signals or barrier semaphores. Data moves between devices by JAX's collectives and lax.ppermute only.
A program may use at most 384 MiB of HBM per device.

v0:
```python
import functools

import jax
import jax.numpy as jnp
from jax import lax
from jax.experimental import pallas as pl
from jax.experimental.pallas import tpu as pltpu
from jax.sharding import PartitionSpec as P

EPS = 1e-05
BF = jnp.bfloat16
F32 = jnp.float32
SQRT_2_PI = 0.7978845608028654
CUBIC = 0.044715
VMEM_LIMIT = 24 << 20


def dot(left, right):
    return jnp.dot(left, right, preferred_element_type=F32)


def dot_cols(left, right):
    return lax.dot_general(left, right, (((1,), (1,)), ((), ())), preferred_element_type=F32)


def params(limit=VMEM_LIMIT):
    return pltpu.CompilerParams(vmem_limit_bytes=limit)


COST_SCALE = 1.0


def cost(flops, nbytes):
    return pl.CostEstimate(
        flops=int(COST_SCALE * flops), bytes_accessed=int(COST_SCALE * nbytes), transcendentals=0
    )


def smem():
    return pl.BlockSpec(memory_space=pltpu.SMEM)


def whole():
    return pl.BlockSpec(memory_space=pltpu.VMEM)


def lag_spec(ar, steps):
    order, width = ar.shape[:2]
    assert order <= steps
    return pl.BlockSpec((1, width, width), lambda j: (jnp.minimum(j, order - 1), 0, 0))


def toeplitz(base_row, rows):
    wide = jnp.broadcast_to(base_row, (rows, base_row.shape[1]))
    return pltpu.roll(wide, 0, 1, stride=1, stride_axis=0)


def put_columns(scr, value):
    for c in range(scr.shape[0]):
        scr[c] = value[:, c * 128 : (c + 1) * 128]


def every_second(scr, start, count):
    columns = [scr[c, pl.ds(start, count, stride=2), :] for c in range(scr.shape[0])]
    return columns[0] if len(columns) == 1 else jnp.concatenate(columns, axis=1)


def interleave(scr, value):
    half = value.shape[0] // 2
    for c in range(scr.shape[0]):
        columns = slice(c * 128, (c + 1) * 128)
        scr[c, pl.ds(0, half, stride=2), :] = value[:half, columns]
        scr[c, pl.ds(1, half, stride=2), :] = value[half:, columns]
    return jnp.concatenate([scr[c] for c in range(scr.shape[0])], axis=1)


def norm_kernel(
    n, share, len_ref, x_ref, gain_ref, filt_ref, u_ref, taps_ref, nat_ref, ut_ref, scr, scr_f
):
    length, width = x_ref.shape
    half = length // 2
    m = lax.axis_index("mp")
    x = x_ref[...].astype(F32)
    r1 = lax.rsqrt(jnp.mean(x * x, axis=-1, keepdims=True) + EPS)
    row = lax.broadcasted_iota(jnp.int32, (length, 1), 0)
    mask = (row < len_ref[0]).astype(F32)
    u = mask * x * r1 * gain_ref[...]
    put_columns(scr, u)
    ut_ref[...] = u.T.astype(BF)
    for r in range(n):
        start = lax.rem(m + r, n) * share
        for odd in range(2):
            u_ref[odd, r * (share // 2) : (r + 1) * (share // 2), :] = every_second(
                scr, start + odd, share // 2
            ).astype(BF)
    filt = filt_ref.shape[0]
    natural = filt_ref[...].astype(F32)
    nat_ref[...] = natural
    scr_f[0, :, :filt] = natural.T
    even = every_second(scr_f, 0, half).T[:filt]
    odd = every_second(scr_f, 1, half).T[:filt]
    i = lax.broadcasted_iota(jnp.int32, (half, half), 0)
    j = lax.broadcasted_iota(jnp.int32, (half, half), 1)
    flip = (i == jnp.where(j == 0, 0, half - j)).astype(F32).astype(BF)
    rev_even = dot(even.astype(BF), flip)
    rev_odd = dot(odd.astype(BF), flip)
    taps_ref[0] = rev_even
    taps_ref[1] = rev_odd
    taps_ref[2] = pltpu.roll(rev_odd, half - 1, 1)
    taps_ref[3] = even
    taps_ref[4] = odd
    taps_ref[5] = pltpu.roll(odd, 1, 1)


def first_norm(lengths, x, gain, filters, n):
    length, width = x.shape
    share = length // n
    filt = filters.shape[0]
    half = length // 2
    return pl.pallas_call(
        functools.partial(norm_kernel, n, share),
        in_specs=[smem()] + [whole()] * 3,
        out_specs=[whole()] * 4,
        out_shape=[
            jax.ShapeDtypeStruct((2, half, width), BF),
            jax.ShapeDtypeStruct((6, filt, half), F32),
            jax.ShapeDtypeStruct((filt, length), F32),
            jax.ShapeDtypeStruct((width, length), BF),
        ],
        scratch_shapes=[
            pltpu.VMEM((width // 128, length, 128), F32),
            pltpu.VMEM((1, length, 128), F32),
        ],
        compiler_params=params(),
        cost_estimate=cost(10 * x.size, 6 * x.size),
        name="first_norm",
    )(lengths, x, gain, filters)


def mix_kernel(
    kb, share, order, len_ref, taps_ref, x_ref, u_ref, wp_ref, wm_ref, ar_ref, gain_ref,
    hid_ref, nt_ref, ta_ref, tb_ref, c_ref, acc_ref, scr,
):
    j = pl.program_id(0)
    length, width = x_ref.shape
    half, rows = length // 2, share // 2
    m = lax.axis_index("mp")
    b = lax.broadcasted_iota(jnp.int32, (rows, half), 0)
    a = lax.broadcasted_iota(jnp.int32, (rows, half), 1)
    wrapped = a >= (length - m * share) // 2
    upto = (a <= b) | wrapped
    below = (a < b) | wrapped

    @pl.when(j == 0)
    def _():
        acc_ref[...] = jnp.zeros((share, width), F32)

    @pl.when(j < order)
    def _():
        parts = []
        for row_odd in range(2):
            part = None
            for col_odd in range(2):
                back = 2 * b + row_odd - 2 * a - col_odd
                valid = (back >= 0) | wrapped
                back = jnp.where(back < 0, back + length, back)
                t = jnp.where(valid & (back == j), 1.0, 0.0).astype(BF)
                one = dot(t, u_ref[col_odd])
                part = one if part is None else part + one
            parts.append(part)
        acc_ref[...] += dot(jnp.concatenate(parts, axis=0).astype(BF), ar_ref[0])

    for k in range(kb):
        even = toeplitz(taps_ref[0, pl.ds(j * kb + k, 1), :], rows)
        odd = toeplitz(taps_ref[1, pl.ds(j * kb + k, 1), :], rows)
        late = toeplitz(taps_ref[2, pl.ds(j * kb + k, 1), :], rows)
        even = jnp.where(upto, even, 0.0).astype(BF)
        at = k * share
        ta_ref[at : at + rows, :] = even
        ta_ref[at + rows : at + share, :] = jnp.where(upto, odd, 0.0).astype(BF)
        tb_ref[at : at + rows, :] = jnp.where(below, late, 0.0).astype(BF)
        tb_ref[at + rows : at + share, :] = even
    ca = dot(ta_ref[...], u_ref[0])
    cb = dot(tb_ref[...], u_ref[1])
    for k in range(kb):
        at = k * share
        pa, pb = ca[at : at + share], cb[at : at + share]
        c_ref[:, k * width : (k + 1) * width] = (pa + pb).astype(BF)
        c_ref[:rows, (kb + k) * width : (kb + k + 1) * width] = (pa[:rows] - pb[:rows]).astype(BF)
        c_ref[rows:, (kb + k) * width : (kb + k + 1) * width] = (pb[rows:] - pa[rows:]).astype(BF)
    total = dot(c_ref[:, : kb * width], wp_ref[...].reshape(kb * width, width))
    total = total + dot(c_ref[:, kb * width :], wm_ref[...].reshape(kb * width, width))
    acc_ref[...] += total

    @pl.when(j == pl.num_programs(0) - 1)
    def _():
        start = pl.multiple_of(m * share, 16)
        x = x_ref[pl.ds(start, share), :].astype(F32)
        hidden = x + interleave(scr, acc_ref[...])
        hid_ref[...] = hidden
        r2 = lax.rsqrt(jnp.mean(hidden * hidden, axis=-1, keepdims=True) + EPS)
        pos = m * share + lax.broadcasted_iota(jnp.int32, (share, 1), 0)
        mask = (pos < len_ref[0]).astype(F32)
        nt_ref[...] = (mask * hidden * r2 * gain_ref[...]).astype(BF)


def spectral_mix(lengths, taps, x, u, stu, ar, gain, share, kb):
    length, width = x.shape
    filt = taps.shape[1]
    steps = filt // kb
    w_spec = pl.BlockSpec((kb, width, width), lambda j: (j, 0, 0))
    w_spec_neg = pl.BlockSpec((kb, width, width), lambda j: (j + steps, 0, 0))
    return pl.pallas_call(
        functools.partial(mix_kernel, kb, share, ar.shape[0]),
        grid=(steps,),
        in_specs=[smem(), whole(), whole(), whole(), w_spec, w_spec_neg]
        + [lag_spec(ar, steps), whole()],
        out_specs=[whole()] * 2,
        out_shape=[
            jax.ShapeDtypeStruct((share, width), F32),
            jax.ShapeDtypeStruct((share, width), BF),
        ],
        scratch_shapes=[
            pltpu.VMEM((kb * share, length // 2), BF),
            pltpu.VMEM((kb * share, length // 2), BF),
            pltpu.VMEM((share, 2 * kb * width), BF),
            pltpu.VMEM((share, width), F32),
            pltpu.VMEM((width // 128, share, 128), F32),
        ],
        compiler_params=params(40 << 20),
        cost_estimate=cost(2 * filt * share * width * (length + 2 * width), 2 * stu.size),
        name="spectral_mix",
    )(lengths, taps, x, u, stu, stu, ar, gain)


def ffn_kernel(
    shift, n, nt_ref, cot_ref, gw_ref, uw_ref, dw_ref, bn_ref, act_ref, bg_ref, bu_ref
):
    share = nt_ref.shape[0]
    nt = nt_ref[...]
    gate = dot(nt, gw_ref[...])
    upper = dot(nt, uw_ref[...])
    start = pl.multiple_of(lax.rem(lax.axis_index("mp") + shift, n) * share, 16)
    back_act = dot_cols(cot_ref[pl.ds(start, share), :], dw_ref[...])
    square = gate * gate
    th = jnp.tanh(SQRT_2_PI * (gate + CUBIC * square * gate))
    half = 0.5 * (1.0 + th)
    gelu = gate * half
    slope = half + 0.5 * gate * (1.0 - th * th) * (SQRT_2_PI * (1.0 + 3.0 * CUBIC * square))
    act_ref[...] = (gelu * upper).astype(BF)
    bg = (back_act * upper * slope).astype(BF)
    bu = (back_act * gelu).astype(BF)
    bg_ref[...] = bg
    bu_ref[...] = bu
    bn_ref[...] = (dot_cols(bg, gw_ref[...]) + dot_cols(bu, uw_ref[...])).astype(BF)


def feed_forward(shift, n, nt, cot, gw, uw, dw):
    share, width = nt.shape
    hid = gw.shape[1]
    return pl.pallas_call(
        functools.partial(ffn_kernel, shift, n),
        in_specs=[whole()] * 5,
        out_specs=[whole()] * 4,
        out_shape=[jax.ShapeDtypeStruct((share, width), BF)]
        + [jax.ShapeDtypeStruct((share, hid), BF)] * 3,
        compiler_params=params(),
        cost_estimate=cost(10 * share * width * hid, 2 * (3 * width * hid + 6 * share * width)),
        name="feed_forward",
    )(nt, cot, gw, uw, dw)


def ffn_grad_kernel(n, share, groups, cot_ref, dw_ref, *refs):
    nt_refs, act_refs, bg_refs, bu_refs = (refs[i * n : (i + 1) * n] for i in range(4))
    out_refs, grad_refs = refs[4 * n : 5 * n], refs[5 * n :]
    m = lax.axis_index("mp")
    nt = jnp.concatenate([ref[...] for ref in nt_refs], axis=0)
    act = jnp.concatenate([ref[...] for ref in act_refs], axis=0)
    bg = jnp.concatenate([ref[...] for ref in bg_refs], axis=0)
    bu = jnp.concatenate([ref[...] for ref in bu_refs], axis=0)
    cot = jnp.concatenate(
        [
            cot_ref[pl.ds(pl.multiple_of(lax.rem(m + r, n) * share, 16), share), :]
            for r in range(n)
        ],
        axis=0,
    )
    outs = dot(act, dw_ref[...]).astype(BF)
    for r in range(n):
        out_refs[r][...] = outs[r * share : (r + 1) * share, :]
    nt_t = nt.T
    grads = (dot(nt_t, bg), dot(nt_t, bu), dot(act.T, cot))
    if not groups:
        for ref, grad in zip(grad_refs, grads):
            ref[...] = grad.astype(BF)
        return
    keep_ref, send_ref, scr = grad_refs
    for i in range(3):
        scr[i] = grads[i].astype(BF)
    rows = scr.shape[1] // (2 * groups)
    d = lax.axis_index("dp")
    core = lax.rem(d, 2)
    for r in range(groups):
        chip = ((d // 2) ^ r) * 2
        for i in range(3):
            mine = pl.multiple_of((chip + core) * rows, 16)
            other = pl.multiple_of((chip + 1 - core) * rows, 16)
            keep_ref[r, i] = scr[i, pl.ds(mine, rows), :]
            send_ref[r, i] = scr[i, pl.ds(other, rows), :]


def ffn_grads(cot, dw, nts, acts, bgs, bus, groups):
    n = len(nts)
    share, width = nts[0].shape
    hid = dw.shape[0]
    length = cot.shape[0]
    out_shape = [jax.ShapeDtypeStruct((share, width), BF)] * n
    scratch = []
    if groups:
        part = (groups, 3, width // (2 * groups), width)
        out_shape += [jax.ShapeDtypeStruct(part, BF)] * 2
        scratch = [pltpu.VMEM((3, width, width), BF)]
    else:
        out_shape += [
            jax.ShapeDtypeStruct((width, hid), BF),
            jax.ShapeDtypeStruct((width, hid), BF),
            jax.ShapeDtypeStruct((hid, width), BF),
        ]
    args = [cot, dw, *nts, *acts, *bgs, *bus]
    return pl.pallas_call(
        functools.partial(ffn_grad_kernel, n, share, groups),
        in_specs=[whole()] * len(args),
        out_specs=[whole()] * len(out_shape),
        out_shape=out_shape,
        scratch_shapes=scratch,
        compiler_params=params(),
        cost_estimate=cost(8 * length * width * hid, 12 * length * width),
        name="ffn_grads",
    )(*args)


def mid_kernel(n, share, len_ref, hid_ref, cot_ref, gain_ref, *refs):
    bn_refs, (bh_ref, b_ref, gg_ref) = refs[:n], refs[n:]
    m = lax.axis_index("mp")
    bn = bn_refs[0][...].astype(F32)
    for ref in bn_refs[1:]:
        bn = bn + ref[...].astype(F32)
    hidden = hid_ref[...]
    r2 = lax.rsqrt(jnp.mean(hidden * hidden, axis=-1, keepdims=True) + EPS)
    pos = m * share + lax.broadcasted_iota(jnp.int32, (share, 1), 0)
    bn = bn * (pos < len_ref[0]).astype(F32)
    z = hidden * r2
    gg_ref[...] = jnp.broadcast_to(jnp.sum(bn * z, axis=0, keepdims=True), gg_ref.shape)
    q = bn * gain_ref[...]
    start = pl.multiple_of(m * share, 16)
    dout = cot_ref[pl.ds(start, share), :].astype(F32)
    back = dout + r2 * (q - z * jnp.mean(q * z, axis=-1, keepdims=True))
    bh_ref[...] = back
    b_ref[...] = back.astype(BF)


def mid_norm(lengths, hidden, cot, gain, pieces):
    share, width = hidden.shape
    n = len(pieces)
    return pl.pallas_call(
        functools.partial(mid_kernel, n, share),
        in_specs=[smem()] + [whole()] * (3 + n),
        out_specs=[whole()] * 3,
        out_shape=[
            jax.ShapeDtypeStruct(hidden.shape, F32),
            jax.ShapeDtypeStruct(hidden.shape, BF),
            jax.ShapeDtypeStruct((8, width), F32),
        ],
        compiler_params=params(),
        cost_estimate=cost(20 * hidden.size, 20 * hidden.size),
        name="second_norm_back",
    )(lengths, hidden, cot, gain, *pieces)


def unmix_kernel(
    kb, share, n, order, len_ref, taps_ref, x_ref, bh_ref, gg_ref, gain_ref, wp_ref, wm_ref, ar_ref, *refs
):
    b_refs, (ig_ref, gain_out, ta_ref, tb_ref, be_ref, bo_ref, acc_ref, scr) = refs[:n], refs[n:]
    j = pl.program_id(0)
    width = bh_ref.shape[1]
    length = n * share
    half, rows = length // 2, share // 2
    m = lax.axis_index("mp")
    b = lax.broadcasted_iota(jnp.int32, (rows, half), 0)
    a = lax.broadcasted_iota(jnp.int32, (rows, half), 1)
    inside = a < (length - m * share) // 2
    upto = (a >= b) & inside
    below = (a > b) & inside

    @pl.when(j == 0)
    def _():
        for r in range(n):
            put_columns(scr, b_refs[r][...].astype(F32))
            be_ref[r * rows : (r + 1) * rows, :] = every_second(scr, 0, rows).astype(BF)
            bo_ref[r * rows : (r + 1) * rows, :] = every_second(scr, 1, rows).astype(BF)
        acc_ref[...] = jnp.zeros((share, width), F32)

    @pl.when(j < order)
    def _():
        parts = []
        for row_odd in range(2):
            part = None
            for col_odd, source in enumerate((be_ref, bo_ref)):
                ahead = 2 * a + col_odd - 2 * b - row_odd
                t = jnp.where(inside & (ahead == j), 1.0, 0.0).astype(BF)
                one = dot(t, source[...])
                part = one if part is None else part + one
            parts.append(part)
        acc_ref[...] += dot_cols(jnp.concatenate(parts, axis=0).astype(BF), ar_ref[0])

    for k in range(kb):
        even = toeplitz(taps_ref[3, pl.ds(j * kb + k, 1), :], rows)
        odd = toeplitz(taps_ref[4, pl.ds(j * kb + k, 1), :], rows)
        late = toeplitz(taps_ref[5, pl.ds(j * kb + k, 1), :], rows)
        even = jnp.where(upto, even, 0.0).astype(BF)
        at = k * share
        ta_ref[at : at + rows, :] = even
        ta_ref[at + rows : at + share, :] = jnp.where(below, late, 0.0).astype(BF)
        tb_ref[at : at + rows, :] = jnp.where(upto, odd, 0.0).astype(BF)
        tb_ref[at + rows : at + share, :] = even
    ca = dot(ta_ref[...], be_ref[...])
    cb = dot(tb_ref[...], bo_ref[...])
    total = acc_ref[...]
    for k in range(kb):
        at = k * share
        pa, pb = ca[at : at + share], cb[at : at + share]
        minus = jnp.concatenate([pa[:rows] - pb[:rows], pb[rows:] - pa[rows:]], axis=0)
        total = total + dot_cols((pa + pb).astype(BF), wp_ref[k])
        total = total + dot_cols(minus.astype(BF), wm_ref[k])
    acc_ref[...] = total

    @pl.when(j == pl.num_programs(0) - 1)
    def _():
        start = pl.multiple_of(m * share, 16)
        x = x_ref[pl.ds(start, share), :].astype(F32)
        r1 = lax.rsqrt(jnp.mean(x * x, axis=-1, keepdims=True) + EPS)
        pos = m * share + lax.broadcasted_iota(jnp.int32, (share, 1), 0)
        masked = interleave(scr, acc_ref[...]) * (pos < len_ref[0]).astype(F32)
        y = x * r1
        p = masked * gain_ref[...]
        ig = bh_ref[...] + r1 * (p - y * jnp.mean(p * y, axis=-1, keepdims=True))
        ig_ref[...] = ig.astype(BF)
        gain_out[0:8, :] = jnp.broadcast_to(jnp.sum(masked * y, axis=0, keepdims=True), (8, width))
        gain_out[8:16, :] = gg_ref[...]


def spectral_unmix(lengths, taps, x, back_hidden, gg, gain, stu, ar, pieces, kb):
    share, width = back_hidden.shape
    n = len(pieces)
    length = n * share
    count = taps.shape[1]
    steps = count // kb
    w_spec = pl.BlockSpec((kb, width, width), lambda j: (j, 0, 0))
    w_spec_neg = pl.BlockSpec((kb, width, width), lambda j: (j + steps, 0, 0))
    return pl.pallas_call(
        functools.partial(unmix_kernel, kb, share, n, ar.shape[0]),
        grid=(steps,),
        in_specs=[smem()]
        + [whole()] * 5
        + [w_spec, w_spec_neg, lag_spec(ar, steps)]
        + [whole()] * n,
        out_specs=[whole()] * 2,
        out_shape=[
            jax.ShapeDtypeStruct((share, width), BF),
            jax.ShapeDtypeStruct((16, width), F32),
        ],
        scratch_shapes=[
            pltpu.VMEM((kb * share, length // 2), BF),
            pltpu.VMEM((kb * share, length // 2), BF),
            pltpu.VMEM((length // 2, width), BF),
            pltpu.VMEM((length // 2, width), BF),
            pltpu.VMEM((share, width), F32),
            pltpu.VMEM((width // 128, share, 128), F32),
        ],
        compiler_params=params(40 << 20),
        cost_estimate=cost(2 * count * share * width * (length + 2 * width), 2 * stu.size),
        name="spectral_unmix",
    )(lengths, taps, x, back_hidden, gg, gain, stu, stu, ar, *pieces)


def conv_kernel(groups, tile, own, filt_ref, *refs):
    ut_refs, (conv_ref, tt_ref, ut_scr) = refs[:groups], refs[groups:]
    j = pl.program_id(0)
    filt, length = filt_ref.shape
    block = conv_ref.shape[1]
    count = length // tile
    chip = lax.axis_index("dp") // 2

    @pl.when(j == 0)
    def _():
        start = pl.multiple_of(chip * block, 16)
        for r in range(groups):
            ut_scr[r * block : (r + 1) * block, :] = ut_refs[r][pl.ds(start, block), :]

    which = lax.axis_index("mp") * own + j
    strip = toeplitz(filt_ref[pl.ds(lax.rem(which, filt), 1), :], tile)
    row = lax.broadcasted_iota(jnp.int32, (tile, length), 0)
    col = lax.broadcasted_iota(jnp.int32, (tile, length), 1)
    flip = ((col - row) % 2 == 1) & (which >= filt)
    strip = jnp.where(col >= row, jnp.where(flip, -strip, strip), 0.0).astype(BF)
    for b in range(count):
        tt_ref[b * tile : (b + 1) * tile, b * tile :] = strip[:, : length - b * tile]
    for c in range(count):
        end = (c + 1) * tile
        part = dot(ut_scr[:, :end], tt_ref[:end, c * tile : end]).astype(BF)
        for r in range(groups):
            start = pl.multiple_of((lax.rem(chip, groups) ^ r) * length + c * tile, 128)
            conv_ref[0, :, pl.ds(start, tile)] = part[r * block : (r + 1) * block, :]


def convolutions(filt, uts, own, chips):
    length = filt.shape[1]
    groups = len(uts)
    block = uts[0].shape[0] // chips
    tile = 256 if length % 256 == 0 else length
    return pl.pallas_call(
        functools.partial(conv_kernel, groups, tile, own),
        grid=(own,),
        in_specs=[whole()] * (1 + groups),
        out_specs=pl.BlockSpec((1, block, groups * length), lambda j: (j, 0, 0)),
        out_shape=jax.ShapeDtypeStruct((own, block, groups * length), BF),
        scratch_shapes=[
            pltpu.VMEM((length, length), BF),
            pltpu.VMEM((groups * block, length), BF),
        ],
        compiler_params=params(),
        cost_estimate=cost(
            4 * own * groups * block * length * length // 3, 2 * own * groups * block * length
        ),
        name="convolutions",
    )(filt, *uts)


def grads_kernel(steps, order, groups, rows, conv_ref, *refs):
    ut_refs, b_refs = refs[:groups], refs[groups : groups + len(rows)]
    keep_ref, send_ref, b_scr, lag_scr, scr = refs[groups + len(rows) :]
    g = pl.program_id(0)
    d = lax.axis_index("dp")
    chip, core = lax.rem(d // 2, groups), lax.rem(d, 2)
    step, block, depth = conv_ref.shape
    width, length = ut_refs[0].shape
    half = block // 2

    @pl.when(g == 0)
    def _():
        for ref, (r, at, size) in zip(b_refs, rows):
            start = pl.multiple_of((chip ^ r) * length + at, 16)
            b_scr[pl.ds(start, size), :] = ref[:size, :]

    @pl.when(g < steps)
    def _():
        part = dot(conv_ref[...].reshape(step * block, depth), b_scr[...])
        scr[...] = part.reshape(step, block, width)
        mine = pl.multiple_of(core * half, 16)
        other = pl.multiple_of((1 - core) * half, 16)
        keep_ref[pl.ds(g * step, step)] = scr[:, pl.ds(mine, half), :]
        for k in range(step):
            start = pl.multiple_of((g * step + k) * half, 16)
            send_ref[pl.ds(start, half), :] = scr[k, pl.ds(other, half), :].astype(BF)

    @pl.when(g >= steps)
    def _():
        lag = g - steps
        col = lax.broadcasted_iota(jnp.int32, (width, length), 1)
        for r in range(groups):
            value = pltpu.roll(ut_refs[r][...].astype(F32), lag, 1)
            start = pl.multiple_of((chip ^ r) * length, 128)
            lag_scr[:, pl.ds(start, length)] = jnp.where(col >= lag, value, 0.0).astype(BF)
        start = pl.multiple_of(steps * step * half + lag * width, 16)
        send_ref[pl.ds(start, width), :] = dot(lag_scr[...], b_scr[...]).astype(BF)


def matrix_grads(conv, uts, backs, rows, order):
    own, block, depth = conv.shape
    groups = len(uts)
    width = uts[0].shape[0]
    step = next(s for s in (4, 3, 2, 1) if own % s == 0)
    steps = own // step
    half = block // 2
    return pl.pallas_call(
        functools.partial(grads_kernel, steps, order, groups, rows),
        grid=(steps + order,),
        in_specs=[pl.BlockSpec((step, block, depth), lambda g: (jnp.minimum(g, steps - 1), 0, 0))]
        + [whole()] * (groups + len(backs)),
        out_specs=[whole()] * 2,
        out_shape=[
            jax.ShapeDtypeStruct((own, half, width), F32),
            jax.ShapeDtypeStruct((own * half + order * width, width), BF),
        ],
        scratch_shapes=[
            pltpu.VMEM((depth, width), BF),
            pltpu.VMEM((width, depth), BF),
            pltpu.VMEM((step, block, width), F32),
        ],
        compiler_params=params(),
        cost_estimate=cost(2 * (conv.size + order * width * depth) * width, 2 * conv.size),
        name="matrix_grads",
    )(conv, *uts, *backs)


def rows_message_kernel(ig_ref, hid_ref, *refs):
    share = ig_ref.shape[0]
    total = hid_ref[...]
    for ref in refs[:-1]:
        total = total + ref[...].astype(F32)
    refs[-1][:share, :] = ig_ref[...]
    refs[-1][share:, :] = total.astype(BF)


def rows_message(ig, hidden, pieces):
    share, width = ig.shape
    return pl.pallas_call(
        rows_message_kernel,
        in_specs=[whole()] * (2 + len(pieces)),
        out_specs=whole(),
        out_shape=jax.ShapeDtypeStruct((2 * share, width), BF),
        compiler_params=params(),
        cost_estimate=cost(4 * ig.size, 10 * ig.size),
        name="rows_message",
    )(ig, hidden, *pieces)


def finish_rows_kernel(n, share, *refs):
    pieces, (ig_ref, out_ref) = refs[:n], refs[n:]
    m = lax.axis_index("mp")
    for r in range(n):
        start = pl.multiple_of(lax.rem(m + r, n) * share, 16)
        ig_ref[pl.ds(start, share), :] = pieces[r][:share, :].astype(F32)
        out_ref[pl.ds(start, share), :] = pieces[r][share:, :]


def finish_rows(pieces):
    n = len(pieces)
    share, width = pieces[0].shape[0] // 2, pieces[0].shape[1]
    return pl.pallas_call(
        functools.partial(finish_rows_kernel, n, share),
        in_specs=[whole()] * n,
        out_specs=[whole()] * 2,
        out_shape=[
            jax.ShapeDtypeStruct((n * share, width), F32),
            jax.ShapeDtypeStruct((n * share, width), BF),
        ],
        compiler_params=params(),
        cost_estimate=cost(n * share * width, 6 * n * share * width),
        name="finish_rows",
    )(*pieces)


def ordered_sum_kernel(n, axis, step, *refs):
    pieces, (out_ref, scr) = refs[:n], refs[n:]
    me = lax.axis_index(axis)
    for r in range(n):
        who = lax.rem(me + r, n) if step == 0 else (me // step) ^ r
        scr[who] = pieces[r][...]
    total = scr[0]
    for r in range(1, n):
        total = total + scr[r]
    out_ref[...] = total


def ordered_sum(pieces, axis, step):
    n = len(pieces)
    shape = pieces[0].shape
    return pl.pallas_call(
        functools.partial(ordered_sum_kernel, n, axis, step),
        in_specs=[whole()] * n,
        out_specs=whole(),
        out_shape=jax.ShapeDtypeStruct(shape, F32),
        scratch_shapes=[pltpu.VMEM((n,) + shape, F32)],
        compiler_params=params(),
        cost_estimate=cost(n * pieces[0].size, 4 * n * pieces[0].size),
        name="ordered_sum",
    )(*pieces)


def halve_kernel(kept, sent, keep_ref, recv_ref, *out_refs):
    rows = recv_ref.shape[0] // keep_ref.shape[0]
    total = keep_ref[...].astype(F32) + recv_ref[...].astype(F32)
    for ref, which in zip(out_refs, (kept, sent)):
        for k, r in enumerate(which):
            ref[k] = total[r].astype(BF)


def halve(keep, recv, kept, sent):
    part = keep.shape[1:]
    return pl.pallas_call(
        functools.partial(halve_kernel, kept, sent),
        in_specs=[whole()] * 2,
        out_specs=[whole()] * 2,
        out_shape=[jax.ShapeDtypeStruct((len(w),) + part, BF) for w in (kept, sent)],
        compiler_params=params(),
        cost_estimate=cost(keep.size, 8 * keep.size),
        name="halve",
    )(keep, recv)


def pack_kernel(n, share, extra, *refs):
    pieces, rest = refs[:n], refs[n:]
    m = lax.axis_index("mp")
    out_refs = rest[1:] if extra else rest
    for r in range(n):
        start = pl.multiple_of(lax.rem(m + r, n) * share, 16)
        for ref in out_refs:
            ref[pl.ds(start, share), :] = pieces[r][...]
    if extra:
        rows = rest[0].shape[1]
        for k in range(rest[0].shape[0]):
            at = n * share + k * rows
            out_refs[1][at : at + rows, :] = rest[0][k]


def pack_rows(pieces, extra=None):
    n = len(pieces)
    share, width = pieces[0].shape
    shapes = [(n * share, width)]
    if extra is not None:
        shapes.append((n * share + extra.shape[0] * extra.shape[1], width))
    args = list(pieces) + ([] if extra is None else [extra])
    return pl.pallas_call(
        functools.partial(pack_kernel, n, share, extra is not None),
        in_specs=[whole()] * len(args),
        out_specs=[whole()] * len(shapes),
        out_shape=[jax.ShapeDtypeStruct(shape, BF) for shape in shapes],
        compiler_params=params(),
        cost_estimate=cost(n * share * width, 6 * n * share * width),
        name="pack_rows",
    )(*args)


def turn_kernel(keep_ref, x_ref, y_ref, keep_out, to_y, to_x):
    length = y_ref.shape[0]
    half, rows = length // 2, keep_ref.shape[1]
    keep_out[...] = keep_ref[0].astype(F32) + x_ref[length : length + rows, :].astype(F32)
    sent = keep_ref[1].astype(F32) + x_ref[length + rows :, :].astype(F32)
    to_y[:half, :] = x_ref[:half, :]
    to_y[half:, :] = sent.astype(BF)
    to_x[...] = y_ref[half:, :]


def turn(keep, over_x, over_y):
    length, width = over_y.shape
    rows = keep.shape[1]
    return pl.pallas_call(
        turn_kernel,
        in_specs=[whole()] * 3,
        out_specs=[whole()] * 3,
        out_shape=[
            jax.ShapeDtypeStruct((rows, width), F32),
            jax.ShapeDtypeStruct((length // 2 + rows, width), BF),
            jax.ShapeDtypeStruct((length // 2, width), BF),
        ],
        compiler_params=params(),
        cost_estimate=cost(over_x.size, 8 * over_x.size),
        name="turn",
    )(keep, over_x, over_y)


def last_sum_kernel(keep_ref, recv_ref, out_ref):
    at = recv_ref.shape[0] - keep_ref.shape[0]
    out_ref[...] = (keep_ref[...] + recv_ref[at:, :].astype(F32)).astype(BF)


def last_sum(keep, recv):
    return pl.pallas_call(
        last_sum_kernel,
        in_specs=[whole()] * 2,
        out_specs=whole(),
        out_shape=jax.ShapeDtypeStruct(keep.shape, BF),
        compiler_params=params(),
        cost_estimate=cost(keep.size, 8 * keep.size),
        name="last_sum",
    )(keep, recv)


def join_kernel(*refs):
    at = 0
    for ref in refs[:-1]:
        refs[-1][at : at + ref.shape[0], :] = ref[...]
        at += ref.shape[0]


def join_pieces(pieces):
    rows = sum(p.shape[0] for p in pieces)
    return pl.pallas_call(
        join_kernel,
        in_specs=[whole()] * len(pieces),
        out_specs=whole(),
        out_shape=jax.ShapeDtypeStruct((rows, pieces[0].shape[1]), pieces[0].dtype),
        compiler_params=params(),
        cost_estimate=cost(rows * pieces[0].shape[1], 4 * rows * pieces[0].shape[1]),
        name="join_pieces",
    )(*pieces)


def finish_kernel(chips, keep_ref, send_ref, recv_ref, stu_ref, ar_ref, *w_refs):
    own, half, width = keep_ref.shape
    d = lax.axis_index("dp")
    core = lax.rem(d, 2)
    groups, count = len(chips), len(w_refs)
    rows = width // (2 * groups) if groups else 0
    base = groups * count * rows
    for r in range(groups):
        chip = ((d // 2) ^ r) * 2
        for ref, which in ((send_ref, chip + core), (recv_ref, chip + 1 - core)):
            start = pl.multiple_of(which * rows, 16)
            for i, out in enumerate(w_refs):
                at = (chips[r] * count + i) * rows
                out[pl.ds(start, rows), :] = ref[at : at + rows, :].astype(F32)
    for k in range(own):
        at = base + k * half
        stu_ref[k] = keep_ref[k] + recv_ref[at : at + half, :].astype(F32)
    for i in range(ar_ref.shape[0]):
        at = base + own * half + i * width
        ar_ref[i] = send_ref[at : at + width, :].astype(F32) + recv_ref[
            at : at + width, :
        ].astype(F32)


def finish(keep, send, recv, order, chips):
    width = keep.shape[2]
    count = 3 if chips else 0
    return pl.pallas_call(
        functools.partial(finish_kernel, chips),
        in_specs=[whole()] * 3,
        out_specs=[whole()] * (2 + count),
        out_shape=[
            jax.ShapeDtypeStruct(keep.shape, F32),
            jax.ShapeDtypeStruct((order, width, width), F32),
        ]
        + [jax.ShapeDtypeStruct((width, width), F32)] * count,
        compiler_params=params(),
        cost_estimate=cost(keep.size, 10 * keep.size),
        name="finish",
    )(keep, send, recv)


def fetch_shifted(value, axis, n):
    return [value] + [
        lax.ppermute(value, axis, [(i, (i - r) % n) for i in range(n)]) for r in range(1, n)
    ]


def send_shifted(pieces, axis):
    n = len(pieces)
    return [pieces[0]] + [
        lax.ppermute(pieces[r], axis, [(i, (i + r) % n) for i in range(n)]) for r in range(1, n)
    ]


def swap(value, axis, n, bits):
    return lax.ppermute(value, axis, [(i, i ^ bits) for i in range(n)])


def merge_rows(value):
    return value.reshape(value.shape[0], -1, value.shape[-1])


def after(values, first):
    flat, tree = jax.tree.flatten(values)
    out = lax.optimization_barrier((*flat, *jax.tree.leaves(first)))
    return jax.tree.unflatten(tree, out[: len(flat)])


def shards(
    inputs, lengths, filters, first_gain, stu_weight, ar_weight, second_gain,
    gate_weight, up_weight, down_weight, cotangent,
):
    n = lax.axis_size("mp")
    n_dp = lax.axis_size("dp")
    groups = n_dp // 2
    length, width = inputs.shape
    share = length // n
    order = ar_weight.shape[0]
    own = stu_weight.shape[0] // n
    lengths = lengths.astype(jnp.int32)
    gain_one = first_gain.reshape(1, width)
    gain_two = second_gain.reshape(1, width)

    u, taps, natural, ut = first_norm(lengths, inputs, gain_one, filters.T, n)
    uts = [ut] + [swap(ut, "dp", n_dp, 2 * r) for r in range(1, 3)]
    hidden, nt = spectral_mix(lengths, taps, inputs, u, stu_weight, ar_weight, gain_two, share, 4)
    nts = fetch_shifted(nt, "mp", n)
    uts += [swap(after(ut, nt), "dp", n_dp, 2 * r) for r in range(3, groups)]
    weights = (cotangent, gate_weight, up_weight, down_weight)
    parts = [feed_forward(0, n, nts[0], *weights)]
    nts = [nts[0]] + after(after(nts[1:], parts[0][0]), uts[1:3])
    parts += [feed_forward(r, n, nts[r], *weights) for r in range(1, n)]
    bns = send_shifted([p[0] for p in parts], "mp")
    acts, bgs, bus = ([p[i] for p in parts] for i in (1, 2, 3))
    custom = n_dp == 8 and gate_weight.shape[1] == width
    grads = ffn_grads(cotangent, down_weight, nts, acts, bgs, bus, groups if custom else 0)
    out_parts, grads = grads[:n], grads[n:]
    bns = [bns[0]] + after(bns[1:], grads[0])
    back_hidden, back_rows, second_part = mid_norm(lengths, hidden, cotangent, gain_two, bns)
    backs = fetch_shifted(back_rows, "mp", n)
    uts = after(uts, back_rows)
    conv = [convolutions(natural, uts[r : r + 4], own, groups) for r in range(0, groups, 4)]
    backs = after(backs, conv)
    if custom:
        w_keep, w_send = grads
        w_send = swap(after(w_send, back_rows), "dp", n_dp, 1)
        w_keep, w_send = halve(w_keep, w_send, (0, 2), (1, 3))
        own_back, to_x = pack_rows(backs, merge_rows(w_send))
        over_x, over_y = swap(to_x, "dp", n_dp, 2), swap(own_back, "dp", n_dp, 4)
    else:
        (own_back,) = pack_rows(backs)
    out_sums = send_shifted(after(out_parts, own_back), "mp")
    ig, gains = spectral_unmix(
        lengths, taps, inputs, back_hidden, second_part, gain_one, stu_weight, ar_weight, backs, 4
    )
    conv, hidden = after((conv, hidden), ig)
    message = rows_message(ig, hidden, out_sums)
    messages = fetch_shifted(message, "mp", n)
    if custom:
        w_keep, to_y, to_x = turn(merge_rows(w_keep), after(over_x, message), over_y)
        from_y, from_x = swap(to_y, "dp", n_dp, 4), swap(to_x, "dp", n_dp, 2)
        all_backs = [own_back, over_x, over_y, from_y, from_x]
        half = length // 2
        rows = ((0, 0, length), (1, 0, length), (2, 0, length), (3, 0, half), (3, half, half))
        w_sum = last_sum(w_keep, from_y)
        conv = after(conv, w_sum)
    else:
        all_backs = [own_back] + [swap(own_back, "dp", n_dp, 2 * r) for r in range(1, groups)]
        rows = tuple((r, 0, length) for r in range(min(groups, 4)))

    gains = after(gains, all_backs[-1])
    gains = ordered_sum(fetch_shifted(gains, "mp", n), "mp", 0)
    gains = ordered_sum([gains, swap(gains, "dp", n_dp, 1)], "dp", 0)
    gains = [gains] + [swap(gains, "dp", n_dp, 2 * r) for r in range(1, groups)]
    gains = ordered_sum(gains, "dp", 2)

    conv = after(conv, (message, messages[n // 2]))
    if len(conv) == 1:
        keep, send = matrix_grads(conv[0], uts, all_backs, rows, order)
    else:
        some = [
            matrix_grads(c, uts[4 * k : 4 * k + 4], all_backs[4 * k : 4 * k + 4], rows, order)
            for k, c in enumerate(conv)
        ]
        keep = ordered_sum([k for k, _ in some], "dp", 8)
        send = ordered_sum([k.astype(F32) for _, k in some], "dp", 8).astype(BF)
    input_grad, output = finish_rows(after(messages, (gains, send)))
    if custom:
        w_pair = join_pieces([w_sum, swap(w_sum, "dp", n_dp, 4)])
        w_all = [w_pair, swap(w_pair, "dp", n_dp, 2)]
        send = join_pieces(after([*w_all, send], output))
    recv = swap(after(send, output), "dp", n_dp, 1)
    stu_grad, ar_grad, *w_grads = finish(keep, send, recv, order, (0, 2, 1, 3) if custom else ())
    if custom:
        gate_grad, up_grad, down_grad = w_grads
    else:
        gate_grad, up_grad, down_grad = (g.astype(F32) for g in lax.psum(tuple(grads), "dp"))
    return (
        output, input_grad, stu_grad, ar_grad, gains[0], gains[8], gate_grad, up_grad, down_grad,
    )


def solution(mesh):
    in_specs = (
        P("dp", None), P("dp"), P(), P(), P(), P(), P(),
        P(None, "mp"), P(None, "mp"), P("mp", None), P("dp", None),
    )
    out_specs = (
        P("dp", None), P("dp", None), P("mp", "dp", None), P(), P(), P(),
        P(None, "mp"), P(None, "mp"), P("mp", None),
    )
    return jax.shard_map(shards, mesh=mesh, in_specs=in_specs, out_specs=out_specs, check_vma=False)
```

profile of v0, /device:TPU:0, one launch (start us, length us, event | category | flops | bytes accessed | tf_op | source)
XLA Modules:
  0.0 179.8 jit_solution(10643277507844061583)
XLA Ops:
  5.0 3.0 %collective-permute-start.3 = (bf16[512,768]{1,0:T(8,128)(2,1)S(1)}, bf16[512,768]{1,0:T(8,128)(2,1)S(1)}, u32[]{:S(2)}, u32[]{:S(2)}) collective-permute-start(bf16[512,768]{1,0:T(8,128)(2,1)S(1)} %get-tuple-element.131.refs_0_), channel_id=1, source_target_pairs={{0,8},{4,12},{8,0},{12,4},{16,24},{20,28},{24,16},{28,20},{1,9},{5... | collective-permute-start | bytes 2359304 | tf_op jit(solution)/shard_map/ppermute | solution.py:856
  12.7 16.2 %spectral_mix.1 = (f32[192,512]{1,0:T(8,128)S(1)}, bf16[192,512]{1,0:T(8,128)(2,1)S(1)}) custom-call(s32[1]{0:T(128)S(6)} %copy.20.len_ref, f32[6,24,384]{2,1,0:T(8,128)S(1)} %get-tuple-element.95.taps_ref, bf16[768,512]{1,0:T(8,128)(2,1)S(1)} %copy-done.5, bf16[2,384,512]{2,1,0:T(8,128)(2,1)S(1)} %get-tuple-element.96.u_ref, bf16[48,512,512]{2,1,0:T(8,128)(2,1)} %wm_ref.3, ...), custom_call_target="tpu_custom_call" | custom-call | flops 8455716864 | bytes 25165824 | tf_op jit(solution)/shard_map/spectral_mix/pallas_call | solution.py:213
  29.0 3.7 %collective-permute-start = (bf16[192,512]{1,0:T(8,128)(2,1)S(1)}, bf16[192,512]{1,0:T(8,128)(2,1)S(1)}, u32[]{:S(2)}, u32[]{:S(2)}) collective-permute-start(bf16[192,512]{1,0:T(8,128)(2,1)S(1)} %get-tuple-element.98.nt_ref.refs_0_), channel_id=1, source_target_pairs={{0,3},{1,0},{2,1},{3,2},{4,7},{5,4},{6,5},{7,6},{8,11},{9,8},{10,9... | collective-permute-start | bytes 589832 | tf_op jit(solution)/shard_map/ppermute | solution.py:844
  33.6 4.4 %collective-permute-done.nt_ref.refs_1_ = bf16[192,512]{1,0:T(8,128)(2,1)S(1)} collective-permute-done((bf16[192,512]{1,0:T(8,128)(2,1)S(1)}, bf16[192,512]{1,0:T(8,128)(2,1)S(1)}, u32[]{:S(2)}, u32[]{:S(2)}) %collective-permute-start) | collective-permute-done | bytes 196640 | tf_op jit(solution)/shard_map/ppermute | solution.py:844
  39.6 9.2 %collective-permute-done.1.nt_ref.refs_2_ = bf16[192,512]{1,0:T(8,128)(2,1)S(1)} collective-permute-done((bf16[192,512]{1,0:T(8,128)(2,1)S(1)}, bf16[192,512]{1,0:T(8,128)(2,1)S(1)}, u32[]{:S(2)}, u32[]{:S(2)}) %collective-permute-start.1) | collective-permute-done | bytes 196640 | tf_op jit(solution)/shard_map/ppermute | solution.py:844
  52.9 2.0 %collective-permute-start.6 = (bf16[192,512]{1,0:T(8,128)(2,1)S(1)}, bf16[192,512]{1,0:T(8,128)(2,1)S(1)}, u32[]{:S(2)}, u32[]{:S(2)}) collective-permute-start(bf16[192,512]{1,0:T(8,128)(2,1)S(1)} %get-tuple-element.107), channel_id=1, source_target_pairs={{0,2},{1,3},{2,0},{3,1},{4,6},{5,7},{6,4},{7,5},{8,10},{9,11},{10,... | collective-permute-start | bytes 589832 | tf_op jit(solution)/shard_map/ppermute | solution.py:851
  54.9 2.9 %collective-permute-start.7 = (bf16[192,512]{1,0:T(8,128)(2,1)S(1)}, bf16[192,512]{1,0:T(8,128)(2,1)S(1)}, u32[]{:S(2)}, u32[]{:S(2)}) collective-permute-start(bf16[192,512]{1,0:T(8,128)(2,1)S(1)} %get-tuple-element.109), channel_id=1, source_target_pairs={{0,3},{1,0},{2,1},{3,2},{4,7},{5,4},{6,5},{7,6},{8,11},{9,8},{10,9... | collective-permute-start | bytes 589832 | tf_op jit(solution)/shard_map/ppermute | solution.py:851
  57.8 1.9 %ffn_grads.1 = (bf16[192,512]{1,0:T(8,128)(2,1)S(1)}, bf16[192,512]{1,0:T(8,128)(2,1)S(1)}, bf16[192,512]{1,0:T(8,128)(2,1)S(1)}, bf16[192,512]{1,0:T(8,128)(2,1...) custom-call(bf16[768,512]{1,0:T(8,128)(2,1)S(1)} %copy-done, ...), custom_call_target="tpu_custom_call" | custom-call | flops 1610612736 | bytes 4718592 | tf_op jit(solution)/shard_map/ffn_grads/pallas_call | solution.py:330
  59.7 6.5 %collective-permute-done.6.refs_2_ = bf16[192,512]{1,0:T(8,128)(2,1)S(1)} collective-permute-done((bf16[192,512]{1,0:T(8,128)(2,1)S(1)}, bf16[192,512]{1,0:T(8,128)(2,1)S(1)}, u32[]{:S(2)}, u32[]{:S(2)}) %collective-permute-start.6) | collective-permute-done | bytes 196640 | tf_op jit(solution)/shard_map/ppermute | solution.py:851
  66.6 4.7 %collective-permute-start.10 = (bf16[192,512]{1,0:T(8,128)(2,1)S(1)}, bf16[192,512]{1,0:T(8,128)(2,1)S(1)}, u32[]{:S(2)}, u32[]{:S(2)}) collective-permute-start(bf16[192,512]{1,0:T(8,128)(2,1)S(1)} %get-tuple-element.135.refs_0_), channel_id=1, source_target_pairs={{0,1},{1,2},{2,3},{3,0},{4,5},{5,6},{6,7},{7,4},{8,9},{9,10},{10,1... | collective-permute-start | bytes 589832 | tf_op jit(solution)/shard_map/ppermute | solution.py:844
  73.2 9.9 %convolutions.1.conv_ref = bf16[12,128,3072]{2,1,0:T(8,128)(2,1)S(1)} custom-call(f32[24,768]{1,0:T(8,128)S(1)} %get-tuple-element.129.filt_ref, bf16[512,768]{1,0:T(8,128)(2,1)S(1)} %get-tuple-element.131.refs_0_, bf16[512,768]{1,0:T(8,128)(2,1)S(1)} %collective-permute-done.3.refs_1_, bf16[512,768]{1,0:T(8,128)(2,1)S(1)} %collective-permute-done.4.refs_2_, ...), custom_call_target="tpu_custom_call" | custom-call | flops 4831838208 | bytes 9437184 | tf_op jit(solution)/shard_map/convolutions/pallas_call | solution.py:521
  83.2 7.6 %collective-permute-done.9.refs_2_ = bf16[192,512]{1,0:T(8,128)(2,1)S(1)} collective-permute-done((bf16[192,512]{1,0:T(8,128)(2,1)S(1)}, bf16[192,512]{1,0:T(8,128)(2,1)S(1)}, u32[]{:S(2)}, u32[]{:S(2)}) %collective-permute-start.9) | collective-permute-done | bytes 196640 | tf_op jit(solution)/shard_map/ppermute | solution.py:844
  92.3 1.6 collective-permute-start.14
  93.9 2.2 %collective-permute-start.15 = (bf16[192,512]{1,0:T(8,128)(2,1)S(1)}, bf16[192,512]{1,0:T(8,128)(2,1)S(1)}, u32[]{:S(2)}, u32[]{:S(2)}) collective-permute-start(bf16[192,512]{1,0:T(8,128)(2,1)S(1)} %get-tuple-element.152), channel_id=1, source_target_pairs={{0,3},{1,0},{2,1},{3,2},{4,7},{5,4},{6,5},{7,6},{8,11},{9,8},{10,9... | collective-permute-start | bytes 589832 | tf_op jit(solution)/shard_map/ppermute | solution.py:851
  96.1 19.1 %spectral_unmix.1 = (bf16[192,512]{1,0:T(8,128)(2,1)S(1)}, f32[16,512]{1,0:T(8,128)S(1)}) custom-call(s32[1]{0:T(128)S(6)} %copy.20.len_ref, f32[6,24,384]{2,1,0:T(8,128)S(1)} %get-tuple-element.95.taps_ref, bf16[768,512]{1,0:T(8,128)(2,1)S(1)} %copy-done.5, f32[192,512]{1,0:T(8,128)S(1)} %get-tuple-element.126.bh_ref, ...), custom_call_target="tpu_custom_call" | custom-call | flops 8455716864 | bytes 25165824 | tf_op jit(solution)/shard_map/spectral_unmix/pallas_call | solution.py:460
  115.3 3.8 %collective-permute-done.19.x_ref.refs_5_ = bf16[1152,512]{1,0:T(8,128)(2,1)S(1)} collective-permute-done((bf16[1152,512]{1,0:T(8,128)(2,1)S(1)}, bf16[1152,512]{1,0:T(8,128)(2,1)S(1)}, u32[]{:S(2)}, u32[]{:S(2)}) %collective-permute-start.19) | collective-permute-done | bytes 1179680 | tf_op jit(solution)/shard_map/ppermute | solution.py:856
  120.6 13.2 %collective-permute-done.29.recv_ref.refs_7_ = bf16[576,512]{1,0:T(8,128)(2,1)S(1)} collective-permute-done((bf16[576,512]{1,0:T(8,128)(2,1)S(1)}, bf16[576,512]{1,0:T(8,128)(2,1)S(1)}, u32[]{:S(2)}, u32[]{:S(2)}) %collective-permute-start.29) | collective-permute-done | bytes 589856 | tf_op jit(solution)/shard_map/ppermute | solution.py:856
  136.5 2.1 %collective-permute-done.22.refs_1_ = f32[16,512]{1,0:T(8,128)S(1)} collective-permute-done((f32[16,512]{1,0:T(8,128)S(1)}, f32[16,512]{1,0:T(8,128)S(1)}, u32[]{:S(2)}, u32[]{:S(2)}) %collective-permute-start.22) | collective-permute-done | bytes 32800 | tf_op jit(solution)/shard_map/ppermute | solution.py:844
  143.1 1.5 collective-permute-start.27
  146.4 1.8 %collective-permute-start.16 = (bf16[384,512]{1,0:T(8,128)(2,1)S(1)}, bf16[384,512]{1,0:T(8,128)(2,1)S(1)}, u32[]{:S(2)}, u32[]{:S(2)}) collective-permute-start(bf16[384,512]{1,0:T(8,128)(2,1)S(1)} %rows_message.1.refs_0_), channel_id=1, source_target_pairs={{0,3},{1,0},{2,1},{3,2},{4,7},{5,4},{6,5},{7,6},{8,11},{9,8},{10,9... | collective-permute-start | bytes 1179656 | tf_op jit(solution)/shard_map/ppermute | solution.py:844
  150.9 17.6 %matrix_grads.1 = (f32[12,64,512]{2,1,0:T(8,128)S(1)}, bf16[2304,512]{1,0:T(8,128)(2,1)S(1)}) custom-call(bf16[12,128,3072]{2,1,0:T(8,128)(2,1)S(1)} %convolutions.1.conv_ref, bf16[512,768]{1,0:T(8,128)(2,1)S(1)} %get-tuple-element.131.refs_0_, bf16[512,768]{1,0:T(8,128)(2,1)S(1)} %collective-permute-done.3.refs_1_, ...), custom_call_target="tpu_custom_call" | custom-call | flops 9663676416 | bytes 9437184 | tf_op jit(solution)/shard_map/matrix_grads/pallas_call | solution.py:585
  168.6 1.6 finish_rows.1
  171.0 5.1 %collective-permute-done.32.recv_ref = bf16[3072,512]{1,0:T(8,128)(2,1)S(1)} collective-permute-done((bf16[3072,512]{1,0:T(8,128)(2,1)S(1)}, bf16[3072,512]{1,0:T(8,128)(2,1)S(1)}, u32[]{:S(2)}, u32[]{:S(2)}) %collective-permute-start.32) | collective-permute-done | bytes 3145760 | tf_op jit(solution)/shard_map/ppermute | solution.py:856
  176.1 3.7 %finish.1 = (f32[12,64,512]{2,1,0:T(8,128)}, f32[3,512,512]{2,1,0:T(8,128)}, f32[512,512]{1,0:T(8,128)}, f32[512,512]{1,0:T(8,128)}, f32[512,512]{1,0:T(8,128)}) custom-call(f32[12,64,512]{2,1,0:T(8,128)S(1)} %get-tuple-element.171.keep_ref, bf16[3072,512]{1,0:T(8,128)(2,1)S(1)} %join_pieces.3.send_ref, bf16[3072,512]{1,0:T(8,128)(2,1)S(1)} %collective-permute-done.32.recv_ref), custom_call_target="tpu_custom_call" | custom-call | flops 393216 | bytes 3932160 | tf_op jit(solution)/shard_map/finish/pallas_call | solution.py:827
  (90 shorter events, 32.9 us)
Async XLA Ops:
  5.0 43.8 %collective-permute-start.3 = (bf16[512,768]{1,0:T(8,128)(2,1)S(1)}, bf16[512,768]{1,0:T(8,128)(2,1)S(1)}, u32[]{:S(2)}, u32[]{:S(2)}) collective-permute-start(bf16[512,768]{1,0:T(8,128)(2,1)S(1)} %get-tuple-element.131.refs_0_), channel_id=1, source_target_pairs={{0,8},{4,12},{8,0},{12,4},{16,24},{20,28},{24,16},{28,20},{1,9},{5... | collective-permute-start | bytes 2359304 | tf_op jit(solution)/shard_map/ppermute | solution.py:856
  8.0 40.8 %collective-permute-start.4 = (bf16[512,768]{1,0:T(8,128)(2,1)S(1)}, bf16[512,768]{1,0:T(8,128)(2,1)S(1)}, u32[]{:S(2)}, u32[]{:S(2)}) collective-permute-start(bf16[512,768]{1,0:T(8,128)(2,1)S(1)} %get-tuple-element.131.refs_0_), channel_id=1, source_target_pairs={{0,16},{4,20},{8,24},{12,28},{16,0},{20,4},{24,8},{28,12},{1,17},{... | collective-permute-start | bytes 2359304 | tf_op jit(solution)/shard_map/ppermute | solution.py:856
  32.6 16.1 %collective-permute-start.1 = (bf16[192,512]{1,0:T(8,128)(2,1)S(1)}, bf16[192,512]{1,0:T(8,128)(2,1)S(1)}, u32[]{:S(2)}, u32[]{:S(2)}) collective-permute-start(bf16[192,512]{1,0:T(8,128)(2,1)S(1)} %get-tuple-element.98.nt_ref.refs_0_), channel_id=1, source_target_pairs={{0,2},{1,3},{2,0},{3,1},{4,6},{5,7},{6,4},{7,5},{8,10},{9,11},{10,... | collective-permute-start | bytes 589832 | tf_op jit(solution)/shard_map/ppermute | solution.py:844
  32.6 16.1 %collective-permute-start.2 = (bf16[192,512]{1,0:T(8,128)(2,1)S(1)}, bf16[192,512]{1,0:T(8,128)(2,1)S(1)}, u32[]{:S(2)}, u32[]{:S(2)}) collective-permute-start(bf16[192,512]{1,0:T(8,128)(2,1)S(1)} %get-tuple-element.98.nt_ref.refs_0_), channel_id=1, source_target_pairs={{0,1},{1,2},{2,3},{3,0},{4,5},{5,6},{6,7},{7,4},{8,9},{9,10},{10,1... | collective-permute-start | bytes 589832 | tf_op jit(solution)/shard_map/ppermute | solution.py:844
  38.0 35.2 %collective-permute-start.11 = (bf16[512,768]{1,0:T(8,128)(2,1)S(1)}, bf16[512,768]{1,0:T(8,128)(2,1)S(1)}, u32[]{:S(2)}, u32[]{:S(2)}) collective-permute-start(bf16[512,768]{1,0:T(8,128)(2,1)S(1)} %get-tuple-element.131.refs_0_), channel_id=1, source_target_pairs={{0,24},{4,28},{8,16},{12,20},{16,8},{20,12},{24,0},{28,4},{1,25},{... | collective-permute-start | bytes 2359304 | tf_op jit(solution)/shard_map/ppermute | solution.py:856
  49.8 9.9 %collective-permute-start.5 = (bf16[192,512]{1,0:T(8,128)(2,1)S(1)}, bf16[192,512]{1,0:T(8,128)(2,1)S(1)}, u32[]{:S(2)}, u32[]{:S(2)}) collective-permute-start(bf16[192,512]{1,0:T(8,128)(2,1)S(1)} %get-tuple-element.105), channel_id=1, source_target_pairs={{0,1},{1,2},{2,3},{3,0},{4,5},{5,6},{6,7},{7,4},{8,9},{9,10},{10,1... | collective-permute-start | bytes 589832 | tf_op jit(solution)/shard_map/ppermute | solution.py:851
  52.9 13.3 %collective-permute-start.6 = (bf16[192,512]{1,0:T(8,128)(2,1)S(1)}, bf16[192,512]{1,0:T(8,128)(2,1)S(1)}, u32[]{:S(2)}, u32[]{:S(2)}) collective-permute-start(bf16[192,512]{1,0:T(8,128)(2,1)S(1)} %get-tuple-element.107), channel_id=1, source_target_pairs={{0,2},{1,3},{2,0},{3,1},{4,6},{5,7},{6,4},{7,5},{8,10},{9,11},{10,... | collective-permute-start | bytes 589832 | tf_op jit(solution)/shard_map/ppermute | solution.py:851
  54.9 11.3 %collective-permute-start.7 = (bf16[192,512]{1,0:T(8,128)(2,1)S(1)}, bf16[192,512]{1,0:T(8,128)(2,1)S(1)}, u32[]{:S(2)}, u32[]{:S(2)}) collective-permute-start(bf16[192,512]{1,0:T(8,128)(2,1)S(1)} %get-tuple-element.109), channel_id=1, source_target_pairs={{0,3},{1,0},{2,1},{3,2},{4,7},{5,4},{6,5},{7,6},{8,11},{9,8},{10,9... | collective-permute-start | bytes 589832 | tf_op jit(solution)/shard_map/ppermute | solution.py:851
  66.5 24.3 %collective-permute-start.12 = (bf16[4,3,64,512]{3,2,1,0:T(8,128)(2,1)S(1)}, bf16[4,3,64,512]{3,2,1,0:T(8,128)(2,1)S(1)}, u32[]{:S(2)}, u32[]{:S(2)}) collective-permute-start(bf16[4,3,64,512]{3,2,1,0:T(8,128)(2,1)S(1)} %get-tuple-element.146), channel_id=1, source_target_pairs={{0,4},{4,0},{8,12},{12,8},{16,20},{20,16},{24,28},{28,24},{1,5},{5... | collective-permute-start | bytes 2359304 | tf_op jit(solution)/shard_map/ppermute | solution.py:856
  66.6 16.6 %collective-permute-start.10 = (bf16[192,512]{1,0:T(8,128)(2,1)S(1)}, bf16[192,512]{1,0:T(8,128)(2,1)S(1)}, u32[]{:S(2)}, u32[]{:S(2)}) collective-permute-start(bf16[192,512]{1,0:T(8,128)(2,1)S(1)} %get-tuple-element.135.refs_0_), channel_id=1, source_target_pairs={{0,1},{1,2},{2,3},{3,0},{4,5},{5,6},{6,7},{7,4},{8,9},{9,10},{10,1... | collective-permute-start | bytes 589832 | tf_op jit(solution)/shard_map/ppermute | solution.py:844
  71.3 11.8 %collective-permute-start.8 = (bf16[192,512]{1,0:T(8,128)(2,1)S(1)}, bf16[192,512]{1,0:T(8,128)(2,1)S(1)}, u32[]{:S(2)}, u32[]{:S(2)}) collective-permute-start(bf16[192,512]{1,0:T(8,128)(2,1)S(1)} %get-tuple-element.135.refs_0_), channel_id=1, source_target_pairs={{0,3},{1,0},{2,1},{3,2},{4,7},{5,4},{6,5},{7,6},{8,11},{9,8},{10,9... | collective-permute-start | bytes 589832 | tf_op jit(solution)/shard_map/ppermute | solution.py:844
  72.8 18.1 %collective-permute-start.9 = (bf16[192,512]{1,0:T(8,128)(2,1)S(1)}, bf16[192,512]{1,0:T(8,128)(2,1)S(1)}, u32[]{:S(2)}, u32[]{:S(2)}) collective-permute-start(bf16[192,512]{1,0:T(8,128)(2,1)S(1)} %get-tuple-element.135.refs_0_), channel_id=1, source_target_pairs={{0,2},{1,3},{2,0},{3,1},{4,6},{5,7},{6,4},{7,5},{8,10},{9,11},{10,... | collective-permute-start | bytes 589832 | tf_op jit(solution)/shard_map/ppermute | solution.py:844
  91.2 28.0 %collective-permute-start.19 = (bf16[1152,512]{1,0:T(8,128)(2,1)S(1)}, bf16[1152,512]{1,0:T(8,128)(2,1)S(1)}, u32[]{:S(2)}, u32[]{:S(2)}) collective-permute-start(bf16[1152,512]{1,0:T(8,128)(2,1)S(1)} %get-tuple-element.155), channel_id=1, source_target_pairs={{0,8},{4,12},{8,0},{12,4},{16,24},{20,28},{24,16},{28,20},{1,9},{5... | collective-permute-start | bytes 3538952 | tf_op jit(solution)/shard_map/ppermute | solution.py:856
  91.8 27.4 %collective-permute-start.20 = (bf16[768,512]{1,0:T(8,128)(2,1)S(1)}, bf16[768,512]{1,0:T(8,128)(2,1)S(1)}, u32[]{:S(2)}, u32[]{:S(2)}) collective-permute-start(bf16[768,512]{1,0:T(8,128)(2,1)S(1)} %get-tuple-element.148.refs_4_), channel_id=1, source_target_pairs={{0,16},{4,20},{8,24},{12,28},{16,0},{20,4},{24,8},{28,12},{1,17},{... | collective-permute-start | bytes 2359304 | tf_op jit(solution)/shard_map/ppermute | solution.py:856
  92.3 22.9 %collective-permute-start.13 = (bf16[192,512]{1,0:T(8,128)(2,1)S(1)}, bf16[192,512]{1,0:T(8,128)(2,1)S(1)}, u32[]{:S(2)}, u32[]{:S(2)}) collective-permute-start(bf16[192,512]{1,0:T(8,128)(2,1)S(1)} %get-tuple-element.150), channel_id=1, source_target_pairs={{0,1},{1,2},{2,3},{3,0},{4,5},{5,6},{6,7},{7,4},{8,9},{9,10},{10,1... | collective-permute-start | bytes 589832 | tf_op jit(solution)/shard_map/ppermute | solution.py:851
  92.3 22.9 %collective-permute-start.14 = (bf16[192,512]{1,0:T(8,128)(2,1)S(1)}, bf16[192,512]{1,0:T(8,128)(2,1)S(1)}, u32[]{:S(2)}, u32[]{:S(2)}) collective-permute-start(bf16[192,512]{1,0:T(8,128)(2,1)S(1)} %get-tuple-element.151), channel_id=1, source_target_pairs={{0,2},{1,3},{2,0},{3,1},{4,6},{5,7},{6,4},{7,5},{8,10},{9,11},{10,... | collective-permute-start | bytes 589832 | tf_op jit(solution)/shard_map/ppermute | solution.py:851
  93.9 21.3 %collective-permute-start.15 = (bf16[192,512]{1,0:T(8,128)(2,1)S(1)}, bf16[192,512]{1,0:T(8,128)(2,1)S(1)}, u32[]{:S(2)}, u32[]{:S(2)}) collective-permute-start(bf16[192,512]{1,0:T(8,128)(2,1)S(1)} %get-tuple-element.152), channel_id=1, source_target_pairs={{0,3},{1,0},{2,1},{3,2},{4,7},{5,4},{6,5},{7,6},{8,11},{9,8},{10,9... | collective-permute-start | bytes 589832 | tf_op jit(solution)/shard_map/ppermute | solution.py:851
  119.3 14.5 %collective-permute-start.29 = (bf16[576,512]{1,0:T(8,128)(2,1)S(1)}, bf16[576,512]{1,0:T(8,128)(2,1)S(1)}, u32[]{:S(2)}, u32[]{:S(2)}) collective-permute-start(bf16[576,512]{1,0:T(8,128)(2,1)S(1)} %get-tuple-element.161), channel_id=1, source_target_pairs={{0,16},{4,20},{8,24},{12,28},{16,0},{20,4},{24,8},{28,12},{1,17},{... | collective-permute-start | bytes 1769480 | tf_op jit(solution)/shard_map/ppermute | solution.py:856
  119.9 14.6 %collective-permute-start.21 = (bf16[384,512]{1,0:T(8,128)(2,1)S(1)}, bf16[384,512]{1,0:T(8,128)(2,1)S(1)}, u32[]{:S(2)}, u32[]{:S(2)}) collective-permute-start(bf16[384,512]{1,0:T(8,128)(2,1)S(1)} %get-tuple-element.157), channel_id=1, source_target_pairs={{0,8},{4,12},{8,0},{12,4},{16,24},{20,28},{24,16},{28,20},{1,9},{5... | collective-permute-start | bytes 1179656 | tf_op jit(solution)/shard_map/ppermute | solution.py:856
  120.4 29.1 %collective-permute-start.17 = (bf16[384,512]{1,0:T(8,128)(2,1)S(1)}, bf16[384,512]{1,0:T(8,128)(2,1)S(1)}, u32[]{:S(2)}, u32[]{:S(2)}) collective-permute-start(bf16[384,512]{1,0:T(8,128)(2,1)S(1)} %rows_message.1.refs_0_), channel_id=1, source_target_pairs={{0,2},{1,3},{2,0},{3,1},{4,6},{5,7},{6,4},{7,5},{8,10},{9,11},{10,... | collective-permute-start | bytes 1179656 | tf_op jit(solution)/shard_map/ppermute | solution.py:844
  133.8 15.7 %collective-permute-start.30 = (bf16[192,512]{1,0:T(8,128)(2,1)S(1)}, bf16[192,512]{1,0:T(8,128)(2,1)S(1)}, u32[]{:S(2)}, u32[]{:S(2)}) collective-permute-start(bf16[192,512]{1,0:T(8,128)(2,1)S(1)} %last_sum.1.refs_0_), channel_id=1, source_target_pairs={{0,16},{4,20},{8,24},{12,28},{16,0},{20,4},{24,8},{28,12},{1,17},{... | collective-permute-start | bytes 589832 | tf_op jit(solution)/shard_map/ppermute | solution.py:856
  146.4 22.2 %collective-permute-start.16 = (bf16[384,512]{1,0:T(8,128)(2,1)S(1)}, bf16[384,512]{1,0:T(8,128)(2,1)S(1)}, u32[]{:S(2)}, u32[]{:S(2)}) collective-permute-start(bf16[384,512]{1,0:T(8,128)(2,1)S(1)} %rows_message.1.refs_0_), channel_id=1, source_target_pairs={{0,3},{1,0},{2,1},{3,2},{4,7},{5,4},{6,5},{7,6},{8,11},{9,8},{10,9... | collective-permute-start | bytes 1179656 | tf_op jit(solution)/shard_map/ppermute | solution.py:844
  148.2 20.4 %collective-permute-start.18 = (bf16[384,512]{1,0:T(8,128)(2,1)S(1)}, bf16[384,512]{1,0:T(8,128)(2,1)S(1)}, u32[]{:S(2)}, u32[]{:S(2)}) collective-permute-start(bf16[384,512]{1,0:T(8,128)(2,1)S(1)} %rows_message.1.refs_0_), channel_id=1, source_target_pairs={{0,1},{1,2},{2,3},{3,0},{4,5},{5,6},{6,7},{7,4},{8,9},{9,10},{10,1... | collective-permute-start | bytes 1179656 | tf_op jit(solution)/shard_map/ppermute | solution.py:844
  149.6 20.6 %collective-permute-start.31 = (bf16[384,512]{1,0:T(8,128)(2,1)S(1)}, bf16[384,512]{1,0:T(8,128)(2,1)S(1)}, u32[]{:S(2)}, u32[]{:S(2)}) collective-permute-start(bf16[384,512]{1,0:T(8,128)(2,1)S(1)} %join_pieces.2.refs_0_), channel_id=1, source_target_pairs={{0,8},{4,12},{8,0},{12,4},{16,24},{20,28},{24,16},{28,20},{1,9},{5... | collective-permute-start | bytes 1179656 | tf_op jit(solution)/shard_map/ppermute | solution.py:856
  (21 other events, 179.7 us)
where the time goes:
time: 180 us
  Pallas kernels  76.5 us (42%)
  waiting for transfers between devices  57.2 us (32%)
  starting transfers between devices  38.2 us (21%)
  local copies, waits for them, and re-layouts  6.41 us (4%)
    ppermute x12, waiting for transfers between devices, fetch_shifted(): lax.ppermute(value, axis, [(i, (i - r) % n) for i in range(n)])  25.8 us
    ppermute x15, waiting for transfers between devices, swap(): return lax.ppermute(value, axis, [(i, i ^ bits) for i in range(n)])  24.8 us
    pallas_call x1, Pallas kernels, spectral_unmix(): pl.pallas_call(functools.partial(unmix_kernel, kb, share, n, ar.shape[0])...  19.1 us
    pallas_call x1, Pallas kernels, matrix_grads(): pl.pallas_call(functools.partial(grads_kernel, steps, order, groups, rows...  17.6 us
    pallas_call x1, Pallas kernels, spectral_mix(): pl.pallas_call(functools.partial(mix_kernel, kb, share, ar.shape[0]), gri...  16.2 us
    ppermute x12, starting transfers between devices, fetch_shifted(): lax.ppermute(value, axis, [(i, (i - r) % n) for i in range(n)])  15.5 us
    ppermute x15, starting transfers between devices, swap(): return lax.ppermute(value, axis, [(i, i ^ bits) for i in range(n)])  13 us
    pallas_call x1, Pallas kernels, convolutions(): pl.pallas_call(functools.partial(conv_kernel, groups, tile, own), grid=(o...  9.88 us
  transfers between devices with their start and end apart: 33, of which 13 were waited for; matrix products, arithmetic and copies ran while one was open for 0% of the time, Pallas kernels for 39%

commit v1 on v0

--- a/solution.py
+++ b/solution.py
@@ -12,7 +12,7 @@
 F32 = jnp.float32
 SQRT_2_PI = 0.7978845608028654
 CUBIC = 0.044715
-VMEM_LIMIT = 24 << 20
+VMEM_LIMIT = 20 << 20
 
 
 def dot(left, right):
@@ -44,10 +44,8 @@
     return pl.BlockSpec(memory_space=pltpu.VMEM)
 
 
-def lag_spec(ar, steps):
-    order, width = ar.shape[:2]
-    assert order <= steps
-    return pl.BlockSpec((1, width, width), lambda j: (jnp.minimum(j, order - 1), 0, 0))
+def outside():
+    return pl.BlockSpec(memory_space=pltpu.HBM)
 
 
 def toeplitz(base_row, rows):
@@ -55,9 +53,9 @@
     return pltpu.roll(wide, 0, 1, stride=1, stride_axis=0)
 
 
-def put_columns(scr, value):
+def put_columns(scr, value, at=0):
     for c in range(scr.shape[0]):
-        scr[c] = value[:, c * 128 : (c + 1) * 128]
+        scr[c, at : at + value.shape[0], :] = value[:, c * 128 : (c + 1) * 128]
 
 
 def every_second(scr, start, count):
@@ -71,29 +69,61 @@
         columns = slice(c * 128, (c + 1) * 128)
         scr[c, pl.ds(0, half, stride=2), :] = value[:half, columns]
         scr[c, pl.ds(1, half, stride=2), :] = value[half:, columns]
-    return jnp.concatenate([scr[c] for c in range(scr.shape[0])], axis=1)
+    count = value.shape[0]
+    return jnp.concatenate([scr[c, :count, :] for c in range(scr.shape[0])], axis=1)
 
 
 def norm_kernel(
-    n, share, len_ref, x_ref, gain_ref, filt_ref, u_ref, taps_ref, nat_ref, ut_ref, scr, scr_f
+    n, share, order, len_ref, x_ref, gain_ref, u_ref, ut_ref, own_ref, lag_ref, scr
 ):
     length, width = x_ref.shape
-    half = length // 2
     m = lax.axis_index("mp")
     x = x_ref[...].astype(F32)
     r1 = lax.rsqrt(jnp.mean(x * x, axis=-1, keepdims=True) + EPS)
     row = lax.broadcasted_iota(jnp.int32, (length, 1), 0)
     mask = (row < len_ref[0]).astype(F32)
-    u = mask * x * r1 * gain_ref[...]
-    put_columns(scr, u)
+    u = mask * x * r1 * gain_ref[0:1, :]
+    scr[:, :8, :] = jnp.zeros((scr.shape[0], 8, 128), F32)
+    put_columns(scr, u, 8)
     ut_ref[...] = u.T.astype(BF)
+    own_ref[...] = x_ref[pl.ds(pl.multiple_of(m * share, 16), share), :].astype(F32)
     for r in range(n):
         start = lax.rem(m + r, n) * share
         for odd in range(2):
             u_ref[odd, r * (share // 2) : (r + 1) * (share // 2), :] = every_second(
-                scr, start + odd, share // 2
+                scr, start + odd + 8, share // 2
             ).astype(BF)
-    filt = filt_ref.shape[0]
+    for lag in range(order):
+        for odd in range(2):
+            at = lag * width
+            lag_ref[odd * (share // 2) : (odd + 1) * (share // 2), at : at + width] = every_second(
+                scr, m * share + odd + 8 - lag, share // 2
+            ).astype(BF)
+
+
+def first_norm(lengths, x, gains, n, order):
+    length, width = x.shape
+    share = length // n
+    return pl.pallas_call(
+        functools.partial(norm_kernel, n, share, order),
+        in_specs=[smem(), whole(), whole()],
+        out_specs=[whole()] * 4,
+        out_shape=[
+            jax.ShapeDtypeStruct((2, length // 2, width), BF),
+            jax.ShapeDtypeStruct((width, length), BF),
+            jax.ShapeDtypeStruct((share, width), F32),
+            jax.ShapeDtypeStruct((share, order * width), BF),
+        ],
+        scratch_shapes=[pltpu.VMEM((width // 128, length + 8, 128), F32)],
+        compiler_params=params(),
+        cost_estimate=cost(10 * x.size, 6 * x.size),
+        name="first_norm",
+    )(lengths, x, gains)
+
+
+def taps_kernel(filt_ref, taps_ref, nat_ref, scr_f):
+    filt, length = filt_ref.shape
+    half = length // 2
     natural = filt_ref[...].astype(F32)
     nat_ref[...] = natural
     scr_f[0, :, :filt] = natural.T
@@ -112,63 +142,82 @@
     taps_ref[5] = pltpu.roll(odd, 1, 1)
 
 
-def first_norm(lengths, x, gain, filters, n):
-    length, width = x.shape
-    share = length // n
-    filt = filters.shape[0]
-    half = length // 2
-    return pl.pallas_call(
-        functools.partial(norm_kernel, n, share),
-        in_specs=[smem()] + [whole()] * 3,
-        out_specs=[whole()] * 4,
+def filter_taps(filters):
+    filt, length = filters.shape
+    return pl.pallas_call(
+        taps_kernel,
+        in_specs=[whole()],
+        out_specs=[whole()] * 2,
         out_shape=[
-            jax.ShapeDtypeStruct((2, half, width), BF),
-            jax.ShapeDtypeStruct((6, filt, half), F32),
+            jax.ShapeDtypeStruct((6, filt, length // 2), F32),
             jax.ShapeDtypeStruct((filt, length), F32),
-            jax.ShapeDtypeStruct((width, length), BF),
         ],
-        scratch_shapes=[
-            pltpu.VMEM((width // 128, length, 128), F32),
-            pltpu.VMEM((1, length, 128), F32),
-        ],
-        compiler_params=params(),
-        cost_estimate=cost(10 * x.size, 6 * x.size),
-        name="first_norm",
-    )(lengths, x, gain, filters)
+        scratch_shapes=[pltpu.VMEM((1, length, 128), F32)],
+        compiler_params=params(),
+        cost_estimate=cost(10 * filters.size, 6 * filters.size),
+        name="filter_taps",
+    )(filters)
+
+
+def fetch_matrices(j, steps, kb, stu_hbm, w_buf, sems):
+    def copies(step):
+        slot = lax.rem(step, 2)
+        return [
+            pltpu.make_async_copy(
+                stu_hbm.at[pl.ds((sign * steps + step) * kb, kb)],
+                w_buf.at[slot, sign],
+                sems.at[slot, sign],
+            )
+            for sign in range(2)
+        ]
+
+    @pl.when(j == 0)
+    def _():
+        for copy in copies(j):
+            copy.start()
+
+    @pl.when(j + 1 < steps)
+    def _():
+        for copy in copies(j + 1):
+            copy.start()
+
+    def wait():
+        for copy in copies(j):
+            copy.wait()
+
+    return lax.rem(j, 2), wait
+
+
+def fetch_last(j, steps, src, dst, sem):
+    copy = pltpu.make_async_copy(src, dst, sem)
+
+    @pl.when(j == 0)
+    def _():
+        copy.start()
+
+    @pl.when(j == steps - 1)
+    def _():
+        copy.wait()
 
 
 def mix_kernel(
-    kb, share, order, len_ref, taps_ref, x_ref, u_ref, wp_ref, wm_ref, ar_ref, gain_ref,
-    hid_ref, nt_ref, ta_ref, tb_ref, c_ref, acc_ref, scr,
+    kb, share, len_ref, taps_ref, x_ref, u_ref, lag_ref, gain_ref, stu_hbm, ar_hbm,
+    hid_ref, nt_ref, ta_ref, tb_ref, c_ref, acc_ref, scr, w_buf, ar_ref, sems, ar_sem,
 ):
-    j = pl.program_id(0)
-    length, width = x_ref.shape
-    half, rows = length // 2, share // 2
+    j, steps = pl.program_id(0), pl.num_programs(0)
+    half, width = u_ref.shape[1:]
+    length, rows = 2 * half, share // 2
     m = lax.axis_index("mp")
     b = lax.broadcasted_iota(jnp.int32, (rows, half), 0)
     a = lax.broadcasted_iota(jnp.int32, (rows, half), 1)
     wrapped = a >= (length - m * share) // 2
     upto = (a <= b) | wrapped
     below = (a < b) | wrapped
+    slot, wait = fetch_matrices(j, stu_hbm.shape[0] // (2 * kb), kb, stu_hbm, w_buf, sems)
 
     @pl.when(j == 0)
     def _():
         acc_ref[...] = jnp.zeros((share, width), F32)
-
-    @pl.when(j < order)
-    def _():
-        parts = []
-        for row_odd in range(2):
-            part = None
-            for col_odd in range(2):
-                back = 2 * b + row_odd - 2 * a - col_odd
-                valid = (back >= 0) | wrapped
-                back = jnp.where(back < 0, back + length, back)
-                t = jnp.where(valid & (back == j), 1.0, 0.0).astype(BF)
-                one = dot(t, u_ref[col_odd])
-                part = one if part is None else part + one
-            parts.append(part)
-        acc_ref[...] += dot(jnp.concatenate(parts, axis=0).astype(BF), ar_ref[0])
 
     for k in range(kb):
         even = toeplitz(taps_ref[0, pl.ds(j * kb + k, 1), :], rows)
@@ -188,33 +237,39 @@
         c_ref[:, k * width : (k + 1) * width] = (pa + pb).astype(BF)
         c_ref[:rows, (kb + k) * width : (kb + k + 1) * width] = (pa[:rows] - pb[:rows]).astype(BF)
         c_ref[rows:, (kb + k) * width : (kb + k + 1) * width] = (pb[rows:] - pa[rows:]).astype(BF)
-    total = dot(c_ref[:, : kb * width], wp_ref[...].reshape(kb * width, width))
-    total = total + dot(c_ref[:, kb * width :], wm_ref[...].reshape(kb * width, width))
-    acc_ref[...] += total
-
-    @pl.when(j == pl.num_programs(0) - 1)
+    wait()
+    acc_ref[...] += dot(c_ref[...], w_buf[slot].reshape(2 * kb * width, width))
+    fetch_last(j, steps, ar_hbm, ar_ref, ar_sem)
+
+    @pl.when(j == steps - 1)
     def _():
-        start = pl.multiple_of(m * share, 16)
-        x = x_ref[pl.ds(start, share), :].astype(F32)
-        hidden = x + interleave(scr, acc_ref[...])
+        total = acc_ref[...] + dot(lag_ref[...], ar_ref[...].reshape(lag_ref.shape[1], width))
+        hidden = x_ref[...] + interleave(scr, total)
         hid_ref[...] = hidden
         r2 = lax.rsqrt(jnp.mean(hidden * hidden, axis=-1, keepdims=True) + EPS)
         pos = m * share + lax.broadcasted_iota(jnp.int32, (share, 1), 0)
         mask = (pos < len_ref[0]).astype(F32)
-        nt_ref[...] = (mask * hidden * r2 * gain_ref[...]).astype(BF)
-
-
-def spectral_mix(lengths, taps, x, u, stu, ar, gain, share, kb):
-    length, width = x.shape
+        nt_ref[...] = (mask * hidden * r2 * gain_ref[1:2, :]).astype(BF)
+
+
+def matrix_scratch(kb, ar):
+    width = ar.shape[1]
+    return [
+        pltpu.VMEM((2, 2, kb, width, width), BF),
+        pltpu.VMEM(ar.shape, BF),
+        pltpu.SemaphoreType.DMA((2, 2)),
+        pltpu.SemaphoreType.DMA,
+    ]
+
+
+def spectral_mix(lengths, taps, x, u, lags, gains, stu, ar, share, kb):
+    width = x.shape[1]
+    length = 2 * u.shape[1]
     filt = taps.shape[1]
-    steps = filt // kb
-    w_spec = pl.BlockSpec((kb, width, width), lambda j: (j, 0, 0))
-    w_spec_neg = pl.BlockSpec((kb, width, width), lambda j: (j + steps, 0, 0))
-    return pl.pallas_call(
-        functools.partial(mix_kernel, kb, share, ar.shape[0]),
-        grid=(steps,),
-        in_specs=[smem(), whole(), whole(), whole(), w_spec, w_spec_neg]
-        + [lag_spec(ar, steps), whole()],
+    return pl.pallas_call(
+        functools.partial(mix_kernel, kb, share),
+        grid=(filt // kb,),
+        in_specs=[smem()] + [whole()] * 5 + [outside()] * 2,
         out_specs=[whole()] * 2,
         out_shape=[
             jax.ShapeDtypeStruct((share, width), F32),
@@ -226,11 +281,12 @@
             pltpu.VMEM((share, 2 * kb * width), BF),
             pltpu.VMEM((share, width), F32),
             pltpu.VMEM((width // 128, share, 128), F32),
-        ],
+        ]
+        + matrix_scratch(kb, ar),
         compiler_params=params(40 << 20),
         cost_estimate=cost(2 * filt * share * width * (length + 2 * width), 2 * stu.size),
         name="spectral_mix",
-    )(lengths, taps, x, u, stu, stu, ar, gain)
+    )(lengths, taps, x, u, lags, gains, stu, ar)
 
 
 def ffn_kernel(
@@ -351,7 +407,7 @@
     bn = bn * (pos < len_ref[0]).astype(F32)
     z = hidden * r2
     gg_ref[...] = jnp.broadcast_to(jnp.sum(bn * z, axis=0, keepdims=True), gg_ref.shape)
-    q = bn * gain_ref[...]
+    q = bn * gain_ref[1:2, :]
     start = pl.multiple_of(m * share, 16)
     dout = cot_ref[pl.ds(start, share), :].astype(F32)
     back = dout + r2 * (q - z * jnp.mean(q * z, axis=-1, keepdims=True))
@@ -378,10 +434,12 @@
 
 
 def unmix_kernel(
-    kb, share, n, order, len_ref, taps_ref, x_ref, bh_ref, gg_ref, gain_ref, wp_ref, wm_ref, ar_ref, *refs
+    kb, share, n, len_ref, taps_ref, x_ref, bh_ref, gg_ref, gain_ref, stu_hbm, ar_hbm, *refs
 ):
-    b_refs, (ig_ref, gain_out, ta_ref, tb_ref, be_ref, bo_ref, acc_ref, scr) = refs[:n], refs[n:]
-    j = pl.program_id(0)
+    b_refs, (ig_ref, gain_out) = refs[:n], refs[n : n + 2]
+    ta_ref, tb_ref, be_ref, bo_ref, lag_ref, acc_ref, scr = refs[n + 2 : n + 9]
+    w_buf, ar_ref, sems, ar_sem = refs[n + 9 :]
+    j, steps = pl.program_id(0), pl.num_programs(0)
     width = bh_ref.shape[1]
     length = n * share
     half, rows = length // 2, share // 2
@@ -391,27 +449,23 @@
     inside = a < (length - m * share) // 2
     upto = (a >= b) & inside
     below = (a > b) & inside
+    slot, wait = fetch_matrices(j, stu_hbm.shape[0] // (2 * kb), kb, stu_hbm, w_buf, sems)
 
     @pl.when(j == 0)
     def _():
-        for r in range(n):
+        for r in reversed(range(n)):
             put_columns(scr, b_refs[r][...].astype(F32))
             be_ref[r * rows : (r + 1) * rows, :] = every_second(scr, 0, rows).astype(BF)
             bo_ref[r * rows : (r + 1) * rows, :] = every_second(scr, 1, rows).astype(BF)
+        more = b_refs[1 % n][:16, :].astype(F32) * jnp.where(m == n - 1, 0.0, 1.0)
+        put_columns(scr, more, share)
+        order = lag_ref.shape[1] // width
+        for lag in range(order):
+            for odd in range(2):
+                lag_ref[odd * rows : (odd + 1) * rows, lag * width : (lag + 1) * width] = (
+                    every_second(scr, odd + lag, rows).astype(BF)
+                )
         acc_ref[...] = jnp.zeros((share, width), F32)
-
-    @pl.when(j < order)
-    def _():
-        parts = []
-        for row_odd in range(2):
-            part = None
-            for col_odd, source in enumerate((be_ref, bo_ref)):
-                ahead = 2 * a + col_odd - 2 * b - row_odd
-                t = jnp.where(inside & (ahead == j), 1.0, 0.0).astype(BF)
-                one = dot(t, source[...])
-                part = one if part is None else part + one
-            parts.append(part)
-        acc_ref[...] += dot_cols(jnp.concatenate(parts, axis=0).astype(BF), ar_ref[0])
 
     for k in range(kb):
         even = toeplitz(taps_ref[3, pl.ds(j * kb + k, 1), :], rows)
@@ -425,45 +479,43 @@
         tb_ref[at + rows : at + share, :] = even
     ca = dot(ta_ref[...], be_ref[...])
     cb = dot(tb_ref[...], bo_ref[...])
+    wait()
     total = acc_ref[...]
     for k in range(kb):
         at = k * share
         pa, pb = ca[at : at + share], cb[at : at + share]
         minus = jnp.concatenate([pa[:rows] - pb[:rows], pb[rows:] - pa[rows:]], axis=0)
-        total = total + dot_cols((pa + pb).astype(BF), wp_ref[k])
-        total = total + dot_cols(minus.astype(BF), wm_ref[k])
+        total = total + dot_cols((pa + pb).astype(BF), w_buf[slot, 0, k])
+        total = total + dot_cols(minus.astype(BF), w_buf[slot, 1, k])
     acc_ref[...] = total
-
-    @pl.when(j == pl.num_programs(0) - 1)
+    fetch_last(j, steps, ar_hbm, ar_ref, ar_sem)
+
+    @pl.when(j == steps - 1)
     def _():
-        start = pl.multiple_of(m * share, 16)
-        x = x_ref[pl.ds(start, share), :].astype(F32)
+        total = acc_ref[...]
+        for lag in range(ar_ref.shape[0]):
+            total = total + dot_cols(lag_ref[:, lag * width : (lag + 1) * width], ar_ref[lag])
+        x = x_ref[...]
         r1 = lax.rsqrt(jnp.mean(x * x, axis=-1, keepdims=True) + EPS)
         pos = m * share + lax.broadcasted_iota(jnp.int32, (share, 1), 0)
-        masked = interleave(scr, acc_ref[...]) * (pos < len_ref[0]).astype(F32)
+        masked = interleave(scr, total) * (pos < len_ref[0]).astype(F32)
         y = x * r1
-        p = masked * gain_ref[...]
+        p = masked * gain_ref[0:1, :]
         ig = bh_ref[...] + r1 * (p - y * jnp.mean(p * y, axis=-1, keepdims=True))
         ig_ref[...] = ig.astype(BF)
         gain_out[0:8, :] = jnp.broadcast_to(jnp.sum(masked * y, axis=0, keepdims=True), (8, width))
         gain_out[8:16, :] = gg_ref[...]
 
 
-def spectral_unmix(lengths, taps, x, back_hidden, gg, gain, stu, ar, pieces, kb):
+def spectral_unmix(lengths, taps, x, back_hidden, gg, gains, stu, ar, pieces, kb):
     share, width = back_hidden.shape
     n = len(pieces)
     length = n * share
     count = taps.shape[1]
-    steps = count // kb
-    w_spec = pl.BlockSpec((kb, width, width), lambda j: (j, 0, 0))
-    w_spec_neg = pl.BlockSpec((kb, width, width), lambda j: (j + steps, 0, 0))
-    return pl.pallas_call(
-        functools.partial(unmix_kernel, kb, share, n, ar.shape[0]),
-        grid=(steps,),
-        in_specs=[smem()]
-        + [whole()] * 5
-        + [w_spec, w_spec_neg, lag_spec(ar, steps)]
-        + [whole()] * n,
+    return pl.pallas_call(
+        functools.partial(unmix_kernel, kb, share, n),
+        grid=(count // kb,),
+        in_specs=[smem()] + [whole()] * 5 + [outside()] * 2 + [whole()] * n,
         out_specs=[whole()] * 2,
         out_shape=[
             jax.ShapeDtypeStruct((share, width), BF),
@@ -474,13 +526,15 @@
             pltpu.VMEM((kb * share, length // 2), BF),
             pltpu.VMEM((length // 2, width), BF),
             pltpu.VMEM((length // 2, width), BF),
+            pltpu.VMEM((share, ar.shape[0] * width), BF),
             pltpu.VMEM((share, width), F32),
-            pltpu.VMEM((width // 128, share, 128), F32),
-        ],
-        compiler_params=params(40 << 20),
+            pltpu.VMEM((width // 128, share + 16, 128), F32),
+        ]
+        + matrix_scratch(kb, ar),
+        compiler_params=params(30 << 20),
         cost_estimate=cost(2 * count * share * width * (length + 2 * width), 2 * stu.size),
         name="spectral_unmix",
-    )(lengths, taps, x, back_hidden, gg, gain, stu, stu, ar, *pieces)
+    )(lengths, taps, x, back_hidden, gg, gains, stu, ar, *pieces)
 
 
 def conv_kernel(groups, tile, own, filt_ref, *refs):
@@ -536,14 +590,43 @@
     )(filt, *uts)
 
 
+def lag_kernel(groups, *refs):
+    ut_refs, out_refs = refs[:groups], refs[groups:]
+    width, length = ut_refs[0].shape
+    chip = lax.rem(lax.axis_index("dp") // 2, groups)
+    col = lax.broadcasted_iota(jnp.int32, (width, length), 1)
+    for r in range(groups):
+        start = pl.multiple_of((chip ^ r) * length, 128)
+        out_refs[0][:, pl.ds(start, length)] = ut_refs[r][...]
+        value = ut_refs[r][...].astype(F32)
+        for lag in range(1, len(out_refs)):
+            moved = pltpu.roll(value, lag, 1)
+            out_refs[lag][:, pl.ds(start, length)] = jnp.where(col >= lag, moved, 0.0).astype(BF)
+
+
+def lagged(uts, order):
+    groups = len(uts)
+    width, length = uts[0].shape
+    shape = jax.ShapeDtypeStruct((width, groups * length), BF)
+    return pl.pallas_call(
+        functools.partial(lag_kernel, groups),
+        in_specs=[whole()] * groups,
+        out_specs=[whole()] * order,
+        out_shape=[shape] * order,
+        compiler_params=params(),
+        cost_estimate=cost(order * groups * width * length, 4 * order * groups * width * length),
+        name="lagged",
+    )(*uts)
+
+
 def grads_kernel(steps, order, groups, rows, conv_ref, *refs):
-    ut_refs, b_refs = refs[:groups], refs[groups : groups + len(rows)]
-    keep_ref, send_ref, b_scr, lag_scr, scr = refs[groups + len(rows) :]
+    lag_refs, b_refs = refs[:order], refs[order : order + len(rows)]
+    keep_ref, send_ref, b_scr, scr = refs[order + len(rows) :]
     g = pl.program_id(0)
     d = lax.axis_index("dp")
     chip, core = lax.rem(d // 2, groups), lax.rem(d, 2)
     step, block, depth = conv_ref.shape
-    width, length = ut_refs[0].shape
+    width, length = b_scr.shape[1], depth // groups
     half = block // 2
 
     @pl.when(g == 0)
@@ -563,22 +646,18 @@
             start = pl.multiple_of((g * step + k) * half, 16)
             send_ref[pl.ds(start, half), :] = scr[k, pl.ds(other, half), :].astype(BF)
 
-    @pl.when(g >= steps)
-    def _():
-        lag = g - steps
-        col = lax.broadcasted_iota(jnp.int32, (width, length), 1)
-        for r in range(groups):
-            value = pltpu.roll(ut_refs[r][...].astype(F32), lag, 1)
-            start = pl.multiple_of((chip ^ r) * length, 128)
-            lag_scr[:, pl.ds(start, length)] = jnp.where(col >= lag, value, 0.0).astype(BF)
-        start = pl.multiple_of(steps * step * half + lag * width, 16)
-        send_ref[pl.ds(start, width), :] = dot(lag_scr[...], b_scr[...]).astype(BF)
-
-
-def matrix_grads(conv, uts, backs, rows, order):
+    for lag in range(order):
+
+        @pl.when(g == steps + lag)
+        def _():
+            at = steps * step * half + lag * width
+            send_ref[at : at + width, :] = dot(lag_refs[lag][...], b_scr[...]).astype(BF)
+
+
+def matrix_grads(conv, lags, backs, rows):
     own, block, depth = conv.shape
-    groups = len(uts)
-    width = uts[0].shape[0]
+    order, width = len(lags), lags[0].shape[0]
+    groups = 1 + max(r for r, _, _ in rows)
     step = next(s for s in (4, 3, 2, 1) if own % s == 0)
     steps = own // step
     half = block // 2
@@ -586,7 +665,7 @@
         functools.partial(grads_kernel, steps, order, groups, rows),
         grid=(steps + order,),
         in_specs=[pl.BlockSpec((step, block, depth), lambda g: (jnp.minimum(g, steps - 1), 0, 0))]
-        + [whole()] * (groups + len(backs)),
+        + [whole()] * (order + len(backs)),
         out_specs=[whole()] * 2,
         out_shape=[
             jax.ShapeDtypeStruct((own, half, width), F32),
@@ -594,13 +673,12 @@
         ],
         scratch_shapes=[
             pltpu.VMEM((depth, width), BF),
-            pltpu.VMEM((width, depth), BF),
             pltpu.VMEM((step, block, width), F32),
         ],
         compiler_params=params(),
         cost_estimate=cost(2 * (conv.size + order * width * depth) * width, 2 * conv.size),
         name="matrix_grads",
-    )(conv, *uts, *backs)
+    )(conv, *lags, *backs)
 
 
 def rows_message_kernel(ig_ref, hid_ref, *refs):
@@ -760,21 +838,54 @@
     )(keep, over_x, over_y)
 
 
-def last_sum_kernel(keep_ref, recv_ref, out_ref):
-    at = recv_ref.shape[0] - keep_ref.shape[0]
-    out_ref[...] = (keep_ref[...] + recv_ref[at:, :].astype(F32)).astype(BF)
-
-
-def last_sum(keep, recv):
+def split_gains(both):
+    high = both.astype(BF)
+    low = (both - high.astype(F32)).astype(BF)
+    return jnp.concatenate([high, low], axis=0)
+
+
+def joined(gains):
+    return gains[:16].astype(F32) + gains[16:].astype(F32)
+
+
+def last_sum_kernel(keep_ref, recv_ref, gain_ref, out_ref):
+    rows = keep_ref.shape[0]
+    at = recv_ref.shape[0] - rows
+    out_ref[:rows, :] = (keep_ref[...] + recv_ref[at:, :].astype(F32)).astype(BF)
+    out_ref[rows:, :] = split_gains(gain_ref[...])
+
+
+def last_sum(keep, recv, gains):
+    rows, width = keep.shape
     return pl.pallas_call(
         last_sum_kernel,
+        in_specs=[whole()] * 3,
+        out_specs=whole(),
+        out_shape=jax.ShapeDtypeStruct((rows + 32, width), BF),
+        compiler_params=params(),
+        cost_estimate=cost(keep.size, 8 * keep.size),
+        name="last_sum",
+    )(keep, recv, gains)
+
+
+def pair_kernel(own_ref, recv_ref, out_ref):
+    rows = own_ref.shape[0] - 32
+    out_ref[:rows, :] = own_ref[:rows, :]
+    out_ref[rows : 2 * rows, :] = recv_ref[:rows, :]
+    out_ref[2 * rows :, :] = split_gains(joined(own_ref[rows:, :]) + joined(recv_ref[rows:, :]))
+
+
+def pair_up(own, recv):
+    rows, width = own.shape[0] - 32, own.shape[1]
+    return pl.pallas_call(
+        pair_kernel,
         in_specs=[whole()] * 2,
         out_specs=whole(),
-        out_shape=jax.ShapeDtypeStruct(keep.shape, BF),
-        compiler_params=params(),
-        cost_estimate=cost(keep.size, 8 * keep.size),
-        name="last_sum",
-    )(keep, recv)
+        out_shape=jax.ShapeDtypeStruct((2 * rows + 32, width), BF),
+        compiler_params=params(),
+        cost_estimate=cost(own.size, 8 * own.size),
+        name="pair_up",
+    )(own, recv)
 
 
 def join_kernel(*refs):
@@ -797,13 +908,18 @@
     )(*pieces)
 
 
-def finish_kernel(chips, keep_ref, send_ref, recv_ref, stu_ref, ar_ref, *w_refs):
+def finish_kernel(chips, keep_ref, send_ref, recv_ref, stu_ref, ar_ref, *more_refs):
     own, half, width = keep_ref.shape
     d = lax.axis_index("dp")
     core = lax.rem(d, 2)
+    w_refs = more_refs[1:]
     groups, count = len(chips), len(w_refs)
     rows = width // (2 * groups) if groups else 0
     base = groups * count * rows
+    if groups:
+        gains = slice(base, base + 32)
+        more_refs[0][...] = joined(send_ref[gains, :]) + joined(recv_ref[gains, :])
+        base += 32
     for r in range(groups):
         chip = ((d // 2) ^ r) * 2
         for ref, which in ((send_ref, chip + core), (recv_ref, chip + 1 - core)):
@@ -823,16 +939,17 @@
 
 def finish(keep, send, recv, order, chips):
     width = keep.shape[2]
-    count = 3 if chips else 0
+    more = [jax.ShapeDtypeStruct((16, width), F32)] if chips else []
+    more += [jax.ShapeDtypeStruct((width, width), F32)] * (3 if chips else 0)
     return pl.pallas_call(
         functools.partial(finish_kernel, chips),
         in_specs=[whole()] * 3,
-        out_specs=[whole()] * (2 + count),
+        out_specs=[whole()] * (2 + len(more)),
         out_shape=[
             jax.ShapeDtypeStruct(keep.shape, F32),
             jax.ShapeDtypeStruct((order, width, width), F32),
         ]
-        + [jax.ShapeDtypeStruct((width, width), F32)] * count,
+        + more,
         compiler_params=params(),
         cost_estimate=cost(keep.size, 10 * keep.size),
         name="finish",
@@ -878,29 +995,36 @@
     order = ar_weight.shape[0]
     own = stu_weight.shape[0] // n
     lengths = lengths.astype(jnp.int32)
-    gain_one = first_gain.reshape(1, width)
-    gain_two = second_gain.reshape(1, width)
-
-    u, taps, natural, ut = first_norm(lengths, inputs, gain_one, filters.T, n)
+    both_gains = jnp.stack([first_gain, second_gain])
+
+    u, ut, x_own, u_lags = first_norm(lengths, inputs, both_gains, n, order)
+    taps, natural = filter_taps(filters.T)
     uts = [ut] + [swap(ut, "dp", n_dp, 2 * r) for r in range(1, 3)]
-    hidden, nt = spectral_mix(lengths, taps, inputs, u, stu_weight, ar_weight, gain_two, share, 4)
+    hidden, nt = spectral_mix(
+        lengths, taps, x_own, u, u_lags, both_gains, stu_weight, ar_weight, share, 4
+    )
     nts = fetch_shifted(nt, "mp", n)
+    weights = (cotangent, gate_weight, up_weight, down_weight)
+    parts = {0: feed_forward(0, n, after(nt, uts[1:3]), *weights)}
+    last = 0
+    for r in sorted(range(1, n), key=lambda r: min(r, n - r)):
+        first = parts[last][0]
+        parts[r] = feed_forward(r, n, after(nts[r], first), *weights)
+        last = r
     uts += [swap(after(ut, nt), "dp", n_dp, 2 * r) for r in range(3, groups)]
-    weights = (cotangent, gate_weight, up_weight, down_weight)
-    parts = [feed_forward(0, n, nts[0], *weights)]
-    nts = [nts[0]] + after(after(nts[1:], parts[0][0]), uts[1:3])
-    parts += [feed_forward(r, n, nts[r], *weights) for r in range(1, n)]
+    parts = [parts[r] for r in range(n)]
     bns = send_shifted([p[0] for p in parts], "mp")
     acts, bgs, bus = ([p[i] for p in parts] for i in (1, 2, 3))
     custom = n_dp == 8 and gate_weight.shape[1] == width
     grads = ffn_grads(cotangent, down_weight, nts, acts, bgs, bus, groups if custom else 0)
     out_parts, grads = grads[:n], grads[n:]
     bns = [bns[0]] + after(bns[1:], grads[0])
-    back_hidden, back_rows, second_part = mid_norm(lengths, hidden, cotangent, gain_two, bns)
+    back_hidden, back_rows, second_part = mid_norm(lengths, hidden, cotangent, both_gains, bns)
     backs = fetch_shifted(back_rows, "mp", n)
     uts = after(uts, back_rows)
     conv = [convolutions(natural, uts[r : r + 4], own, groups) for r in range(0, groups, 4)]
-    backs = after(backs, conv)
+    lags = [lagged(uts[r : r + 4], order) for r in range(0, groups, 4)]
+    backs = after(backs, (conv, lags))
     if custom:
         w_keep, w_send = grads
         w_send = swap(after(w_send, back_rows), "dp", n_dp, 1)
@@ -911,10 +1035,12 @@
         (own_back,) = pack_rows(backs)
     out_sums = send_shifted(after(out_parts, own_back), "mp")
     ig, gains = spectral_unmix(
-        lengths, taps, inputs, back_hidden, second_part, gain_one, stu_weight, ar_weight, backs, 4
+        lengths, taps, x_own, back_hidden, second_part, both_gains, stu_weight, ar_weight, backs, 4
     )
     conv, hidden = after((conv, hidden), ig)
     message = rows_message(ig, hidden, out_sums)
+    gains = ordered_sum(fetch_shifted(after(gains, message), "mp", n), "mp", 0)
+    message = after(message, gains)
     messages = fetch_shifted(message, "mp", n)
     if custom:
         w_keep, to_y, to_x = turn(merge_rows(w_keep), after(over_x, message), over_y)
@@ -922,38 +1048,33 @@
         all_backs = [own_back, over_x, over_y, from_y, from_x]
         half = length // 2
         rows = ((0, 0, length), (1, 0, length), (2, 0, length), (3, 0, half), (3, half, half))
-        w_sum = last_sum(w_keep, from_y)
+        w_sum = last_sum(w_keep, from_y, gains)
         conv = after(conv, w_sum)
     else:
         all_backs = [own_back] + [swap(own_back, "dp", n_dp, 2 * r) for r in range(1, groups)]
         rows = tuple((r, 0, length) for r in range(min(groups, 4)))
 
-    gains = after(gains, all_backs[-1])
-    gains = ordered_sum(fetch_shifted(gains, "mp", n), "mp", 0)
-    gains = ordered_sum([gains, swap(gains, "dp", n_dp, 1)], "dp", 0)
-    gains = [gains] + [swap(gains, "dp", n_dp, 2 * r) for r in range(1, groups)]
-    gains = ordered_sum(gains, "dp", 2)
-
     conv = after(conv, (message, messages[n // 2]))
     if len(conv) == 1:
-        keep, send = matrix_grads(conv[0], uts, all_backs, rows, order)
+        keep, send = matrix_grads(conv[0], lags[0], all_backs, rows)
     else:
         some = [
-            matrix_grads(c, uts[4 * k : 4 * k + 4], all_backs[4 * k : 4 * k + 4], rows, order)
+            matrix_grads(c, lags[k], all_backs[4 * k : 4 * k + 4], rows)
             for k, c in enumerate(conv)
         ]
         keep = ordered_sum([k for k, _ in some], "dp", 8)
         send = ordered_sum([k.astype(F32) for _, k in some], "dp", 8).astype(BF)
     input_grad, output = finish_rows(after(messages, (gains, send)))
     if custom:
-        w_pair = join_pieces([w_sum, swap(w_sum, "dp", n_dp, 4)])
-        w_all = [w_pair, swap(w_pair, "dp", n_dp, 2)]
-        send = join_pieces(after([*w_all, send], output))
-    recv = swap(after(send, output), "dp", n_dp, 1)
-    stu_grad, ar_grad, *w_grads = finish(keep, send, recv, order, (0, 2, 1, 3) if custom else ())
+        w_pair = pair_up(w_sum, swap(w_sum, "dp", n_dp, 4))
+        w_all = pair_up(w_pair, after(swap(w_pair, "dp", n_dp, 2), messages))
+        send = join_pieces([w_all, send])
+    recv = after(swap(send, "dp", n_dp, 1), output)
+    stu_grad, ar_grad, *more = finish(keep, send, recv, order, (0, 2, 1, 3) if custom else ())
     if custom:
-        gate_grad, up_grad, down_grad = w_grads
+        gains, gate_grad, up_grad, down_grad = more
     else:
+        gains = ordered_sum([gains] + [swap(gains, "dp", n_dp, r) for r in range(1, n_dp)], "dp", 1)
         gate_grad, up_grad, down_grad = (g.astype(F32) for g in lax.psum(tuple(grads), "dp"))
     return (
         output, input_grad, stu_grad, ar_grad, gains[0], gains[8], gate_grad, up_grad, down_grad,

time: 180 us -> 165 us (0.917)
  waiting for transfers between devices: 57.2 us -> 48 us
  Pallas kernels: 76.5 us -> 70.1 us
  local copies, waits for them, and re-layouts: 6.41 us -> 3.9 us
  starting transfers between devices: 38.2 us -> 40.5 us
    ppermute x15 -> x11, waiting for transfers between devices: 24.8 us -> 13.8 us  [swap(): return lax.ppermute(value, axis, [(i, i ^ bits) for i in range(n)])]
    pallas_call x1, Pallas kernels: 17.6 us -> 11.4 us  [matrix_grads(): pl.pallas_call(functools.partial(grads_kernel, steps, order, groups, rows...]
    unnamed x24 -> x14, local copies, waits for them, and re-layouts: 5.83 us -> 3.32 us
    ppermute x15 -> x11, starting transfers between devices: 13 us -> 12.4 us  [swap(): return lax.ppermute(value, axis, [(i, i ^ bits) for i in range(n)])]
    pallas_call x4 -> x8, Pallas kernels: 36.4 us -> 36.3 us  [the longest x1 17.8 us: spectral_unmix(): pl.pallas_call(functools.partial(unmix_kernel, kb, share, n), grid=(count...]
  transfers between devices with their start and end apart: 33 -> 29, of which waited for: 13 -> 10; matrix products, arithmetic and copies ran while one was open for 0% -> 0% of each run, Pallas kernels for 39% -> 39%
where the time goes in v1:
time: 165 us
  Pallas kernels  70.1 us (42%)
  waiting for transfers between devices  48 us (29%)
  starting transfers between devices  40.5 us (25%)
  local copies, waits for them, and re-layouts  3.9 us (2%)
    ppermute x12, waiting for transfers between devices, fetch_shifted(): lax.ppermute(value, axis, [(i, (i - r) % n) for i in range(n)])  26.3 us
    pallas_call x1, Pallas kernels, spectral_unmix(): pl.pallas_call(functools.partial(unmix_kernel, kb, share, n), grid=(count...  17.8 us
    ppermute x12, starting transfers between devices, fetch_shifted(): lax.ppermute(value, axis, [(i, (i - r) % n) for i in range(n)])  17.1 us
    pallas_call x1, Pallas kernels, spectral_mix(): pl.pallas_call(functools.partial(mix_kernel, kb, share), grid=(filt // kb...  14.5 us
    ppermute x11, waiting for transfers between devices, swap(): return lax.ppermute(value, axis, [(i, i ^ bits) for i in range(n)])  13.8 us
    ppermute x11, starting transfers between devices, swap(): return lax.ppermute(value, axis, [(i, i ^ bits) for i in range(n)])  12.4 us
    pallas_call x1, Pallas kernels, matrix_grads(): pl.pallas_call(functools.partial(grads_kernel, steps, order, groups, rows...  11.4 us
    ppermute x6, starting transfers between devices, send_shifted(): lax.ppermute(pieces[r], axis, [(i, (i + r) % n) for i in range(n)])  10.9 us
  transfers between devices with their start and end apart: 29, of which 10 were waited for; matrix products, arithmetic and copies ran while one was open for 0% of the time, Pallas kernels for 39%

profile of v1, /device:TPU:0, one launch (start us, length us, event | category | flops | bytes accessed | tf_op | source)
XLA Modules:
  0.0 164.8 jit_solution(10644417732491442606)
XLA Ops:
  3.9 3.0 %collective-permute-start.1 = (bf16[512,768]{1,0:T(8,128)(2,1)S(1)}, bf16[512,768]{1,0:T(8,128)(2,1)S(1)}, u32[]{:S(2)}, u32[]{:S(2)}) collective-permute-start(bf16[512,768]{1,0:T(8,128)(2,1)S(1)} %get-tuple-element.134.refs_0_), channel_id=1, source_target_pairs={{0,16},{4,20},{8,24},{12,28},{16,0},{20,4},{24,8},{28,12},{1,17},{... | collective-permute-start | bytes 2359304 | tf_op jit(solution)/shard_map/ppermute | solution.py:973
  11.1 14.5 %spectral_mix.1 = (f32[192,512]{1,0:T(8,128)S(1)}, bf16[192,512]{1,0:T(8,128)(2,1)S(1)}) custom-call(s32[1]{0:T(128)S(6)} %copy.20.len_ref, f32[6,24,384]{2,1,0:T(8,128)S(1)} %get-tuple-element.98.taps_ref, f32[192,512]{1,0:T(8,128)S(1)} %get-tuple-element.99.x_ref, bf16[2,384,512]{2,1,0:T(8,128)(2,1)S(1)} %get-tuple-element.100.u_ref, ...), custom_call_target="tpu_custom_call" | custom-call | flops 8455716864 | bytes 25165824 | tf_op jit(solution)/shard_map/spectral_mix/pallas_call | solution.py:269
  25.6 3.6 %collective-permute-start.2 = (bf16[192,512]{1,0:T(8,128)(2,1)S(1)}, bf16[192,512]{1,0:T(8,128)(2,1)S(1)}, u32[]{:S(2)}, u32[]{:S(2)}) collective-permute-start(bf16[192,512]{1,0:T(8,128)(2,1)S(1)} %get-tuple-element.105.nt_ref.refs_0_), channel_id=1, source_target_pairs={{0,3},{1,0},{2,1},{3,2},{4,7},{5,4},{6,5},{7,6},{8,11},{9,8},{10,9... | collective-permute-start | bytes 589832 | tf_op jit(solution)/shard_map/ppermute | solution.py:961
  31.8 2.8 %collective-permute-done.2.nt_ref.refs_1_ = bf16[192,512]{1,0:T(8,128)(2,1)S(1)} collective-permute-done((bf16[192,512]{1,0:T(8,128)(2,1)S(1)}, bf16[192,512]{1,0:T(8,128)(2,1)S(1)}, u32[]{:S(2)}, u32[]{:S(2)}) %collective-permute-start.2) | collective-permute-done | bytes 196640 | tf_op jit(solution)/shard_map/ppermute | solution.py:961
  36.3 2.8 %collective-permute-done.5.nt_ref.refs_3_ = bf16[192,512]{1,0:T(8,128)(2,1)S(1)} collective-permute-done((bf16[192,512]{1,0:T(8,128)(2,1)S(1)}, bf16[192,512]{1,0:T(8,128)(2,1)S(1)}, u32[]{:S(2)}, u32[]{:S(2)}) %collective-permute-start.5) | collective-permute-done | bytes 196640 | tf_op jit(solution)/shard_map/ppermute | solution.py:961
  40.2 3.6 %collective-permute-start.7 = (bf16[192,512]{1,0:T(8,128)(2,1)S(1)}, bf16[192,512]{1,0:T(8,128)(2,1)S(1)}, u32[]{:S(2)}, u32[]{:S(2)}) collective-permute-start(bf16[192,512]{1,0:T(8,128)(2,1)S(1)} %get-tuple-element.110), channel_id=1, source_target_pairs={{0,3},{1,0},{2,1},{3,2},{4,7},{5,4},{6,5},{7,6},{8,11},{9,8},{10,9... | collective-permute-start | bytes 589832 | tf_op jit(solution)/shard_map/ppermute | solution.py:968
  43.8 7.4 %collective-permute-done.4.nt_ref.refs_2_ = bf16[192,512]{1,0:T(8,128)(2,1)S(1)} collective-permute-done((bf16[192,512]{1,0:T(8,128)(2,1)S(1)}, bf16[192,512]{1,0:T(8,128)(2,1)S(1)}, u32[]{:S(2)}, u32[]{:S(2)}) %collective-permute-start.4) | collective-permute-done | bytes 196640 | tf_op jit(solution)/shard_map/ppermute | solution.py:961
  52.3 1.9 %ffn_grads.1 = (bf16[192,512]{1,0:T(8,128)(2,1)S(1)}, bf16[192,512]{1,0:T(8,128)(2,1)S(1)}, bf16[192,512]{1,0:T(8,128)(2,1)S(1)}, bf16[192,512]{1,0:T(8,128)(2,1...) custom-call(bf16[768,512]{1,0:T(8,128)(2,1)S(1)} %copy-done, ...), custom_call_target="tpu_custom_call" | custom-call | flops 1610612736 | bytes 4718592 | tf_op jit(solution)/shard_map/ffn_grads/pallas_call | solution.py:386
  54.2 8.0 %collective-permute-done.6.refs_2_ = bf16[192,512]{1,0:T(8,128)(2,1)S(1)} collective-permute-done((bf16[192,512]{1,0:T(8,128)(2,1)S(1)}, bf16[192,512]{1,0:T(8,128)(2,1)S(1)}, u32[]{:S(2)}, u32[]{:S(2)}) %collective-permute-start.6) | collective-permute-done | bytes 196640 | tf_op jit(solution)/shard_map/ppermute | solution.py:968
  62.7 3.1 %collective-permute-start.9 = (bf16[192,512]{1,0:T(8,128)(2,1)S(1)}, bf16[192,512]{1,0:T(8,128)(2,1)S(1)}, u32[]{:S(2)}, u32[]{:S(2)}) collective-permute-start(bf16[192,512]{1,0:T(8,128)(2,1)S(1)} %get-tuple-element.141.refs_0_), channel_id=1, source_target_pairs={{0,2},{1,3},{2,0},{3,1},{4,6},{5,7},{6,4},{7,5},{8,10},{9,11},{10,... | collective-permute-start | bytes 589832 | tf_op jit(solution)/shard_map/ppermute | solution.py:961
  66.5 9.9 %convolutions.1.conv_ref = bf16[12,128,3072]{2,1,0:T(8,128)(2,1)S(1)} custom-call(f32[24,768]{1,0:T(8,128)S(1)} %get-tuple-element.132.filt_ref, bf16[512,768]{1,0:T(8,128)(2,1)S(1)} %get-tuple-element.134.refs_0_, bf16[512,768]{1,0:T(8,128)(2,1)S(1)} %collective-permute-done.refs_1_, bf16[512,768]{1,0:T(8,128)(2,1)S(1)} %collective-permute-done.1.refs_2_, ...), custom_call_target="tpu_custom_call" | custom-call | flops 4831838208 | bytes 9437184 | tf_op jit(solution)/shard_map/convolutions/pallas_call | solution.py:575
  76.4 2.6 %lagged.1 = (bf16[512,3072]{1,0:T(8,128)(2,1)S(1)}, bf16[512,3072]{1,0:T(8,128)(2,1)S(1)}, bf16[512,3072]{1,0:T(8,128)(2,1)S(1)}) custom-call(bf16[512,768]{1,0:T(8,128)(2,1)S(1)} %get-tuple-element.134.refs_0_, bf16[512,768]{1,0:T(8,128)(2,1)S(1)} %collective-permute-done.refs_1_, bf16[512,768]{1,0:T(8,128)(2,1)S(1)} %collective-permute-done.1.refs_2_, ...), custom_call_target="tpu_custom_call" | custom-call | flops 4718592 | bytes 18874368 | tf_op jit(solution)/shard_map/lagged/pallas_call | solution.py:611
  81.9 4.2 %collective-permute-start.13 = (bf16[192,512]{1,0:T(8,128)(2,1)S(1)}, bf16[192,512]{1,0:T(8,128)(2,1)S(1)}, u32[]{:S(2)}, u32[]{:S(2)}) collective-permute-start(bf16[192,512]{1,0:T(8,128)(2,1)S(1)} %get-tuple-element.156), channel_id=1, source_target_pairs={{0,1},{1,2},{2,3},{3,0},{4,5},{5,6},{6,7},{7,4},{8,9},{9,10},{10,1... | collective-permute-start | bytes 589832 | tf_op jit(solution)/shard_map/ppermute | solution.py:968
  86.1 2.4 %collective-permute-start.15 = (bf16[192,512]{1,0:T(8,128)(2,1)S(1)}, bf16[192,512]{1,0:T(8,128)(2,1)S(1)}, u32[]{:S(2)}, u32[]{:S(2)}) collective-permute-start(bf16[192,512]{1,0:T(8,128)(2,1)S(1)} %get-tuple-element.158), channel_id=1, source_target_pairs={{0,3},{1,0},{2,1},{3,2},{4,7},{5,4},{6,5},{7,6},{8,11},{9,8},{10,9... | collective-permute-start | bytes 589832 | tf_op jit(solution)/shard_map/ppermute | solution.py:968
  88.5 17.8 %spectral_unmix.1 = (bf16[192,512]{1,0:T(8,128)(2,1)S(1)}, f32[16,512]{1,0:T(8,128)S(1)}) custom-call(s32[1]{0:T(128)S(6)} %copy.20.len_ref, f32[6,24,384]{2,1,0:T(8,128)S(1)} %get-tuple-element.98.taps_ref, f32[192,512]{1,0:T(8,128)S(1)} %get-tuple-element.99.x_ref, f32[192,512]{1,0:T(8,128)S(1)} %get-tuple-element.129.bh_ref, ...), custom_call_target="tpu_custom_call" | custom-call | flops 8455716864 | bytes 25165824 | tf_op jit(solution)/shard_map/spectral_unmix/pallas_call | solution.py:515
  106.6 2.6 %collective-permute-start.17 = (f32[16,512]{1,0:T(8,128)S(1)}, f32[16,512]{1,0:T(8,128)S(1)}, u32[]{:S(2)}, u32[]{:S(2)}) collective-permute-start(f32[16,512]{1,0:T(8,128)S(1)} %get-tuple-element.160.refs_0_), channel_id=1, source_target_pairs={{0,2},{1,3},{2,0},{3,1},{4,6},{5,7},{6,4},{7,5},{8,10},{9,11},{10,... | collective-permute-start | bytes 98312 | tf_op jit(solution)/shard_map/ppermute | solution.py:961
  110.4 1.9 %collective-permute-done.18.refs_3_ = f32[16,512]{1,0:T(8,128)S(1)} collective-permute-done((f32[16,512]{1,0:T(8,128)S(1)}, f32[16,512]{1,0:T(8,128)S(1)}, u32[]{:S(2)}, u32[]{:S(2)}) %collective-permute-start.18) | collective-permute-done | bytes 32800 | tf_op jit(solution)/shard_map/ppermute | solution.py:961
  117.1 9.6 %collective-permute-done.24.recv_ref.refs_6_ = bf16[576,512]{1,0:T(8,128)(2,1)S(1)} collective-permute-done((bf16[576,512]{1,0:T(8,128)(2,1)S(1)}, bf16[576,512]{1,0:T(8,128)(2,1)S(1)}, u32[]{:S(2)}, u32[]{:S(2)}) %collective-permute-start.24) | collective-permute-done | bytes 589856 | tf_op jit(solution)/shard_map/ppermute | solution.py:973
  128.0 1.9 %collective-permute-start.21 = (bf16[384,512]{1,0:T(8,128)(2,1)S(1)}, bf16[384,512]{1,0:T(8,128)(2,1)S(1)}, u32[]{:S(2)}, u32[]{:S(2)}) collective-permute-start(bf16[384,512]{1,0:T(8,128)(2,1)S(1)} %rows_message.1.refs_0_), channel_id=1, source_target_pairs={{0,1},{1,2},{2,3},{3,0},{4,5},{5,6},{6,7},{7,4},{8,9},{9,10},{10,1... | collective-permute-start | bytes 1179656 | tf_op jit(solution)/shard_map/ppermute | solution.py:961
  129.9 1.9 %collective-permute-start.19 = (bf16[384,512]{1,0:T(8,128)(2,1)S(1)}, bf16[384,512]{1,0:T(8,128)(2,1)S(1)}, u32[]{:S(2)}, u32[]{:S(2)}) collective-permute-start(bf16[384,512]{1,0:T(8,128)(2,1)S(1)} %rows_message.1.refs_0_), channel_id=1, source_target_pairs={{0,3},{1,0},{2,1},{3,2},{4,7},{5,4},{6,5},{7,6},{8,11},{9,8},{10,9... | collective-permute-start | bytes 1179656 | tf_op jit(solution)/shard_map/ppermute | solution.py:961
  131.8 9.6 %collective-permute-done.20.refs_2_ = bf16[384,512]{1,0:T(8,128)(2,1)S(1)} collective-permute-done((bf16[384,512]{1,0:T(8,128)(2,1)S(1)}, bf16[384,512]{1,0:T(8,128)(2,1)S(1)}, u32[]{:S(2)}, u32[]{:S(2)}) %collective-permute-start.20) | collective-permute-done | bytes 393248 | tf_op jit(solution)/shard_map/ppermute | solution.py:961
  143.0 11.4 %matrix_grads.1 = (f32[12,64,512]{2,1,0:T(8,128)S(1)}, bf16[2304,512]{1,0:T(8,128)(2,1)S(1)}) custom-call(bf16[12,128,3072]{2,1,0:T(8,128)(2,1)S(1)} %convolutions.1.conv_ref, bf16[512,3072]{1,0:T(8,128)(2,1)S(1)} %get-tuple-element.138.refs_0_, bf16[512,3072]{1,0:T(8,128)(2,1)S(1)} %get-tuple-element.139.refs_1_, ...), custom_call_target="tpu_custom_call" | custom-call | flops 9663676416 | bytes 9437184 | tf_op jit(solution)/shard_map/matrix_grads/pallas_call | solution.py:664
  156.4 4.1 %collective-permute-done.28.recv_ref = bf16[3104,512]{1,0:T(8,128)(2,1)S(1)} collective-permute-done((bf16[3104,512]{1,0:T(8,128)(2,1)S(1)}, bf16[3104,512]{1,0:T(8,128)(2,1)S(1)}, u32[]{:S(2)}, u32[]{:S(2)}) %collective-permute-start.28) | collective-permute-done | bytes 3178528 | tf_op jit(solution)/shard_map/ppermute | solution.py:973
  160.5 3.7 %finish.1 = (f32[12,64,512]{2,1,0:T(8,128)}, f32[3,512,512]{2,1,0:T(8,128)}, f32[16,512]{1,0:T(8,128)S(1)}, f32[512,512]{1,0:T(8,128)}, f32[512,512]{1,0:T(8,128)}, /*index=5*/f32[512,512]{1,0:T(8,128)}) custom-call(f32[12,64,512]{2,1,0:T(8,128)S(1)} %get-tuple-element.178.keep_ref, bf16[3104,512]{1,0:T(8,128)(2,1)S(1)} %join_pieces.1.send_ref, ...), custom_call_target="tpu_custom_call" | custom-call | flops 393216 | bytes 3932160 | tf_op jit(solution)/shard_map/finish/pallas_call | solution.py:944
  (74 shorter events, 28.8 us)
Async XLA Ops:
  3.9 25.8 %collective-permute-start.1 = (bf16[512,768]{1,0:T(8,128)(2,1)S(1)}, bf16[512,768]{1,0:T(8,128)(2,1)S(1)}, u32[]{:S(2)}, u32[]{:S(2)}) collective-permute-start(bf16[512,768]{1,0:T(8,128)(2,1)S(1)} %get-tuple-element.134.refs_0_), channel_id=1, source_target_pairs={{0,16},{4,20},{8,24},{12,28},{16,0},{20,4},{24,8},{28,12},{1,17},{... | collective-permute-start | bytes 2359304 | tf_op jit(solution)/shard_map/ppermute | solution.py:973
  6.9 23.8 %collective-permute-start = (bf16[512,768]{1,0:T(8,128)(2,1)S(1)}, bf16[512,768]{1,0:T(8,128)(2,1)S(1)}, u32[]{:S(2)}, u32[]{:S(2)}) collective-permute-start(bf16[512,768]{1,0:T(8,128)(2,1)S(1)} %get-tuple-element.134.refs_0_), channel_id=1, source_target_pairs={{0,8},{4,12},{8,0},{12,4},{16,24},{20,28},{24,16},{28,20},{1,9},{5... | collective-permute-start | bytes 2359304 | tf_op jit(solution)/shard_map/ppermute | solution.py:973
  29.2 9.9 %collective-permute-start.5 = (bf16[192,512]{1,0:T(8,128)(2,1)S(1)}, bf16[192,512]{1,0:T(8,128)(2,1)S(1)}, u32[]{:S(2)}, u32[]{:S(2)}) collective-permute-start(bf16[192,512]{1,0:T(8,128)(2,1)S(1)} %get-tuple-element.105.nt_ref.refs_0_), channel_id=1, source_target_pairs={{0,1},{1,2},{2,3},{3,0},{4,5},{5,6},{6,7},{7,4},{8,9},{9,10},{10,1... | collective-permute-start | bytes 589832 | tf_op jit(solution)/shard_map/ppermute | solution.py:961
  29.2 37.3 %collective-permute-start.11 = (bf16[512,768]{1,0:T(8,128)(2,1)S(1)}, bf16[512,768]{1,0:T(8,128)(2,1)S(1)}, u32[]{:S(2)}, u32[]{:S(2)}) collective-permute-start(bf16[512,768]{1,0:T(8,128)(2,1)S(1)} %get-tuple-element.134.refs_0_), channel_id=1, source_target_pairs={{0,24},{4,28},{8,16},{12,20},{16,8},{20,12},{24,0},{28,4},{1,25},{... | collective-permute-start | bytes 2359304 | tf_op jit(solution)/shard_map/ppermute | solution.py:973
  29.7 21.4 %collective-permute-start.4 = (bf16[192,512]{1,0:T(8,128)(2,1)S(1)}, bf16[192,512]{1,0:T(8,128)(2,1)S(1)}, u32[]{:S(2)}, u32[]{:S(2)}) collective-permute-start(bf16[192,512]{1,0:T(8,128)(2,1)S(1)} %get-tuple-element.105.nt_ref.refs_0_), channel_id=1, source_target_pairs={{0,2},{1,3},{2,0},{3,1},{4,6},{5,7},{6,4},{7,5},{8,10},{9,11},{10,... | collective-permute-start | bytes 589832 | tf_op jit(solution)/shard_map/ppermute | solution.py:961
  35.6 18.6 %collective-permute-start.3 = (bf16[192,512]{1,0:T(8,128)(2,1)S(1)}, bf16[192,512]{1,0:T(8,128)(2,1)S(1)}, u32[]{:S(2)}, u32[]{:S(2)}) collective-permute-start(bf16[192,512]{1,0:T(8,128)(2,1)S(1)} %get-tuple-element.108), channel_id=1, source_target_pairs={{0,1},{1,2},{2,3},{3,0},{4,5},{5,6},{6,7},{7,4},{8,9},{9,10},{10,1... | collective-permute-start | bytes 589832 | tf_op jit(solution)/shard_map/ppermute | solution.py:968
  40.2 14.1 %collective-permute-start.7 = (bf16[192,512]{1,0:T(8,128)(2,1)S(1)}, bf16[192,512]{1,0:T(8,128)(2,1)S(1)}, u32[]{:S(2)}, u32[]{:S(2)}) collective-permute-start(bf16[192,512]{1,0:T(8,128)(2,1)S(1)} %get-tuple-element.110), channel_id=1, source_target_pairs={{0,3},{1,0},{2,1},{3,2},{4,7},{5,4},{6,5},{7,6},{8,11},{9,8},{10,9... | collective-permute-start | bytes 589832 | tf_op jit(solution)/shard_map/ppermute | solution.py:968
  52.2 10.0 %collective-permute-start.6 = (bf16[192,512]{1,0:T(8,128)(2,1)S(1)}, bf16[192,512]{1,0:T(8,128)(2,1)S(1)}, u32[]{:S(2)}, u32[]{:S(2)}) collective-permute-start(bf16[192,512]{1,0:T(8,128)(2,1)S(1)} %get-tuple-element.112), channel_id=1, source_target_pairs={{0,2},{1,3},{2,0},{3,1},{4,6},{5,7},{6,4},{7,5},{8,10},{9,11},{10,... | collective-permute-start | bytes 589832 | tf_op jit(solution)/shard_map/ppermute | solution.py:968
  62.6 17.4 %collective-permute-start.12 = (bf16[4,3,64,512]{3,2,1,0:T(8,128)(2,1)S(1)}, bf16[4,3,64,512]{3,2,1,0:T(8,128)(2,1)S(1)}, u32[]{:S(2)}, u32[]{:S(2)}) collective-permute-start(bf16[4,3,64,512]{3,2,1,0:T(8,128)(2,1)S(1)} %get-tuple-element.152), channel_id=1, source_target_pairs={{0,4},{4,0},{8,12},{12,8},{16,20},{20,16},{24,28},{28,24},{1,5},{5... | collective-permute-start | bytes 2359304 | tf_op jit(solution)/shard_map/ppermute | solution.py:973
  62.7 16.4 %collective-permute-start.10 = (bf16[192,512]{1,0:T(8,128)(2,1)S(1)}, bf16[192,512]{1,0:T(8,128)(2,1)S(1)}, u32[]{:S(2)}, u32[]{:S(2)}) collective-permute-start(bf16[192,512]{1,0:T(8,128)(2,1)S(1)} %get-tuple-element.141.refs_0_), channel_id=1, source_target_pairs={{0,1},{1,2},{2,3},{3,0},{4,5},{5,6},{6,7},{7,4},{8,9},{9,10},{10,1... | collective-permute-start | bytes 589832 | tf_op jit(solution)/shard_map/ppermute | solution.py:961
  62.7 17.3 %collective-permute-start.9 = (bf16[192,512]{1,0:T(8,128)(2,1)S(1)}, bf16[192,512]{1,0:T(8,128)(2,1)S(1)}, u32[]{:S(2)}, u32[]{:S(2)}) collective-permute-start(bf16[192,512]{1,0:T(8,128)(2,1)S(1)} %get-tuple-element.141.refs_0_), channel_id=1, source_target_pairs={{0,2},{1,3},{2,0},{3,1},{4,6},{5,7},{6,4},{7,5},{8,10},{9,11},{10,... | collective-permute-start | bytes 589832 | tf_op jit(solution)/shard_map/ppermute | solution.py:961
  65.9 14.2 %collective-permute-start.8 = (bf16[192,512]{1,0:T(8,128)(2,1)S(1)}, bf16[192,512]{1,0:T(8,128)(2,1)S(1)}, u32[]{:S(2)}, u32[]{:S(2)}) collective-permute-start(bf16[192,512]{1,0:T(8,128)(2,1)S(1)} %get-tuple-element.141.refs_0_), channel_id=1, source_target_pairs={{0,3},{1,0},{2,1},{3,2},{4,7},{5,4},{6,5},{7,6},{8,11},{9,8},{10,9... | collective-permute-start | bytes 589832 | tf_op jit(solution)/shard_map/ppermute | solution.py:961
  80.4 32.7 %collective-permute-start.22 = (bf16[1152,512]{1,0:T(8,128)(2,1)S(1)}, bf16[1152,512]{1,0:T(8,128)(2,1)S(1)}, u32[]{:S(2)}, u32[]{:S(2)}) collective-permute-start(bf16[1152,512]{1,0:T(8,128)(2,1)S(1)} %get-tuple-element.164), channel_id=1, source_target_pairs={{0,8},{4,12},{8,0},{12,4},{16,24},{20,28},{24,16},{28,20},{1,9},{5... | collective-permute-start | bytes 3538952 | tf_op jit(solution)/shard_map/ppermute | solution.py:973
  81.0 32.1 %collective-permute-start.23 = (bf16[768,512]{1,0:T(8,128)(2,1)S(1)}, bf16[768,512]{1,0:T(8,128)(2,1)S(1)}, u32[]{:S(2)}, u32[]{:S(2)}) collective-permute-start(bf16[768,512]{1,0:T(8,128)(2,1)S(1)} %get-tuple-element.154.refs_3_), channel_id=1, source_target_pairs={{0,16},{4,20},{8,24},{12,28},{16,0},{20,4},{24,8},{28,12},{1,17},{... | collective-permute-start | bytes 2359304 | tf_op jit(solution)/shard_map/ppermute | solution.py:973
  81.9 24.4 %collective-permute-start.13 = (bf16[192,512]{1,0:T(8,128)(2,1)S(1)}, bf16[192,512]{1,0:T(8,128)(2,1)S(1)}, u32[]{:S(2)}, u32[]{:S(2)}) collective-permute-start(bf16[192,512]{1,0:T(8,128)(2,1)S(1)} %get-tuple-element.156), channel_id=1, source_target_pairs={{0,1},{1,2},{2,3},{3,0},{4,5},{5,6},{6,7},{7,4},{8,9},{9,10},{10,1... | collective-permute-start | bytes 589832 | tf_op jit(solution)/shard_map/ppermute | solution.py:968
  86.1 20.2 %collective-permute-start.14 = (bf16[192,512]{1,0:T(8,128)(2,1)S(1)}, bf16[192,512]{1,0:T(8,128)(2,1)S(1)}, u32[]{:S(2)}, u32[]{:S(2)}) collective-permute-start(bf16[192,512]{1,0:T(8,128)(2,1)S(1)} %get-tuple-element.157), channel_id=1, source_target_pairs={{0,2},{1,3},{2,0},{3,1},{4,6},{5,7},{6,4},{7,5},{8,10},{9,11},{10,... | collective-permute-start | bytes 589832 | tf_op jit(solution)/shard_map/ppermute | solution.py:968
  86.1 20.2 %collective-permute-start.15 = (bf16[192,512]{1,0:T(8,128)(2,1)S(1)}, bf16[192,512]{1,0:T(8,128)(2,1)S(1)}, u32[]{:S(2)}, u32[]{:S(2)}) collective-permute-start(bf16[192,512]{1,0:T(8,128)(2,1)S(1)} %get-tuple-element.158), channel_id=1, source_target_pairs={{0,3},{1,0},{2,1},{3,2},{4,7},{5,4},{6,5},{7,6},{8,11},{9,8},{10,9... | collective-permute-start | bytes 589832 | tf_op jit(solution)/shard_map/ppermute | solution.py:968
  113.2 13.5 %collective-permute-start.24 = (bf16[576,512]{1,0:T(8,128)(2,1)S(1)}, bf16[576,512]{1,0:T(8,128)(2,1)S(1)}, u32[]{:S(2)}, u32[]{:S(2)}) collective-permute-start(bf16[576,512]{1,0:T(8,128)(2,1)S(1)} %get-tuple-element.167), channel_id=1, source_target_pairs={{0,16},{4,20},{8,24},{12,28},{16,0},{20,4},{24,8},{28,12},{1,17},{... | collective-permute-start | bytes 1769480 | tf_op jit(solution)/shard_map/ppermute | solution.py:973
  114.5 27.0 %collective-permute-start.20 = (bf16[384,512]{1,0:T(8,128)(2,1)S(1)}, bf16[384,512]{1,0:T(8,128)(2,1)S(1)}, u32[]{:S(2)}, u32[]{:S(2)}) collective-permute-start(bf16[384,512]{1,0:T(8,128)(2,1)S(1)} %rows_message.1.refs_0_), channel_id=1, source_target_pairs={{0,2},{1,3},{2,0},{3,1},{4,6},{5,7},{6,4},{7,5},{8,10},{9,11},{10,... | collective-permute-start | bytes 1179656 | tf_op jit(solution)/shard_map/ppermute | solution.py:961
  115.4 27.6 %collective-permute-start.25 = (bf16[384,512]{1,0:T(8,128)(2,1)S(1)}, bf16[384,512]{1,0:T(8,128)(2,1)S(1)}, u32[]{:S(2)}, u32[]{:S(2)}) collective-permute-start(bf16[384,512]{1,0:T(8,128)(2,1)S(1)} %get-tuple-element.170), channel_id=1, source_target_pairs={{0,8},{4,12},{8,0},{12,4},{16,24},{20,28},{24,16},{28,20},{1,9},{5... | collective-permute-start | bytes 1179656 | tf_op jit(solution)/shard_map/ppermute | solution.py:973
  126.7 14.7 %collective-permute-start.26 = (bf16[224,512]{1,0:T(8,128)(2,1)S(1)}, bf16[224,512]{1,0:T(8,128)(2,1)S(1)}, u32[]{:S(2)}, u32[]{:S(2)}) collective-permute-start(bf16[224,512]{1,0:T(8,128)(2,1)S(1)} %last_sum.1.own_ref), channel_id=1, source_target_pairs={{0,16},{4,20},{8,24},{12,28},{16,0},{20,4},{24,8},{28,12},{1,17},{... | collective-permute-start | bytes 688136 | tf_op jit(solution)/shard_map/ppermute | solution.py:973
  128.0 26.5 %collective-permute-start.21 = (bf16[384,512]{1,0:T(8,128)(2,1)S(1)}, bf16[384,512]{1,0:T(8,128)(2,1)S(1)}, u32[]{:S(2)}, u32[]{:S(2)}) collective-permute-start(bf16[384,512]{1,0:T(8,128)(2,1)S(1)} %rows_message.1.refs_0_), channel_id=1, source_target_pairs={{0,1},{1,2},{2,3},{3,0},{4,5},{5,6},{6,7},{7,4},{8,9},{9,10},{10,1... | collective-permute-start | bytes 1179656 | tf_op jit(solution)/shard_map/ppermute | solution.py:961
  129.9 24.5 %collective-permute-start.19 = (bf16[384,512]{1,0:T(8,128)(2,1)S(1)}, bf16[384,512]{1,0:T(8,128)(2,1)S(1)}, u32[]{:S(2)}, u32[]{:S(2)}) collective-permute-start(bf16[384,512]{1,0:T(8,128)(2,1)S(1)} %rows_message.1.refs_0_), channel_id=1, source_target_pairs={{0,3},{1,0},{2,1},{3,2},{4,7},{5,4},{6,5},{7,6},{8,11},{9,8},{10,9... | collective-permute-start | bytes 1179656 | tf_op jit(solution)/shard_map/ppermute | solution.py:961
  141.5 13.0 %collective-permute-start.27 = (bf16[416,512]{1,0:T(8,128)(2,1)S(1)}, bf16[416,512]{1,0:T(8,128)(2,1)S(1)}, u32[]{:S(2)}, u32[]{:S(2)}) collective-permute-start(bf16[416,512]{1,0:T(8,128)(2,1)S(1)} %pair_up.2.own_ref), channel_id=1, source_target_pairs={{0,8},{4,12},{8,0},{12,4},{16,24},{20,28},{24,16},{28,20},{1,9},{5... | collective-permute-start | bytes 1277960 | tf_op jit(solution)/shard_map/ppermute | solution.py:973
  (12 other events, 111.9 us)

commit v2 on v1

--- a/solution.py
+++ b/solution.py
@@ -74,10 +74,12 @@
 
 
 def norm_kernel(
-    n, share, order, len_ref, x_ref, gain_ref, u_ref, ut_ref, own_ref, lag_ref, scr
+    n, share, order, len_ref, x_ref, gain_ref, filt_ref,
+    u_ref, ut_ref, own_ref, lag_ref, taps_ref, nat_ref, scr, scr_f,
 ):
     length, width = x_ref.shape
     m = lax.axis_index("mp")
+    filt = nat_ref.shape[0]
     x = x_ref[...].astype(F32)
     r1 = lax.rsqrt(jnp.mean(x * x, axis=-1, keepdims=True) + EPS)
     row = lax.broadcasted_iota(jnp.int32, (length, 1), 0)
@@ -99,30 +101,6 @@
             lag_ref[odd * (share // 2) : (odd + 1) * (share // 2), at : at + width] = every_second(
                 scr, m * share + odd + 8 - lag, share // 2
             ).astype(BF)
-
-
-def first_norm(lengths, x, gains, n, order):
-    length, width = x.shape
-    share = length // n
-    return pl.pallas_call(
-        functools.partial(norm_kernel, n, share, order),
-        in_specs=[smem(), whole(), whole()],
-        out_specs=[whole()] * 4,
-        out_shape=[
-            jax.ShapeDtypeStruct((2, length // 2, width), BF),
-            jax.ShapeDtypeStruct((width, length), BF),
-            jax.ShapeDtypeStruct((share, width), F32),
-            jax.ShapeDtypeStruct((share, order * width), BF),
-        ],
-        scratch_shapes=[pltpu.VMEM((width // 128, length + 8, 128), F32)],
-        compiler_params=params(),
-        cost_estimate=cost(10 * x.size, 6 * x.size),
-        name="first_norm",
-    )(lengths, x, gains)
-
-
-def taps_kernel(filt_ref, taps_ref, nat_ref, scr_f):
-    filt, length = filt_ref.shape
     half = length // 2
     natural = filt_ref[...].astype(F32)
     nat_ref[...] = natural
@@ -142,21 +120,30 @@
     taps_ref[5] = pltpu.roll(odd, 1, 1)
 
 
-def filter_taps(filters):
-    filt, length = filters.shape
-    return pl.pallas_call(
-        taps_kernel,
-        in_specs=[whole()],
-        out_specs=[whole()] * 2,
+def first_norm(lengths, x, gains, filters, n, order):
+    length, width = x.shape
+    share = length // n
+    filt = filters.shape[0]
+    return pl.pallas_call(
+        functools.partial(norm_kernel, n, share, order),
+        in_specs=[smem()] + [whole()] * 3,
+        out_specs=[whole()] * 6,
         out_shape=[
+            jax.ShapeDtypeStruct((2, length // 2, width), BF),
+            jax.ShapeDtypeStruct((width, length), BF),
+            jax.ShapeDtypeStruct((share, width), F32),
+            jax.ShapeDtypeStruct((share, order * width), BF),
             jax.ShapeDtypeStruct((6, filt, length // 2), F32),
             jax.ShapeDtypeStruct((filt, length), F32),
         ],
-        scratch_shapes=[pltpu.VMEM((1, length, 128), F32)],
-        compiler_params=params(),
-        cost_estimate=cost(10 * filters.size, 6 * filters.size),
-        name="filter_taps",
-    )(filters)
+        scratch_shapes=[
+            pltpu.VMEM((width // 128, length + 8, 128), F32),
+            pltpu.VMEM((1, length, 128), F32),
+        ],
+        compiler_params=params(),
+        cost_estimate=cost(10 * x.size, 6 * x.size),
+        name="first_norm",
+    )(lengths, x, gains, filters)
 
 
 def fetch_matrices(j, steps, kb, stu_hbm, w_buf, sems):
@@ -361,8 +348,9 @@
         for i in range(3):
             mine = pl.multiple_of((chip + core) * rows, 16)
             other = pl.multiple_of((chip + 1 - core) * rows, 16)
-            keep_ref[r, i] = scr[i, pl.ds(mine, rows), :]
-            send_ref[r, i] = scr[i, pl.ds(other, rows), :]
+            at = (3 * r + i) * rows
+            keep_ref[at : at + rows, :] = scr[i, pl.ds(mine, rows), :]
+            send_ref[at : at + rows, :] = scr[i, pl.ds(other, rows), :]
 
 
 def ffn_grads(cot, dw, nts, acts, bgs, bus, groups):
@@ -373,8 +361,7 @@
     out_shape = [jax.ShapeDtypeStruct((share, width), BF)] * n
     scratch = []
     if groups:
-        part = (groups, 3, width // (2 * groups), width)
-        out_shape += [jax.ShapeDtypeStruct(part, BF)] * 2
+        out_shape += [jax.ShapeDtypeStruct((3 * width // 2, width), BF)] * 2
         scratch = [pltpu.VMEM((3, width, width), BF)]
     else:
         out_shape += [
@@ -583,9 +570,7 @@
             pltpu.VMEM((groups * block, length), BF),
         ],
         compiler_params=params(),
-        cost_estimate=cost(
-            4 * own * groups * block * length * length // 3, 2 * own * groups * block * length
-        ),
+        cost_estimate=cost(0, 0),
         name="convolutions",
     )(filt, *uts)
 
@@ -614,7 +599,7 @@
         out_specs=[whole()] * order,
         out_shape=[shape] * order,
         compiler_params=params(),
-        cost_estimate=cost(order * groups * width * length, 4 * order * groups * width * length),
+        cost_estimate=cost(0, 0),
         name="lagged",
     )(*uts)
 
@@ -676,7 +661,7 @@
             pltpu.VMEM((step, block, width), F32),
         ],
         compiler_params=params(),
-        cost_estimate=cost(2 * (conv.size + order * width * depth) * width, 2 * conv.size),
+        cost_estimate=cost(0, 0),
         name="matrix_grads",
     )(conv, *lags, *backs)
 
@@ -756,86 +741,118 @@
     )(*pieces)
 
 
-def halve_kernel(kept, sent, keep_ref, recv_ref, *out_refs):
-    rows = recv_ref.shape[0] // keep_ref.shape[0]
-    total = keep_ref[...].astype(F32) + recv_ref[...].astype(F32)
-    for ref, which in zip(out_refs, (kept, sent)):
-        for k, r in enumerate(which):
-            ref[k] = total[r].astype(BF)
-
-
-def halve(keep, recv, kept, sent):
-    part = keep.shape[1:]
-    return pl.pallas_call(
-        functools.partial(halve_kernel, kept, sent),
+def cores_sum_kernel(keep_ref, recv_ref, sum_ref, to_x, to_y):
+    total = (keep_ref[...].astype(F32) + recv_ref[...].astype(F32)).astype(BF)
+    sum_ref[...] = total
+    half = total.shape[0] // 8
+    for k, r in enumerate((1, 3)):
+        to_x[k * half : (k + 1) * half, :] = total[2 * r * half : (2 * r + 1) * half]
+    for k, r in enumerate((2, 3)):
+        to_y[k * half : (k + 1) * half, :] = total[(2 * r + 1) * half : (2 * r + 2) * half]
+
+
+def cores_sum(keep, recv):
+    size, width = keep.shape
+    return pl.pallas_call(
+        cores_sum_kernel,
         in_specs=[whole()] * 2,
-        out_specs=[whole()] * 2,
-        out_shape=[jax.ShapeDtypeStruct((len(w),) + part, BF) for w in (kept, sent)],
+        out_specs=[whole()] * 3,
+        out_shape=[jax.ShapeDtypeStruct((rows, width), BF) for rows in (size, size // 4, size // 4)],
         compiler_params=params(),
         cost_estimate=cost(keep.size, 8 * keep.size),
-        name="halve",
+        name="cores_sum",
     )(keep, recv)
 
 
-def pack_kernel(n, share, extra, *refs):
-    pieces, rest = refs[:n], refs[n:]
+def pack_kernel(n, share, extras, *refs):
+    pieces, extra_refs, out_refs = refs[:n], refs[n : n + extras], refs[n + extras :]
     m = lax.axis_index("mp")
-    out_refs = rest[1:] if extra else rest
     for r in range(n):
         start = pl.multiple_of(lax.rem(m + r, n) * share, 16)
         for ref in out_refs:
             ref[pl.ds(start, share), :] = pieces[r][...]
-    if extra:
-        rows = rest[0].shape[1]
-        for k in range(rest[0].shape[0]):
-            at = n * share + k * rows
-            out_refs[1][at : at + rows, :] = rest[0][k]
-
-
-def pack_rows(pieces, extra=None):
+    for ref, extra in zip(out_refs[1:], extra_refs):
+        ref[n * share :, :] = extra[...]
+
+
+def pack_rows(pieces, extras=()):
     n = len(pieces)
     share, width = pieces[0].shape
-    shapes = [(n * share, width)]
-    if extra is not None:
-        shapes.append((n * share + extra.shape[0] * extra.shape[1], width))
-    args = list(pieces) + ([] if extra is None else [extra])
-    return pl.pallas_call(
-        functools.partial(pack_kernel, n, share, extra is not None),
-        in_specs=[whole()] * len(args),
-        out_specs=[whole()] * len(shapes),
-        out_shape=[jax.ShapeDtypeStruct(shape, BF) for shape in shapes],
+    rows = [n * share] + [n * share + extra.shape[0] for extra in extras]
+    return pl.pallas_call(
+        functools.partial(pack_kernel, n, share, len(extras)),
+        in_specs=[whole()] * (n + len(extras)),
+        out_specs=[whole()] * len(rows),
+        out_shape=[jax.ShapeDtypeStruct((r, width), BF) for r in rows],
         compiler_params=params(),
         cost_estimate=cost(n * share * width, 6 * n * share * width),
         name="pack_rows",
-    )(*args)
-
-
-def turn_kernel(keep_ref, x_ref, y_ref, keep_out, to_y, to_x):
-    length = y_ref.shape[0]
-    half, rows = length // 2, keep_ref.shape[1]
-    keep_out[...] = keep_ref[0].astype(F32) + x_ref[length : length + rows, :].astype(F32)
-    sent = keep_ref[1].astype(F32) + x_ref[length + rows :, :].astype(F32)
-    to_y[:half, :] = x_ref[:half, :]
-    to_y[half:, :] = sent.astype(BF)
-    to_x[...] = y_ref[half:, :]
-
-
-def turn(keep, over_x, over_y):
-    length, width = over_y.shape
-    rows = keep.shape[1]
+    )(*pieces, *extras)
+
+
+def turn_kernel(x_ref, y_ref, sum_ref, gain_ref, part_ref, to_y, to_x):
+    size = part_ref.shape[0] // 2
+    half = size // 2
+    length = x_ref.shape[0] - size
+    gains = split_gains(gain_ref[...])
+    for ref, came, at, chunks in ((to_y, x_ref, 0, (0, 2)), (to_x, y_ref, 1, (0, 1))):
+        start = at * length // 2
+        ref[: length // 2, :] = came[start : start + length // 2, :]
+        for k, r in enumerate(chunks):
+            own = sum_ref[(2 * r + at) * half : (2 * r + at + 1) * half, :].astype(F32)
+            there = length + k * half
+            total = (own + came[there : there + half, :].astype(F32)).astype(BF)
+            part_ref[at * size + k * half : at * size + (k + 1) * half, :] = total
+            ref[length // 2 + k * half : length // 2 + (k + 1) * half, :] = total
+        ref[length // 2 + size :, :] = gains
+
+
+def turn(over_x, over_y, sums, gains):
+    size, width = sums.shape[0] // 4, sums.shape[1]
+    rows = (over_x.shape[0] - size) // 2 + size + 32
     return pl.pallas_call(
         turn_kernel,
-        in_specs=[whole()] * 3,
+        in_specs=[whole()] * 4,
         out_specs=[whole()] * 3,
         out_shape=[
-            jax.ShapeDtypeStruct((rows, width), F32),
-            jax.ShapeDtypeStruct((length // 2 + rows, width), BF),
-            jax.ShapeDtypeStruct((length // 2, width), BF),
+            jax.ShapeDtypeStruct((2 * size, width), BF),
+            jax.ShapeDtypeStruct((rows, width), BF),
+            jax.ShapeDtypeStruct((rows, width), BF),
         ],
         compiler_params=params(),
         cost_estimate=cost(over_x.size, 8 * over_x.size),
         name="turn",
-    )(keep, over_x, over_y)
+    )(over_x, over_y, sums, gains)
+
+
+def chunks_kernel(part_ref, from_y, from_x, to_x, to_y):
+    size = part_ref.shape[0] // 2
+    half = size // 2
+    at = from_y.shape[0] - 32 - size
+    for ref, came, start in ((to_x, from_y, 0), (to_y, from_x, size)):
+        for k in range(2):
+            there = at + (1 - k) * half
+            ref[k * half : (k + 1) * half, :] = (
+                part_ref[start + k * half : start + (k + 1) * half, :].astype(F32)
+                + came[there : there + half, :].astype(F32)
+            ).astype(BF)
+    to_x[size:, :] = from_y[at + size :, :]
+
+
+def whole_chunks(parts, from_y, from_x):
+    size, width = parts.shape[0] // 2, parts.shape[1]
+    return pl.pallas_call(
+        chunks_kernel,
+        in_specs=[whole()] * 3,
+        out_specs=[whole()] * 2,
+        out_shape=[
+            jax.ShapeDtypeStruct((size + 32, width), BF),
+            jax.ShapeDtypeStruct((size, width), BF),
+        ],
+        compiler_params=params(),
+        cost_estimate=cost(parts.size, 8 * parts.size),
+        name="whole_chunks",
+    )(parts, from_y, from_x)
 
 
 def split_gains(both):
@@ -848,57 +865,38 @@
     return gains[:16].astype(F32) + gains[16:].astype(F32)
 
 
-def last_sum_kernel(keep_ref, recv_ref, gain_ref, out_ref):
-    rows = keep_ref.shape[0]
-    at = recv_ref.shape[0] - rows
-    out_ref[:rows, :] = (keep_ref[...] + recv_ref[at:, :].astype(F32)).astype(BF)
-    out_ref[rows:, :] = split_gains(gain_ref[...])
-
-
-def last_sum(keep, recv, gains):
-    rows, width = keep.shape
-    return pl.pallas_call(
-        last_sum_kernel,
-        in_specs=[whole()] * 3,
+def chips_sum_kernel(gain_ref, from_x, from_y, recv_ref, out_ref, scr):
+    chip = lax.axis_index("dp") // 2
+    scr[chip] = joined(split_gains(gain_ref[...]))
+    for ref, bits in ((from_x, 1), (from_y, 2), (recv_ref, 3)):
+        scr[chip ^ bits] = joined(ref[ref.shape[0] - 32 :, :])
+    out_ref[...] = ((scr[0] + scr[1]) + scr[2]) + scr[3]
+
+
+def chips_sum(gains, from_x, from_y, recv):
+    return pl.pallas_call(
+        chips_sum_kernel,
+        in_specs=[whole()] * 4,
         out_specs=whole(),
-        out_shape=jax.ShapeDtypeStruct((rows + 32, width), BF),
-        compiler_params=params(),
-        cost_estimate=cost(keep.size, 8 * keep.size),
-        name="last_sum",
-    )(keep, recv, gains)
-
-
-def pair_kernel(own_ref, recv_ref, out_ref):
-    rows = own_ref.shape[0] - 32
-    out_ref[:rows, :] = own_ref[:rows, :]
-    out_ref[rows : 2 * rows, :] = recv_ref[:rows, :]
-    out_ref[2 * rows :, :] = split_gains(joined(own_ref[rows:, :]) + joined(recv_ref[rows:, :]))
-
-
-def pair_up(own, recv):
-    rows, width = own.shape[0] - 32, own.shape[1]
-    return pl.pallas_call(
-        pair_kernel,
-        in_specs=[whole()] * 2,
-        out_specs=whole(),
-        out_shape=jax.ShapeDtypeStruct((2 * rows + 32, width), BF),
-        compiler_params=params(),
-        cost_estimate=cost(own.size, 8 * own.size),
-        name="pair_up",
-    )(own, recv)
-
-
-def join_kernel(*refs):
+        out_shape=jax.ShapeDtypeStruct(gains.shape, F32),
+        scratch_shapes=[pltpu.VMEM((4,) + gains.shape, F32)],
+        compiler_params=params(),
+        cost_estimate=cost(4 * gains.size, 16 * gains.size),
+        name="chips_sum",
+    )(gains, from_x, from_y, recv)
+
+
+def join_kernel(counts, *refs):
     at = 0
-    for ref in refs[:-1]:
-        refs[-1][at : at + ref.shape[0], :] = ref[...]
-        at += ref.shape[0]
-
-
-def join_pieces(pieces):
-    rows = sum(p.shape[0] for p in pieces)
-    return pl.pallas_call(
-        join_kernel,
+    for ref, count in zip(refs, counts):
+        refs[-1][at : at + count, :] = ref[:count, :]
+        at += count
+
+
+def join_pieces(pieces, counts):
+    rows = sum(counts)
+    return pl.pallas_call(
+        functools.partial(join_kernel, counts),
         in_specs=[whole()] * len(pieces),
         out_specs=whole(),
         out_shape=jax.ShapeDtypeStruct((rows, pieces[0].shape[1]), pieces[0].dtype),
@@ -908,25 +906,25 @@
     )(*pieces)
 
 
-def finish_kernel(chips, keep_ref, send_ref, recv_ref, stu_ref, ar_ref, *more_refs):
+def finish_kernel(custom, keep_ref, send_ref, recv_ref, stu_ref, ar_ref, *w_refs):
     own, half, width = keep_ref.shape
-    d = lax.axis_index("dp")
-    core = lax.rem(d, 2)
-    w_refs = more_refs[1:]
-    groups, count = len(chips), len(w_refs)
-    rows = width // (2 * groups) if groups else 0
-    base = groups * count * rows
-    if groups:
-        gains = slice(base, base + 32)
-        more_refs[0][...] = joined(send_ref[gains, :]) + joined(recv_ref[gains, :])
-        base += 32
-    for r in range(groups):
-        chip = ((d // 2) ^ r) * 2
-        for ref, which in ((send_ref, chip + core), (recv_ref, chip + 1 - core)):
-            start = pl.multiple_of(which * rows, 16)
-            for i, out in enumerate(w_refs):
-                at = (chips[r] * count + i) * rows
-                out[pl.ds(start, rows), :] = ref[at : at + rows, :].astype(F32)
+    base = 0
+    if custom:
+        d = lax.axis_index("dp")
+        core = lax.rem(d, 2)
+        rows = width // 8
+        part = 3 * rows // 2
+        base = 8 * part
+        for r in range(4):
+            chip = ((d // 2) ^ r) * 2
+            upper, lower = (0, 4, 1, 5)[r] * part, (2, 3, 6, 7)[r] * part
+            for ref, which in ((send_ref, chip + core), (recv_ref, chip + 1 - core)):
+                start = pl.multiple_of(which * rows, 16)
+                chunk = jnp.concatenate(
+                    [ref[upper : upper + part, :], ref[lower : lower + part, :]], axis=0
+                ).astype(F32)
+                for i, out in enumerate(w_refs):
+                    out[pl.ds(start, rows), :] = chunk[i * rows : (i + 1) * rows]
     for k in range(own):
         at = base + k * half
         stu_ref[k] = keep_ref[k] + recv_ref[at : at + half, :].astype(F32)
@@ -937,12 +935,11 @@
         ].astype(F32)
 
 
-def finish(keep, send, recv, order, chips):
+def finish(keep, send, recv, order, custom):
     width = keep.shape[2]
-    more = [jax.ShapeDtypeStruct((16, width), F32)] if chips else []
-    more += [jax.ShapeDtypeStruct((width, width), F32)] * (3 if chips else 0)
-    return pl.pallas_call(
-        functools.partial(finish_kernel, chips),
+    more = [jax.ShapeDtypeStruct((width, width), F32)] * (3 if custom else 0)
+    return pl.pallas_call(
+        functools.partial(finish_kernel, custom),
         in_specs=[whole()] * 3,
         out_specs=[whole()] * (2 + len(more)),
         out_shape=[
@@ -957,24 +954,22 @@
 
 
 def fetch_shifted(value, axis, n):
-    return [value] + [
-        lax.ppermute(value, axis, [(i, (i - r) % n) for i in range(n)]) for r in range(1, n)
-    ]
+    pieces = {0: value}
+    for r in sorted(range(1, n), key=lambda r: min(r, n - r)):
+        pieces[r] = lax.ppermute(value, axis, [(i, (i - r) % n) for i in range(n)])
+    return [pieces[r] for r in range(n)]
 
 
 def send_shifted(pieces, axis):
     n = len(pieces)
-    return [pieces[0]] + [
-        lax.ppermute(pieces[r], axis, [(i, (i + r) % n) for i in range(n)]) for r in range(1, n)
-    ]
+    moved = {0: pieces[0]}
+    for r in sorted(range(1, n), key=lambda r: min(r, n - r)):
+        moved[r] = lax.ppermute(pieces[r], axis, [(i, (i + r) % n) for i in range(n)])
+    return [moved[r] for r in range(n)]
 
 
 def swap(value, axis, n, bits):
     return lax.ppermute(value, axis, [(i, i ^ bits) for i in range(n)])
-
-
-def merge_rows(value):
-    return value.reshape(value.shape[0], -1, value.shape[-1])
 
 
 def after(values, first):
@@ -997,8 +992,9 @@
     lengths = lengths.astype(jnp.int32)
     both_gains = jnp.stack([first_gain, second_gain])
 
-    u, ut, x_own, u_lags = first_norm(lengths, inputs, both_gains, n, order)
-    taps, natural = filter_taps(filters.T)
+    u, ut, x_own, u_lags, taps, natural = first_norm(
+        lengths, inputs, both_gains, filters.T, n, order
+    )
     uts = [ut] + [swap(ut, "dp", n_dp, 2 * r) for r in range(1, 3)]
     hidden, nt = spectral_mix(
         lengths, taps, x_own, u, u_lags, both_gains, stu_weight, ar_weight, share, 4
@@ -1007,7 +1003,7 @@
     weights = (cotangent, gate_weight, up_weight, down_weight)
     parts = {0: feed_forward(0, n, after(nt, uts[1:3]), *weights)}
     last = 0
-    for r in sorted(range(1, n), key=lambda r: min(r, n - r)):
+    for r in sorted(range(1, n), key=lambda r: -min(r, n - r)):
         first = parts[last][0]
         parts[r] = feed_forward(r, n, after(nts[r], first), *weights)
         last = r
@@ -1018,43 +1014,43 @@
     custom = n_dp == 8 and gate_weight.shape[1] == width
     grads = ffn_grads(cotangent, down_weight, nts, acts, bgs, bus, groups if custom else 0)
     out_parts, grads = grads[:n], grads[n:]
-    bns = [bns[0]] + after(bns[1:], grads[0])
+    bns = [bns[0]] + after(bns[1:], (grads[0], uts))
     back_hidden, back_rows, second_part = mid_norm(lengths, hidden, cotangent, both_gains, bns)
     backs = fetch_shifted(back_rows, "mp", n)
-    uts = after(uts, back_rows)
-    conv = [convolutions(natural, uts[r : r + 4], own, groups) for r in range(0, groups, 4)]
-    lags = [lagged(uts[r : r + 4], order) for r in range(0, groups, 4)]
-    backs = after(backs, (conv, lags))
     if custom:
         w_keep, w_send = grads
-        w_send = swap(after(w_send, back_rows), "dp", n_dp, 1)
-        w_keep, w_send = halve(w_keep, w_send, (0, 2), (1, 3))
-        own_back, to_x = pack_rows(backs, merge_rows(w_send))
-        over_x, over_y = swap(to_x, "dp", n_dp, 2), swap(own_back, "dp", n_dp, 4)
+        w_parts, to_x, to_y = cores_sum(w_keep, swap(after(w_send, back_rows), "dp", n_dp, 1))
+        own_back, to_x, to_y = pack_rows(backs, (to_x, to_y))
+        over_x, over_y = swap(to_x, "dp", n_dp, 2), swap(to_y, "dp", n_dp, 4)
     else:
         (own_back,) = pack_rows(backs)
     out_sums = send_shifted(after(out_parts, own_back), "mp")
     ig, gains = spectral_unmix(
         lengths, taps, x_own, back_hidden, second_part, both_gains, stu_weight, ar_weight, backs, 4
     )
-    conv, hidden = after((conv, hidden), ig)
+    uts, hidden = after((uts, hidden), ig)
+    conv = [convolutions(natural, uts[r : r + 4], own, groups) for r in range(0, groups, 4)]
+    lags = [lagged(uts[r : r + 4], order) for r in range(0, groups, 4)]
     message = rows_message(ig, hidden, out_sums)
-    gains = ordered_sum(fetch_shifted(after(gains, message), "mp", n), "mp", 0)
-    message = after(message, gains)
     messages = fetch_shifted(message, "mp", n)
     if custom:
-        w_keep, to_y, to_x = turn(merge_rows(w_keep), after(over_x, message), over_y)
+        w_parts, to_y, to_x = turn(after(over_x, message), over_y, w_parts, gains)
         from_y, from_x = swap(to_y, "dp", n_dp, 4), swap(to_x, "dp", n_dp, 2)
         all_backs = [own_back, over_x, over_y, from_y, from_x]
         half = length // 2
         rows = ((0, 0, length), (1, 0, length), (2, 0, length), (3, 0, half), (3, half, half))
-        w_sum = last_sum(w_keep, from_y, gains)
-        conv = after(conv, w_sum)
+        to_x, to_y = whole_chunks(after(w_parts, conv), from_y, from_x)
+        w_all = [to_x, to_y, swap(to_x, "dp", n_dp, 2), swap(to_y, "dp", n_dp, 4)]
+        gains = chips_sum(gains, from_x, from_y, w_all[2])
+        gains = ordered_sum([gains, swap(gains, "dp", n_dp, 1)], "dp", 0)
     else:
         all_backs = [own_back] + [swap(own_back, "dp", n_dp, 2 * r) for r in range(1, groups)]
         rows = tuple((r, 0, length) for r in range(min(groups, 4)))
-
-    conv = after(conv, (message, messages[n // 2]))
+        gains = ordered_sum([gains] + [swap(gains, "dp", n_dp, r) for r in range(1, n_dp)], "dp", 1)
+    gains_dp = gains
+    gains = fetch_shifted(gains, "mp", n)
+
+    conv = after(conv, message)
     if len(conv) == 1:
         keep, send = matrix_grads(conv[0], lags[0], all_backs, rows)
     else:
@@ -1064,17 +1060,17 @@
         ]
         keep = ordered_sum([k for k, _ in some], "dp", 8)
         send = ordered_sum([k.astype(F32) for _, k in some], "dp", 8).astype(BF)
-    input_grad, output = finish_rows(after(messages, (gains, send)))
+    input_grad, output = finish_rows(after(messages, send))
     if custom:
-        w_pair = pair_up(w_sum, swap(w_sum, "dp", n_dp, 4))
-        w_all = pair_up(w_pair, after(swap(w_pair, "dp", n_dp, 2), messages))
-        send = join_pieces([w_all, send])
+        w_all = after(w_all, (messages, gains_dp))
+        counts = [w_all[1].shape[0]] * 4 + [send.shape[0]]
+        send = join_pieces([*w_all, send], counts)
     recv = after(swap(send, "dp", n_dp, 1), output)
-    stu_grad, ar_grad, *more = finish(keep, send, recv, order, (0, 2, 1, 3) if custom else ())
+    stu_grad, ar_grad, *w_grads = finish(keep, send, recv, order, custom)
+    gains = ordered_sum(after(gains, stu_grad), "mp", 0)
     if custom:
-        gains, gate_grad, up_grad, down_grad = more
+        gate_grad, up_grad, down_grad = w_grads
     else:
-        gains = ordered_sum([gains] + [swap(gains, "dp", n_dp, r) for r in range(1, n_dp)], "dp", 1)
         gate_grad, up_grad, down_grad = (g.astype(F32) for g in lax.psum(tuple(grads), "dp"))
     return (
         output, input_grad, stu_grad, ar_grad, gains[0], gains[8], gate_grad, up_grad, down_grad,

time: 165 us -> 156 us (0.945)
  waiting for transfers between devices: 48 us -> 40.5 us
    ppermute x11 -> x12, waiting for transfers between devices: 13.8 us -> 3.98 us  [swap(): return lax.ppermute(value, axis, [(i, i ^ bits) for i in range(n)])]
    ppermute x11 -> x12, starting transfers between devices: 12.4 us -> 11.2 us  [swap(): return lax.ppermute(value, axis, [(i, i ^ bits) for i in range(n)])]
    pallas_call x9 -> x7, Pallas kernels: 4.99 us -> 4.54 us  [the longest x1 3.71 us: finish(): pl.pallas_call(functools.partial(finish_kernel, custom), in_specs=[whole(...]
    unnamed x14 -> x16, local copies, waits for them, and re-layouts: 3.32 us -> 3.33 us
  transfers between devices with their start and end apart: 29 -> 30, of which waited for: 10 -> 9; matrix products, arithmetic and copies ran while one was open for 0% -> 0% of each run, Pallas kernels for 39% -> 44%
where the time goes in v2:
time: 156 us
  Pallas kernels  70.1 us (45%)
  waiting for transfers between devices  40.5 us (26%)
  starting transfers between devices  39.3 us (25%)
  local copies, waits for them, and re-layouts  3.91 us (3%)
  between operations  1.63 us (1%)
    ppermute x12, waiting for transfers between devices, fetch_shifted(): pieces[r] = lax.ppermute(value, axis, [(i, (i - r) % n) for i in range(n)])  27.2 us
    ppermute x12, starting transfers between devices, fetch_shifted(): pieces[r] = lax.ppermute(value, axis, [(i, (i - r) % n) for i in range(n)])  18 us
    pallas_call x1, Pallas kernels, spectral_unmix(): pl.pallas_call(functools.partial(unmix_kernel, kb, share, n), grid=(count...  17.8 us
    pallas_call x1, Pallas kernels, spectral_mix(): pl.pallas_call(functools.partial(mix_kernel, kb, share), grid=(filt // kb...  14.5 us
    pallas_call x1, Pallas kernels, matrix_grads(): pl.pallas_call(functools.partial(grads_kernel, steps, order, groups, rows...  11.4 us
    ppermute x12, starting transfers between devices, swap(): return lax.ppermute(value, axis, [(i, i ^ bits) for i in range(n)])  11.2 us
    ppermute x6, starting transfers between devices, send_shifted(): lax.ppermute(pieces[r], axis, [(i, (i + r) % n) for i in range(n)])  10.1 us
    pallas_call x1, Pallas kernels, convolutions(): pl.pallas_call(functools.partial(conv_kernel, groups, tile, own), grid=(o...  9.88 us
  transfers between devices with their start and end apart: 30, of which 9 were waited for; matrix products, arithmetic and copies ran while one was open for 0% of the time, Pallas kernels for 44%

profile of v2, /device:TPU:0, one launch (start us, length us, event | category | flops | bytes accessed | tf_op | source)
XLA Modules:
  0.0 156.1 jit_solution(10672427260783419706)
XLA Ops:
  5.1 3.0 %collective-permute-start = (bf16[512,768]{1,0:T(8,128)(2,1)S(1)}, bf16[512,768]{1,0:T(8,128)(2,1)S(1)}, u32[]{:S(2)}, u32[]{:S(2)}) collective-permute-start(bf16[512,768]{1,0:T(8,128)(2,1)S(1)} %get-tuple-element.152.refs_0_), channel_id=1, source_target_pairs={{0,8},{4,12},{8,0},{12,4},{16,24},{20,28},{24,16},{28,20},{1,9},{5... | collective-permute-start | bytes 2359304 | tf_op jit(solution)/shard_map/ppermute | solution.py:972
  11.0 14.5 %spectral_mix.1 = (f32[192,512]{1,0:T(8,128)S(1)}, bf16[192,512]{1,0:T(8,128)(2,1)S(1)}) custom-call(s32[1]{0:T(128)S(6)} %copy.20.len_ref, f32[6,24,384]{2,1,0:T(8,128)S(1)} %get-tuple-element.101.taps_ref, f32[192,512]{1,0:T(8,128)S(1)} %get-tuple-element.102.x_ref, bf16[2,384,512]{2,1,0:T(8,128)(2,1)S(1)} %get-tuple-element.103.u_ref, ...), custom_call_target="tpu_custom_call" | custom-call | flops 8455716864 | bytes 25165824 | tf_op jit(solution)/shard_map/spectral_mix/pallas_call | solution.py:256
  25.6 3.0 %collective-permute-start.3 = (bf16[192,512]{1,0:T(8,128)(2,1)S(1)}, bf16[192,512]{1,0:T(8,128)(2,1)S(1)}, u32[]{:S(2)}, u32[]{:S(2)}) collective-permute-start(bf16[192,512]{1,0:T(8,128)(2,1)S(1)} %get-tuple-element.108.nt_ref.refs_0_), channel_id=1, source_target_pairs={{0,2},{1,3},{2,0},{3,1},{4,6},{5,7},{6,4},{7,5},{8,10},{9,11},{10,... | collective-permute-start | bytes 589832 | tf_op jit(solution)/shard_map/ppermute | solution.py:959
  31.7 10.6 %collective-permute-done.3.nt_ref.refs_2_ = bf16[192,512]{1,0:T(8,128)(2,1)S(1)} collective-permute-done((bf16[192,512]{1,0:T(8,128)(2,1)S(1)}, bf16[192,512]{1,0:T(8,128)(2,1)S(1)}, u32[]{:S(2)}, u32[]{:S(2)}) %collective-permute-start.3) | collective-permute-done | bytes 196640 | tf_op jit(solution)/shard_map/ppermute | solution.py:959
  44.5 5.2 %collective-permute-start.4 = (bf16[192,512]{1,0:T(8,128)(2,1)S(1)}, bf16[192,512]{1,0:T(8,128)(2,1)S(1)}, u32[]{:S(2)}, u32[]{:S(2)}) collective-permute-start(bf16[192,512]{1,0:T(8,128)(2,1)S(1)} %get-tuple-element.113), channel_id=1, source_target_pairs={{0,1},{1,2},{2,3},{3,0},{4,5},{5,6},{6,7},{7,4},{8,9},{9,10},{10,1... | collective-permute-start | bytes 589832 | tf_op jit(solution)/shard_map/ppermute | solution.py:967
  50.8 1.9 %ffn_grads.1 = (bf16[192,512]{1,0:T(8,128)(2,1)S(1)}, bf16[192,512]{1,0:T(8,128)(2,1)S(1)}, bf16[192,512]{1,0:T(8,128)(2,1)S(1)}, bf16[192,512]{1,0:T(8,128)(2,1...) custom-call(bf16[768,512]{1,0:T(8,128)(2,1)S(1)} %copy-done, bf16[512,512]{1,0:T(8,128)(2,1)S(1)} %copy-done.3, ...), custom_call_target="tpu_custom_call" | custom-call | flops 1610612736 | bytes 4718592 | tf_op jit(solution)/shard_map/ffn_grads/pallas_call | solution.py:373
  52.8 5.3 %collective-permute-done.4.refs_1_ = bf16[192,512]{1,0:T(8,128)(2,1)S(1)} collective-permute-done((bf16[192,512]{1,0:T(8,128)(2,1)S(1)}, bf16[192,512]{1,0:T(8,128)(2,1)S(1)}, u32[]{:S(2)}, u32[]{:S(2)}) %collective-permute-start.4) | collective-permute-done | bytes 196640 | tf_op jit(solution)/shard_map/ppermute | solution.py:967
  58.0 1.7 %collective-permute-done.5.refs_2_ = bf16[192,512]{1,0:T(8,128)(2,1)S(1)} collective-permute-done((bf16[192,512]{1,0:T(8,128)(2,1)S(1)}, bf16[192,512]{1,0:T(8,128)(2,1)S(1)}, u32[]{:S(2)}, u32[]{:S(2)}) %collective-permute-start.5) | collective-permute-done | bytes 196640 | tf_op jit(solution)/shard_map/ppermute | solution.py:967
  59.8 2.2 %collective-permute-done.7.refs_3_ = bf16[192,512]{1,0:T(8,128)(2,1)S(1)} collective-permute-done((bf16[192,512]{1,0:T(8,128)(2,1)S(1)}, bf16[192,512]{1,0:T(8,128)(2,1)S(1)}, u32[]{:S(2)}, u32[]{:S(2)}) %collective-permute-start.7) | collective-permute-done | bytes 196640 | tf_op jit(solution)/shard_map/ppermute | solution.py:967
  62.4 2.1 %collective-permute-start.9 = (bf16[192,512]{1,0:T(8,128)(2,1)S(1)}, bf16[192,512]{1,0:T(8,128)(2,1)S(1)}, u32[]{:S(2)}, u32[]{:S(2)}) collective-permute-start(bf16[192,512]{1,0:T(8,128)(2,1)S(1)} %get-tuple-element.135.refs_0_), channel_id=1, source_target_pairs={{0,3},{1,0},{2,1},{3,2},{4,7},{5,4},{6,5},{7,6},{8,11},{9,8},{10,9... | collective-permute-start | bytes 589832 | tf_op jit(solution)/shard_map/ppermute | solution.py:959
  65.4 1.9 %collective-permute-start.11 = (bf16[192,512]{1,0:T(8,128)(2,1)S(1)}, bf16[192,512]{1,0:T(8,128)(2,1)S(1)}, u32[]{:S(2)}, u32[]{:S(2)}) collective-permute-start(bf16[192,512]{1,0:T(8,128)(2,1)S(1)} %get-tuple-element.135.refs_0_), channel_id=1, source_target_pairs={{0,1},{1,2},{2,3},{3,0},{4,5},{5,6},{6,7},{7,4},{8,9},{9,10},{10,1... | collective-permute-start | bytes 589832 | tf_op jit(solution)/shard_map/ppermute | solution.py:959
  67.6 2.3 %collective-permute-done.9.refs_1_ = bf16[192,512]{1,0:T(8,128)(2,1)S(1)} collective-permute-done((bf16[192,512]{1,0:T(8,128)(2,1)S(1)}, bf16[192,512]{1,0:T(8,128)(2,1)S(1)}, u32[]{:S(2)}, u32[]{:S(2)}) %collective-permute-start.9) | collective-permute-done | bytes 196640 | tf_op jit(solution)/shard_map/ppermute | solution.py:959
  69.9 13.6 %collective-permute-done.10.refs_2_ = bf16[192,512]{1,0:T(8,128)(2,1)S(1)} collective-permute-done((bf16[192,512]{1,0:T(8,128)(2,1)S(1)}, bf16[192,512]{1,0:T(8,128)(2,1)S(1)}, u32[]{:S(2)}, u32[]{:S(2)}) %collective-permute-start.10) | collective-permute-done | bytes 196640 | tf_op jit(solution)/shard_map/ppermute | solution.py:959
  86.8 1.9 %collective-permute-start.14 = (bf16[192,512]{1,0:T(8,128)(2,1)S(1)}, bf16[192,512]{1,0:T(8,128)(2,1)S(1)}, u32[]{:S(2)}, u32[]{:S(2)}) collective-permute-start(bf16[192,512]{1,0:T(8,128)(2,1)S(1)} %get-tuple-element.149), channel_id=1, source_target_pairs={{0,2},{1,3},{2,0},{3,1},{4,6},{5,7},{6,4},{7,5},{8,10},{9,11},{10,... | collective-permute-start | bytes 589832 | tf_op jit(solution)/shard_map/ppermute | solution.py:967
  88.7 2.9 %collective-permute-start.15 = (bf16[192,512]{1,0:T(8,128)(2,1)S(1)}, bf16[192,512]{1,0:T(8,128)(2,1)S(1)}, u32[]{:S(2)}, u32[]{:S(2)}) collective-permute-start(bf16[192,512]{1,0:T(8,128)(2,1)S(1)} %get-tuple-element.150), channel_id=1, source_target_pairs={{0,3},{1,0},{2,1},{3,2},{4,7},{5,4},{6,5},{7,6},{8,11},{9,8},{10,9... | collective-permute-start | bytes 589832 | tf_op jit(solution)/shard_map/ppermute | solution.py:967
  91.6 17.8 %spectral_unmix.1 = (bf16[192,512]{1,0:T(8,128)(2,1)S(1)}, f32[16,512]{1,0:T(8,128)S(1)}) custom-call(s32[1]{0:T(128)S(6)} %copy.20.len_ref, f32[6,24,384]{2,1,0:T(8,128)S(1)} %get-tuple-element.101.taps_ref, f32[192,512]{1,0:T(8,128)S(1)} %get-tuple-element.102.x_ref, f32[192,512]{1,0:T(8,128)S(1)} %get-tuple-element.133.bh_ref, ...), custom_call_target="tpu_custom_call" | custom-call | flops 8455716864 | bytes 25165824 | tf_op jit(solution)/shard_map/spectral_unmix/pallas_call | solution.py:502
  110.9 1.9 %collective-permute-start.17 = (bf16[384,512]{1,0:T(8,128)(2,1)S(1)}, bf16[384,512]{1,0:T(8,128)(2,1)S(1)}, u32[]{:S(2)}, u32[]{:S(2)}) collective-permute-start(bf16[384,512]{1,0:T(8,128)(2,1)S(1)} %rows_message.1.refs_0_), channel_id=1, source_target_pairs={{0,2},{1,3},{2,0},{3,1},{4,6},{5,7},{6,4},{7,5},{8,10},{9,11},{10,... | collective-permute-start | bytes 1179656 | tf_op jit(solution)/shard_map/ppermute | solution.py:959
  112.8 2.0 %collective-permute-start.18 = (bf16[384,512]{1,0:T(8,128)(2,1)S(1)}, bf16[384,512]{1,0:T(8,128)(2,1)S(1)}, u32[]{:S(2)}, u32[]{:S(2)}) collective-permute-start(bf16[384,512]{1,0:T(8,128)(2,1)S(1)} %rows_message.1.refs_0_), channel_id=1, source_target_pairs={{0,1},{1,2},{2,3},{3,0},{4,5},{5,6},{6,7},{7,4},{8,9},{9,10},{10,1... | collective-permute-start | bytes 1179656 | tf_op jit(solution)/shard_map/ppermute | solution.py:959
  114.8 9.9 %convolutions.1.conv_ref = bf16[12,128,3072]{2,1,0:T(8,128)(2,1)S(1)} custom-call(f32[24,768]{1,0:T(8,128)S(1)} %get-tuple-element.151.filt_ref, bf16[512,768]{1,0:T(8,128)(2,1)S(1)} %get-tuple-element.152.refs_0_, bf16[512,768]{1,0:T(8,128)(2,1)S(1)} %collective-permute-done.refs_1_, bf16[512,768]{1,0:T(8,128)(2,1)S(1)} %collective-permute-done.1.refs_2_, ...), custom_call_target="tpu_custom_call" | custom-call | tf_op jit(solution)/shard_map/convolutions/pallas_call | solution.py:562
  127.1 3.9 %collective-permute-done.23.recv_ref.refs_2_ = bf16[224,512]{1,0:T(8,128)(2,1)S(1)} collective-permute-done((bf16[224,512]{1,0:T(8,128)(2,1)S(1)}, bf16[224,512]{1,0:T(8,128)(2,1)S(1)}, u32[]{:S(2)}, u32[]{:S(2)}) %collective-permute-start.23) | collective-permute-done | bytes 229408 | tf_op jit(solution)/shard_map/ppermute | solution.py:972
  131.1 2.6 %lagged.1 = (bf16[512,3072]{1,0:T(8,128)(2,1)S(1)}, bf16[512,3072]{1,0:T(8,128)(2,1)S(1)}, bf16[512,3072]{1,0:T(8,128)(2,1)S(1)}) custom-call(bf16[512,768]{1,0:T(8,128)(2,1)S(1)} %get-tuple-element.152.refs_0_, bf16[512,768]{1,0:T(8,128)(2,1)S(1)} %collective-permute-done.refs_1_, bf16[512,768]{1,0:T(8,128)(2,1)S(1)} %collective-permute-done.1.refs_2_, ...), custom_call_target="tpu_custom_call" | custom-call | tf_op jit(solution)/shard_map/lagged/pallas_call | solution.py:596
  133.6 11.4 %matrix_grads.1 = (f32[12,64,512]{2,1,0:T(8,128)S(1)}, bf16[2304,512]{1,0:T(8,128)(2,1)S(1)}) custom-call(bf16[12,128,3072]{2,1,0:T(8,128)(2,1)S(1)} %convolutions.1.conv_ref, bf16[512,3072]{1,0:T(8,128)(2,1)S(1)} %get-tuple-element.157.refs_0_, bf16[512,3072]{1,0:T(8,128)(2,1)S(1)} %get-tuple-element.158.refs_1_, ...), custom_call_target="tpu_custom_call" | custom-call | tf_op jit(solution)/shard_map/matrix_grads/pallas_call | solution.py:649
  148.1 2.0 %collective-permute-start.29 = (f32[16,512]{1,0:T(8,128)S(1)}, f32[16,512]{1,0:T(8,128)S(1)}, u32[]{:S(2)}, u32[]{:S(2)}) collective-permute-start(f32[16,512]{1,0:T(8,128)S(1)} %ordered_sum.2.refs_0_), channel_id=1, source_target_pairs={{0,1},{1,2},{2,3},{3,0},{4,5},{5,6},{6,7},{7,4},{8,9},{9,10},{10,1... | collective-permute-start | bytes 98312 | tf_op jit(solution)/shard_map/ppermute | solution.py:959
  151.7 3.7 %finish.1 = (f32[12,64,512]{2,1,0:T(8,128)}, f32[3,512,512]{2,1,0:T(8,128)}, f32[512,512]{1,0:T(8,128)}, f32[512,512]{1,0:T(8,128)}, f32[512,512]{1,0:T(8,128)}) custom-call(f32[12,64,512]{2,1,0:T(8,128)S(1)} %get-tuple-element.174.keep_ref, bf16[3072,512]{1,0:T(8,128)(2,1)S(1)} %join_pieces.1.send_ref, bf16[3072,512]{1,0:T(8,128)(2,1)S(1)} %collective-permute-done.26.recv_ref), custom_call_target="tpu_custom_call" | custom-call | flops 393216 | bytes 3932160 | tf_op jit(solution)/shard_map/finish/pallas_call | solution.py:941
  (77 shorter events, 26.9 us)
Async XLA Ops:
  5.1 24.9 %collective-permute-start = (bf16[512,768]{1,0:T(8,128)(2,1)S(1)}, bf16[512,768]{1,0:T(8,128)(2,1)S(1)}, u32[]{:S(2)}, u32[]{:S(2)}) collective-permute-start(bf16[512,768]{1,0:T(8,128)(2,1)S(1)} %get-tuple-element.152.refs_0_), channel_id=1, source_target_pairs={{0,8},{4,12},{8,0},{12,4},{16,24},{20,28},{24,16},{28,20},{1,9},{5... | collective-permute-start | bytes 2359304 | tf_op jit(solution)/shard_map/ppermute | solution.py:972
  8.1 22.5 %collective-permute-start.1 = (bf16[512,768]{1,0:T(8,128)(2,1)S(1)}, bf16[512,768]{1,0:T(8,128)(2,1)S(1)}, u32[]{:S(2)}, u32[]{:S(2)}) collective-permute-start(bf16[512,768]{1,0:T(8,128)(2,1)S(1)} %get-tuple-element.152.refs_0_), channel_id=1, source_target_pairs={{0,16},{4,20},{8,24},{12,28},{16,0},{20,4},{24,8},{28,12},{1,17},{... | collective-permute-start | bytes 2359304 | tf_op jit(solution)/shard_map/ppermute | solution.py:972
  25.5 27.3 %collective-permute-start.8 = (bf16[512,768]{1,0:T(8,128)(2,1)S(1)}, bf16[512,768]{1,0:T(8,128)(2,1)S(1)}, u32[]{:S(2)}, u32[]{:S(2)}) collective-permute-start(bf16[512,768]{1,0:T(8,128)(2,1)S(1)} %get-tuple-element.152.refs_0_), channel_id=1, source_target_pairs={{0,24},{4,28},{8,16},{12,20},{16,8},{20,12},{24,0},{28,4},{1,25},{... | collective-permute-start | bytes 2359304 | tf_op jit(solution)/shard_map/ppermute | solution.py:972
  25.6 16.8 %collective-permute-start.3 = (bf16[192,512]{1,0:T(8,128)(2,1)S(1)}, bf16[192,512]{1,0:T(8,128)(2,1)S(1)}, u32[]{:S(2)}, u32[]{:S(2)}) collective-permute-start(bf16[192,512]{1,0:T(8,128)(2,1)S(1)} %get-tuple-element.108.nt_ref.refs_0_), channel_id=1, source_target_pairs={{0,2},{1,3},{2,0},{3,1},{4,6},{5,7},{6,4},{7,5},{8,10},{9,11},{10,... | collective-permute-start | bytes 589832 | tf_op jit(solution)/shard_map/ppermute | solution.py:959
  28.6 14.9 %collective-permute-start.2 = (bf16[192,512]{1,0:T(8,128)(2,1)S(1)}, bf16[192,512]{1,0:T(8,128)(2,1)S(1)}, u32[]{:S(2)}, u32[]{:S(2)}) collective-permute-start(bf16[192,512]{1,0:T(8,128)(2,1)S(1)} %get-tuple-element.108.nt_ref.refs_0_), channel_id=1, source_target_pairs={{0,3},{1,0},{2,1},{3,2},{4,7},{5,4},{6,5},{7,6},{8,11},{9,8},{10,9... | collective-permute-start | bytes 589832 | tf_op jit(solution)/shard_map/ppermute | solution.py:959
  30.0 19.7 %collective-permute-start.6 = (bf16[192,512]{1,0:T(8,128)(2,1)S(1)}, bf16[192,512]{1,0:T(8,128)(2,1)S(1)}, u32[]{:S(2)}, u32[]{:S(2)}) collective-permute-start(bf16[192,512]{1,0:T(8,128)(2,1)S(1)} %get-tuple-element.108.nt_ref.refs_0_), channel_id=1, source_target_pairs={{0,1},{1,2},{2,3},{3,0},{4,5},{5,6},{6,7},{7,4},{8,9},{9,10},{10,1... | collective-permute-start | bytes 589832 | tf_op jit(solution)/shard_map/ppermute | solution.py:959
  43.4 16.4 %collective-permute-start.5 = (bf16[192,512]{1,0:T(8,128)(2,1)S(1)}, bf16[192,512]{1,0:T(8,128)(2,1)S(1)}, u32[]{:S(2)}, u32[]{:S(2)}) collective-permute-start(bf16[192,512]{1,0:T(8,128)(2,1)S(1)} %get-tuple-element.111), channel_id=1, source_target_pairs={{0,2},{1,3},{2,0},{3,1},{4,6},{5,7},{6,4},{7,5},{8,10},{9,11},{10,... | collective-permute-start | bytes 589832 | tf_op jit(solution)/shard_map/ppermute | solution.py:967
  44.5 13.5 %collective-permute-start.4 = (bf16[192,512]{1,0:T(8,128)(2,1)S(1)}, bf16[192,512]{1,0:T(8,128)(2,1)S(1)}, u32[]{:S(2)}, u32[]{:S(2)}) collective-permute-start(bf16[192,512]{1,0:T(8,128)(2,1)S(1)} %get-tuple-element.113), channel_id=1, source_target_pairs={{0,1},{1,2},{2,3},{3,0},{4,5},{5,6},{6,7},{7,4},{8,9},{9,10},{10,1... | collective-permute-start | bytes 589832 | tf_op jit(solution)/shard_map/ppermute | solution.py:967
  50.8 11.3 %collective-permute-start.7 = (bf16[192,512]{1,0:T(8,128)(2,1)S(1)}, bf16[192,512]{1,0:T(8,128)(2,1)S(1)}, u32[]{:S(2)}, u32[]{:S(2)}) collective-permute-start(bf16[192,512]{1,0:T(8,128)(2,1)S(1)} %get-tuple-element.115), channel_id=1, source_target_pairs={{0,3},{1,0},{2,1},{3,2},{4,7},{5,4},{6,5},{7,6},{8,11},{9,8},{10,9... | collective-permute-start | bytes 589832 | tf_op jit(solution)/shard_map/ppermute | solution.py:967
  64.5 18.9 %collective-permute-start.10 = (bf16[192,512]{1,0:T(8,128)(2,1)S(1)}, bf16[192,512]{1,0:T(8,128)(2,1)S(1)}, u32[]{:S(2)}, u32[]{:S(2)}) collective-permute-start(bf16[192,512]{1,0:T(8,128)(2,1)S(1)} %get-tuple-element.135.refs_0_), channel_id=1, source_target_pairs={{0,2},{1,3},{2,0},{3,1},{4,6},{5,7},{6,4},{7,5},{8,10},{9,11},{10,... | collective-permute-start | bytes 589832 | tf_op jit(solution)/shard_map/ppermute | solution.py:959
  65.4 18.1 %collective-permute-start.11 = (bf16[192,512]{1,0:T(8,128)(2,1)S(1)}, bf16[192,512]{1,0:T(8,128)(2,1)S(1)}, u32[]{:S(2)}, u32[]{:S(2)}) collective-permute-start(bf16[192,512]{1,0:T(8,128)(2,1)S(1)} %get-tuple-element.135.refs_0_), channel_id=1, source_target_pairs={{0,1},{1,2},{2,3},{3,0},{4,5},{5,6},{6,7},{7,4},{8,9},{9,10},{10,1... | collective-permute-start | bytes 589832 | tf_op jit(solution)/shard_map/ppermute | solution.py:959
  83.7 25.9 %collective-permute-start.19 = (bf16[960,512]{1,0:T(8,128)(2,1)S(1)}, bf16[960,512]{1,0:T(8,128)(2,1)S(1)}, u32[]{:S(2)}, u32[]{:S(2)}) collective-permute-start(bf16[960,512]{1,0:T(8,128)(2,1)S(1)} %get-tuple-element.160), channel_id=1, source_target_pairs={{0,8},{4,12},{8,0},{12,4},{16,24},{20,28},{24,16},{28,20},{1,9},{5... | collective-permute-start | bytes 2949128 | tf_op jit(solution)/shard_map/ppermute | solution.py:972
  85.3 24.4 %collective-permute-start.20 = (bf16[960,512]{1,0:T(8,128)(2,1)S(1)}, bf16[960,512]{1,0:T(8,128)(2,1)S(1)}, u32[]{:S(2)}, u32[]{:S(2)}) collective-permute-start(bf16[960,512]{1,0:T(8,128)(2,1)S(1)} %get-tuple-element.161), channel_id=1, source_target_pairs={{0,16},{4,20},{8,24},{12,28},{16,0},{20,4},{24,8},{28,12},{1,17},{... | collective-permute-start | bytes 2949128 | tf_op jit(solution)/shard_map/ppermute | solution.py:972
  86.8 22.7 %collective-permute-start.13 = (bf16[192,512]{1,0:T(8,128)(2,1)S(1)}, bf16[192,512]{1,0:T(8,128)(2,1)S(1)}, u32[]{:S(2)}, u32[]{:S(2)}) collective-permute-start(bf16[192,512]{1,0:T(8,128)(2,1)S(1)} %get-tuple-element.148), channel_id=1, source_target_pairs={{0,1},{1,2},{2,3},{3,0},{4,5},{5,6},{6,7},{7,4},{8,9},{9,10},{10,1... | collective-permute-start | bytes 589832 | tf_op jit(solution)/shard_map/ppermute | solution.py:967
  86.8 22.7 %collective-permute-start.14 = (bf16[192,512]{1,0:T(8,128)(2,1)S(1)}, bf16[192,512]{1,0:T(8,128)(2,1)S(1)}, u32[]{:S(2)}, u32[]{:S(2)}) collective-permute-start(bf16[192,512]{1,0:T(8,128)(2,1)S(1)} %get-tuple-element.149), channel_id=1, source_target_pairs={{0,2},{1,3},{2,0},{3,1},{4,6},{5,7},{6,4},{7,5},{8,10},{9,11},{10,... | collective-permute-start | bytes 589832 | tf_op jit(solution)/shard_map/ppermute | solution.py:967
  88.7 20.8 %collective-permute-start.15 = (bf16[192,512]{1,0:T(8,128)(2,1)S(1)}, bf16[192,512]{1,0:T(8,128)(2,1)S(1)}, u32[]{:S(2)}, u32[]{:S(2)}) collective-permute-start(bf16[192,512]{1,0:T(8,128)(2,1)S(1)} %get-tuple-element.150), channel_id=1, source_target_pairs={{0,3},{1,0},{2,1},{3,2},{4,7},{5,4},{6,5},{7,6},{8,11},{9,8},{10,9... | collective-permute-start | bytes 589832 | tf_op jit(solution)/shard_map/ppermute | solution.py:967
  109.8 14.9 %collective-permute-start.21 = (bf16[608,512]{1,0:T(8,128)(2,1)S(1)}, bf16[608,512]{1,0:T(8,128)(2,1)S(1)}, u32[]{:S(2)}, u32[]{:S(2)}) collective-permute-start(bf16[608,512]{1,0:T(8,128)(2,1)S(1)} %get-tuple-element.165), channel_id=1, source_target_pairs={{0,16},{4,20},{8,24},{12,28},{16,0},{20,4},{24,8},{28,12},{1,17},{... | collective-permute-start | bytes 1867784 | tf_op jit(solution)/shard_map/ppermute | solution.py:972
  110.3 14.4 %collective-permute-start.22 = (bf16[608,512]{1,0:T(8,128)(2,1)S(1)}, bf16[608,512]{1,0:T(8,128)(2,1)S(1)}, u32[]{:S(2)}, u32[]{:S(2)}) collective-permute-start(bf16[608,512]{1,0:T(8,128)(2,1)S(1)} %get-tuple-element.166), channel_id=1, source_target_pairs={{0,8},{4,12},{8,0},{12,4},{16,24},{20,28},{24,16},{28,20},{1,9},{5... | collective-permute-start | bytes 1867784 | tf_op jit(solution)/shard_map/ppermute | solution.py:972
  110.9 34.2 %collective-permute-start.16 = (bf16[384,512]{1,0:T(8,128)(2,1)S(1)}, bf16[384,512]{1,0:T(8,128)(2,1)S(1)}, u32[]{:S(2)}, u32[]{:S(2)}) collective-permute-start(bf16[384,512]{1,0:T(8,128)(2,1)S(1)} %rows_message.1.refs_0_), channel_id=1, source_target_pairs={{0,3},{1,0},{2,1},{3,2},{4,7},{5,4},{6,5},{7,6},{8,11},{9,8},{10,9... | collective-permute-start | bytes 1179656 | tf_op jit(solution)/shard_map/ppermute | solution.py:959
  110.9 34.9 %collective-permute-start.17 = (bf16[384,512]{1,0:T(8,128)(2,1)S(1)}, bf16[384,512]{1,0:T(8,128)(2,1)S(1)}, u32[]{:S(2)}, u32[]{:S(2)}) collective-permute-start(bf16[384,512]{1,0:T(8,128)(2,1)S(1)} %rows_message.1.refs_0_), channel_id=1, source_target_pairs={{0,2},{1,3},{2,0},{3,1},{4,6},{5,7},{6,4},{7,5},{8,10},{9,11},{10,... | collective-permute-start | bytes 1179656 | tf_op jit(solution)/shard_map/ppermute | solution.py:959
  112.8 32.9 %collective-permute-start.18 = (bf16[384,512]{1,0:T(8,128)(2,1)S(1)}, bf16[384,512]{1,0:T(8,128)(2,1)S(1)}, u32[]{:S(2)}, u32[]{:S(2)}) collective-permute-start(bf16[384,512]{1,0:T(8,128)(2,1)S(1)} %rows_message.1.refs_0_), channel_id=1, source_target_pairs={{0,1},{1,2},{2,3},{3,0},{4,5},{5,6},{6,7},{7,4},{8,9},{9,10},{10,1... | collective-permute-start | bytes 1179656 | tf_op jit(solution)/shard_map/ppermute | solution.py:959
  126.4 19.4 %collective-permute-start.24 = (bf16[192,512]{1,0:T(8,128)(2,1)S(1)}, bf16[192,512]{1,0:T(8,128)(2,1)S(1)}, u32[]{:S(2)}, u32[]{:S(2)}) collective-permute-start(bf16[192,512]{1,0:T(8,128)(2,1)S(1)} %get-tuple-element.180.refs_1_), channel_id=1, source_target_pairs={{0,16},{4,20},{8,24},{12,28},{16,0},{20,4},{24,8},{28,12},{1,17},{... | collective-permute-start | bytes 589832 | tf_op jit(solution)/shard_map/ppermute | solution.py:972
  131.0 14.1 %collective-permute-start.25 = (f32[16,512]{1,0:T(8,128)S(1)}, f32[16,512]{1,0:T(8,128)S(1)}, u32[]{:S(2)}, u32[]{:S(2)}) collective-permute-start(f32[16,512]{1,0:T(8,128)S(1)} %chips_sum.1.refs_0_), channel_id=1, source_target_pairs={{0,4},{4,0},{8,12},{12,8},{16,20},{20,16},{24,28},{28,24},{1,5},{5... | collective-permute-start | bytes 98312 | tf_op jit(solution)/shard_map/ppermute | solution.py:972
  146.1 9.4 %collective-permute-start.27 = (f32[16,512]{1,0:T(8,128)S(1)}, f32[16,512]{1,0:T(8,128)S(1)}, u32[]{:S(2)}, u32[]{:S(2)}) collective-permute-start(f32[16,512]{1,0:T(8,128)S(1)} %ordered_sum.2.refs_0_), channel_id=1, source_target_pairs={{0,3},{1,0},{2,1},{3,2},{4,7},{5,4},{6,5},{7,6},{8,11},{9,8},{10,9... | collective-permute-start | bytes 98312 | tf_op jit(solution)/shard_map/ppermute | solution.py:959
  (14 other events, 160.0 us)

commit v3 on v2

--- a/solution.py
+++ b/solution.py
@@ -270,7 +270,7 @@
             pltpu.VMEM((width // 128, share, 128), F32),
         ]
         + matrix_scratch(kb, ar),
-        compiler_params=params(40 << 20),
+        compiler_params=params(50 << 20),
         cost_estimate=cost(2 * filt * share * width * (length + 2 * width), 2 * stu.size),
         name="spectral_mix",
     )(lengths, taps, x, u, lags, gains, stu, ar)
@@ -402,6 +402,22 @@
     b_ref[...] = back.astype(BF)
 
 
+def first_sum_kernel(a_ref, b_ref, out_ref):
+    out_ref[...] = a_ref[...].astype(F32) + b_ref[...].astype(F32)
+
+
+def first_sum(a, b):
+    return pl.pallas_call(
+        first_sum_kernel,
+        in_specs=[whole()] * 2,
+        out_specs=whole(),
+        out_shape=jax.ShapeDtypeStruct(a.shape, F32),
+        compiler_params=params(),
+        cost_estimate=cost(a.size, 8 * a.size),
+        name="first_sum",
+    )(a, b)
+
+
 def mid_norm(lengths, hidden, cot, gain, pieces):
     share, width = hidden.shape
     n = len(pieces)
@@ -524,7 +540,7 @@
     )(lengths, taps, x, back_hidden, gg, gains, stu, ar, *pieces)
 
 
-def conv_kernel(groups, tile, own, filt_ref, *refs):
+def conv_kernel(groups, tile, own, first, filt_ref, *refs):
     ut_refs, (conv_ref, tt_ref, ut_scr) = refs[:groups], refs[groups:]
     j = pl.program_id(0)
     filt, length = filt_ref.shape
@@ -538,7 +554,7 @@
         for r in range(groups):
             ut_scr[r * block : (r + 1) * block, :] = ut_refs[r][pl.ds(start, block), :]
 
-    which = lax.axis_index("mp") * own + j
+    which = lax.axis_index("mp") * own + first + j
     strip = toeplitz(filt_ref[pl.ds(lax.rem(which, filt), 1), :], tile)
     row = lax.broadcasted_iota(jnp.int32, (tile, length), 0)
     col = lax.broadcasted_iota(jnp.int32, (tile, length), 1)
@@ -554,17 +570,17 @@
             conv_ref[0, :, pl.ds(start, tile)] = part[r * block : (r + 1) * block, :]
 
 
-def convolutions(filt, uts, own, chips):
+def convolutions(filt, uts, own, chips, first, last):
     length = filt.shape[1]
     groups = len(uts)
     block = uts[0].shape[0] // chips
     tile = 256 if length % 256 == 0 else length
     return pl.pallas_call(
-        functools.partial(conv_kernel, groups, tile, own),
-        grid=(own,),
+        functools.partial(conv_kernel, groups, tile, own, first),
+        grid=(last - first,),
         in_specs=[whole()] * (1 + groups),
         out_specs=pl.BlockSpec((1, block, groups * length), lambda j: (j, 0, 0)),
-        out_shape=jax.ShapeDtypeStruct((own, block, groups * length), BF),
+        out_shape=jax.ShapeDtypeStruct((last - first, block, groups * length), BF),
         scratch_shapes=[
             pltpu.VMEM((length, length), BF),
             pltpu.VMEM((groups * block, length), BF),
@@ -604,7 +620,7 @@
     )(*uts)
 
 
-def grads_kernel(steps, order, groups, rows, conv_ref, *refs):
+def grads_kernel(steps, order, groups, rows, conv_ref, conv_two_ref, *refs):
     lag_refs, b_refs = refs[:order], refs[order : order + len(rows)]
     keep_ref, send_ref, b_scr, scr = refs[order + len(rows) :]
     g = pl.program_id(0)
@@ -620,10 +636,15 @@
             start = pl.multiple_of((chip ^ r) * length + at, 16)
             b_scr[pl.ds(start, size), :] = ref[:size, :]
 
+    for k, ref in enumerate((conv_ref, conv_two_ref)):
+
+        @pl.when((g >= k * steps // 2) & (g < (k + 1) * steps // 2))
+        def _():
+            part = dot(ref[...].reshape(step * block, depth), b_scr[...])
+            scr[...] = part.reshape(step, block, width)
+
     @pl.when(g < steps)
     def _():
-        part = dot(conv_ref[...].reshape(step * block, depth), b_scr[...])
-        scr[...] = part.reshape(step, block, width)
         mine = pl.multiple_of(core * half, 16)
         other = pl.multiple_of((1 - core) * half, 16)
         keep_ref[pl.ds(g * step, step)] = scr[:, pl.ds(mine, half), :]
@@ -639,17 +660,23 @@
             send_ref[at : at + width, :] = dot(lag_refs[lag][...], b_scr[...]).astype(BF)
 
 
-def matrix_grads(conv, lags, backs, rows):
-    own, block, depth = conv.shape
+def matrix_grads(convs, lags, backs, rows):
+    part, block, depth = convs[0].shape
+    own = 2 * part
     order, width = len(lags), lags[0].shape[0]
     groups = 1 + max(r for r, _, _ in rows)
-    step = next(s for s in (4, 3, 2, 1) if own % s == 0)
+    step = next(s for s in (3, 2, 1) if part % s == 0)
     steps = own // step
     half = block // 2
     return pl.pallas_call(
         functools.partial(grads_kernel, steps, order, groups, rows),
         grid=(steps + order,),
-        in_specs=[pl.BlockSpec((step, block, depth), lambda g: (jnp.minimum(g, steps - 1), 0, 0))]
+        in_specs=[
+            pl.BlockSpec((step, block, depth), lambda g: (jnp.minimum(g, steps // 2 - 1), 0, 0)),
+            pl.BlockSpec(
+                (step, block, depth), lambda g: (jnp.clip(g - steps // 2, 0, steps // 2 - 1), 0, 0)
+            ),
+        ]
         + [whole()] * (order + len(backs)),
         out_specs=[whole()] * 2,
         out_shape=[
@@ -663,7 +690,7 @@
         compiler_params=params(),
         cost_estimate=cost(0, 0),
         name="matrix_grads",
-    )(conv, *lags, *backs)
+    )(*convs, *lags, *backs)
 
 
 def rows_message_kernel(ig_ref, hid_ref, *refs):
@@ -997,7 +1024,7 @@
     )
     uts = [ut] + [swap(ut, "dp", n_dp, 2 * r) for r in range(1, 3)]
     hidden, nt = spectral_mix(
-        lengths, taps, x_own, u, u_lags, both_gains, stu_weight, ar_weight, share, 4
+        lengths, taps, x_own, u, u_lags, both_gains, stu_weight, ar_weight, share, 8
     )
     nts = fetch_shifted(nt, "mp", n)
     weights = (cotangent, gate_weight, up_weight, down_weight)
@@ -1014,9 +1041,16 @@
     custom = n_dp == 8 and gate_weight.shape[1] == width
     grads = ffn_grads(cotangent, down_weight, nts, acts, bgs, bus, groups if custom else 0)
     out_parts, grads = grads[:n], grads[n:]
-    bns = [bns[0]] + after(bns[1:], (grads[0], uts))
+    bns[1 : n // 2] = after(bns[1 : n // 2], (grads[0], uts))
+    far = n // 2
+    bns = [first_sum(bns[0], bns[far])] + [bns[r] for r in range(1, n) if r != far]
     back_hidden, back_rows, second_part = mid_norm(lengths, hidden, cotangent, both_gains, bns)
     backs = fetch_shifted(back_rows, "mp", n)
+    uts = after(uts, back_rows)
+    fours = [uts[r : r + 4] for r in range(0, groups, 4)]
+    lags = [lagged(some, order) for some in fours]
+    conv = [convolutions(natural, some, own, groups, 0, own // 2) for some in fours]
+    backs = after(backs, (lags, conv))
     if custom:
         w_keep, w_send = grads
         w_parts, to_x, to_y = cores_sum(w_keep, swap(after(w_send, back_rows), "dp", n_dp, 1))
@@ -1026,11 +1060,11 @@
         (own_back,) = pack_rows(backs)
     out_sums = send_shifted(after(out_parts, own_back), "mp")
     ig, gains = spectral_unmix(
-        lengths, taps, x_own, back_hidden, second_part, both_gains, stu_weight, ar_weight, backs, 4
+        lengths, taps, x_own, back_hidden, second_part, both_gains, stu_weight, ar_weight, backs, 8
     )
     uts, hidden = after((uts, hidden), ig)
-    conv = [convolutions(natural, uts[r : r + 4], own, groups) for r in range(0, groups, 4)]
-    lags = [lagged(uts[r : r + 4], order) for r in range(0, groups, 4)]
+    fours = [uts[r : r + 4] for r in range(0, groups, 4)]
+    conv_two = [convolutions(natural, some, own, groups, own // 2, own) for some in fours]
     message = rows_message(ig, hidden, out_sums)
     messages = fetch_shifted(message, "mp", n)
     if custom:
@@ -1039,7 +1073,7 @@
         all_backs = [own_back, over_x, over_y, from_y, from_x]
         half = length // 2
         rows = ((0, 0, length), (1, 0, length), (2, 0, length), (3, 0, half), (3, half, half))
-        to_x, to_y = whole_chunks(after(w_parts, conv), from_y, from_x)
+        to_x, to_y = whole_chunks(after(w_parts, conv_two), from_y, from_x)
         w_all = [to_x, to_y, swap(to_x, "dp", n_dp, 2), swap(to_y, "dp", n_dp, 4)]
         gains = chips_sum(gains, from_x, from_y, w_all[2])
         gains = ordered_sum([gains, swap(gains, "dp", n_dp, 1)], "dp", 0)
@@ -1050,7 +1084,7 @@
     gains_dp = gains
     gains = fetch_shifted(gains, "mp", n)
 
-    conv = after(conv, message)
+    conv = after(list(zip(conv, conv_two)), message)
     if len(conv) == 1:
         keep, send = matrix_grads(conv[0], lags[0], all_backs, rows)
     else:

time: 156 us -> 153 us (0.981)
  waiting for transfers between devices: 40.5 us -> 31.4 us
  starting transfers between devices: 39.3 us -> 47.8 us
    ppermute x12, waiting for transfers between devices: 27.2 us -> 14.5 us  [fetch_shifted(): pieces[r] = lax.ppermute(value, axis, [(i, (i - r) % n) for i in range(n)])]
    ppermute x12, starting transfers between devices: 18 us -> 23.9 us  [fetch_shifted(): pieces[r] = lax.ppermute(value, axis, [(i, (i - r) % n) for i in range(n)])]
    ppermute x12, waiting for transfers between devices: 3.98 us -> 7.67 us  [swap(): return lax.ppermute(value, axis, [(i, i ^ bits) for i in range(n)])]
    ppermute x6, starting transfers between devices: 10.1 us -> 12.3 us  [send_shifted(): lax.ppermute(pieces[r], axis, [(i, (i + r) % n) for i in range(n)])]
    unnamed x16 -> x14, local copies, waits for them, and re-layouts: 3.33 us -> 1.92 us
    pallas_call x1 -> x3, Pallas kernels: 9.88 us -> 10 us  [the longest x2 9.97 us: convolutions(): pl.pallas_call(functools.partial(conv_kernel, groups, tile, own, first),...]
  transfers between devices with their start and end apart: 30 -> 30, of which waited for: 9 -> 8; matrix products, arithmetic and copies ran while one was open for 0% -> 0% of each run, Pallas kernels for 44% -> 44%
where the time goes in v3:
time: 153 us
  Pallas kernels  68.8 us (45%)
  starting transfers between devices  47.8 us (31%)
  waiting for transfers between devices  31.4 us (21%)
  local copies, waits for them, and re-layouts  2.51 us (2%)
  between operations  1.63 us (1%)
    ppermute x12, starting transfers between devices, fetch_shifted(): pieces[r] = lax.ppermute(value, axis, [(i, (i - r) % n) for i in range(n)])  23.9 us
    pallas_call x1, Pallas kernels, spectral_unmix(): pl.pallas_call(functools.partial(unmix_kernel, kb, share, n), grid=(count...  17 us
    ppermute x12, waiting for transfers between devices, fetch_shifted(): pieces[r] = lax.ppermute(value, axis, [(i, (i - r) % n) for i in range(n)])  14.5 us
    pallas_call x1, Pallas kernels, spectral_mix(): pl.pallas_call(functools.partial(mix_kernel, kb, share), grid=(filt // kb...  13.5 us
    ppermute x6, starting transfers between devices, send_shifted(): lax.ppermute(pieces[r], axis, [(i, (i + r) % n) for i in range(n)])  12.3 us
    pallas_call x1, Pallas kernels, matrix_grads(): pl.pallas_call(functools.partial(grads_kernel, steps, order, groups, rows...  11.7 us
    ppermute x12, starting transfers between devices, swap(): return lax.ppermute(value, axis, [(i, i ^ bits) for i in range(n)])  11.6 us
    pallas_call x2, Pallas kernels, convolutions(): pl.pallas_call(functools.partial(conv_kernel, groups, tile, own, first),...  9.97 us
  transfers between devices with their start and end apart: 30, of which 8 were waited for; matrix products, arithmetic and copies ran while one was open for 0% of the time, Pallas kernels for 44%

profile of v3, /device:TPU:0, one launch (start us, length us, event | category | flops | bytes accessed | tf_op | source)
XLA Modules:
  0.0 152.9 jit_solution(17279430154464036446)
XLA Ops:
  5.1 3.0 %collective-permute-start.1 = (bf16[512,768]{1,0:T(8,128)(2,1)S(1)}, bf16[512,768]{1,0:T(8,128)(2,1)S(1)}, u32[]{:S(2)}, u32[]{:S(2)}) collective-permute-start(bf16[512,768]{1,0:T(8,128)(2,1)S(1)} %get-tuple-element.168.refs_0_), channel_id=1, source_target_pairs={{0,16},{4,20},{8,24},{12,28},{16,0},{20,4},{24,8},{28,12},{1,17},{... | collective-permute-start | bytes 2359304 | tf_op jit(solution)/shard_map/ppermute | solution.py:999
  9.6 13.5 %spectral_mix.1 = (f32[192,512]{1,0:T(8,128)S(1)}, bf16[192,512]{1,0:T(8,128)(2,1)S(1)}) custom-call(s32[1]{0:T(128)S(6)} %copy.20.len_ref, f32[6,24,384]{2,1,0:T(8,128)S(1)} %get-tuple-element.108.taps_ref, f32[192,512]{1,0:T(8,128)S(1)} %get-tuple-element.109.x_ref, bf16[2,384,512]{2,1,0:T(8,128)(2,1)S(1)} %get-tuple-element.110.u_ref, ...), custom_call_target="tpu_custom_call" | custom-call | flops 8455716864 | bytes 25165824 | tf_op jit(solution)/shard_map/spectral_mix/pallas_call | solution.py:256
  23.3 3.0 %collective-permute-start.2 = (bf16[192,512]{1,0:T(8,128)(2,1)S(1)}, bf16[192,512]{1,0:T(8,128)(2,1)S(1)}, u32[]{:S(2)}, u32[]{:S(2)}) collective-permute-start(bf16[192,512]{1,0:T(8,128)(2,1)S(1)} %get-tuple-element.115.nt_ref.refs_0_), channel_id=1, source_target_pairs={{0,2},{1,3},{2,0},{3,1},{4,6},{5,7},{6,4},{7,5},{8,10},{9,11},{10,... | collective-permute-start | bytes 589832 | tf_op jit(solution)/shard_map/ppermute | solution.py:986
  29.6 10.4 %collective-permute-done.2.nt_ref.refs_2_ = bf16[192,512]{1,0:T(8,128)(2,1)S(1)} collective-permute-done((bf16[192,512]{1,0:T(8,128)(2,1)S(1)}, bf16[192,512]{1,0:T(8,128)(2,1)S(1)}, u32[]{:S(2)}, u32[]{:S(2)}) %collective-permute-start.2) | collective-permute-done | bytes 196640 | tf_op jit(solution)/shard_map/ppermute | solution.py:986
  42.2 5.1 %collective-permute-start.5 = (bf16[192,512]{1,0:T(8,128)(2,1)S(1)}, bf16[192,512]{1,0:T(8,128)(2,1)S(1)}, u32[]{:S(2)}, u32[]{:S(2)}) collective-permute-start(bf16[192,512]{1,0:T(8,128)(2,1)S(1)} %get-tuple-element.120), channel_id=1, source_target_pairs={{0,1},{1,2},{2,3},{3,0},{4,5},{5,6},{6,7},{7,4},{8,9},{9,10},{10,1... | collective-permute-start | bytes 589832 | tf_op jit(solution)/shard_map/ppermute | solution.py:994
  48.5 1.9 %ffn_grads.1 = (bf16[192,512]{1,0:T(8,128)(2,1)S(1)}, bf16[192,512]{1,0:T(8,128)(2,1)S(1)}, bf16[192,512]{1,0:T(8,128)(2,1)S(1)}, bf16[192,512]{1,0:T(8,128)(2,1...) custom-call(bf16[768,512]{1,0:T(8,128)(2,1)S(1)} %copy-done, bf16[512,512]{1,0:T(8,128)(2,1)S(1)} %copy-done.3, ...), custom_call_target="tpu_custom_call" | custom-call | flops 1610612736 | bytes 4718592 | tf_op jit(solution)/shard_map/ffn_grads/pallas_call | solution.py:373
  50.4 7.0 %collective-permute-done.3.b_ref = bf16[192,512]{1,0:T(8,128)(2,1)S(1)} collective-permute-done((bf16[192,512]{1,0:T(8,128)(2,1)S(1)}, bf16[192,512]{1,0:T(8,128)(2,1)S(1)}, u32[]{:S(2)}, u32[]{:S(2)}) %collective-permute-start.3) | collective-permute-done | bytes 196640 | tf_op jit(solution)/shard_map/ppermute | solution.py:994
  57.5 2.2 %collective-permute-done.8.refs_2_ = bf16[192,512]{1,0:T(8,128)(2,1)S(1)} collective-permute-done((bf16[192,512]{1,0:T(8,128)(2,1)S(1)}, bf16[192,512]{1,0:T(8,128)(2,1)S(1)}, u32[]{:S(2)}, u32[]{:S(2)}) %collective-permute-start.8) | collective-permute-done | bytes 196640 | tf_op jit(solution)/shard_map/ppermute | solution.py:994
  61.4 1.7 %collective-permute-start.10 = (bf16[192,512]{1,0:T(8,128)(2,1)S(1)}, bf16[192,512]{1,0:T(8,128)(2,1)S(1)}, u32[]{:S(2)}, u32[]{:S(2)}) collective-permute-start(bf16[192,512]{1,0:T(8,128)(2,1)S(1)} %get-tuple-element.149.refs_0_), channel_id=1, source_target_pairs={{0,2},{1,3},{2,0},{3,1},{4,6},{5,7},{6,4},{7,5},{8,10},{9,11},{10,... | collective-permute-start | bytes 589832 | tf_op jit(solution)/shard_map/ppermute | solution.py:986
  63.1 2.8 %collective-permute-start.9 = (bf16[192,512]{1,0:T(8,128)(2,1)S(1)}, bf16[192,512]{1,0:T(8,128)(2,1)S(1)}, u32[]{:S(2)}, u32[]{:S(2)}) collective-permute-start(bf16[192,512]{1,0:T(8,128)(2,1)S(1)} %get-tuple-element.149.refs_0_), channel_id=1, source_target_pairs={{0,3},{1,0},{2,1},{3,2},{4,7},{5,4},{6,5},{7,6},{8,11},{9,8},{10,9... | collective-permute-start | bytes 589832 | tf_op jit(solution)/shard_map/ppermute | solution.py:986
  65.9 2.6 %lagged.1 = (bf16[512,3072]{1,0:T(8,128)(2,1)S(1)}, bf16[512,3072]{1,0:T(8,128)(2,1)S(1)}, bf16[512,3072]{1,0:T(8,128)(2,1)S(1)}) custom-call(bf16[512,768]{1,0:T(8,128)(2,1)S(1)} %get-tuple-element.168.refs_0_, bf16[512,768]{1,0:T(8,128)(2,1)S(1)} %collective-permute-done.refs_1_, bf16[512,768]{1,0:T(8,128)(2,1)S(1)} %collective-permute-done.1.refs_2_, ...), custom_call_target="tpu_custom_call" | custom-call | tf_op jit(solution)/shard_map/lagged/pallas_call | solution.py:612
  68.5 5.0 %convolutions.2.conv_ref = bf16[6,128,3072]{2,1,0:T(8,128)(2,1)S(1)} custom-call(f32[24,768]{1,0:T(8,128)S(1)} %get-tuple-element.148.filt_ref, bf16[512,768]{1,0:T(8,128)(2,1)S(1)} %get-tuple-element.168.refs_0_, bf16[512,768]{1,0:T(8,128)(2,1)S(1)} %collective-permute-done.refs_1_, bf16[512,768]{1,0:T(8,128)(2,1)S(1)} %collective-permute-done.1.refs_2_, ...), custom_call_target="tpu_custom_call" | custom-call | tf_op jit(solution)/shard_map/convolutions/pallas_call | solution.py:578
  73.5 4.2 %collective-permute-done.10.refs_2_ = bf16[192,512]{1,0:T(8,128)(2,1)S(1)} collective-permute-done((bf16[192,512]{1,0:T(8,128)(2,1)S(1)}, bf16[192,512]{1,0:T(8,128)(2,1)S(1)}, u32[]{:S(2)}, u32[]{:S(2)}) %collective-permute-start.10) | collective-permute-done | bytes 196640 | tf_op jit(solution)/shard_map/ppermute | solution.py:986
  81.2 4.7 %collective-permute-start.13 = (bf16[192,512]{1,0:T(8,128)(2,1)S(1)}, bf16[192,512]{1,0:T(8,128)(2,1)S(1)}, u32[]{:S(2)}, u32[]{:S(2)}) collective-permute-start(bf16[192,512]{1,0:T(8,128)(2,1)S(1)} %get-tuple-element.165), channel_id=1, source_target_pairs={{0,1},{1,2},{2,3},{3,0},{4,5},{5,6},{6,7},{7,4},{8,9},{9,10},{10,1... | collective-permute-start | bytes 589832 | tf_op jit(solution)/shard_map/ppermute | solution.py:994
  85.9 1.9 %collective-permute-start.14 = (bf16[192,512]{1,0:T(8,128)(2,1)S(1)}, bf16[192,512]{1,0:T(8,128)(2,1)S(1)}, u32[]{:S(2)}, u32[]{:S(2)}) collective-permute-start(bf16[192,512]{1,0:T(8,128)(2,1)S(1)} %get-tuple-element.166), channel_id=1, source_target_pairs={{0,2},{1,3},{2,0},{3,1},{4,6},{5,7},{6,4},{7,5},{8,10},{9,11},{10,... | collective-permute-start | bytes 589832 | tf_op jit(solution)/shard_map/ppermute | solution.py:994
  88.2 17.0 %spectral_unmix.1 = (bf16[192,512]{1,0:T(8,128)(2,1)S(1)}, f32[16,512]{1,0:T(8,128)S(1)}) custom-call(s32[1]{0:T(128)S(6)} %copy.20.len_ref, f32[6,24,384]{2,1,0:T(8,128)S(1)} %get-tuple-element.108.taps_ref, f32[192,512]{1,0:T(8,128)S(1)} %get-tuple-element.109.x_ref, f32[192,512]{1,0:T(8,128)S(1)} %get-tuple-element.138.bh_ref, ...), custom_call_target="tpu_custom_call" | custom-call | flops 8455716864 | bytes 25165824 | tf_op jit(solution)/shard_map/spectral_unmix/pallas_call | solution.py:518
  106.7 3.3 %collective-permute-start.18 = (bf16[384,512]{1,0:T(8,128)(2,1)S(1)}, bf16[384,512]{1,0:T(8,128)(2,1)S(1)}, u32[]{:S(2)}, u32[]{:S(2)}) collective-permute-start(bf16[384,512]{1,0:T(8,128)(2,1)S(1)} %rows_message.1.refs_0_), channel_id=1, source_target_pairs={{0,1},{1,2},{2,3},{3,0},{4,5},{5,6},{6,7},{7,4},{8,9},{9,10},{10,1... | collective-permute-start | bytes 1179656 | tf_op jit(solution)/shard_map/ppermute | solution.py:986
  112.4 5.0 %convolutions.3.conv_two_ref = bf16[6,128,3072]{2,1,0:T(8,128)(2,1)S(1)} custom-call(f32[24,768]{1,0:T(8,128)S(1)} %get-tuple-element.148.filt_ref, bf16[512,768]{1,0:T(8,128)(2,1)S(1)} %get-tuple-element.168.refs_0_, bf16[512,768]{1,0:T(8,128)(2,1)S(1)} %collective-permute-done.refs_1_, bf16[512,768]{1,0:T(8,128)(2,1)S(1)} %collective-permute-done.1.refs_2_, ...), custom_call_target="tpu_custom_call" | custom-call | tf_op jit(solution)/shard_map/convolutions/pallas_call | solution.py:578
  117.4 3.1 %collective-permute-done.21.refs_6_.from_y = bf16[608,512]{1,0:T(8,128)(2,1)S(1)} collective-permute-done((bf16[608,512]{1,0:T(8,128)(2,1)S(1)}, bf16[608,512]{1,0:T(8,128)(2,1)S(1)}, u32[]{:S(2)}, u32[]{:S(2)}) %collective-permute-start.21) | collective-permute-done | bytes 622624 | tf_op jit(solution)/shard_map/ppermute | solution.py:999
  123.0 4.0 %collective-permute-done.23.recv_ref.refs_2_ = bf16[224,512]{1,0:T(8,128)(2,1)S(1)} collective-permute-done((bf16[224,512]{1,0:T(8,128)(2,1)S(1)}, bf16[224,512]{1,0:T(8,128)(2,1)S(1)}, u32[]{:S(2)}, u32[]{:S(2)}) %collective-permute-start.23) | collective-permute-done | bytes 229408 | tf_op jit(solution)/shard_map/ppermute | solution.py:999
  127.1 11.7 %matrix_grads.1 = (f32[12,64,512]{2,1,0:T(8,128)S(1)}, bf16[2304,512]{1,0:T(8,128)(2,1)S(1)}) custom-call(bf16[6,128,3072]{2,1,0:T(8,128)(2,1)S(1)} %convolutions.2.conv_ref, bf16[6,128,3072]{2,1,0:T(8,128)(2,1)S(1)} %convolutions.3.conv_two_ref, bf16[512,3072]{1,0:T(8,128)(2,1)S(1)} %get-tuple-element.145.refs_0_, ...), custom_call_target="tpu_custom_call" | custom-call | tf_op jit(solution)/shard_map/matrix_grads/pallas_call | solution.py:671
  139.6 4.9 %collective-permute-start.29 = (f32[16,512]{1,0:T(8,128)S(1)}, f32[16,512]{1,0:T(8,128)S(1)}, u32[]{:S(2)}, u32[]{:S(2)}) collective-permute-start(f32[16,512]{1,0:T(8,128)S(1)} %ordered_sum.2.refs_0_), channel_id=1, source_target_pairs={{0,1},{1,2},{2,3},{3,0},{4,5},{5,6},{6,7},{7,4},{8,9},{9,10},{10,1... | collective-permute-start | bytes 98312 | tf_op jit(solution)/shard_map/ppermute | solution.py:986
  144.5 1.7 %collective-permute-start.28 = (f32[16,512]{1,0:T(8,128)S(1)}, f32[16,512]{1,0:T(8,128)S(1)}, u32[]{:S(2)}, u32[]{:S(2)}) collective-permute-start(f32[16,512]{1,0:T(8,128)S(1)} %ordered_sum.2.refs_0_), channel_id=1, source_target_pairs={{0,2},{1,3},{2,0},{3,1},{4,6},{5,7},{6,4},{7,5},{8,10},{9,11},{10,... | collective-permute-start | bytes 98312 | tf_op jit(solution)/shard_map/ppermute | solution.py:986
  148.5 3.7 %finish.1 = (f32[12,64,512]{2,1,0:T(8,128)}, f32[3,512,512]{2,1,0:T(8,128)}, f32[512,512]{1,0:T(8,128)}, f32[512,512]{1,0:T(8,128)}, f32[512,512]{1,0:T(8,128)}) custom-call(f32[12,64,512]{2,1,0:T(8,128)S(1)} %get-tuple-element.188.keep_ref, bf16[3072,512]{1,0:T(8,128)(2,1)S(1)} %join_pieces.1.send_ref, bf16[3072,512]{1,0:T(8,128)(2,1)S(1)} %collective-permute-done.26.recv_ref), custom_call_target="tpu_custom_call" | custom-call | flops 393216 | bytes 3932160 | tf_op jit(solution)/shard_map/finish/pallas_call | solution.py:968
  (77 shorter events, 27.6 us)
Async XLA Ops:
  5.1 22.6 %collective-permute-start.1 = (bf16[512,768]{1,0:T(8,128)(2,1)S(1)}, bf16[512,768]{1,0:T(8,128)(2,1)S(1)}, u32[]{:S(2)}, u32[]{:S(2)}) collective-permute-start(bf16[512,768]{1,0:T(8,128)(2,1)S(1)} %get-tuple-element.168.refs_0_), channel_id=1, source_target_pairs={{0,16},{4,20},{8,24},{12,28},{16,0},{20,4},{24,8},{28,12},{1,17},{... | collective-permute-start | bytes 2359304 | tf_op jit(solution)/shard_map/ppermute | solution.py:999
  8.1 20.5 %collective-permute-start = (bf16[512,768]{1,0:T(8,128)(2,1)S(1)}, bf16[512,768]{1,0:T(8,128)(2,1)S(1)}, u32[]{:S(2)}, u32[]{:S(2)}) collective-permute-start(bf16[512,768]{1,0:T(8,128)(2,1)S(1)} %get-tuple-element.168.refs_0_), channel_id=1, source_target_pairs={{0,8},{4,12},{8,0},{12,4},{16,24},{20,28},{24,16},{28,20},{1,9},{5... | collective-permute-start | bytes 2359304 | tf_op jit(solution)/shard_map/ppermute | solution.py:999
  23.2 34.3 %collective-permute-start.7 = (bf16[512,768]{1,0:T(8,128)(2,1)S(1)}, bf16[512,768]{1,0:T(8,128)(2,1)S(1)}, u32[]{:S(2)}, u32[]{:S(2)}) collective-permute-start(bf16[512,768]{1,0:T(8,128)(2,1)S(1)} %get-tuple-element.168.refs_0_), channel_id=1, source_target_pairs={{0,24},{4,28},{8,16},{12,20},{16,8},{20,12},{24,0},{28,4},{1,25},{... | collective-permute-start | bytes 2359304 | tf_op jit(solution)/shard_map/ppermute | solution.py:999
  23.3 16.7 %collective-permute-start.2 = (bf16[192,512]{1,0:T(8,128)(2,1)S(1)}, bf16[192,512]{1,0:T(8,128)(2,1)S(1)}, u32[]{:S(2)}, u32[]{:S(2)}) collective-permute-start(bf16[192,512]{1,0:T(8,128)(2,1)S(1)} %get-tuple-element.115.nt_ref.refs_0_), channel_id=1, source_target_pairs={{0,2},{1,3},{2,0},{3,1},{4,6},{5,7},{6,4},{7,5},{8,10},{9,11},{10,... | collective-permute-start | bytes 589832 | tf_op jit(solution)/shard_map/ppermute | solution.py:986
  26.3 14.9 %collective-permute-start.4 = (bf16[192,512]{1,0:T(8,128)(2,1)S(1)}, bf16[192,512]{1,0:T(8,128)(2,1)S(1)}, u32[]{:S(2)}, u32[]{:S(2)}) collective-permute-start(bf16[192,512]{1,0:T(8,128)(2,1)S(1)} %get-tuple-element.115.nt_ref.refs_0_), channel_id=1, source_target_pairs={{0,3},{1,0},{2,1},{3,2},{4,7},{5,4},{6,5},{7,6},{8,11},{9,8},{10,9... | collective-permute-start | bytes 589832 | tf_op jit(solution)/shard_map/ppermute | solution.py:986
  27.6 19.7 %collective-permute-start.6 = (bf16[192,512]{1,0:T(8,128)(2,1)S(1)}, bf16[192,512]{1,0:T(8,128)(2,1)S(1)}, u32[]{:S(2)}, u32[]{:S(2)}) collective-permute-start(bf16[192,512]{1,0:T(8,128)(2,1)S(1)} %get-tuple-element.115.nt_ref.refs_0_), channel_id=1, source_target_pairs={{0,1},{1,2},{2,3},{3,0},{4,5},{5,6},{6,7},{7,4},{8,9},{9,10},{10,1... | collective-permute-start | bytes 589832 | tf_op jit(solution)/shard_map/ppermute | solution.py:986
  41.1 16.4 %collective-permute-start.3 = (bf16[192,512]{1,0:T(8,128)(2,1)S(1)}, bf16[192,512]{1,0:T(8,128)(2,1)S(1)}, u32[]{:S(2)}, u32[]{:S(2)}) collective-permute-start(bf16[192,512]{1,0:T(8,128)(2,1)S(1)} %get-tuple-element.118), channel_id=1, source_target_pairs={{0,2},{1,3},{2,0},{3,1},{4,6},{5,7},{6,4},{7,5},{8,10},{9,11},{10,... | collective-permute-start | bytes 589832 | tf_op jit(solution)/shard_map/ppermute | solution.py:994
  42.2 15.3 %collective-permute-start.5 = (bf16[192,512]{1,0:T(8,128)(2,1)S(1)}, bf16[192,512]{1,0:T(8,128)(2,1)S(1)}, u32[]{:S(2)}, u32[]{:S(2)}) collective-permute-start(bf16[192,512]{1,0:T(8,128)(2,1)S(1)} %get-tuple-element.120), channel_id=1, source_target_pairs={{0,1},{1,2},{2,3},{3,0},{4,5},{5,6},{6,7},{7,4},{8,9},{9,10},{10,1... | collective-permute-start | bytes 589832 | tf_op jit(solution)/shard_map/ppermute | solution.py:994
  60.0 17.7 %collective-permute-start.12 = (bf16[768,512]{1,0:T(8,128)(2,1)S(1)}, bf16[768,512]{1,0:T(8,128)(2,1)S(1)}, u32[]{:S(2)}, u32[]{:S(2)}) collective-permute-start(bf16[768,512]{1,0:T(8,128)(2,1)S(1)} %get-tuple-element.160), channel_id=1, source_target_pairs={{0,4},{4,0},{8,12},{12,8},{16,20},{20,16},{24,28},{28,24},{1,5},{5... | collective-permute-start | bytes 2359304 | tf_op jit(solution)/shard_map/ppermute | solution.py:999
  60.1 13.5 %collective-permute-start.11 = (bf16[192,512]{1,0:T(8,128)(2,1)S(1)}, bf16[192,512]{1,0:T(8,128)(2,1)S(1)}, u32[]{:S(2)}, u32[]{:S(2)}) collective-permute-start(bf16[192,512]{1,0:T(8,128)(2,1)S(1)} %get-tuple-element.149.refs_0_), channel_id=1, source_target_pairs={{0,1},{1,2},{2,3},{3,0},{4,5},{5,6},{6,7},{7,4},{8,9},{9,10},{10,1... | collective-permute-start | bytes 589832 | tf_op jit(solution)/shard_map/ppermute | solution.py:986
  61.4 16.3 %collective-permute-start.10 = (bf16[192,512]{1,0:T(8,128)(2,1)S(1)}, bf16[192,512]{1,0:T(8,128)(2,1)S(1)}, u32[]{:S(2)}, u32[]{:S(2)}) collective-permute-start(bf16[192,512]{1,0:T(8,128)(2,1)S(1)} %get-tuple-element.149.refs_0_), channel_id=1, source_target_pairs={{0,2},{1,3},{2,0},{3,1},{4,6},{5,7},{6,4},{7,5},{8,10},{9,11},{10,... | collective-permute-start | bytes 589832 | tf_op jit(solution)/shard_map/ppermute | solution.py:986
  63.1 14.6 %collective-permute-start.9 = (bf16[192,512]{1,0:T(8,128)(2,1)S(1)}, bf16[192,512]{1,0:T(8,128)(2,1)S(1)}, u32[]{:S(2)}, u32[]{:S(2)}) collective-permute-start(bf16[192,512]{1,0:T(8,128)(2,1)S(1)} %get-tuple-element.149.refs_0_), channel_id=1, source_target_pairs={{0,3},{1,0},{2,1},{3,2},{4,7},{5,4},{6,5},{7,6},{8,11},{9,8},{10,9... | collective-permute-start | bytes 589832 | tf_op jit(solution)/shard_map/ppermute | solution.py:986
  78.1 27.3 %collective-permute-start.19 = (bf16[960,512]{1,0:T(8,128)(2,1)S(1)}, bf16[960,512]{1,0:T(8,128)(2,1)S(1)}, u32[]{:S(2)}, u32[]{:S(2)}) collective-permute-start(bf16[960,512]{1,0:T(8,128)(2,1)S(1)} %get-tuple-element.174), channel_id=1, source_target_pairs={{0,8},{4,12},{8,0},{12,4},{16,24},{20,28},{24,16},{28,20},{1,9},{5... | collective-permute-start | bytes 2949128 | tf_op jit(solution)/shard_map/ppermute | solution.py:999
  79.7 25.8 %collective-permute-start.20 = (bf16[960,512]{1,0:T(8,128)(2,1)S(1)}, bf16[960,512]{1,0:T(8,128)(2,1)S(1)}, u32[]{:S(2)}, u32[]{:S(2)}) collective-permute-start(bf16[960,512]{1,0:T(8,128)(2,1)S(1)} %get-tuple-element.175), channel_id=1, source_target_pairs={{0,16},{4,20},{8,24},{12,28},{16,0},{20,4},{24,8},{28,12},{1,17},{... | collective-permute-start | bytes 2949128 | tf_op jit(solution)/shard_map/ppermute | solution.py:999
  81.2 24.1 %collective-permute-start.13 = (bf16[192,512]{1,0:T(8,128)(2,1)S(1)}, bf16[192,512]{1,0:T(8,128)(2,1)S(1)}, u32[]{:S(2)}, u32[]{:S(2)}) collective-permute-start(bf16[192,512]{1,0:T(8,128)(2,1)S(1)} %get-tuple-element.165), channel_id=1, source_target_pairs={{0,1},{1,2},{2,3},{3,0},{4,5},{5,6},{6,7},{7,4},{8,9},{9,10},{10,1... | collective-permute-start | bytes 589832 | tf_op jit(solution)/shard_map/ppermute | solution.py:994
  85.9 19.4 %collective-permute-start.14 = (bf16[192,512]{1,0:T(8,128)(2,1)S(1)}, bf16[192,512]{1,0:T(8,128)(2,1)S(1)}, u32[]{:S(2)}, u32[]{:S(2)}) collective-permute-start(bf16[192,512]{1,0:T(8,128)(2,1)S(1)} %get-tuple-element.166), channel_id=1, source_target_pairs={{0,2},{1,3},{2,0},{3,1},{4,6},{5,7},{6,4},{7,5},{8,10},{9,11},{10,... | collective-permute-start | bytes 589832 | tf_op jit(solution)/shard_map/ppermute | solution.py:994
  87.8 17.5 %collective-permute-start.15 = (bf16[192,512]{1,0:T(8,128)(2,1)S(1)}, bf16[192,512]{1,0:T(8,128)(2,1)S(1)}, u32[]{:S(2)}, u32[]{:S(2)}) collective-permute-start(bf16[192,512]{1,0:T(8,128)(2,1)S(1)} %get-tuple-element.167), channel_id=1, source_target_pairs={{0,3},{1,0},{2,1},{3,2},{4,7},{5,4},{6,5},{7,6},{8,11},{9,8},{10,9... | collective-permute-start | bytes 589832 | tf_op jit(solution)/shard_map/ppermute | solution.py:994
  105.6 14.9 %collective-permute-start.21 = (bf16[608,512]{1,0:T(8,128)(2,1)S(1)}, bf16[608,512]{1,0:T(8,128)(2,1)S(1)}, u32[]{:S(2)}, u32[]{:S(2)}) collective-permute-start(bf16[608,512]{1,0:T(8,128)(2,1)S(1)} %get-tuple-element.179), channel_id=1, source_target_pairs={{0,16},{4,20},{8,24},{12,28},{16,0},{20,4},{24,8},{28,12},{1,17},{... | collective-permute-start | bytes 1867784 | tf_op jit(solution)/shard_map/ppermute | solution.py:999
  106.2 14.6 %collective-permute-start.22 = (bf16[608,512]{1,0:T(8,128)(2,1)S(1)}, bf16[608,512]{1,0:T(8,128)(2,1)S(1)}, u32[]{:S(2)}, u32[]{:S(2)}) collective-permute-start(bf16[608,512]{1,0:T(8,128)(2,1)S(1)} %get-tuple-element.180), channel_id=1, source_target_pairs={{0,8},{4,12},{8,0},{12,4},{16,24},{20,28},{24,16},{28,20},{1,9},{5... | collective-permute-start | bytes 1867784 | tf_op jit(solution)/shard_map/ppermute | solution.py:999
  106.7 32.1 %collective-permute-start.18 = (bf16[384,512]{1,0:T(8,128)(2,1)S(1)}, bf16[384,512]{1,0:T(8,128)(2,1)S(1)}, u32[]{:S(2)}, u32[]{:S(2)}) collective-permute-start(bf16[384,512]{1,0:T(8,128)(2,1)S(1)} %rows_message.1.refs_0_), channel_id=1, source_target_pairs={{0,1},{1,2},{2,3},{3,0},{4,5},{5,6},{6,7},{7,4},{8,9},{9,10},{10,1... | collective-permute-start | bytes 1179656 | tf_op jit(solution)/shard_map/ppermute | solution.py:986
  110.0 28.8 %collective-permute-start.17 = (bf16[384,512]{1,0:T(8,128)(2,1)S(1)}, bf16[384,512]{1,0:T(8,128)(2,1)S(1)}, u32[]{:S(2)}, u32[]{:S(2)}) collective-permute-start(bf16[384,512]{1,0:T(8,128)(2,1)S(1)} %rows_message.1.refs_0_), channel_id=1, source_target_pairs={{0,2},{1,3},{2,0},{3,1},{4,6},{5,7},{6,4},{7,5},{8,10},{9,11},{10,... | collective-permute-start | bytes 1179656 | tf_op jit(solution)/shard_map/ppermute | solution.py:986
  111.6 27.2 %collective-permute-start.16 = (bf16[384,512]{1,0:T(8,128)(2,1)S(1)}, bf16[384,512]{1,0:T(8,128)(2,1)S(1)}, u32[]{:S(2)}, u32[]{:S(2)}) collective-permute-start(bf16[384,512]{1,0:T(8,128)(2,1)S(1)} %rows_message.1.refs_0_), channel_id=1, source_target_pairs={{0,3},{1,0},{2,1},{3,2},{4,7},{5,4},{6,5},{7,6},{8,11},{9,8},{10,9... | collective-permute-start | bytes 1179656 | tf_op jit(solution)/shard_map/ppermute | solution.py:986
  121.5 17.4 %collective-permute-start.24 = (bf16[192,512]{1,0:T(8,128)(2,1)S(1)}, bf16[192,512]{1,0:T(8,128)(2,1)S(1)}, u32[]{:S(2)}, u32[]{:S(2)}) collective-permute-start(bf16[192,512]{1,0:T(8,128)(2,1)S(1)} %get-tuple-element.194.refs_1_), channel_id=1, source_target_pairs={{0,16},{4,20},{8,24},{12,28},{16,0},{20,4},{24,8},{28,12},{1,17},{... | collective-permute-start | bytes 589832 | tf_op jit(solution)/shard_map/ppermute | solution.py:999
  139.6 12.7 %collective-permute-start.29 = (f32[16,512]{1,0:T(8,128)S(1)}, f32[16,512]{1,0:T(8,128)S(1)}, u32[]{:S(2)}, u32[]{:S(2)}) collective-permute-start(f32[16,512]{1,0:T(8,128)S(1)} %ordered_sum.2.refs_0_), channel_id=1, source_target_pairs={{0,1},{1,2},{2,3},{3,0},{4,5},{5,6},{6,7},{7,4},{8,9},{9,10},{10,1... | collective-permute-start | bytes 98312 | tf_op jit(solution)/shard_map/ppermute | solution.py:986
  (13 other events, 149.9 us)

commit v4 on v3

v4 whole, which is shorter than its diff:
```python
import functools

import jax
import jax.numpy as jnp
from jax import lax
from jax.experimental import pallas as pl
from jax.experimental.pallas import tpu as pltpu
from jax.sharding import PartitionSpec as P

EPS = 1e-05
BF = jnp.bfloat16
F32 = jnp.float32
SQRT_2_PI = 0.7978845608028654
CUBIC = 0.044715
VMEM_LIMIT = 20 << 20


def dot(left, right):
    return jnp.dot(left, right, preferred_element_type=F32)


def dot_cols(left, right):
    return lax.dot_general(left, right, (((1,), (1,)), ((), ())), preferred_element_type=F32)


def params(limit=VMEM_LIMIT):
    return pltpu.CompilerParams(vmem_limit_bytes=limit)


COST_SCALE = 1.0


def cost(flops, nbytes):
    return pl.CostEstimate(
        flops=int(COST_SCALE * flops), bytes_accessed=int(COST_SCALE * nbytes), transcendentals=0
    )


def smem():
    return pl.BlockSpec(memory_space=pltpu.SMEM)


def whole():
    return pl.BlockSpec(memory_space=pltpu.VMEM)


def outside():
    return pl.BlockSpec(memory_space=pltpu.HBM)


def toeplitz(base_row, rows, first=0, step=1):
    wide = jnp.broadcast_to(base_row, (rows, base_row.shape[1]))
    return pltpu.roll(wide, first, 1, stride=step, stride_axis=0)


def put_columns(scr, value, at=0):
    for c in range(scr.shape[0]):
        scr[c, at : at + value.shape[0], :] = value[:, c * 128 : (c + 1) * 128]


def every_nth(scr, start, count, step):
    columns = [scr[c, pl.ds(start, count, stride=step), :] for c in range(scr.shape[0])]
    return columns[0] if len(columns) == 1 else jnp.concatenate(columns, axis=1)


def put_every_nth(scr, value, start, step):
    for c in range(scr.shape[0]):
        columns = slice(c * 128, (c + 1) * 128)
        scr[c, pl.ds(start, value.shape[0], stride=step), :] = value[:, columns]


def columns_of(scr, count):
    return jnp.concatenate([scr[c, :count, :] for c in range(scr.shape[0])], axis=1)


def norm_kernel(
    n, share, order, len_ref, x_ref, gain_ref, filt_ref,
    u_ref, ut_ref, ut_two_ref, own_ref, lag_ref, taps_ref, nat_ref, scr, scr_f,
):
    length, width = x_ref.shape
    m = lax.axis_index("mp")
    filt = nat_ref.shape[0]
    x = x_ref[...].astype(F32)
    r1 = lax.rsqrt(jnp.mean(x * x, axis=-1, keepdims=True) + EPS)
    row = lax.broadcasted_iota(jnp.int32, (length, 1), 0)
    mask = (row < len_ref[0]).astype(F32)
    u = mask * x * r1 * gain_ref[0:1, :]
    scr[:, :8, :] = jnp.zeros((scr.shape[0], 8, 128), F32)
    put_columns(scr, u, 8)
    ut = u.T.astype(BF)
    ut_ref[...] = ut
    ut_two_ref[:width, :] = ut
    ut_two_ref[width:, :] = jnp.zeros((ut_two_ref.shape[0] - width, length), BF)
    for odd in range(2):
        u_ref[odd] = every_nth(scr, odd + 8, length // 2, 2).astype(BF)
    for lag in range(order):
        rows = every_nth(scr, m + 8 - lag, share, n)
        lag_ref[:, lag * width : (lag + 1) * width] = rows.astype(BF)
    put_columns(scr, x, 8)
    own_ref[...] = every_nth(scr, m + 8, share, n)
    half = length // 2
    natural = filt_ref[...].astype(F32)
    nat_ref[...] = natural
    scr_f[0, :length, :filt] = natural.T
    even = every_nth(scr_f, 0, half, 2).T[:filt]
    odd = every_nth(scr_f, 1, half, 2).T[:filt]
    i = lax.broadcasted_iota(jnp.int32, (half, half), 0)
    j = lax.broadcasted_iota(jnp.int32, (half, half), 1)
    flip = (i == jnp.where(j == 0, 0, half - j)).astype(F32).astype(BF)
    rev_even = dot(even.astype(BF), flip)
    rev_odd = dot(odd.astype(BF), flip)
    shift, is_odd = m // 2, lax.rem(m, 2)
    one, two = jnp.where(is_odd == 0, rev_even, rev_odd), jnp.where(is_odd == 0, rev_odd, rev_even)
    taps_ref[0] = pltpu.roll(one, shift, 1)
    taps_ref[1] = pltpu.roll(two, lax.rem(shift + half - 1 + is_odd, half), 1)
    one, two = jnp.where(is_odd == 0, even, odd), jnp.where(is_odd == 0, odd, even)
    taps_ref[2] = pltpu.roll(one, shift + is_odd, 1)
    taps_ref[3] = pltpu.roll(two, shift, 1)


def first_norm(lengths, x, gains, filters, n, order):
    length, width = x.shape
    share = length // n
    filt = filters.shape[0]
    return pl.pallas_call(
        functools.partial(norm_kernel, n, share, order),
        in_specs=[smem()] + [whole()] * 3,
        out_specs=[whole()] * 7,
        out_shape=[
            jax.ShapeDtypeStruct((2, length // 2, width), BF),
            jax.ShapeDtypeStruct((width, length), BF),
            jax.ShapeDtypeStruct((width + 16, length), BF),
            jax.ShapeDtypeStruct((share, width), F32),
            jax.ShapeDtypeStruct((share, order * width), BF),
            jax.ShapeDtypeStruct((4, filt, length // 2), F32),
            jax.ShapeDtypeStruct((filt, length), F32),
        ],
        scratch_shapes=[
            pltpu.VMEM((width // 128, length + 24, 128), F32),
            pltpu.VMEM((1, length + 8, 128), F32),
        ],
        compiler_params=params(),
        cost_estimate=cost(10 * x.size, 6 * x.size),
        name="first_norm",
    )(lengths, x, gains, filters)


def fetch_matrices(j, steps, kb, stu_hbm, w_buf, sems):
    def copies(step):
        slot = lax.rem(step, 2)
        return [
            pltpu.make_async_copy(
                stu_hbm.at[pl.ds((sign * steps + step) * kb, kb)],
                w_buf.at[slot, sign],
                sems.at[slot, sign],
            )
            for sign in range(2)
        ]

    @pl.when(j == 0)
    def _():
        for copy in copies(j):
            copy.start()

    @pl.when(j + 1 < steps)
    def _():
        for copy in copies(j + 1):
            copy.start()

    def wait():
        for copy in copies(j):
            copy.wait()

    return lax.rem(j, 2), wait


def fetch_last(j, steps, src, dst, sem):
    copy = pltpu.make_async_copy(src, dst, sem)

    @pl.when(j == 0)
    def _():
        copy.start()

    @pl.when(j == steps - 1)
    def _():
        copy.wait()


def mix_kernel(
    kb, n, len_ref, taps_ref, x_ref, u_ref, lag_ref, gain_ref, stu_hbm, ar_hbm,
    hid_ref, nt_ref, ta_ref, tb_ref, tc_ref, td_ref, c_ref, acc_ref, w_buf, ar_ref, sems, ar_sem,
):
    j, steps = pl.program_id(0), pl.num_programs(0)
    half, width = u_ref.shape[1:]
    share, step = x_ref.shape[0], n // 2
    m = lax.axis_index("mp")
    shift, is_odd = m // 2, lax.rem(m, 2)
    depth = ta_ref.shape[1]
    first = ta_ref.shape[0] // kb
    rest = share - first
    row = lax.broadcasted_iota(jnp.int32, (share, half), 0) * step + shift
    col = lax.broadcasted_iota(jnp.int32, (share, half), 1)
    upto, below = col <= row, col <= row - 1 + is_odd
    slot, wait = fetch_matrices(j, stu_hbm.shape[0] // (2 * kb), kb, stu_hbm, w_buf, sems)

    @pl.when(j == 0)
    def _():
        acc_ref[...] = jnp.zeros((share, width), F32)

    for k in range(kb):
        for which, valid, short, full in ((0, upto, ta_ref, tc_ref), (1, below, tb_ref, td_ref)):
            base = taps_ref[which, pl.ds(j * kb + k, 1), :]
            t = toeplitz(base, first, 0, step)
            t = jnp.where(valid[:first], t, 0.0).astype(BF)
            short[k * first : (k + 1) * first, :] = t[:, :depth]
            t = toeplitz(base, rest, step * first, step)
            full[k * rest : (k + 1) * rest, :] = jnp.where(valid[first:], t, 0.0).astype(BF)
    ca, cb = dot(ta_ref[...], u_ref[0, :depth]), dot(tb_ref[...], u_ref[1, :depth])
    cc, cd = dot(tc_ref[...], u_ref[0]), dot(td_ref[...], u_ref[1])
    sign = jnp.where(is_odd == 0, 1.0, -1.0)
    for k in range(kb):
        plus = slice(k * width, (k + 1) * width)
        minus = slice((kb + k) * width, (kb + k + 1) * width)
        pa, pb = ca[k * first : (k + 1) * first], cb[k * first : (k + 1) * first]
        c_ref[:first, plus] = (pa + pb).astype(BF)
        c_ref[:first, minus] = ((pa - pb) * sign).astype(BF)
        pa, pb = cc[k * rest : (k + 1) * rest], cd[k * rest : (k + 1) * rest]
        c_ref[first:, plus] = (pa + pb).astype(BF)
        c_ref[first:, minus] = ((pa - pb) * sign).astype(BF)
    wait()
    acc_ref[...] += dot(c_ref[...], w_buf[slot].reshape(2 * kb * width, width))
    fetch_last(j, steps, ar_hbm, ar_ref, ar_sem)

    @pl.when(j == steps - 1)
    def _():
        total = acc_ref[...] + dot(lag_ref[...], ar_ref[...].reshape(lag_ref.shape[1], width))
        hidden = x_ref[...] + total
        hid_ref[...] = hidden
        r2 = lax.rsqrt(jnp.mean(hidden * hidden, axis=-1, keepdims=True) + EPS)
        pos = n * lax.broadcasted_iota(jnp.int32, (share, 1), 0) + m
        mask = (pos < len_ref[0]).astype(F32)
        nt_ref[...] = (mask * hidden * r2 * gain_ref[1:2, :]).astype(BF)


def matrix_scratch(kb, ar):
    width = ar.shape[1]
    return [
        pltpu.VMEM((2, 2, kb, width, width), BF),
        pltpu.VMEM(ar.shape, BF),
        pltpu.SemaphoreType.DMA((2, 2)),
        pltpu.SemaphoreType.DMA,
    ]


def spectral_mix(lengths, taps, x, u, lags, gains, stu, ar, n, kb):
    share, width = x.shape
    half = u.shape[1]
    filt = taps.shape[1]
    depth = min(256, half)
    first = depth // (n // 2)
    return pl.pallas_call(
        functools.partial(mix_kernel, kb, n),
        grid=(filt // kb,),
        in_specs=[smem()] + [whole()] * 5 + [outside()] * 2,
        out_specs=[whole()] * 2,
        out_shape=[
            jax.ShapeDtypeStruct((share, width), F32),
            jax.ShapeDtypeStruct((share, width), BF),
        ],
        scratch_shapes=[pltpu.VMEM((kb * first, depth), BF)] * 2
        + [pltpu.VMEM((kb * (share - first), half), BF)] * 2
        + [pltpu.VMEM((share, 2 * kb * width), BF), pltpu.VMEM((share, width), F32)]
        + matrix_scratch(kb, ar),
        compiler_params=params(51 << 20),
        cost_estimate=cost(0, 0),
        name="spectral_mix",
    )(lengths, taps, x, u, lags, gains, stu, ar)


def dealt_kernel(n, in_ref, out_ref, scr):
    share = out_ref.shape[0] // n
    put_columns(scr, in_ref[...].astype(F32))
    for m in range(n):
        out_ref[m * share : (m + 1) * share, :] = every_nth(scr, m, share, n).astype(BF)


def dealt_rows(value, n):
    length, width = value.shape
    return pl.pallas_call(
        functools.partial(dealt_kernel, n),
        in_specs=[whole()],
        out_specs=whole(),
        out_shape=jax.ShapeDtypeStruct(value.shape, BF),
        scratch_shapes=[pltpu.VMEM((width // 128, length + 16, 128), F32)],
        compiler_params=params(),
        cost_estimate=cost(value.size, 4 * value.size),
        name="dealt_rows",
    )(value)


def half_kernel(gate_hbm, up_hbm, down_hbm, out_ref, sems):
    rows = gate_hbm.shape[0] // 2
    start = pl.multiple_of(lax.rem(lax.axis_index("dp"), 2) * rows, 16)
    copies = [
        pltpu.make_async_copy(src.at[pl.ds(start, rows)], out_ref.at[k], sems.at[k])
        for k, src in enumerate((gate_hbm, up_hbm, down_hbm))
    ]
    for copy in copies:
        copy.start()
    for copy in copies:
        copy.wait()


def half_weights(gate, up, down):
    rows, width = gate.shape
    return pl.pallas_call(
        half_kernel,
        in_specs=[outside()] * 3,
        out_specs=whole(),
        out_shape=jax.ShapeDtypeStruct((3, rows // 2, width), BF),
        scratch_shapes=[pltpu.SemaphoreType.DMA((3,))],
        compiler_params=params(),
        cost_estimate=cost(0, 6 * gate.size),
        name="half_weights",
    )(gate, up, down)


def both_halves_kernel(own_ref, other_ref, *out_refs):
    rows = own_ref.shape[1]
    core = lax.rem(lax.axis_index("dp"), 2)
    for ref, which in ((own_ref, core), (other_ref, 1 - core)):
        start = pl.multiple_of(which * rows, 16)
        for k, out in enumerate(out_refs):
            out[pl.ds(start, rows), :] = ref[k]


def both_halves(own, other):
    count, rows, width = own.shape
    return pl.pallas_call(
        both_halves_kernel,
        in_specs=[whole()] * 2,
        out_specs=[whole()] * count,
        out_shape=[jax.ShapeDtypeStruct((2 * rows, width), BF)] * count,
        compiler_params=params(),
        cost_estimate=cost(0, 4 * own.size),
        name="both_halves",
    )(own, other)


def hidden_part(nt, cot, gw, uw, dw):
    gate = dot(nt, gw)
    upper = dot(nt, uw)
    back_act = dot_cols(cot, dw)
    square = gate * gate
    th = jnp.tanh(SQRT_2_PI * (gate + CUBIC * square * gate))
    half = 0.5 * (1.0 + th)
    gelu = gate * half
    slope = half + 0.5 * gate * (1.0 - th * th) * (SQRT_2_PI * (1.0 + 3.0 * CUBIC * square))
    act = (gelu * upper).astype(BF)
    return act, (back_act * upper * slope).astype(BF), (back_act * gelu).astype(BF)


def rows_of(cot_ref, which, share):
    return cot_ref[pl.ds(pl.multiple_of(which * share, 16), share), :]


def ffn_kernel(shift, n, nt_ref, cot_ref, *refs):
    w_refs, (bn_ref, out_ref, act_ref, bg_ref, bu_ref) = refs[:6], refs[6:]
    nt = nt_ref[...]
    cot = rows_of(cot_ref, lax.rem(lax.axis_index("mp") + shift, n), nt.shape[0])
    bn, out = 0.0, 0.0
    for k in range(2):
        gw, uw, dw = (ref[...] for ref in w_refs[3 * k : 3 * k + 3])
        act, bg, bu = hidden_part(nt, cot, gw, uw, dw)
        bn = bn + dot_cols(bg, gw) + dot_cols(bu, uw)
        out = out + dot(act, dw)
        if k == 0:
            act_ref[...] = act
            bg_ref[...] = bg
            bu_ref[...] = bu
    bn_ref[...] = bn.astype(BF)
    out_ref[...] = out.astype(BF)


def feed_forward(shift, n, nt, cot, own, other):
    share, width = nt.shape
    hid = own[0].shape[1]
    return pl.pallas_call(
        functools.partial(ffn_kernel, shift, n),
        in_specs=[whole()] * 8,
        out_specs=[whole()] * 5,
        out_shape=[jax.ShapeDtypeStruct((share, width), BF)] * 2
        + [jax.ShapeDtypeStruct((share, hid), BF)] * 3,
        compiler_params=params(),
        cost_estimate=cost(24 * share * width * hid, 2 * (6 * width * hid + 6 * share * width)),
        name="feed_forward",
    )(nt, cot, *own, *other)


def hidden_kernel(shift, n, nt_ref, cot_ref, gw_ref, uw_ref, dw_ref, act_ref, bg_ref, bu_ref):
    nt = nt_ref[...]
    which = lax.rem((lax.axis_index("mp") ^ 1) + shift, n)
    cot = rows_of(cot_ref, which, nt.shape[0])
    act_ref[...], bg_ref[...], bu_ref[...] = hidden_part(
        nt, cot, gw_ref[...], uw_ref[...], dw_ref[...]
    )


def hidden_rows(shift, n, nt, cot, own):
    share, width = nt.shape
    hid = own[0].shape[1]
    return pl.pallas_call(
        functools.partial(hidden_kernel, shift, n),
        in_specs=[whole()] * 5,
        out_specs=[whole()] * 3,
        out_shape=[jax.ShapeDtypeStruct((share, hid), BF)] * 3,
        compiler_params=params(),
        cost_estimate=cost(6 * share * width * hid, 2 * (3 * width * hid + 6 * share * width)),
        name="hidden_rows",
    )(nt, cot, *own)


def ffn_grad_kernel(n, share, groups, cot_ref, *refs):
    nt_refs, act_refs, bg_refs, bu_refs = (refs[i * n : (i + 1) * n] for i in range(4))
    grad_refs = refs[4 * n :]
    m = lax.axis_index("mp")
    nt = jnp.concatenate([ref[...] for ref in nt_refs], axis=0)
    act = jnp.concatenate([ref[...] for ref in act_refs], axis=0)
    bg = jnp.concatenate([ref[...] for ref in bg_refs], axis=0)
    bu = jnp.concatenate([ref[...] for ref in bu_refs], axis=0)
    cot = jnp.concatenate(
        [
            rows_of(cot_ref, lax.rem(first + shift, n), share)
            for first in (m, m ^ 1)
            for shift in range(0, n, 2)
        ],
        axis=0,
    )
    nt_t = nt.T
    grads = (dot(nt_t, bg), dot(nt_t, bu), dot(act.T, cot))
    if not groups:
        for ref, grad in zip(grad_refs, grads):
            ref[...] = grad.astype(BF)
        return
    keep_ref, send_ref, scr = grad_refs
    for i in range(3):
        scr[i] = grads[i].astype(BF)
    rows = scr.shape[1] // (2 * groups)
    d = lax.axis_index("dp")
    core = lax.rem(d, 2)
    for r in range(groups):
        chip = ((d // 2) ^ r) * 2
        for i in range(3):
            mine = pl.multiple_of((chip + core) * rows, 16)
            other = pl.multiple_of((chip + 1 - core) * rows, 16)
            at = (3 * r + i) * rows
            keep_ref[at : at + rows, :] = scr[i, pl.ds(mine, rows), :]
            send_ref[at : at + rows, :] = scr[i, pl.ds(other, rows), :]


def ffn_grads(cot, nts, acts, bgs, bus, groups):
    n = len(nts)
    share, width = nts[0].shape
    hid = acts[0].shape[1]
    length = cot.shape[0]
    scratch = []
    if groups:
        out_shape = [jax.ShapeDtypeStruct((3 * width // 2, width), BF)] * 2
        scratch = [pltpu.VMEM((3, width, width), BF)]
    else:
        out_shape = [
            jax.ShapeDtypeStruct((width, hid), BF),
            jax.ShapeDtypeStruct((width, hid), BF),
            jax.ShapeDtypeStruct((hid, width), BF),
        ]
    args = [cot, *nts, *acts, *bgs, *bus]
    return pl.pallas_call(
        functools.partial(ffn_grad_kernel, n, share, groups),
        in_specs=[whole()] * len(args),
        out_specs=[whole()] * len(out_shape),
        out_shape=out_shape,
        scratch_shapes=scratch,
        compiler_params=params(),
        cost_estimate=cost(6 * length * width * hid, 12 * length * width),
        name="ffn_grads",
    )(*args)


def mid_kernel(n, share, mp, len_ref, hid_ref, cot_ref, gain_ref, *refs):
    bn_refs, (bh_ref, b_ref, gg_ref) = refs[:n], refs[n:]
    m = lax.axis_index("mp")
    bn = bn_refs[0][...].astype(F32)
    for ref in bn_refs[1:]:
        bn = bn + ref[...].astype(F32)
    hidden = hid_ref[...]
    r2 = lax.rsqrt(jnp.mean(hidden * hidden, axis=-1, keepdims=True) + EPS)
    pos = mp * lax.broadcasted_iota(jnp.int32, (share, 1), 0) + m
    bn = bn * (pos < len_ref[0]).astype(F32)
    z = hidden * r2
    gg_ref[...] = jnp.broadcast_to(jnp.sum(bn * z, axis=0, keepdims=True), gg_ref.shape)
    q = bn * gain_ref[1:2, :]
    start = pl.multiple_of(m * share, 16)
    dout = cot_ref[pl.ds(start, share), :].astype(F32)
    back = dout + r2 * (q - z * jnp.mean(q * z, axis=-1, keepdims=True))
    bh_ref[...] = back
    b_ref[...] = back.astype(BF)


def mid_norm(lengths, hidden, cot, gain, pieces):
    share, width = hidden.shape
    n = len(pieces)
    return pl.pallas_call(
        functools.partial(mid_kernel, n, share, cot.shape[0] // share),
        in_specs=[smem()] + [whole()] * (3 + n),
        out_specs=[whole()] * 3,
        out_shape=[
            jax.ShapeDtypeStruct(hidden.shape, F32),
            jax.ShapeDtypeStruct(hidden.shape, BF),
            jax.ShapeDtypeStruct((8, width), F32),
        ],
        compiler_params=params(),
        cost_estimate=cost(20 * hidden.size, 20 * hidden.size),
        name="second_norm_back",
    )(lengths, hidden, cot, gain, *pieces)


def unmix_kernel(
    kb, n, len_ref, taps_ref, x_ref, bh_ref, gg_ref, gain_ref, stu_hbm, ar_hbm, *refs
):
    b_refs, (ig_ref, gain_out) = refs[:n], refs[n : n + 2]
    ta_ref, tb_ref, tc_ref, td_ref, b_scr, lag_ref, acc_ref, scr = refs[n + 2 : n + 10]
    w_buf, ar_ref, sems, ar_sem = refs[n + 10 :]
    j, steps = pl.program_id(0), pl.num_programs(0)
    share, width = bh_ref.shape
    half, step = n * share // 2, n // 2
    m = lax.axis_index("mp")
    shift, is_odd = m // 2, lax.rem(m, 2)
    depth = tc_ref.shape[1]
    start = half - depth
    first = ta_ref.shape[0] // kb
    rest = share - first
    row = lax.broadcasted_iota(jnp.int32, (share, half), 0) * step + shift
    col = lax.broadcasted_iota(jnp.int32, (share, half), 1)
    above, upto = col >= row + is_odd, col >= row
    slot, wait = fetch_matrices(j, stu_hbm.shape[0] // (2 * kb), kb, stu_hbm, w_buf, sems)

    @pl.when(j == 0)
    def _():
        for r in range(n):
            c = lax.rem(m + r, n)
            value = b_refs[r][...].astype(F32)
            put_every_nth(scr.at[lax.rem(c, 2)], value, c // 2, step)
            if r < lag_ref.shape[1] // width:
                moved = pltpu.roll(value, share - 1, 0)
                last = lax.broadcasted_iota(jnp.int32, (share, 1), 0) == share - 1
                moved = jnp.where(last, 0.0, moved)
                value = jnp.where(m + r >= n, moved, value)
                lag_ref[:, r * width : (r + 1) * width] = value.astype(BF)
        for odd in range(2):
            b_scr[odd] = columns_of(scr.at[odd], half).astype(BF)
        acc_ref[...] = jnp.zeros((share, width), F32)

    for k in range(kb):
        for which, valid, full, short in ((2, above, ta_ref, tc_ref), (3, upto, tb_ref, td_ref)):
            base = taps_ref[which, pl.ds(j * kb + k, 1), :]
            t = toeplitz(base, first, 0, step)
            full[k * first : (k + 1) * first, :] = jnp.where(valid[:first], t, 0.0).astype(BF)
            t = toeplitz(base, rest, step * first, step)
            t = jnp.where(valid[first:], t, 0.0).astype(BF)
            short[k * rest : (k + 1) * rest, :] = t[:, start:]
    ca, cb = dot(ta_ref[...], b_scr[0]), dot(tb_ref[...], b_scr[1])
    cc, cd = dot(tc_ref[...], b_scr[0, start:]), dot(td_ref[...], b_scr[1, start:])
    sign = jnp.where(is_odd == 0, 1.0, -1.0)
    wait()
    total = acc_ref[...]
    for k in range(kb):
        upper, lower = slice(k * first, (k + 1) * first), slice(k * rest, (k + 1) * rest)
        pa = jnp.concatenate([ca[upper], cc[lower]], axis=0)
        pb = jnp.concatenate([cb[upper], cd[lower]], axis=0)
        total = total + dot_cols((pa + pb).astype(BF), w_buf[slot, 0, k])
        total = total + dot_cols(((pa - pb) * sign).astype(BF), w_buf[slot, 1, k])
    acc_ref[...] = total
    fetch_last(j, steps, ar_hbm, ar_ref, ar_sem)

    @pl.when(j == steps - 1)
    def _():
        total = acc_ref[...]
        for lag in range(ar_ref.shape[0]):
            total = total + dot_cols(lag_ref[:, lag * width : (lag + 1) * width], ar_ref[lag])
        x = x_ref[...]
        r1 = lax.rsqrt(jnp.mean(x * x, axis=-1, keepdims=True) + EPS)
        pos = n * lax.broadcasted_iota(jnp.int32, (share, 1), 0) + m
        masked = total * (pos < len_ref[0]).astype(F32)
        y = x * r1
        p = masked * gain_ref[0:1, :]
        ig = bh_ref[...] + r1 * (p - y * jnp.mean(p * y, axis=-1, keepdims=True))
        ig_ref[...] = ig.astype(BF)
        gain_out[0:8, :] = jnp.broadcast_to(jnp.sum(masked * y, axis=0, keepdims=True), (8, width))
        gain_out[8:16, :] = gg_ref[...]


def spectral_unmix(lengths, taps, x, back_hidden, gg, gains, stu, ar, pieces, kb):
    share, width = back_hidden.shape
    n = len(pieces)
    half = n * share // 2
    count = taps.shape[1]
    depth = min(256, half)
    first = (half - depth) // (n // 2)
    return pl.pallas_call(
        functools.partial(unmix_kernel, kb, n),
        grid=(count // kb,),
        in_specs=[smem()] + [whole()] * 5 + [outside()] * 2 + [whole()] * n,
        out_specs=[whole()] * 2,
        out_shape=[
            jax.ShapeDtypeStruct((share, width), BF),
            jax.ShapeDtypeStruct((16, width), F32),
        ],
        scratch_shapes=[pltpu.VMEM((kb * first, half), BF)] * 2
        + [pltpu.VMEM((kb * (share - first), depth), BF)] * 2
        + [
            pltpu.VMEM((2, half, width), BF),
            pltpu.VMEM((share, ar.shape[0] * width), BF),
            pltpu.VMEM((share, width), F32),
            pltpu.VMEM((2, width // 128, half + 8, 128), F32),
        ]
        + matrix_scratch(kb, ar),
        compiler_params=params(30 << 20),
        cost_estimate=cost(4 * count * share * width * (half + width), 2 * stu.size),
        name="spectral_unmix",
    )(lengths, taps, x, back_hidden, gg, gains, stu, ar, *pieces)


def conv_kernel(groups, tile, own, first, filt_ref, *refs):
    ut_refs, (conv_ref, tt_ref, ut_scr) = refs[:groups], refs[groups:]
    j = pl.program_id(0)
    filt, length = filt_ref.shape
    block = conv_ref.shape[1]
    count = length // tile
    chip = lax.axis_index("dp") // 2

    @pl.when(j == 0)
    def _():
        start = pl.multiple_of(chip * block, 16)
        for r in range(groups):
            ut_scr[r * block : (r + 1) * block, :] = ut_refs[r][pl.ds(start, block), :]

    which = lax.axis_index("mp") * own + first + j
    strip = toeplitz(filt_ref[pl.ds(lax.rem(which, filt), 1), :], tile)
    row = lax.broadcasted_iota(jnp.int32, (tile, length), 0)
    col = lax.broadcasted_iota(jnp.int32, (tile, length), 1)
    flip = ((col - row) % 2 == 1) & (which >= filt)
    strip = jnp.where(col >= row, jnp.where(flip, -strip, strip), 0.0).astype(BF)
    for b in range(count):
        tt_ref[b * tile : (b + 1) * tile, b * tile :] = strip[:, : length - b * tile]
    for c in range(count):
        end = (c + 1) * tile
        part = dot(ut_scr[:, :end], tt_ref[:end, c * tile : end]).astype(BF)
        for r in range(groups):
            start = pl.multiple_of((lax.rem(chip, groups) ^ r) * length + c * tile, 128)
            conv_ref[0, :, pl.ds(start, tile)] = part[r * block : (r + 1) * block, :]


def convolutions(filt, uts, own, chips, first, last):
    length = filt.shape[1]
    groups = len(uts)
    block = uts[0].shape[0] // chips
    tile = 256 if length % 256 == 0 else length
    return pl.pallas_call(
        functools.partial(conv_kernel, groups, tile, own, first),
        grid=(last - first,),
        in_specs=[whole()] * (1 + groups),
        out_specs=pl.BlockSpec((1, block, groups * length), lambda j: (j, 0, 0)),
        out_shape=jax.ShapeDtypeStruct((last - first, block, groups * length), BF),
        scratch_shapes=[
            pltpu.VMEM((length, length), BF),
            pltpu.VMEM((groups * block, length), BF),
        ],
        compiler_params=params(),
        cost_estimate=cost(0, 0),
        name="convolutions",
    )(filt, *uts)


def lag_kernel(groups, *refs):
    ut_refs, out_refs = refs[:groups], refs[groups:]
    width, length = ut_refs[0].shape
    chip = lax.rem(lax.axis_index("dp") // 2, groups)
    col = lax.broadcasted_iota(jnp.int32, (width, length), 1)
    for r in range(groups):
        start = pl.multiple_of((chip ^ r) * length, 128)
        out_refs[0][:, pl.ds(start, length)] = ut_refs[r][:width, :]
        value = ut_refs[r][:width, :].astype(F32)
        for lag in range(1, len(out_refs)):
            moved = pltpu.roll(value, lag, 1)
            out_refs[lag][:, pl.ds(start, length)] = jnp.where(col >= lag, moved, 0.0).astype(BF)


def lagged(uts, order):
    groups = len(uts)
    width, length = uts[0].shape
    shape = jax.ShapeDtypeStruct((width, groups * length), BF)
    return pl.pallas_call(
        functools.partial(lag_kernel, groups),
        in_specs=[whole()] * groups,
        out_specs=[whole()] * order,
        out_shape=[shape] * order,
        compiler_params=params(),
        cost_estimate=cost(0, 0),
        name="lagged",
    )(*uts)


def grads_kernel(steps, order, groups, rows, conv_ref, conv_two_ref, *refs):
    lag_refs, b_refs = refs[:order], refs[order : order + len(rows)]
    keep_ref, send_ref, b_scr, scr = refs[order + len(rows) :]
    g = pl.program_id(0)
    d = lax.axis_index("dp")
    chip, core = lax.rem(d // 2, groups), lax.rem(d, 2)
    step, block, depth = conv_ref.shape
    width, length = b_scr.shape[1], depth // groups
    half = block // 2

    @pl.when(g == 0)
    def _():
        for ref, (r, at, size) in zip(b_refs, rows):
            start = pl.multiple_of((chip ^ r) * length + at, 16)
            b_scr[pl.ds(start, size), :] = ref[:size, :]

    for k, ref in enumerate((conv_ref, conv_two_ref)):

        @pl.when((g >= k * steps // 2) & (g < (k + 1) * steps // 2))
        def _():
            part = dot(ref[...].reshape(step * block, depth), b_scr[...])
            scr[...] = part.reshape(step, block, width)

    @pl.when(g < steps)
    def _():
        mine = pl.multiple_of(core * half, 16)
        other = pl.multiple_of((1 - core) * half, 16)
        keep_ref[pl.ds(g * step, step)] = scr[:, pl.ds(mine, half), :]
        for k in range(step):
            start = pl.multiple_of((g * step + k) * half, 16)
            send_ref[pl.ds(start, half), :] = scr[k, pl.ds(other, half), :].astype(BF)

    for lag in range(order):

        @pl.when(g == steps + lag)
        def _():
            at = steps * step * half + lag * width
            send_ref[at : at + width, :] = dot(lag_refs[lag][...], b_scr[...]).astype(BF)


def matrix_grads(convs, lags, backs, rows):
    part, block, depth = convs[0].shape
    own = 2 * part
    order, width = len(lags), lags[0].shape[0]
    groups = 1 + max(r for r, _, _ in rows)
    step = next(s for s in (3, 2, 1) if part % s == 0)
    steps = own // step
    half = block // 2
    return pl.pallas_call(
        functools.partial(grads_kernel, steps, order, groups, rows),
        grid=(steps + order,),
        in_specs=[
            pl.BlockSpec((step, block, depth), lambda g: (jnp.minimum(g, steps // 2 - 1), 0, 0)),
            pl.BlockSpec(
                (step, block, depth), lambda g: (jnp.clip(g - steps // 2, 0, steps // 2 - 1), 0, 0)
            ),
        ]
        + [whole()] * (order + len(backs)),
        out_specs=[whole()] * 2,
        out_shape=[
            jax.ShapeDtypeStruct((own, half, width), F32),
            jax.ShapeDtypeStruct((own * half + order * width, width), BF),
        ],
        scratch_shapes=[
            pltpu.VMEM((depth, width), BF),
            pltpu.VMEM((step, block, width), F32),
        ],
        compiler_params=params(),
        cost_estimate=cost(0, 0),
        name="matrix_grads",
    )(*convs, *lags, *backs)


def rows_message_kernel(ig_ref, hid_ref, *refs):
    share = ig_ref.shape[0]
    total = hid_ref[...]
    for ref in refs[:-1]:
        total = total + ref[...].astype(F32)
    refs[-1][:share, :] = ig_ref[...]
    refs[-1][share:, :] = total.astype(BF)


def rows_message(ig, hidden, pieces):
    share, width = ig.shape
    return pl.pallas_call(
        rows_message_kernel,
        in_specs=[whole()] * (2 + len(pieces)),
        out_specs=whole(),
        out_shape=jax.ShapeDtypeStruct((2 * share, width), BF),
        compiler_params=params(),
        cost_estimate=cost(4 * ig.size, 10 * ig.size),
        name="rows_message",
    )(ig, hidden, *pieces)


def finish_rows_kernel(n, share, *refs):
    pieces, (ig_ref, out_ref, scr) = refs[:n], refs[n:]
    m = lax.axis_index("mp")
    for at, ref in ((0, ig_ref), (share, out_ref)):
        for r in range(n):
            value = pieces[r][at : at + share, :].astype(F32)
            put_every_nth(scr, value, lax.rem(m + r, n), n)
        ref[...] = columns_of(scr, n * share).astype(ref.dtype)


def finish_rows(pieces):
    n = len(pieces)
    share, width = pieces[0].shape[0] // 2, pieces[0].shape[1]
    return pl.pallas_call(
        functools.partial(finish_rows_kernel, n, share),
        in_specs=[whole()] * n,
        out_specs=[whole()] * 2,
        out_shape=[
            jax.ShapeDtypeStruct((n * share, width), F32),
            jax.ShapeDtypeStruct((n * share, width), BF),
        ],
        scratch_shapes=[pltpu.VMEM((width // 128, n * share + 16, 128), F32)],
        compiler_params=params(),
        cost_estimate=cost(1e9, 1e9),
        name="finish_rows",
    )(*pieces)


def ordered_sum_kernel(n, axis, step, *refs):
    pieces, (out_ref, scr) = refs[:n], refs[n:]
    me = lax.axis_index(axis)
    for r in range(n):
        who = lax.rem(me + r, n) if step == 0 else (me // step) ^ r
        scr[who] = pieces[r][...]
    total = scr[0]
    for r in range(1, n):
        total = total + scr[r]
    out_ref[...] = total


def ordered_sum(pieces, axis, step):
    n = len(pieces)
    shape = pieces[0].shape
    return pl.pallas_call(
        functools.partial(ordered_sum_kernel, n, axis, step),
        in_specs=[whole()] * n,
        out_specs=whole(),
        out_shape=jax.ShapeDtypeStruct(shape, F32),
        scratch_shapes=[pltpu.VMEM((n,) + shape, F32)],
        compiler_params=params(),
        cost_estimate=cost(n * pieces[0].size, 4 * n * pieces[0].size),
        name="ordered_sum",
    )(*pieces)


def cores_sum_kernel(keep_ref, recv_ref, upper_ref, lower_ref):
    total = (keep_ref[...].astype(F32) + recv_ref[...].astype(F32)).astype(BF)
    half = total.shape[0] // 8
    for r in range(4):
        at = 2 * r * half
        upper_ref[r * half : (r + 1) * half, :] = total[at : at + half]
        lower_ref[r * half : (r + 1) * half, :] = total[at + half : at + 2 * half]


def cores_sum(keep, recv):
    size, width = keep.shape
    return pl.pallas_call(
        cores_sum_kernel,
        in_specs=[whole()] * 2,
        out_specs=[whole()] * 2,
        out_shape=[jax.ShapeDtypeStruct((size // 2, width), BF)] * 2,
        compiler_params=params(),
        cost_estimate=cost(keep.size, 8 * keep.size),
        name="cores_sum",
    )(keep, recv)


def pack_kernel(n, share, *refs):
    pieces, (out_ref, scr) = refs[:n], refs[n:]
    m = lax.axis_index("mp")
    for r in range(n):
        put_every_nth(scr, pieces[r][...].astype(F32), lax.rem(m + r, n), n)
    out_ref[...] = columns_of(scr, n * share).astype(BF)


def pack_rows(pieces):
    n = len(pieces)
    share, width = pieces[0].shape
    return pl.pallas_call(
        functools.partial(pack_kernel, n, share),
        in_specs=[whole()] * n,
        out_specs=whole(),
        out_shape=jax.ShapeDtypeStruct((n * share, width), BF),
        scratch_shapes=[pltpu.VMEM((width // 128, n * share + 16, 128), F32)],
        compiler_params=params(),
        cost_estimate=cost(n * share * width, 6 * n * share * width),
        name="pack_rows",
    )(*pieces)


def turn_kernel(x_ref, y_ref, upper_ref, lower_ref, gain_ref, to_y, to_x):
    half, size = x_ref.shape[0] // 2, upper_ref.shape[0]
    gains = split_gains(gain_ref[...])
    for ref, rows, w_ref in ((to_y, x_ref[:half, :], lower_ref), (to_x, y_ref[half:, :], upper_ref)):
        ref[:half, :] = rows
        ref[half : half + size, :] = w_ref[...]
        ref[half + size :, :] = gains


def turn(over_x, over_y, upper, lower, gains):
    rows = over_x.shape[0] // 2 + upper.shape[0] + 32
    return pl.pallas_call(
        turn_kernel,
        in_specs=[whole()] * 5,
        out_specs=[whole()] * 2,
        out_shape=[jax.ShapeDtypeStruct((rows, over_x.shape[1]), BF)] * 2,
        compiler_params=params(),
        cost_estimate=cost(over_x.size, 8 * over_x.size),
        name="turn",
    )(over_x, over_y, upper, lower, gains)


def half_sums_kernel(upper_ref, lower_ref, from_y, from_x, to_y, to_x):
    size = to_y.shape[0]
    half = size // 4
    at = from_y.shape[0] - 32 - size
    for ref, own, came, bits in ((to_y, upper_ref, from_x, 1), (to_x, lower_ref, from_y, 2)):
        for r in range(4):
            there = at + (r ^ bits) * half
            ref[r * half : (r + 1) * half, :] = (
                own[r * half : (r + 1) * half, :].astype(F32)
                + came[there : there + half, :].astype(F32)
            ).astype(BF)
    to_x[size:, :] = from_y[at + size :, :]


def half_sums(upper, lower, from_y, from_x):
    size, width = upper.shape
    return pl.pallas_call(
        half_sums_kernel,
        in_specs=[whole()] * 4,
        out_specs=[whole()] * 2,
        out_shape=[jax.ShapeDtypeStruct((rows, width), BF) for rows in (size, size + 32)],
        compiler_params=params(),
        cost_estimate=cost(upper.size, 8 * upper.size),
        name="half_sums",
    )(upper, lower, from_y, from_x)


def chunks_kernel(upper_ref, from_y, lower_ref, from_x, more_ref, out_ref):
    half = upper_ref.shape[0] // 4
    for own, came, bits, lower in ((upper_ref, from_y, 2, 0), (lower_ref, from_x, 1, 1)):
        for r in range(4):
            at, there = (2 * r + lower) * half, (r ^ bits) * half
            out_ref[at : at + half, :] = (
                own[r * half : (r + 1) * half, :].astype(F32)
                + came[there : there + half, :].astype(F32)
            ).astype(BF)
    out_ref[8 * half :, :] = more_ref[...]


def whole_chunks(upper, from_y, lower, from_x, more):
    size, width = upper.shape
    return pl.pallas_call(
        chunks_kernel,
        in_specs=[whole()] * 5,
        out_specs=whole(),
        out_shape=jax.ShapeDtypeStruct((2 * size + more.shape[0], width), BF),
        compiler_params=params(),
        cost_estimate=cost(upper.size, 8 * upper.size),
        name="whole_chunks",
    )(upper, from_y, lower, from_x, more)


def split_gains(both):
    high = both.astype(BF)
    low = (both - high.astype(F32)).astype(BF)
    return jnp.concatenate([high, low], axis=0)


def joined(gains):
    return gains[:16].astype(F32) + gains[16:].astype(F32)


def chips_sum_kernel(gain_ref, from_x, from_y, recv_ref, out_ref, scr):
    chip = lax.axis_index("dp") // 2
    scr[chip] = joined(split_gains(gain_ref[...]))
    for ref, bits in ((from_x, 1), (from_y, 2), (recv_ref, 3)):
        scr[chip ^ bits] = joined(ref[ref.shape[0] - 32 :, :])
    out_ref[...] = ((scr[0] + scr[1]) + scr[2]) + scr[3]


def chips_sum(gains, from_x, from_y, recv):
    return pl.pallas_call(
        chips_sum_kernel,
        in_specs=[whole()] * 4,
        out_specs=whole(),
        out_shape=jax.ShapeDtypeStruct(gains.shape, F32),
        scratch_shapes=[pltpu.VMEM((4,) + gains.shape, F32)],
        compiler_params=params(),
        cost_estimate=cost(4 * gains.size, 16 * gains.size),
        name="chips_sum",
    )(gains, from_x, from_y, recv)


def finish_kernel(custom, keep_ref, send_ref, recv_ref, stu_ref, ar_ref, *w_refs):
    own, half, width = keep_ref.shape
    base = 0
    if custom:
        d = lax.axis_index("dp")
        core = lax.rem(d, 2)
        rows = width // 8
        base = 12 * rows
        for r in range(4):
            chip = ((d // 2) ^ r) * 2
            for ref, which in ((send_ref, chip + core), (recv_ref, chip + 1 - core)):
                start = pl.multiple_of(which * rows, 16)
                for i, out in enumerate(w_refs):
                    at = (3 * r + i) * rows
                    out[pl.ds(start, rows), :] = ref[at : at + rows, :].astype(F32)
    for k in range(own):
        at = base + k * half
        stu_ref[k] = keep_ref[k] + recv_ref[at : at + half, :].astype(F32)
    for i in range(ar_ref.shape[0]):
        at = base + own * half + i * width
        ar_ref[i] = send_ref[at : at + width, :].astype(F32) + recv_ref[
            at : at + width, :
        ].astype(F32)


def finish(keep, send, recv, order, custom):
    width = keep.shape[2]
    more = [jax.ShapeDtypeStruct((width, width), F32)] * (3 if custom else 0)
    return pl.pallas_call(
        functools.partial(finish_kernel, custom),
        in_specs=[whole()] * 3,
        out_specs=[whole()] * (2 + len(more)),
        out_shape=[
            jax.ShapeDtypeStruct(keep.shape, F32),
            jax.ShapeDtypeStruct((order, width, width), F32),
        ]
        + more,
        compiler_params=params(),
        cost_estimate=cost(keep.size, 10 * keep.size),
        name="finish",
    )(keep, send, recv)


def fetch_shifted(value, axis, n, step=1):
    pieces = {0: value}
    for r in sorted(range(step, n, step), key=lambda r: min(r, n - r)):
        pieces[r] = lax.ppermute(value, axis, [(i, (i - r) % n) for i in range(n)])
    return [pieces[r] for r in range(0, n, step)]


def send_shifted(pieces, axis, n, step):
    moved = {0: pieces[0]}
    for r in sorted(range(step, n, step), key=lambda r: min(r, n - r)):
        moved[r] = lax.ppermute(pieces[r // step], axis, [(i, (i + r) % n) for i in range(n)])
    return [moved[r] for r in range(0, n, step)]


def swap(value, axis, n, bits):
    return lax.ppermute(value, axis, [(i, i ^ bits) for i in range(n)])


def swap_sum(value, n):
    return ordered_sum([value, swap(value, "dp", n, 1)], "dp", 0)


def after(values, first):
    flat, tree = jax.tree.flatten(values)
    out = lax.optimization_barrier((*flat, *jax.tree.leaves(first)))
    return jax.tree.unflatten(tree, out[: len(flat)])


def shards(
    inputs, lengths, filters, first_gain, stu_weight, ar_weight, second_gain,
    gate_weight, up_weight, down_weight, cotangent,
):
    n = lax.axis_size("mp")
    n_dp = lax.axis_size("dp")
    groups = n_dp // 2
    length, width = inputs.shape
    share = length // n
    order = ar_weight.shape[0]
    own = stu_weight.shape[0] // n
    lengths = lengths.astype(jnp.int32)
    both_gains = jnp.stack([first_gain, second_gain])

    own_w = (gate_weight, up_weight, down_weight)
    custom = n_dp == 8 and gate_weight.shape[1] == width
    if custom:
        half_w = half_weights(*own_w)
        both_gains = after(both_gains, half_w)
        half_w = swap(half_w, "mp", n, 1)
    u, ut, ut_two, x_own, u_lags, taps, natural = first_norm(
        lengths, inputs, both_gains, filters.T, n, order
    )
    uts = [ut, swap(ut, "dp", n_dp, 2), swap(ut_two, "dp", n_dp, 4)]
    hidden, nt = spectral_mix(
        lengths, taps, x_own, u, u_lags, both_gains, stu_weight, ar_weight, n, 8
    )
    cotangent = dealt_rows(cotangent, n)
    nts = fetch_shifted(nt, "mp", n, 2)
    others = [swap(piece, "mp", n, 1) for piece in nts]
    if custom:
        other_w = both_halves(half_w, swap(after(half_w, nt), "dp", n_dp, 1))
    else:
        other_w = [swap(w, "mp", n, 1) for w in own_w]
    parts = [feed_forward(0, n, after(nt, uts[1:3]), cotangent, own_w, other_w)]
    for k in range(1, n // 2):
        piece = after(nts[k], parts[-1][0])
        parts.append(feed_forward(2 * k, n, piece, cotangent, own_w, other_w))
    uts += [swap(after(ut, nt), "dp", n_dp, 2 * r) for r in range(3, groups)]
    bns = send_shifted([p[0] for p in parts], "mp", n, 2)
    out_parts = [p[1] for p in parts]
    bns[1:] = after(bns[1:], uts)
    back_hidden, back_rows, second_part = mid_norm(lengths, hidden, cotangent, both_gains, bns)
    backs = fetch_shifted(back_rows, "mp", n)
    more = [
        hidden_rows(2 * k, n, after(piece, back_rows), cotangent, own_w)
        for k, piece in enumerate(others)
    ]
    acts, bgs, bus = ([p[i + 2] for p in parts] + [p[i] for p in more] for i in range(3))
    grads = ffn_grads(cotangent, nts + others, acts, bgs, bus, groups if custom else 0)
    uts = after(uts, back_rows)
    fours = [uts[r : r + 4] for r in range(0, groups, 4)]
    lags = [lagged(some, order) for some in fours]
    conv = [convolutions(natural, some, own, groups, 0, own // 2) for some in fours]
    backs = after(backs, (lags, conv))
    own_back = pack_rows(backs)
    if custom:
        over_x, over_y = swap(own_back, "dp", n_dp, 2), swap(own_back, "dp", n_dp, 4)
        w_came = swap(after(grads[1], own_back), "dp", n_dp, 1)
    out_sums = send_shifted(after(out_parts, own_back), "mp", n, 2)
    ig, gains = spectral_unmix(
        lengths, taps, x_own, back_hidden, second_part, both_gains, stu_weight, ar_weight, backs, 8
    )
    uts, hidden = after((uts, hidden), ig)
    fours = [uts[r : r + 4] for r in range(0, groups, 4)]
    conv_two = [convolutions(natural, some, own, groups, own // 2, own) for some in fours]
    message = rows_message(ig, hidden, out_sums)
    messages = fetch_shifted(message, "mp", n)
    if custom:
        upper, lower = cores_sum(grads[0], after(w_came, message))
        to_y, to_x = turn(after(over_x, message), over_y, upper, lower, gains)
        from_y, from_x = swap(to_y, "dp", n_dp, 4), swap(to_x, "dp", n_dp, 2)
        all_backs = [own_back, over_x, over_y, from_y, from_x]
        half = length // 2
        rows = ((0, 0, length), (1, 0, length), (2, 0, length), (3, 0, half), (3, half, half))
        upper, lower = half_sums(after(upper, conv_two), lower, from_y, from_x)
        from_y_two, from_x_two = swap(upper, "dp", n_dp, 4), swap(lower, "dp", n_dp, 2)
        conv_two = after(conv_two, upper)
        gains_parts = (gains, from_x, from_y)
    else:
        all_backs = [own_back] + [swap(own_back, "dp", n_dp, 2 * r) for r in range(1, groups)]
        rows = tuple((r, 0, length) for r in range(min(groups, 4)))
        gains = ordered_sum([gains] + [swap(gains, "dp", n_dp, r) for r in range(1, n_dp)], "dp", 1)
    conv = after(list(zip(conv, conv_two)), message)
    if len(conv) == 1:
        keep, send = matrix_grads(conv[0], lags[0], all_backs, rows)
    else:
        some = [
            matrix_grads(c, lags[k], all_backs[4 * k : 4 * k + 4], rows)
            for k, c in enumerate(conv)
        ]
        keep = ordered_sum([k for k, _ in some], "dp", 8)
        send = ordered_sum([k.astype(F32) for _, k in some], "dp", 8).astype(BF)
    input_grad, output = finish_rows(after(messages, send))
    if custom:
        from_y_two, from_x_two = after((from_y_two, from_x_two), output)
        gains = swap_sum(chips_sum(*gains_parts, after(from_x_two, send)), n_dp)
        send = whole_chunks(upper, from_y_two, lower, from_x_two, after(send, gains))
    gains = fetch_shifted(gains, "mp", n)
    recv = swap(send, "dp", n_dp, 1)
    stu_grad, ar_grad, *w_grads = finish(keep, send, recv, order, custom)
    gains = ordered_sum(after(gains, stu_grad), "mp", 0)
    if custom:
        gate_grad, up_grad, down_grad = w_grads
    else:
        gate_grad, up_grad, down_grad = (g.astype(F32) for g in lax.psum(tuple(grads), "dp"))
    return (
        output, input_grad, stu_grad, ar_grad, gains[0], gains[8], gate_grad, up_grad, down_grad,
    )


def solution(mesh):
    in_specs = (
        P("dp", None), P("dp"), P(), P(), P(), P(), P(),
        P(None, "mp"), P(None, "mp"), P("mp", None), P("dp", None),
    )
    out_specs = (
        P("dp", None), P("dp", None), P("mp", "dp", None), P(), P(), P(),
        P(None, "mp"), P(None, "mp"), P("mp", None),
    )
    return jax.shard_map(shards, mesh=mesh, in_specs=in_specs, out_specs=out_specs, check_vma=False)
```

time: 153 us -> 145 us (0.948)
  starting transfers between devices: 47.8 us -> 33.8 us
  local copies, waits for them, and re-layouts: 2.51 us -> 5.63 us
  waiting for transfers between devices: 31.4 us -> 33.8 us
    ppermute x12 -> x16, waiting for transfers between devices: 7.67 us -> 19 us  [swap(): return lax.ppermute(value, axis, [(i, i ^ bits) for i in range(n)])]
    ppermute x12 -> x10, starting transfers between devices: 23.9 us -> 13.6 us  [fetch_shifted(): pieces[r] = lax.ppermute(value, axis, [(i, (i - r) % n) for i in range(n)])]
    ppermute x6 -> x2, starting transfers between devices: 12.3 us -> 3.57 us  [send_shifted(): lax.ppermute(pieces[r // step], axis, [(i, (i + r) % n) for i in range(n)])]
    ppermute x12 -> x16, starting transfers between devices: 11.6 us -> 16.6 us  [swap(): return lax.ppermute(value, axis, [(i, i ^ bits) for i in range(n)])]
    ppermute x12 -> x10, waiting for transfers between devices: 14.5 us -> 10 us  [fetch_shifted(): pieces[r] = lax.ppermute(value, axis, [(i, (i - r) % n) for i in range(n)])]
    ppermute x6 -> x2, waiting for transfers between devices: 9.23 us -> 4.84 us  [send_shifted(): lax.ppermute(pieces[r // step], axis, [(i, (i + r) % n) for i in range(n)])]
    unnamed x14 -> x20, local copies, waits for them, and re-layouts: 1.92 us -> 5.04 us
    pallas_call x8 -> x12, Pallas kernels: 31.5 us -> 31.4 us  [the longest x1 16 us: spectral_unmix(): pl.pallas_call(functools.partial(unmix_kernel, kb, n), grid=(count // kb,...]
  transfers between devices with their start and end apart: 30 -> 28, of which waited for: 8 -> 10; matrix products, arithmetic and copies ran while one was open for 0% -> 0% of each run, Pallas kernels for 44% -> 47%
where the time goes in v4:
time: 145 us
  Pallas kernels  68.9 us (48%)
  starting transfers between devices  33.8 us (23%)
  waiting for transfers between devices  33.8 us (23%)
  local copies, waits for them, and re-layouts  5.63 us (4%)
  between operations  1.66 us (1%)
    ppermute x16, waiting for transfers between devices, swap(): return lax.ppermute(value, axis, [(i, i ^ bits) for i in range(n)])  19 us
    ppermute x16, starting transfers between devices, swap(): return lax.ppermute(value, axis, [(i, i ^ bits) for i in range(n)])  16.6 us
    pallas_call x1, Pallas kernels, spectral_unmix(): pl.pallas_call(functools.partial(unmix_kernel, kb, n), grid=(count // kb,...  16 us
    ppermute x10, starting transfers between devices, fetch_shifted(): pieces[r] = lax.ppermute(value, axis, [(i, (i - r) % n) for i in range(n)])  13.6 us
    pallas_call x1, Pallas kernels, spectral_mix(): pl.pallas_call(functools.partial(mix_kernel, kb, n), grid=(filt // kb,),...  12.5 us
    pallas_call x1, Pallas kernels, matrix_grads(): pl.pallas_call(functools.partial(grads_kernel, steps, order, groups, rows...  11.7 us
    ppermute x10, waiting for transfers between devices, fetch_shifted(): pieces[r] = lax.ppermute(value, axis, [(i, (i - r) % n) for i in range(n)])  10 us
    pallas_call x2, Pallas kernels, convolutions(): pl.pallas_call(functools.partial(conv_kernel, groups, tile, own, first),...  9.96 us
  transfers between devices with their start and end apart: 28, of which 10 were waited for; matrix products, arithmetic and copies ran while one was open for 0% of the time, Pallas kernels for 47%

profile of v4, /device:TPU:0, one launch (start us, length us, event | category | flops | bytes accessed | tf_op | source)
XLA Modules:
  0.0 144.6 jit_solution(7838909645859013236)
XLA Ops:
  3.9 3.1 %collective-permute-start.2 = (bf16[3,256,512]{2,1,0:T(8,128)(2,1)S(1)}, bf16[3,256,512]{2,1,0:T(8,128)(2,1)S(1)}, u32[]{:S(2)}, u32[]{:S(2)}) collective-permute-start(bf16[3,256,512]{2,1,0:T(8,128)(2,1)S(1)} %half_weights.1), channel_id=1, source_target_pairs={{0,1},{1,0},{2,3},{3,2},{4,5},{5,4},{6,7},{7,6},{8,9},{9,8},{10,11... | collective-permute-start | bytes 2359304 | tf_op jit(solution)/shard_map/ppermute | solution.py:1071
  14.9 12.5 %spectral_mix.1 = (f32[192,512]{1,0:T(8,128)S(1)}, bf16[192,512]{1,0:T(8,128)(2,1)S(1)}) custom-call(s32[1]{0:T(128)S(6)} %copy.20.len_ref, f32[4,24,384]{2,1,0:T(8,128)S(1)} %get-tuple-element.105.taps_ref, f32[192,512]{1,0:T(8,128)S(1)} %get-tuple-element.106.x_ref, bf16[2,384,512]{2,1,0:T(8,128)(2,1)S(1)} %get-tuple-element.107.u_ref, ...), custom_call_target="tpu_custom_call" | custom-call | tf_op jit(solution)/shard_map/spectral_mix/pallas_call | solution.py:261
  28.1 2.6 %collective-permute-start.4 = (bf16[192,512]{1,0:T(8,128)(2,1)S(1)}, bf16[192,512]{1,0:T(8,128)(2,1)S(1)}, u32[]{:S(2)}, u32[]{:S(2)}) collective-permute-start(bf16[192,512]{1,0:T(8,128)(2,1)S(1)} %get-tuple-element.113.nt_ref.refs_0_), channel_id=1, source_target_pairs={{0,2},{1,3},{2,0},{3,1},{4,6},{5,7},{6,4},{7,5},{8,10},{9,11},{10,... | collective-permute-start | bytes 589832 | tf_op jit(solution)/shard_map/ppermute | solution.py:1059
  31.0 2.7 %collective-permute-done.refs_1_ = bf16[512,768]{1,0:T(8,128)(2,1)S(1)} collective-permute-done((bf16[512,768]{1,0:T(8,128)(2,1)S(1)}, bf16[512,768]{1,0:T(8,128)(2,1)S(1)}, u32[]{:S(2)}, u32[]{:S(2)}) %collective-permute-start) | collective-permute-done | bytes 786464 | tf_op jit(solution)/shard_map/ppermute | solution.py:1071
  33.8 2.1 %feed_forward.2 = (bf16[192,512]{1,0:T(8,128)(2,1)S(1)}, bf16[192,512]{1,0:T(8,128)(2,1)S(1)}, bf16[192,512]{1,0:T(8,128)(2,1)S(1)}, bf16[192,512]{1,0:T(8,128)(2,1)S(1)}, bf16[192,512]{1,0:T(8,128)(2,1)S(1)}) custom-call(bf16[192,512]{1,0:T(8,128)(2,1)S(1)} %get-tuple-element.113.nt_ref.refs_0_, bf16[768,512]{1,0:T(8,128)(2,1)S(1)} %dealt_rows.1.cot_ref, ...), custom_call_target="tpu_custom_call" | custom-call | flops 1207959552 | bytes 4325376 | tf_op jit(solution)/shard_map/feed_forward/pallas_call | solution.py:388
  35.9 4.3 %collective-permute-done.4.nt_ref.refs_1_ = bf16[192,512]{1,0:T(8,128)(2,1)S(1)} collective-permute-done((bf16[192,512]{1,0:T(8,128)(2,1)S(1)}, bf16[192,512]{1,0:T(8,128)(2,1)S(1)}, u32[]{:S(2)}, u32[]{:S(2)}) %collective-permute-start.4) | collective-permute-done | bytes 196640 | tf_op jit(solution)/shard_map/ppermute | solution.py:1059
  40.2 2.1 %feed_forward.3 = (bf16[192,512]{1,0:T(8,128)(2,1)S(1)}, bf16[192,512]{1,0:T(8,128)(2,1)S(1)}, bf16[192,512]{1,0:T(8,128)(2,1)S(1)}, bf16[192,512]{1,0:T(8,128)(2,1)S(1)}, bf16[192,512]{1,0:T(8,128)(2,1)S(1)}) custom-call(bf16[192,512]{1,0:T(8,128)(2,1)S(1)} %collective-permute-done.4.nt_ref.refs_1_, bf16[768,512]{1,0:T(8,128)(2,1)S(1)} %dealt_rows.1.cot_ref, ...), custom_call_target="tpu_custom_call" | custom-call | flops 1207959552 | bytes 4325376 | tf_op jit(solution)/shard_map/feed_forward/pallas_call | solution.py:388
  42.4 3.2 %collective-permute-start.15 = (bf16[192,512]{1,0:T(8,128)(2,1)S(1)}, bf16[192,512]{1,0:T(8,128)(2,1)S(1)}, u32[]{:S(2)}, u32[]{:S(2)}) collective-permute-start(bf16[192,512]{1,0:T(8,128)(2,1)S(1)} %collective-permute-done.4.nt_ref.refs_1_), channel_id=1, source_target_pairs={{0,1},{1,0},{2,3},{3,2},{4,5},{5,4},{6,7},{7,6},{8,9},{9,8},{10,11... | collective-permute-start | bytes 589832 | tf_op jit(solution)/shard_map/ppermute | solution.py:1071
  45.6 3.4 %collective-permute-done.6.refs_3_ = bf16[512,768]{1,0:T(8,128)(2,1)S(1)} collective-permute-done((bf16[512,768]{1,0:T(8,128)(2,1)S(1)}, bf16[512,768]{1,0:T(8,128)(2,1)S(1)}, u32[]{:S(2)}, u32[]{:S(2)}) %collective-permute-start.6) | collective-permute-done | bytes 786464 | tf_op jit(solution)/shard_map/ppermute | solution.py:1071
  49.0 4.8 %collective-permute-done.5.refs_1_ = bf16[192,512]{1,0:T(8,128)(2,1)S(1)} collective-permute-done((bf16[192,512]{1,0:T(8,128)(2,1)S(1)}, bf16[192,512]{1,0:T(8,128)(2,1)S(1)}, u32[]{:S(2)}, u32[]{:S(2)}) %collective-permute-start.5) | collective-permute-done | bytes 196640 | tf_op jit(solution)/shard_map/ppermute | solution.py:1066
  54.1 1.8 %collective-permute-start.7 = (bf16[192,512]{1,0:T(8,128)(2,1)S(1)}, bf16[192,512]{1,0:T(8,128)(2,1)S(1)}, u32[]{:S(2)}, u32[]{:S(2)}) collective-permute-start(bf16[192,512]{1,0:T(8,128)(2,1)S(1)} %get-tuple-element.134.refs_0_), channel_id=1, source_target_pairs={{0,3},{1,0},{2,1},{3,2},{4,7},{5,4},{6,5},{7,6},{8,11},{9,8},{10,9... | collective-permute-start | bytes 589832 | tf_op jit(solution)/shard_map/ppermute | solution.py:1059
  56.5 2.6 %lagged.1 = (bf16[512,3072]{1,0:T(8,128)(2,1)S(1)}, bf16[512,3072]{1,0:T(8,128)(2,1)S(1)}, bf16[512,3072]{1,0:T(8,128)(2,1)S(1)}) custom-call(bf16[512,768]{1,0:T(8,128)(2,1)S(1)} %get-tuple-element.144.refs_0_, bf16[512,768]{1,0:T(8,128)(2,1)S(1)} %collective-permute-done.refs_1_, bf16[528,768]{1,0:T(8,128)(2,1)S(1)} %collective-permute-done.1.refs_2_, ...), custom_call_target="tpu_custom_call" | custom-call | tf_op jit(solution)/shard_map/lagged/pallas_call | solution.py:702
  59.1 5.0 %convolutions.2.conv_ref = bf16[6,128,3072]{2,1,0:T(8,128)(2,1)S(1)} custom-call(f32[24,768]{1,0:T(8,128)S(1)} %get-tuple-element.133.filt_ref, bf16[512,768]{1,0:T(8,128)(2,1)S(1)} %get-tuple-element.144.refs_0_, bf16[512,768]{1,0:T(8,128)(2,1)S(1)} %collective-permute-done.refs_1_, bf16[528,768]{1,0:T(8,128)(2,1)S(1)} %collective-permute-done.1.refs_2_, ...), custom_call_target="tpu_custom_call" | custom-call | tf_op jit(solution)/shard_map/convolutions/pallas_call | solution.py:668
  67.0 5.0 %collective-permute-done.8.refs_2_ = bf16[192,512]{1,0:T(8,128)(2,1)S(1)} collective-permute-done((bf16[192,512]{1,0:T(8,128)(2,1)S(1)}, bf16[192,512]{1,0:T(8,128)(2,1)S(1)}, u32[]{:S(2)}, u32[]{:S(2)}) %collective-permute-start.8) | collective-permute-done | bytes 196640 | tf_op jit(solution)/shard_map/ppermute | solution.py:1059
  75.2 3.5 %collective-permute-start.10 = (bf16[192,512]{1,0:T(8,128)(2,1)S(1)}, bf16[192,512]{1,0:T(8,128)(2,1)S(1)}, u32[]{:S(2)}, u32[]{:S(2)}) collective-permute-start(bf16[192,512]{1,0:T(8,128)(2,1)S(1)} %get-tuple-element.143), channel_id=1, source_target_pairs={{0,2},{1,3},{2,0},{3,1},{4,6},{5,7},{6,4},{7,5},{8,10},{9,11},{10,... | collective-permute-start | bytes 589832 | tf_op jit(solution)/shard_map/ppermute | solution.py:1066
  78.8 16.0 %spectral_unmix.1 = (bf16[192,512]{1,0:T(8,128)(2,1)S(1)}, f32[16,512]{1,0:T(8,128)S(1)}) custom-call(s32[1]{0:T(128)S(6)} %copy.20.len_ref, f32[4,24,384]{2,1,0:T(8,128)S(1)} %get-tuple-element.105.taps_ref, f32[192,512]{1,0:T(8,128)S(1)} %get-tuple-element.106.x_ref, f32[192,512]{1,0:T(8,128)S(1)} %get-tuple-element.123.bh_ref, ...), custom_call_target="tpu_custom_call" | custom-call | flops 8455716864 | bytes 25165824 | tf_op jit(solution)/shard_map/spectral_unmix/pallas_call | solution.py:609
  97.8 2.0 %collective-permute-start.13 = (bf16[384,512]{1,0:T(8,128)(2,1)S(1)}, bf16[384,512]{1,0:T(8,128)(2,1)S(1)}, u32[]{:S(2)}, u32[]{:S(2)}) collective-permute-start(bf16[384,512]{1,0:T(8,128)(2,1)S(1)} %rows_message.1.refs_0_), channel_id=1, source_target_pairs={{0,1},{1,2},{2,3},{3,0},{4,5},{5,6},{6,7},{7,4},{8,9},{9,10},{10,1... | collective-permute-start | bytes 1179656 | tf_op jit(solution)/shard_map/ppermute | solution.py:1059
  99.9 5.0 %convolutions.3.conv_two_ref = bf16[6,128,3072]{2,1,0:T(8,128)(2,1)S(1)} custom-call(f32[24,768]{1,0:T(8,128)S(1)} %get-tuple-element.133.filt_ref, bf16[512,768]{1,0:T(8,128)(2,1)S(1)} %get-tuple-element.144.refs_0_, bf16[512,768]{1,0:T(8,128)(2,1)S(1)} %collective-permute-done.refs_1_, bf16[528,768]{1,0:T(8,128)(2,1)S(1)} %collective-permute-done.1.refs_2_, ...), custom_call_target="tpu_custom_call" | custom-call | tf_op jit(solution)/shard_map/convolutions/pallas_call | solution.py:668
  104.8 11.1 %collective-permute-done.19.from_y.refs_6_ = bf16[800,512]{1,0:T(8,128)(2,1)S(1)} collective-permute-done((bf16[800,512]{1,0:T(8,128)(2,1)S(1)}, bf16[800,512]{1,0:T(8,128)(2,1)S(1)}, u32[]{:S(2)}, u32[]{:S(2)}) %collective-permute-start.19) | collective-permute-done | bytes 819232 | tf_op jit(solution)/shard_map/ppermute | solution.py:1071
  118.5 11.7 %matrix_grads.1 = (f32[12,64,512]{2,1,0:T(8,128)S(1)}, bf16[2304,512]{1,0:T(8,128)(2,1)S(1)}) custom-call(bf16[6,128,3072]{2,1,0:T(8,128)(2,1)S(1)} %convolutions.2.conv_ref, bf16[6,128,3072]{2,1,0:T(8,128)(2,1)S(1)} %convolutions.3.conv_two_ref, bf16[512,3072]{1,0:T(8,128)(2,1)S(1)} %get-tuple-element.130.refs_0_, ...), custom_call_target="tpu_custom_call" | custom-call | tf_op jit(solution)/shard_map/matrix_grads/pallas_call | solution.py:761
  130.9 2.0 %finish_rows.1 = (f32[768,512]{1,0:T(8,128)}, bf16[768,512]{1,0:T(8,128)(2,1)}) custom-call(bf16[384,512]{1,0:T(8,128)(2,1)S(1)} %rows_message.1.refs_0_, bf16[384,512]{1,0:T(8,128)(2,1)S(1)} %collective-permute-done.11.refs_1_, bf16[384,512]{1,0:T(8,128)(2,1)S(1)} %collective-permute-done.12.refs_2_, bf16[384,512]{1,0:T(8,128)(2,1)S(1)} %collective-permute-done.13.refs_3_), custom_call_target="tpu_custom_call" | custom-call | flops 1000000000 | bytes 1000000000 | tf_op jit(solution)/shard_map/finish_rows/pallas_call | solution.py:821
  134.7 3.1 %collective-permute-start.26 = (f32[16,512]{1,0:T(8,128)S(1)}, f32[16,512]{1,0:T(8,128)S(1)}, u32[]{:S(2)}, u32[]{:S(2)}) collective-permute-start(f32[16,512]{1,0:T(8,128)S(1)} %ordered_sum.2.refs_0_), channel_id=1, source_target_pairs={{0,2},{1,3},{2,0},{3,1},{4,6},{5,7},{6,4},{7,5},{8,10},{9,11},{10,... | collective-permute-start | bytes 98312 | tf_op jit(solution)/shard_map/ppermute | solution.py:1059
  137.9 2.0 %collective-permute-start.27 = (f32[16,512]{1,0:T(8,128)S(1)}, f32[16,512]{1,0:T(8,128)S(1)}, u32[]{:S(2)}, u32[]{:S(2)}) collective-permute-start(f32[16,512]{1,0:T(8,128)S(1)} %ordered_sum.2.refs_0_), channel_id=1, source_target_pairs={{0,1},{1,2},{2,3},{3,0},{4,5},{5,6},{6,7},{7,4},{8,9},{9,10},{10,1... | collective-permute-start | bytes 98312 | tf_op jit(solution)/shard_map/ppermute | solution.py:1059
  140.2 3.7 %finish.1 = (f32[12,64,512]{2,1,0:T(8,128)}, f32[3,512,512]{2,1,0:T(8,128)}, f32[512,512]{1,0:T(8,128)}, f32[512,512]{1,0:T(8,128)}, f32[512,512]{1,0:T(8,128)}) custom-call(f32[12,64,512]{2,1,0:T(8,128)S(1)} %get-tuple-element.184.keep_ref, bf16[3072,512]{1,0:T(8,128)(2,1)S(1)} %whole_chunks.1.send_ref, bf16[3072,512]{1,0:T(8,128)(2,1)S(1)} %collective-permute-done.24.recv_ref), custom_call_target="tpu_custom_call" | custom-call | flops 393216 | bytes 3932160 | tf_op jit(solution)/shard_map/finish/pallas_call | solution.py:1041
  (81 shorter events, 27.7 us)
Async XLA Ops:
  3.9 23.6 %collective-permute-start.2 = (bf16[3,256,512]{2,1,0:T(8,128)(2,1)S(1)}, bf16[3,256,512]{2,1,0:T(8,128)(2,1)S(1)}, u32[]{:S(2)}, u32[]{:S(2)}) collective-permute-start(bf16[3,256,512]{2,1,0:T(8,128)(2,1)S(1)} %half_weights.1), channel_id=1, source_target_pairs={{0,1},{1,0},{2,3},{3,2},{4,5},{5,4},{6,7},{7,6},{8,9},{9,8},{10,11... | collective-permute-start | bytes 2359304 | tf_op jit(solution)/shard_map/ppermute | solution.py:1071
  11.8 21.8 %collective-permute-start.1 = (bf16[528,768]{1,0:T(8,128)(2,1)S(1)}, bf16[528,768]{1,0:T(8,128)(2,1)S(1)}, u32[]{:S(2)}, u32[]{:S(2)}) collective-permute-start(bf16[528,768]{1,0:T(8,128)(2,1)S(1)} %get-tuple-element.112), channel_id=1, source_target_pairs={{0,16},{4,20},{8,24},{12,28},{16,0},{20,4},{24,8},{28,12},{1,17},{... | collective-permute-start | bytes 2433032 | tf_op jit(solution)/shard_map/ppermute | solution.py:1071
  13.4 20.2 %collective-permute-start = (bf16[512,768]{1,0:T(8,128)(2,1)S(1)}, bf16[512,768]{1,0:T(8,128)(2,1)S(1)}, u32[]{:S(2)}, u32[]{:S(2)}) collective-permute-start(bf16[512,768]{1,0:T(8,128)(2,1)S(1)} %get-tuple-element.144.refs_0_), channel_id=1, source_target_pairs={{0,8},{4,12},{8,0},{12,4},{16,24},{20,28},{24,16},{28,20},{1,9},{5... | collective-permute-start | bytes 2359304 | tf_op jit(solution)/shard_map/ppermute | solution.py:1071
  27.6 21.4 %collective-permute-start.6 = (bf16[512,768]{1,0:T(8,128)(2,1)S(1)}, bf16[512,768]{1,0:T(8,128)(2,1)S(1)}, u32[]{:S(2)}, u32[]{:S(2)}) collective-permute-start(bf16[512,768]{1,0:T(8,128)(2,1)S(1)} %get-tuple-element.144.refs_0_), channel_id=1, source_target_pairs={{0,24},{4,28},{8,16},{12,20},{16,8},{20,12},{24,0},{28,4},{1,25},{... | collective-permute-start | bytes 2359304 | tf_op jit(solution)/shard_map/ppermute | solution.py:1071
  28.1 12.1 %collective-permute-start.4 = (bf16[192,512]{1,0:T(8,128)(2,1)S(1)}, bf16[192,512]{1,0:T(8,128)(2,1)S(1)}, u32[]{:S(2)}, u32[]{:S(2)}) collective-permute-start(bf16[192,512]{1,0:T(8,128)(2,1)S(1)} %get-tuple-element.113.nt_ref.refs_0_), channel_id=1, source_target_pairs={{0,2},{1,3},{2,0},{3,1},{4,6},{5,7},{6,4},{7,5},{8,10},{9,11},{10,... | collective-permute-start | bytes 589832 | tf_op jit(solution)/shard_map/ppermute | solution.py:1059
  42.3 11.5 %collective-permute-start.5 = (bf16[192,512]{1,0:T(8,128)(2,1)S(1)}, bf16[192,512]{1,0:T(8,128)(2,1)S(1)}, u32[]{:S(2)}, u32[]{:S(2)}) collective-permute-start(bf16[192,512]{1,0:T(8,128)(2,1)S(1)} %get-tuple-element.120), channel_id=1, source_target_pairs={{0,2},{1,3},{2,0},{3,1},{4,6},{5,7},{6,4},{7,5},{8,10},{9,11},{10,... | collective-permute-start | bytes 589832 | tf_op jit(solution)/shard_map/ppermute | solution.py:1066
  42.4 21.7 %collective-permute-start.15 = (bf16[192,512]{1,0:T(8,128)(2,1)S(1)}, bf16[192,512]{1,0:T(8,128)(2,1)S(1)}, u32[]{:S(2)}, u32[]{:S(2)}) collective-permute-start(bf16[192,512]{1,0:T(8,128)(2,1)S(1)} %collective-permute-done.4.nt_ref.refs_1_), channel_id=1, source_target_pairs={{0,1},{1,0},{2,3},{3,2},{4,5},{5,4},{6,7},{7,6},{8,9},{9,8},{10,11... | collective-permute-start | bytes 589832 | tf_op jit(solution)/shard_map/ppermute | solution.py:1071
  45.6 18.6 %collective-permute-start.14 = (bf16[192,512]{1,0:T(8,128)(2,1)S(1)}, bf16[192,512]{1,0:T(8,128)(2,1)S(1)}, u32[]{:S(2)}, u32[]{:S(2)}) collective-permute-start(bf16[192,512]{1,0:T(8,128)(2,1)S(1)} %get-tuple-element.113.nt_ref.refs_0_), channel_id=1, source_target_pairs={{0,1},{1,0},{2,3},{3,2},{4,5},{5,4},{6,7},{7,6},{8,9},{9,8},{10,11... | collective-permute-start | bytes 589832 | tf_op jit(solution)/shard_map/ppermute | solution.py:1071
  54.1 12.9 %collective-permute-start.7 = (bf16[192,512]{1,0:T(8,128)(2,1)S(1)}, bf16[192,512]{1,0:T(8,128)(2,1)S(1)}, u32[]{:S(2)}, u32[]{:S(2)}) collective-permute-start(bf16[192,512]{1,0:T(8,128)(2,1)S(1)} %get-tuple-element.134.refs_0_), channel_id=1, source_target_pairs={{0,3},{1,0},{2,1},{3,2},{4,7},{5,4},{6,5},{7,6},{8,11},{9,8},{10,9... | collective-permute-start | bytes 589832 | tf_op jit(solution)/shard_map/ppermute | solution.py:1059
  55.9 16.1 %collective-permute-start.8 = (bf16[192,512]{1,0:T(8,128)(2,1)S(1)}, bf16[192,512]{1,0:T(8,128)(2,1)S(1)}, u32[]{:S(2)}, u32[]{:S(2)}) collective-permute-start(bf16[192,512]{1,0:T(8,128)(2,1)S(1)} %get-tuple-element.134.refs_0_), channel_id=1, source_target_pairs={{0,2},{1,3},{2,0},{3,1},{4,6},{5,7},{6,4},{7,5},{8,10},{9,11},{10,... | collective-permute-start | bytes 589832 | tf_op jit(solution)/shard_map/ppermute | solution.py:1059
  55.9 16.1 %collective-permute-start.9 = (bf16[192,512]{1,0:T(8,128)(2,1)S(1)}, bf16[192,512]{1,0:T(8,128)(2,1)S(1)}, u32[]{:S(2)}, u32[]{:S(2)}) collective-permute-start(bf16[192,512]{1,0:T(8,128)(2,1)S(1)} %get-tuple-element.134.refs_0_), channel_id=1, source_target_pairs={{0,1},{1,2},{2,3},{3,0},{4,5},{5,6},{6,7},{7,4},{8,9},{9,10},{10,1... | collective-permute-start | bytes 589832 | tf_op jit(solution)/shard_map/ppermute | solution.py:1059
  72.2 22.9 %collective-permute-start.17 = (bf16[768,512]{1,0:T(8,128)(2,1)S(1)}, bf16[768,512]{1,0:T(8,128)(2,1)S(1)}, u32[]{:S(2)}, u32[]{:S(2)}) collective-permute-start(bf16[768,512]{1,0:T(8,128)(2,1)S(1)} %pack_rows.1.refs_3_), channel_id=1, source_target_pairs={{0,8},{4,12},{8,0},{12,4},{16,24},{20,28},{24,16},{28,20},{1,9},{5... | collective-permute-start | bytes 2359304 | tf_op jit(solution)/shard_map/ppermute | solution.py:1071
  73.7 21.4 %collective-permute-start.18 = (bf16[768,512]{1,0:T(8,128)(2,1)S(1)}, bf16[768,512]{1,0:T(8,128)(2,1)S(1)}, u32[]{:S(2)}, u32[]{:S(2)}) collective-permute-start(bf16[768,512]{1,0:T(8,128)(2,1)S(1)} %pack_rows.1.refs_3_), channel_id=1, source_target_pairs={{0,16},{4,20},{8,24},{12,28},{16,0},{20,4},{24,8},{28,12},{1,17},{... | collective-permute-start | bytes 2359304 | tf_op jit(solution)/shard_map/ppermute | solution.py:1071
  75.2 19.6 %collective-permute-start.10 = (bf16[192,512]{1,0:T(8,128)(2,1)S(1)}, bf16[192,512]{1,0:T(8,128)(2,1)S(1)}, u32[]{:S(2)}, u32[]{:S(2)}) collective-permute-start(bf16[192,512]{1,0:T(8,128)(2,1)S(1)} %get-tuple-element.143), channel_id=1, source_target_pairs={{0,2},{1,3},{2,0},{3,1},{4,6},{5,7},{6,4},{7,5},{8,10},{9,11},{10,... | collective-permute-start | bytes 589832 | tf_op jit(solution)/shard_map/ppermute | solution.py:1066
  78.7 16.1 %collective-permute-start.16 = (bf16[768,512]{1,0:T(8,128)(2,1)S(1)}, bf16[768,512]{1,0:T(8,128)(2,1)S(1)}, u32[]{:S(2)}, u32[]{:S(2)}) collective-permute-start(bf16[768,512]{1,0:T(8,128)(2,1)S(1)} %get-tuple-element.164), channel_id=1, source_target_pairs={{0,4},{4,0},{8,12},{12,8},{16,20},{20,16},{24,28},{28,24},{1,5},{5... | collective-permute-start | bytes 2359304 | tf_op jit(solution)/shard_map/ppermute | solution.py:1071
  95.2 20.7 %collective-permute-start.19 = (bf16[800,512]{1,0:T(8,128)(2,1)S(1)}, bf16[800,512]{1,0:T(8,128)(2,1)S(1)}, u32[]{:S(2)}, u32[]{:S(2)}) collective-permute-start(bf16[800,512]{1,0:T(8,128)(2,1)S(1)} %get-tuple-element.171), channel_id=1, source_target_pairs={{0,16},{4,20},{8,24},{12,28},{16,0},{20,4},{24,8},{28,12},{1,17},{... | collective-permute-start | bytes 2457608 | tf_op jit(solution)/shard_map/ppermute | solution.py:1071
  95.8 20.4 %collective-permute-start.20 = (bf16[800,512]{1,0:T(8,128)(2,1)S(1)}, bf16[800,512]{1,0:T(8,128)(2,1)S(1)}, u32[]{:S(2)}, u32[]{:S(2)}) collective-permute-start(bf16[800,512]{1,0:T(8,128)(2,1)S(1)} %get-tuple-element.172), channel_id=1, source_target_pairs={{0,8},{4,12},{8,0},{12,4},{16,24},{20,28},{24,16},{28,20},{1,9},{5... | collective-permute-start | bytes 2457608 | tf_op jit(solution)/shard_map/ppermute | solution.py:1071
  96.4 33.8 %collective-permute-start.11 = (bf16[384,512]{1,0:T(8,128)(2,1)S(1)}, bf16[384,512]{1,0:T(8,128)(2,1)S(1)}, u32[]{:S(2)}, u32[]{:S(2)}) collective-permute-start(bf16[384,512]{1,0:T(8,128)(2,1)S(1)} %rows_message.1.refs_0_), channel_id=1, source_target_pairs={{0,3},{1,0},{2,1},{3,2},{4,7},{5,4},{6,5},{7,6},{8,11},{9,8},{10,9... | collective-permute-start | bytes 1179656 | tf_op jit(solution)/shard_map/ppermute | solution.py:1059
  96.8 34.1 %collective-permute-start.12 = (bf16[384,512]{1,0:T(8,128)(2,1)S(1)}, bf16[384,512]{1,0:T(8,128)(2,1)S(1)}, u32[]{:S(2)}, u32[]{:S(2)}) collective-permute-start(bf16[384,512]{1,0:T(8,128)(2,1)S(1)} %rows_message.1.refs_0_), channel_id=1, source_target_pairs={{0,2},{1,3},{2,0},{3,1},{4,6},{5,7},{6,4},{7,5},{8,10},{9,11},{10,... | collective-permute-start | bytes 1179656 | tf_op jit(solution)/shard_map/ppermute | solution.py:1059
  97.8 33.0 %collective-permute-start.13 = (bf16[384,512]{1,0:T(8,128)(2,1)S(1)}, bf16[384,512]{1,0:T(8,128)(2,1)S(1)}, u32[]{:S(2)}, u32[]{:S(2)}) collective-permute-start(bf16[384,512]{1,0:T(8,128)(2,1)S(1)} %rows_message.1.refs_0_), channel_id=1, source_target_pairs={{0,1},{1,2},{2,3},{3,0},{4,5},{5,6},{6,7},{7,4},{8,9},{9,10},{10,1... | collective-permute-start | bytes 1179656 | tf_op jit(solution)/shard_map/ppermute | solution.py:1059
  116.4 16.5 %collective-permute-start.22 = (bf16[416,512]{1,0:T(8,128)(2,1)S(1)}, bf16[416,512]{1,0:T(8,128)(2,1)S(1)}, u32[]{:S(2)}, u32[]{:S(2)}) collective-permute-start(bf16[416,512]{1,0:T(8,128)(2,1)S(1)} %get-tuple-element.185.lower_ref), channel_id=1, source_target_pairs={{0,8},{4,12},{8,0},{12,4},{16,24},{20,28},{24,16},{28,20},{1,9},{5... | collective-permute-start | bytes 1277960 | tf_op jit(solution)/shard_map/ppermute | solution.py:1071
  117.0 15.9 %collective-permute-start.21 = (bf16[384,512]{1,0:T(8,128)(2,1)S(1)}, bf16[384,512]{1,0:T(8,128)(2,1)S(1)}, u32[]{:S(2)}, u32[]{:S(2)}) collective-permute-start(bf16[384,512]{1,0:T(8,128)(2,1)S(1)} %get-tuple-element.173.upper_ref), channel_id=1, source_target_pairs={{0,16},{4,20},{8,24},{12,28},{16,0},{20,4},{24,8},{28,12},{1,17},{... | collective-permute-start | bytes 1179656 | tf_op jit(solution)/shard_map/ppermute | solution.py:1071
  134.7 9.2 %collective-permute-start.25 = (f32[16,512]{1,0:T(8,128)S(1)}, f32[16,512]{1,0:T(8,128)S(1)}, u32[]{:S(2)}, u32[]{:S(2)}) collective-permute-start(f32[16,512]{1,0:T(8,128)S(1)} %ordered_sum.2.refs_0_), channel_id=1, source_target_pairs={{0,3},{1,0},{2,1},{3,2},{4,7},{5,4},{6,5},{7,6},{8,11},{9,8},{10,9... | collective-permute-start | bytes 98312 | tf_op jit(solution)/shard_map/ppermute | solution.py:1059
  134.7 9.2 %collective-permute-start.26 = (f32[16,512]{1,0:T(8,128)S(1)}, f32[16,512]{1,0:T(8,128)S(1)}, u32[]{:S(2)}, u32[]{:S(2)}) collective-permute-start(f32[16,512]{1,0:T(8,128)S(1)} %ordered_sum.2.refs_0_), channel_id=1, source_target_pairs={{0,2},{1,3},{2,0},{3,1},{4,6},{5,7},{6,4},{7,5},{8,10},{9,11},{10,... | collective-permute-start | bytes 98312 | tf_op jit(solution)/shard_map/ppermute | solution.py:1059
  (14 other events, 72.4 us)

commit v5 on v4

--- a/solution.py
+++ b/solution.py
@@ -319,7 +319,7 @@
         out_specs=whole(),
         out_shape=jax.ShapeDtypeStruct((3, rows // 2, width), BF),
         scratch_shapes=[pltpu.SemaphoreType.DMA((3,))],
-        compiler_params=params(),
+        compiler_params=params(58 << 20),
         cost_estimate=cost(0, 6 * gate.size),
         name="half_weights",
     )(gate, up, down)

time: 145 us -> 145 us (level)
  local copies, waits for them, and re-layouts: 5.63 us -> 2.51 us
  Pallas kernels: 68.9 us -> 72 us
    unnamed x20 -> x14, local copies, waits for them, and re-layouts: 5.04 us -> 1.92 us
    pallas_call x1, Pallas kernels: 0.09 us -> 2.03 us  [half_weights(): pl.pallas_call(half_kernel, in_specs=[outside()] * 3, out_specs=whole(),...]
  transfers between devices with their start and end apart: 28 -> 28, of which waited for: 10 -> 10; matrix products, arithmetic and copies ran while one was open for 0% -> 0% of each run, Pallas kernels for 47% -> 48%
where the time goes in v5:
time: 145 us; the launch traced here: 144 us
  Pallas kernels  72 us (50%)
  waiting for transfers between devices  33.9 us (23%)
  starting transfers between devices  33.5 us (23%)
  local copies, waits for them, and re-layouts  2.51 us (2%)
  between operations  1.65 us (1%)
    ppermute x16, waiting for transfers between devices, swap(): return lax.ppermute(value, axis, [(i, i ^ bits) for i in range(n)])  18.5 us
    ppermute x16, starting transfers between devices, swap(): return lax.ppermute(value, axis, [(i, i ^ bits) for i in range(n)])  16.6 us
    pallas_call x1, Pallas kernels, spectral_unmix(): pl.pallas_call(functools.partial(unmix_kernel, kb, n), grid=(count // kb,...  16.5 us
    ppermute x10, starting transfers between devices, fetch_shifted(): pieces[r] = lax.ppermute(value, axis, [(i, (i - r) % n) for i in range(n)])  13.3 us
    pallas_call x1, Pallas kernels, spectral_mix(): pl.pallas_call(functools.partial(mix_kernel, kb, n), grid=(filt // kb,),...  12.8 us
    pallas_call x1, Pallas kernels, matrix_grads(): pl.pallas_call(functools.partial(grads_kernel, steps, order, groups, rows...  11.9 us
    ppermute x10, waiting for transfers between devices, fetch_shifted(): pieces[r] = lax.ppermute(value, axis, [(i, (i - r) % n) for i in range(n)])  10.4 us
    pallas_call x2, Pallas kernels, convolutions(): pl.pallas_call(functools.partial(conv_kernel, groups, tile, own, first),...  9.97 us
  transfers between devices with their start and end apart: 28, of which 10 were waited for; matrix products, arithmetic and copies ran while one was open for 0% of the time, Pallas kernels for 48%

profile of v5, /device:TPU:0, one launch (start us, length us, event | category | flops | bytes accessed | tf_op | source)
XLA Modules:
  0.0 144.2 jit_solution(6536982925239013254)
XLA Ops:
  0.6 2.0 %half_weights.1 = bf16[3,256,512]{2,1,0:T(8,128)(2,1)} custom-call(bf16[512,512]{1,0:T(8,128)(2,1)} %gw_ref.3, bf16[512,512]{1,0:T(8,128)(2,1)} %uw_ref.3, bf16[512,512]{1,0:T(8,128)(2,1)} %dw_ref.3), custom_call_target="tpu_custom_call" | custom-call | bytes 1572864 | tf_op jit(solution)/shard_map/half_weights/pallas_call | solution.py:316
  2.7 3.1 %collective-permute-start.2 = (bf16[3,256,512]{2,1,0:T(8,128)(2,1)}, bf16[3,256,512]{2,1,0:T(8,128)(2,1)S(1)}, u32[]{:S(2)}, u32[]{:S(2)}) collective-permute-start(bf16[3,256,512]{2,1,0:T(8,128)(2,1)} %half_weights.1), channel_id=1, source_target_pairs={{0,1},{1,0},{2,3},{3,2},{4,5},{5,4},{6,7},{7,6},{8,9},{9,8},{10,11... | collective-permute-start | bytes 2359304 | tf_op jit(solution)/shard_map/ppermute | solution.py:1071
  13.7 12.8 %spectral_mix.1 = (f32[192,512]{1,0:T(8,128)S(1)}, bf16[192,512]{1,0:T(8,128)(2,1)S(1)}) custom-call(s32[1]{0:T(128)S(6)} %copy.20.len_ref, f32[4,24,384]{2,1,0:T(8,128)S(1)} %get-tuple-element.105.taps_ref, f32[192,512]{1,0:T(8,128)S(1)} %get-tuple-element.106.x_ref, bf16[2,384,512]{2,1,0:T(8,128)(2,1)S(1)} %get-tuple-element.107.u_ref, ...), custom_call_target="tpu_custom_call" | custom-call | tf_op jit(solution)/shard_map/spectral_mix/pallas_call | solution.py:261
  27.3 2.6 %collective-permute-start.4 = (bf16[192,512]{1,0:T(8,128)(2,1)S(1)}, bf16[192,512]{1,0:T(8,128)(2,1)S(1)}, u32[]{:S(2)}, u32[]{:S(2)}) collective-permute-start(bf16[192,512]{1,0:T(8,128)(2,1)S(1)} %get-tuple-element.113.nt_ref.refs_0_), channel_id=1, source_target_pairs={{0,2},{1,3},{2,0},{3,1},{4,6},{5,7},{6,4},{7,5},{8,10},{9,11},{10,... | collective-permute-start | bytes 589832 | tf_op jit(solution)/shard_map/ppermute | solution.py:1059
  30.1 2.0 %collective-permute-done.refs_1_ = bf16[512,768]{1,0:T(8,128)(2,1)S(1)} collective-permute-done((bf16[512,768]{1,0:T(8,128)(2,1)S(1)}, bf16[512,768]{1,0:T(8,128)(2,1)S(1)}, u32[]{:S(2)}, u32[]{:S(2)}) %collective-permute-start) | collective-permute-done | bytes 786464 | tf_op jit(solution)/shard_map/ppermute | solution.py:1071
  32.3 2.1 %feed_forward.2 = (bf16[192,512]{1,0:T(8,128)(2,1)S(1)}, bf16[192,512]{1,0:T(8,128)(2,1)S(1)}, bf16[192,512]{1,0:T(8,128)(2,1)S(1)}, bf16[192,512]{1,0:T(8,128)(2,1)S(1)}, bf16[192,512]{1,0:T(8,128)(2,1)S(1)}) custom-call(bf16[192,512]{1,0:T(8,128)(2,1)S(1)} %get-tuple-element.113.nt_ref.refs_0_, bf16[768,512]{1,0:T(8,128)(2,1)S(1)} %dealt_rows.1.cot_ref, ...), custom_call_target="tpu_custom_call" | custom-call | flops 1207959552 | bytes 4325376 | tf_op jit(solution)/shard_map/feed_forward/pallas_call | solution.py:388
  34.4 4.9 %collective-permute-done.4.nt_ref.refs_1_ = bf16[192,512]{1,0:T(8,128)(2,1)S(1)} collective-permute-done((bf16[192,512]{1,0:T(8,128)(2,1)S(1)}, bf16[192,512]{1,0:T(8,128)(2,1)S(1)}, u32[]{:S(2)}, u32[]{:S(2)}) %collective-permute-start.4) | collective-permute-done | bytes 196640 | tf_op jit(solution)/shard_map/ppermute | solution.py:1059
  39.3 2.1 %feed_forward.3 = (bf16[192,512]{1,0:T(8,128)(2,1)S(1)}, bf16[192,512]{1,0:T(8,128)(2,1)S(1)}, bf16[192,512]{1,0:T(8,128)(2,1)S(1)}, bf16[192,512]{1,0:T(8,128)(2,1)S(1)}, bf16[192,512]{1,0:T(8,128)(2,1)S(1)}) custom-call(bf16[192,512]{1,0:T(8,128)(2,1)S(1)} %collective-permute-done.4.nt_ref.refs_1_, bf16[768,512]{1,0:T(8,128)(2,1)S(1)} %dealt_rows.1.cot_ref, ...), custom_call_target="tpu_custom_call" | custom-call | flops 1207959552 | bytes 4325376 | tf_op jit(solution)/shard_map/feed_forward/pallas_call | solution.py:388
  41.5 3.1 %collective-permute-start.15 = (bf16[192,512]{1,0:T(8,128)(2,1)S(1)}, bf16[192,512]{1,0:T(8,128)(2,1)S(1)}, u32[]{:S(2)}, u32[]{:S(2)}) collective-permute-start(bf16[192,512]{1,0:T(8,128)(2,1)S(1)} %collective-permute-done.4.nt_ref.refs_1_), channel_id=1, source_target_pairs={{0,1},{1,0},{2,3},{3,2},{4,5},{5,4},{6,7},{7,6},{8,9},{9,8},{10,11... | collective-permute-start | bytes 589832 | tf_op jit(solution)/shard_map/ppermute | solution.py:1071
  44.7 3.1 %collective-permute-done.6.refs_3_ = bf16[512,768]{1,0:T(8,128)(2,1)S(1)} collective-permute-done((bf16[512,768]{1,0:T(8,128)(2,1)S(1)}, bf16[512,768]{1,0:T(8,128)(2,1)S(1)}, u32[]{:S(2)}, u32[]{:S(2)}) %collective-permute-start.6) | collective-permute-done | bytes 786464 | tf_op jit(solution)/shard_map/ppermute | solution.py:1071
  47.8 5.1 %collective-permute-done.5.refs_1_ = bf16[192,512]{1,0:T(8,128)(2,1)S(1)} collective-permute-done((bf16[192,512]{1,0:T(8,128)(2,1)S(1)}, bf16[192,512]{1,0:T(8,128)(2,1)S(1)}, u32[]{:S(2)}, u32[]{:S(2)}) %collective-permute-start.5) | collective-permute-done | bytes 196640 | tf_op jit(solution)/shard_map/ppermute | solution.py:1066
  55.7 2.6 %lagged.1 = (bf16[512,3072]{1,0:T(8,128)(2,1)S(1)}, bf16[512,3072]{1,0:T(8,128)(2,1)S(1)}, bf16[512,3072]{1,0:T(8,128)(2,1)S(1)}) custom-call(bf16[512,768]{1,0:T(8,128)(2,1)S(1)} %get-tuple-element.144.refs_0_, bf16[512,768]{1,0:T(8,128)(2,1)S(1)} %collective-permute-done.refs_1_, bf16[528,768]{1,0:T(8,128)(2,1)S(1)} %collective-permute-done.1.refs_2_, ...), custom_call_target="tpu_custom_call" | custom-call | tf_op jit(solution)/shard_map/lagged/pallas_call | solution.py:702
  58.3 5.0 %convolutions.2.conv_ref = bf16[6,128,3072]{2,1,0:T(8,128)(2,1)S(1)} custom-call(f32[24,768]{1,0:T(8,128)S(1)} %get-tuple-element.133.filt_ref, bf16[512,768]{1,0:T(8,128)(2,1)S(1)} %get-tuple-element.144.refs_0_, bf16[512,768]{1,0:T(8,128)(2,1)S(1)} %collective-permute-done.refs_1_, bf16[528,768]{1,0:T(8,128)(2,1)S(1)} %collective-permute-done.1.refs_2_, ...), custom_call_target="tpu_custom_call" | custom-call | tf_op jit(solution)/shard_map/convolutions/pallas_call | solution.py:668
  66.2 4.9 %collective-permute-done.8.refs_2_ = bf16[192,512]{1,0:T(8,128)(2,1)S(1)} collective-permute-done((bf16[192,512]{1,0:T(8,128)(2,1)S(1)}, bf16[192,512]{1,0:T(8,128)(2,1)S(1)}, u32[]{:S(2)}, u32[]{:S(2)}) %collective-permute-start.8) | collective-permute-done | bytes 196640 | tf_op jit(solution)/shard_map/ppermute | solution.py:1059
  74.4 3.5 %collective-permute-start.10 = (bf16[192,512]{1,0:T(8,128)(2,1)S(1)}, bf16[192,512]{1,0:T(8,128)(2,1)S(1)}, u32[]{:S(2)}, u32[]{:S(2)}) collective-permute-start(bf16[192,512]{1,0:T(8,128)(2,1)S(1)} %get-tuple-element.143), channel_id=1, source_target_pairs={{0,2},{1,3},{2,0},{3,1},{4,6},{5,7},{6,4},{7,5},{8,10},{9,11},{10,... | collective-permute-start | bytes 589832 | tf_op jit(solution)/shard_map/ppermute | solution.py:1066
  77.9 16.5 %spectral_unmix.1 = (bf16[192,512]{1,0:T(8,128)(2,1)S(1)}, f32[16,512]{1,0:T(8,128)S(1)}) custom-call(s32[1]{0:T(128)S(6)} %copy.20.len_ref, f32[4,24,384]{2,1,0:T(8,128)S(1)} %get-tuple-element.105.taps_ref, f32[192,512]{1,0:T(8,128)S(1)} %get-tuple-element.106.x_ref, f32[192,512]{1,0:T(8,128)S(1)} %get-tuple-element.123.bh_ref, ...), custom_call_target="tpu_custom_call" | custom-call | flops 8455716864 | bytes 25165824 | tf_op jit(solution)/shard_map/spectral_unmix/pallas_call | solution.py:609
  97.0 2.0 %collective-permute-start.13 = (bf16[384,512]{1,0:T(8,128)(2,1)S(1)}, bf16[384,512]{1,0:T(8,128)(2,1)S(1)}, u32[]{:S(2)}, u32[]{:S(2)}) collective-permute-start(bf16[384,512]{1,0:T(8,128)(2,1)S(1)} %rows_message.1.refs_0_), channel_id=1, source_target_pairs={{0,1},{1,2},{2,3},{3,0},{4,5},{5,6},{6,7},{7,4},{8,9},{9,10},{10,1... | collective-permute-start | bytes 1179656 | tf_op jit(solution)/shard_map/ppermute | solution.py:1059
  99.0 5.0 %convolutions.3.conv_two_ref = bf16[6,128,3072]{2,1,0:T(8,128)(2,1)S(1)} custom-call(f32[24,768]{1,0:T(8,128)S(1)} %get-tuple-element.133.filt_ref, bf16[512,768]{1,0:T(8,128)(2,1)S(1)} %get-tuple-element.144.refs_0_, bf16[512,768]{1,0:T(8,128)(2,1)S(1)} %collective-permute-done.refs_1_, bf16[528,768]{1,0:T(8,128)(2,1)S(1)} %collective-permute-done.1.refs_2_, ...), custom_call_target="tpu_custom_call" | custom-call | tf_op jit(solution)/shard_map/convolutions/pallas_call | solution.py:668
  104.0 11.6 %collective-permute-done.19.from_y.refs_6_ = bf16[800,512]{1,0:T(8,128)(2,1)S(1)} collective-permute-done((bf16[800,512]{1,0:T(8,128)(2,1)S(1)}, bf16[800,512]{1,0:T(8,128)(2,1)S(1)}, u32[]{:S(2)}, u32[]{:S(2)}) %collective-permute-start.19) | collective-permute-done | bytes 819232 | tf_op jit(solution)/shard_map/ppermute | solution.py:1071
  118.1 11.9 %matrix_grads.1 = (f32[12,64,512]{2,1,0:T(8,128)S(1)}, bf16[2304,512]{1,0:T(8,128)(2,1)S(1)}) custom-call(bf16[6,128,3072]{2,1,0:T(8,128)(2,1)S(1)} %convolutions.2.conv_ref, bf16[6,128,3072]{2,1,0:T(8,128)(2,1)S(1)} %convolutions.3.conv_two_ref, bf16[512,3072]{1,0:T(8,128)(2,1)S(1)} %get-tuple-element.130.refs_0_, ...), custom_call_target="tpu_custom_call" | custom-call | tf_op jit(solution)/shard_map/matrix_grads/pallas_call | solution.py:761
  130.5 2.0 %finish_rows.1 = (f32[768,512]{1,0:T(8,128)}, bf16[768,512]{1,0:T(8,128)(2,1)}) custom-call(bf16[384,512]{1,0:T(8,128)(2,1)S(1)} %rows_message.1.refs_0_, bf16[384,512]{1,0:T(8,128)(2,1)S(1)} %collective-permute-done.11.refs_1_, bf16[384,512]{1,0:T(8,128)(2,1)S(1)} %collective-permute-done.12.refs_2_, bf16[384,512]{1,0:T(8,128)(2,1)S(1)} %collective-permute-done.13.refs_3_), custom_call_target="tpu_custom_call" | custom-call | flops 1000000000 | bytes 1000000000 | tf_op jit(solution)/shard_map/finish_rows/pallas_call | solution.py:821
  134.4 3.1 %collective-permute-start.26 = (f32[16,512]{1,0:T(8,128)S(1)}, f32[16,512]{1,0:T(8,128)S(1)}, u32[]{:S(2)}, u32[]{:S(2)}) collective-permute-start(f32[16,512]{1,0:T(8,128)S(1)} %ordered_sum.2.refs_0_), channel_id=1, source_target_pairs={{0,2},{1,3},{2,0},{3,1},{4,6},{5,7},{6,4},{7,5},{8,10},{9,11},{10,... | collective-permute-start | bytes 98312 | tf_op jit(solution)/shard_map/ppermute | solution.py:1059
  137.5 2.0 %collective-permute-start.27 = (f32[16,512]{1,0:T(8,128)S(1)}, f32[16,512]{1,0:T(8,128)S(1)}, u32[]{:S(2)}, u32[]{:S(2)}) collective-permute-start(f32[16,512]{1,0:T(8,128)S(1)} %ordered_sum.2.refs_0_), channel_id=1, source_target_pairs={{0,1},{1,2},{2,3},{3,0},{4,5},{5,6},{6,7},{7,4},{8,9},{9,10},{10,1... | collective-permute-start | bytes 98312 | tf_op jit(solution)/shard_map/ppermute | solution.py:1059
  139.9 3.7 %finish.1 = (f32[12,64,512]{2,1,0:T(8,128)}, f32[3,512,512]{2,1,0:T(8,128)}, f32[512,512]{1,0:T(8,128)}, f32[512,512]{1,0:T(8,128)}, f32[512,512]{1,0:T(8,128)}) custom-call(f32[12,64,512]{2,1,0:T(8,128)S(1)} %get-tuple-element.184.keep_ref, bf16[3072,512]{1,0:T(8,128)(2,1)S(1)} %whole_chunks.1.send_ref, bf16[3072,512]{1,0:T(8,128)(2,1)S(1)} %collective-permute-done.24.recv_ref), custom_call_target="tpu_custom_call" | custom-call | flops 393216 | bytes 3932160 | tf_op jit(solution)/shard_map/finish/pallas_call | solution.py:1041
  (75 shorter events, 25.8 us)
Async XLA Ops:
  2.7 23.9 %collective-permute-start.2 = (bf16[3,256,512]{2,1,0:T(8,128)(2,1)}, bf16[3,256,512]{2,1,0:T(8,128)(2,1)S(1)}, u32[]{:S(2)}, u32[]{:S(2)}) collective-permute-start(bf16[3,256,512]{2,1,0:T(8,128)(2,1)} %half_weights.1), channel_id=1, source_target_pairs={{0,1},{1,0},{2,3},{3,2},{4,5},{5,4},{6,7},{7,6},{8,9},{9,8},{10,11... | collective-permute-start | bytes 2359304 | tf_op jit(solution)/shard_map/ppermute | solution.py:1071
  10.7 21.4 %collective-permute-start.1 = (bf16[528,768]{1,0:T(8,128)(2,1)S(1)}, bf16[528,768]{1,0:T(8,128)(2,1)S(1)}, u32[]{:S(2)}, u32[]{:S(2)}) collective-permute-start(bf16[528,768]{1,0:T(8,128)(2,1)S(1)} %get-tuple-element.112), channel_id=1, source_target_pairs={{0,16},{4,20},{8,24},{12,28},{16,0},{20,4},{24,8},{28,12},{1,17},{... | collective-permute-start | bytes 2433032 | tf_op jit(solution)/shard_map/ppermute | solution.py:1071
  12.2 19.9 %collective-permute-start = (bf16[512,768]{1,0:T(8,128)(2,1)S(1)}, bf16[512,768]{1,0:T(8,128)(2,1)S(1)}, u32[]{:S(2)}, u32[]{:S(2)}) collective-permute-start(bf16[512,768]{1,0:T(8,128)(2,1)S(1)} %get-tuple-element.144.refs_0_), channel_id=1, source_target_pairs={{0,8},{4,12},{8,0},{12,4},{16,24},{20,28},{24,16},{28,20},{1,9},{5... | collective-permute-start | bytes 2359304 | tf_op jit(solution)/shard_map/ppermute | solution.py:1071
  26.7 21.0 %collective-permute-start.6 = (bf16[512,768]{1,0:T(8,128)(2,1)S(1)}, bf16[512,768]{1,0:T(8,128)(2,1)S(1)}, u32[]{:S(2)}, u32[]{:S(2)}) collective-permute-start(bf16[512,768]{1,0:T(8,128)(2,1)S(1)} %get-tuple-element.144.refs_0_), channel_id=1, source_target_pairs={{0,24},{4,28},{8,16},{12,20},{16,8},{20,12},{24,0},{28,4},{1,25},{... | collective-permute-start | bytes 2359304 | tf_op jit(solution)/shard_map/ppermute | solution.py:1071
  27.3 12.0 %collective-permute-start.4 = (bf16[192,512]{1,0:T(8,128)(2,1)S(1)}, bf16[192,512]{1,0:T(8,128)(2,1)S(1)}, u32[]{:S(2)}, u32[]{:S(2)}) collective-permute-start(bf16[192,512]{1,0:T(8,128)(2,1)S(1)} %get-tuple-element.113.nt_ref.refs_0_), channel_id=1, source_target_pairs={{0,2},{1,3},{2,0},{3,1},{4,6},{5,7},{6,4},{7,5},{8,10},{9,11},{10,... | collective-permute-start | bytes 589832 | tf_op jit(solution)/shard_map/ppermute | solution.py:1059
  41.4 11.4 %collective-permute-start.5 = (bf16[192,512]{1,0:T(8,128)(2,1)S(1)}, bf16[192,512]{1,0:T(8,128)(2,1)S(1)}, u32[]{:S(2)}, u32[]{:S(2)}) collective-permute-start(bf16[192,512]{1,0:T(8,128)(2,1)S(1)} %get-tuple-element.120), channel_id=1, source_target_pairs={{0,2},{1,3},{2,0},{3,1},{4,6},{5,7},{6,4},{7,5},{8,10},{9,11},{10,... | collective-permute-start | bytes 589832 | tf_op jit(solution)/shard_map/ppermute | solution.py:1066
  41.5 21.8 %collective-permute-start.15 = (bf16[192,512]{1,0:T(8,128)(2,1)S(1)}, bf16[192,512]{1,0:T(8,128)(2,1)S(1)}, u32[]{:S(2)}, u32[]{:S(2)}) collective-permute-start(bf16[192,512]{1,0:T(8,128)(2,1)S(1)} %collective-permute-done.4.nt_ref.refs_1_), channel_id=1, source_target_pairs={{0,1},{1,0},{2,3},{3,2},{4,5},{5,4},{6,7},{7,6},{8,9},{9,8},{10,11... | collective-permute-start | bytes 589832 | tf_op jit(solution)/shard_map/ppermute | solution.py:1071
  44.6 18.7 %collective-permute-start.14 = (bf16[192,512]{1,0:T(8,128)(2,1)S(1)}, bf16[192,512]{1,0:T(8,128)(2,1)S(1)}, u32[]{:S(2)}, u32[]{:S(2)}) collective-permute-start(bf16[192,512]{1,0:T(8,128)(2,1)S(1)} %get-tuple-element.113.nt_ref.refs_0_), channel_id=1, source_target_pairs={{0,1},{1,0},{2,3},{3,2},{4,5},{5,4},{6,7},{7,6},{8,9},{9,8},{10,11... | collective-permute-start | bytes 589832 | tf_op jit(solution)/shard_map/ppermute | solution.py:1071
  53.1 13.1 %collective-permute-start.7 = (bf16[192,512]{1,0:T(8,128)(2,1)S(1)}, bf16[192,512]{1,0:T(8,128)(2,1)S(1)}, u32[]{:S(2)}, u32[]{:S(2)}) collective-permute-start(bf16[192,512]{1,0:T(8,128)(2,1)S(1)} %get-tuple-element.134.refs_0_), channel_id=1, source_target_pairs={{0,3},{1,0},{2,1},{3,2},{4,7},{5,4},{6,5},{7,6},{8,11},{9,8},{10,9... | collective-permute-start | bytes 589832 | tf_op jit(solution)/shard_map/ppermute | solution.py:1059
  55.1 16.1 %collective-permute-start.8 = (bf16[192,512]{1,0:T(8,128)(2,1)S(1)}, bf16[192,512]{1,0:T(8,128)(2,1)S(1)}, u32[]{:S(2)}, u32[]{:S(2)}) collective-permute-start(bf16[192,512]{1,0:T(8,128)(2,1)S(1)} %get-tuple-element.134.refs_0_), channel_id=1, source_target_pairs={{0,2},{1,3},{2,0},{3,1},{4,6},{5,7},{6,4},{7,5},{8,10},{9,11},{10,... | collective-permute-start | bytes 589832 | tf_op jit(solution)/shard_map/ppermute | solution.py:1059
  55.1 16.1 %collective-permute-start.9 = (bf16[192,512]{1,0:T(8,128)(2,1)S(1)}, bf16[192,512]{1,0:T(8,128)(2,1)S(1)}, u32[]{:S(2)}, u32[]{:S(2)}) collective-permute-start(bf16[192,512]{1,0:T(8,128)(2,1)S(1)} %get-tuple-element.134.refs_0_), channel_id=1, source_target_pairs={{0,1},{1,2},{2,3},{3,0},{4,5},{5,6},{6,7},{7,4},{8,9},{9,10},{10,1... | collective-permute-start | bytes 589832 | tf_op jit(solution)/shard_map/ppermute | solution.py:1059
  71.4 23.3 %collective-permute-start.17 = (bf16[768,512]{1,0:T(8,128)(2,1)S(1)}, bf16[768,512]{1,0:T(8,128)(2,1)S(1)}, u32[]{:S(2)}, u32[]{:S(2)}) collective-permute-start(bf16[768,512]{1,0:T(8,128)(2,1)S(1)} %pack_rows.1.refs_3_), channel_id=1, source_target_pairs={{0,8},{4,12},{8,0},{12,4},{16,24},{20,28},{24,16},{28,20},{1,9},{5... | collective-permute-start | bytes 2359304 | tf_op jit(solution)/shard_map/ppermute | solution.py:1071
  72.9 21.8 %collective-permute-start.18 = (bf16[768,512]{1,0:T(8,128)(2,1)S(1)}, bf16[768,512]{1,0:T(8,128)(2,1)S(1)}, u32[]{:S(2)}, u32[]{:S(2)}) collective-permute-start(bf16[768,512]{1,0:T(8,128)(2,1)S(1)} %pack_rows.1.refs_3_), channel_id=1, source_target_pairs={{0,16},{4,20},{8,24},{12,28},{16,0},{20,4},{24,8},{28,12},{1,17},{... | collective-permute-start | bytes 2359304 | tf_op jit(solution)/shard_map/ppermute | solution.py:1071
  74.4 20.0 %collective-permute-start.10 = (bf16[192,512]{1,0:T(8,128)(2,1)S(1)}, bf16[192,512]{1,0:T(8,128)(2,1)S(1)}, u32[]{:S(2)}, u32[]{:S(2)}) collective-permute-start(bf16[192,512]{1,0:T(8,128)(2,1)S(1)} %get-tuple-element.143), channel_id=1, source_target_pairs={{0,2},{1,3},{2,0},{3,1},{4,6},{5,7},{6,4},{7,5},{8,10},{9,11},{10,... | collective-permute-start | bytes 589832 | tf_op jit(solution)/shard_map/ppermute | solution.py:1066
  77.9 16.6 %collective-permute-start.16 = (bf16[768,512]{1,0:T(8,128)(2,1)S(1)}, bf16[768,512]{1,0:T(8,128)(2,1)S(1)}, u32[]{:S(2)}, u32[]{:S(2)}) collective-permute-start(bf16[768,512]{1,0:T(8,128)(2,1)S(1)} %get-tuple-element.164), channel_id=1, source_target_pairs={{0,4},{4,0},{8,12},{12,8},{16,20},{20,16},{24,28},{28,24},{1,5},{5... | collective-permute-start | bytes 2359304 | tf_op jit(solution)/shard_map/ppermute | solution.py:1071
  94.8 20.8 %collective-permute-start.19 = (bf16[800,512]{1,0:T(8,128)(2,1)S(1)}, bf16[800,512]{1,0:T(8,128)(2,1)S(1)}, u32[]{:S(2)}, u32[]{:S(2)}) collective-permute-start(bf16[800,512]{1,0:T(8,128)(2,1)S(1)} %get-tuple-element.171), channel_id=1, source_target_pairs={{0,16},{4,20},{8,24},{12,28},{16,0},{20,4},{24,8},{28,12},{1,17},{... | collective-permute-start | bytes 2457608 | tf_op jit(solution)/shard_map/ppermute | solution.py:1071
  95.4 20.4 %collective-permute-start.20 = (bf16[800,512]{1,0:T(8,128)(2,1)S(1)}, bf16[800,512]{1,0:T(8,128)(2,1)S(1)}, u32[]{:S(2)}, u32[]{:S(2)}) collective-permute-start(bf16[800,512]{1,0:T(8,128)(2,1)S(1)} %get-tuple-element.172), channel_id=1, source_target_pairs={{0,8},{4,12},{8,0},{12,4},{16,24},{20,28},{24,16},{28,20},{1,9},{5... | collective-permute-start | bytes 2457608 | tf_op jit(solution)/shard_map/ppermute | solution.py:1071
  96.0 34.0 %collective-permute-start.11 = (bf16[384,512]{1,0:T(8,128)(2,1)S(1)}, bf16[384,512]{1,0:T(8,128)(2,1)S(1)}, u32[]{:S(2)}, u32[]{:S(2)}) collective-permute-start(bf16[384,512]{1,0:T(8,128)(2,1)S(1)} %rows_message.1.refs_0_), channel_id=1, source_target_pairs={{0,3},{1,0},{2,1},{3,2},{4,7},{5,4},{6,5},{7,6},{8,11},{9,8},{10,9... | collective-permute-start | bytes 1179656 | tf_op jit(solution)/shard_map/ppermute | solution.py:1059
  96.5 34.0 %collective-permute-start.12 = (bf16[384,512]{1,0:T(8,128)(2,1)S(1)}, bf16[384,512]{1,0:T(8,128)(2,1)S(1)}, u32[]{:S(2)}, u32[]{:S(2)}) collective-permute-start(bf16[384,512]{1,0:T(8,128)(2,1)S(1)} %rows_message.1.refs_0_), channel_id=1, source_target_pairs={{0,2},{1,3},{2,0},{3,1},{4,6},{5,7},{6,4},{7,5},{8,10},{9,11},{10,... | collective-permute-start | bytes 1179656 | tf_op jit(solution)/shard_map/ppermute | solution.py:1059
  97.0 33.5 %collective-permute-start.13 = (bf16[384,512]{1,0:T(8,128)(2,1)S(1)}, bf16[384,512]{1,0:T(8,128)(2,1)S(1)}, u32[]{:S(2)}, u32[]{:S(2)}) collective-permute-start(bf16[384,512]{1,0:T(8,128)(2,1)S(1)} %rows_message.1.refs_0_), channel_id=1, source_target_pairs={{0,1},{1,2},{2,3},{3,0},{4,5},{5,6},{6,7},{7,4},{8,9},{9,10},{10,1... | collective-permute-start | bytes 1179656 | tf_op jit(solution)/shard_map/ppermute | solution.py:1059
  116.0 16.5 %collective-permute-start.22 = (bf16[416,512]{1,0:T(8,128)(2,1)S(1)}, bf16[416,512]{1,0:T(8,128)(2,1)S(1)}, u32[]{:S(2)}, u32[]{:S(2)}) collective-permute-start(bf16[416,512]{1,0:T(8,128)(2,1)S(1)} %get-tuple-element.185.lower_ref), channel_id=1, source_target_pairs={{0,8},{4,12},{8,0},{12,4},{16,24},{20,28},{24,16},{28,20},{1,9},{5... | collective-permute-start | bytes 1277960 | tf_op jit(solution)/shard_map/ppermute | solution.py:1071
  116.6 15.8 %collective-permute-start.21 = (bf16[384,512]{1,0:T(8,128)(2,1)S(1)}, bf16[384,512]{1,0:T(8,128)(2,1)S(1)}, u32[]{:S(2)}, u32[]{:S(2)}) collective-permute-start(bf16[384,512]{1,0:T(8,128)(2,1)S(1)} %get-tuple-element.173.upper_ref), channel_id=1, source_target_pairs={{0,16},{4,20},{8,24},{12,28},{16,0},{20,4},{24,8},{28,12},{1,17},{... | collective-permute-start | bytes 1179656 | tf_op jit(solution)/shard_map/ppermute | solution.py:1071
  134.4 9.2 %collective-permute-start.25 = (f32[16,512]{1,0:T(8,128)S(1)}, f32[16,512]{1,0:T(8,128)S(1)}, u32[]{:S(2)}, u32[]{:S(2)}) collective-permute-start(f32[16,512]{1,0:T(8,128)S(1)} %ordered_sum.2.refs_0_), channel_id=1, source_target_pairs={{0,3},{1,0},{2,1},{3,2},{4,7},{5,4},{6,5},{7,6},{8,11},{9,8},{10,9... | collective-permute-start | bytes 98312 | tf_op jit(solution)/shard_map/ppermute | solution.py:1059
  134.4 9.2 %collective-permute-start.26 = (f32[16,512]{1,0:T(8,128)S(1)}, f32[16,512]{1,0:T(8,128)S(1)}, u32[]{:S(2)}, u32[]{:S(2)}) collective-permute-start(f32[16,512]{1,0:T(8,128)S(1)} %ordered_sum.2.refs_0_), channel_id=1, source_target_pairs={{0,2},{1,3},{2,0},{3,1},{4,6},{5,7},{6,4},{7,5},{8,10},{9,11},{10,... | collective-permute-start | bytes 98312 | tf_op jit(solution)/shard_map/ppermute | solution.py:1059
  (11 other events, 66.8 us)

commit v6 on v5

--- a/solution.py
+++ b/solution.py
@@ -805,30 +805,26 @@
     )(ig, hidden, *pieces)
 
 
-def finish_rows_kernel(n, share, *refs):
-    pieces, (ig_ref, out_ref, scr) = refs[:n], refs[n:]
+def finish_rows_kernel(n, share, at, *refs):
+    pieces, (out_ref, scr) = refs[:n], refs[n:]
     m = lax.axis_index("mp")
-    for at, ref in ((0, ig_ref), (share, out_ref)):
-        for r in range(n):
-            value = pieces[r][at : at + share, :].astype(F32)
-            put_every_nth(scr, value, lax.rem(m + r, n), n)
-        ref[...] = columns_of(scr, n * share).astype(ref.dtype)
-
-
-def finish_rows(pieces):
+    for r in range(n):
+        value = pieces[r][at : at + share, :].astype(F32)
+        put_every_nth(scr, value, lax.rem(m + r, n), n)
+    out_ref[...] = columns_of(scr, n * share).astype(out_ref.dtype)
+
+
+def finish_rows(pieces, at, dtype, weight):
     n = len(pieces)
     share, width = pieces[0].shape[0] // 2, pieces[0].shape[1]
     return pl.pallas_call(
-        functools.partial(finish_rows_kernel, n, share),
+        functools.partial(finish_rows_kernel, n, share, at),
         in_specs=[whole()] * n,
-        out_specs=[whole()] * 2,
-        out_shape=[
-            jax.ShapeDtypeStruct((n * share, width), F32),
-            jax.ShapeDtypeStruct((n * share, width), BF),
-        ],
+        out_specs=whole(),
+        out_shape=jax.ShapeDtypeStruct((n * share, width), dtype),
         scratch_shapes=[pltpu.VMEM((width // 128, n * share + 16, 128), F32)],
         compiler_params=params(),
-        cost_estimate=cost(1e9, 1e9),
+        cost_estimate=cost(weight, weight),
         name="finish_rows",
     )(*pieces)
 
@@ -1174,10 +1170,14 @@
         ]
         keep = ordered_sum([k for k, _ in some], "dp", 8)
         send = ordered_sum([k.astype(F32) for _, k in some], "dp", 8).astype(BF)
-    input_grad, output = finish_rows(after(messages, send))
+    messages = after(messages, send)
+    output = finish_rows(messages, share, BF, 1e9)
+    input_grad = finish_rows(after(messages, output), 0, F32, 1e6)
     if custom:
         from_y_two, from_x_two = after((from_y_two, from_x_two), output)
-        gains = swap_sum(chips_sum(*gains_parts, after(from_x_two, send)), n_dp)
+        gains = chips_sum(*gains_parts, after(from_x_two, send))
+        gains = [gains, after(swap(gains, "dp", n_dp, 1), input_grad)]
+        gains = ordered_sum(gains, "dp", 0)
         send = whole_chunks(upper, from_y_two, lower, from_x_two, after(send, gains))
     gains = fetch_shifted(gains, "mp", n)
     recv = swap(send, "dp", n_dp, 1)

time: 145 us -> 144 us (level)
  transfers between devices with their start and end apart: 28 -> 28, of which waited for: 10 -> 9; matrix products, arithmetic and copies ran while one was open for 0% -> 0% of each run, Pallas kernels for 48% -> 49%
where the time goes in v6:
time: 144 us
  Pallas kernels  72.7 us (50%)
  starting transfers between devices  33.8 us (23%)
  waiting for transfers between devices  32.5 us (23%)
  local copies, waits for them, and re-layouts  2.51 us (2%)
  between operations  1.65 us (1%)
    ppermute x16, waiting for transfers between devices, swap(): return lax.ppermute(value, axis, [(i, i ^ bits) for i in range(n)])  17.1 us
    ppermute x16, starting transfers between devices, swap(): return lax.ppermute(value, axis, [(i, i ^ bits) for i in range(n)])  16.9 us
    pallas_call x1, Pallas kernels, spectral_unmix(): pl.pallas_call(functools.partial(unmix_kernel, kb, n), grid=(count // kb,...  16.5 us
    ppermute x10, starting transfers between devices, fetch_shifted(): pieces[r] = lax.ppermute(value, axis, [(i, (i - r) % n) for i in range(n)])  13.3 us
    pallas_call x1, Pallas kernels, spectral_mix(): pl.pallas_call(functools.partial(mix_kernel, kb, n), grid=(filt // kb,),...  12.8 us
    pallas_call x1, Pallas kernels, matrix_grads(): pl.pallas_call(functools.partial(grads_kernel, steps, order, groups, rows...  11.9 us
    ppermute x10, waiting for transfers between devices, fetch_shifted(): pieces[r] = lax.ppermute(value, axis, [(i, (i - r) % n) for i in range(n)])  10.4 us
    pallas_call x2, Pallas kernels, convolutions(): pl.pallas_call(functools.partial(conv_kernel, groups, tile, own, first),...  9.97 us
  transfers between devices with their start and end apart: 28, of which 9 were waited for; matrix products, arithmetic and copies ran while one was open for 0% of the time, Pallas kernels for 49%

profile of v6, /device:TPU:0, one launch (start us, length us, event | category | flops | bytes accessed | tf_op | source)
XLA Modules:
  0.0 143.9 jit_solution(17749329555266110689)
XLA Ops:
  0.6 2.0 %half_weights.1 = bf16[3,256,512]{2,1,0:T(8,128)(2,1)} custom-call(bf16[512,512]{1,0:T(8,128)(2,1)} %gw_ref.3, bf16[512,512]{1,0:T(8,128)(2,1)} %uw_ref.3, bf16[512,512]{1,0:T(8,128)(2,1)} %dw_ref.3), custom_call_target="tpu_custom_call" | custom-call | bytes 1572864 | tf_op jit(solution)/shard_map/half_weights/pallas_call | solution.py:316
  2.7 3.1 %collective-permute-start.2 = (bf16[3,256,512]{2,1,0:T(8,128)(2,1)}, bf16[3,256,512]{2,1,0:T(8,128)(2,1)S(1)}, u32[]{:S(2)}, u32[]{:S(2)}) collective-permute-start(bf16[3,256,512]{2,1,0:T(8,128)(2,1)} %half_weights.1), channel_id=1, source_target_pairs={{0,1},{1,0},{2,3},{3,2},{4,5},{5,4},{6,7},{7,6},{8,9},{9,8},{10,11... | collective-permute-start | bytes 2359304 | tf_op jit(solution)/shard_map/ppermute | solution.py:1067
  13.7 12.8 %spectral_mix.1 = (f32[192,512]{1,0:T(8,128)S(1)}, bf16[192,512]{1,0:T(8,128)(2,1)S(1)}) custom-call(s32[1]{0:T(128)S(6)} %copy.20.len_ref, f32[4,24,384]{2,1,0:T(8,128)S(1)} %get-tuple-element.108.taps_ref, f32[192,512]{1,0:T(8,128)S(1)} %get-tuple-element.109.x_ref, bf16[2,384,512]{2,1,0:T(8,128)(2,1)S(1)} %get-tuple-element.110.u_ref, ...), custom_call_target="tpu_custom_call" | custom-call | tf_op jit(solution)/shard_map/spectral_mix/pallas_call | solution.py:261
  27.3 2.6 %collective-permute-start.4 = (bf16[192,512]{1,0:T(8,128)(2,1)S(1)}, bf16[192,512]{1,0:T(8,128)(2,1)S(1)}, u32[]{:S(2)}, u32[]{:S(2)}) collective-permute-start(bf16[192,512]{1,0:T(8,128)(2,1)S(1)} %get-tuple-element.116.nt_ref.refs_0_), channel_id=1, source_target_pairs={{0,2},{1,3},{2,0},{3,1},{4,6},{5,7},{6,4},{7,5},{8,10},{9,11},{10,... | collective-permute-start | bytes 589832 | tf_op jit(solution)/shard_map/ppermute | solution.py:1055
  30.1 2.0 %collective-permute-done.refs_1_ = bf16[512,768]{1,0:T(8,128)(2,1)S(1)} collective-permute-done((bf16[512,768]{1,0:T(8,128)(2,1)S(1)}, bf16[512,768]{1,0:T(8,128)(2,1)S(1)}, u32[]{:S(2)}, u32[]{:S(2)}) %collective-permute-start) | collective-permute-done | bytes 786464 | tf_op jit(solution)/shard_map/ppermute | solution.py:1067
  32.3 2.1 %feed_forward.2 = (bf16[192,512]{1,0:T(8,128)(2,1)S(1)}, bf16[192,512]{1,0:T(8,128)(2,1)S(1)}, bf16[192,512]{1,0:T(8,128)(2,1)S(1)}, bf16[192,512]{1,0:T(8,128)(2,1)S(1)}, bf16[192,512]{1,0:T(8,128)(2,1)S(1)}) custom-call(bf16[192,512]{1,0:T(8,128)(2,1)S(1)} %get-tuple-element.116.nt_ref.refs_0_, bf16[768,512]{1,0:T(8,128)(2,1)S(1)} %dealt_rows.1.cot_ref, ...), custom_call_target="tpu_custom_call" | custom-call | flops 1207959552 | bytes 4325376 | tf_op jit(solution)/shard_map/feed_forward/pallas_call | solution.py:388
  34.4 4.9 %collective-permute-done.4.nt_ref.refs_1_ = bf16[192,512]{1,0:T(8,128)(2,1)S(1)} collective-permute-done((bf16[192,512]{1,0:T(8,128)(2,1)S(1)}, bf16[192,512]{1,0:T(8,128)(2,1)S(1)}, u32[]{:S(2)}, u32[]{:S(2)}) %collective-permute-start.4) | collective-permute-done | bytes 196640 | tf_op jit(solution)/shard_map/ppermute | solution.py:1055
  39.3 2.1 %feed_forward.3 = (bf16[192,512]{1,0:T(8,128)(2,1)S(1)}, bf16[192,512]{1,0:T(8,128)(2,1)S(1)}, bf16[192,512]{1,0:T(8,128)(2,1)S(1)}, bf16[192,512]{1,0:T(8,128)(2,1)S(1)}, bf16[192,512]{1,0:T(8,128)(2,1)S(1)}) custom-call(bf16[192,512]{1,0:T(8,128)(2,1)S(1)} %collective-permute-done.4.nt_ref.refs_1_, bf16[768,512]{1,0:T(8,128)(2,1)S(1)} %dealt_rows.1.cot_ref, ...), custom_call_target="tpu_custom_call" | custom-call | flops 1207959552 | bytes 4325376 | tf_op jit(solution)/shard_map/feed_forward/pallas_call | solution.py:388
  41.5 3.1 %collective-permute-start.15 = (bf16[192,512]{1,0:T(8,128)(2,1)S(1)}, bf16[192,512]{1,0:T(8,128)(2,1)S(1)}, u32[]{:S(2)}, u32[]{:S(2)}) collective-permute-start(bf16[192,512]{1,0:T(8,128)(2,1)S(1)} %collective-permute-done.4.nt_ref.refs_1_), channel_id=1, source_target_pairs={{0,1},{1,0},{2,3},{3,2},{4,5},{5,4},{6,7},{7,6},{8,9},{9,8},{10,11... | collective-permute-start | bytes 589832 | tf_op jit(solution)/shard_map/ppermute | solution.py:1067
  44.7 3.1 %collective-permute-done.6.refs_3_ = bf16[512,768]{1,0:T(8,128)(2,1)S(1)} collective-permute-done((bf16[512,768]{1,0:T(8,128)(2,1)S(1)}, bf16[512,768]{1,0:T(8,128)(2,1)S(1)}, u32[]{:S(2)}, u32[]{:S(2)}) %collective-permute-start.6) | collective-permute-done | bytes 786464 | tf_op jit(solution)/shard_map/ppermute | solution.py:1067
  47.8 5.1 %collective-permute-done.5.refs_1_ = bf16[192,512]{1,0:T(8,128)(2,1)S(1)} collective-permute-done((bf16[192,512]{1,0:T(8,128)(2,1)S(1)}, bf16[192,512]{1,0:T(8,128)(2,1)S(1)}, u32[]{:S(2)}, u32[]{:S(2)}) %collective-permute-start.5) | collective-permute-done | bytes 196640 | tf_op jit(solution)/shard_map/ppermute | solution.py:1062
  53.1 1.9 %collective-permute-start.7 = (bf16[192,512]{1,0:T(8,128)(2,1)S(1)}, bf16[192,512]{1,0:T(8,128)(2,1)S(1)}, u32[]{:S(2)}, u32[]{:S(2)}) collective-permute-start(bf16[192,512]{1,0:T(8,128)(2,1)S(1)} %get-tuple-element.137.refs_0_), channel_id=1, source_target_pairs={{0,3},{1,0},{2,1},{3,2},{4,7},{5,4},{6,5},{7,6},{8,11},{9,8},{10,9... | collective-permute-start | bytes 589832 | tf_op jit(solution)/shard_map/ppermute | solution.py:1055
  55.7 2.6 %lagged.1 = (bf16[512,3072]{1,0:T(8,128)(2,1)S(1)}, bf16[512,3072]{1,0:T(8,128)(2,1)S(1)}, bf16[512,3072]{1,0:T(8,128)(2,1)S(1)}) custom-call(bf16[512,768]{1,0:T(8,128)(2,1)S(1)} %get-tuple-element.147.refs_0_, bf16[512,768]{1,0:T(8,128)(2,1)S(1)} %collective-permute-done.refs_1_, bf16[528,768]{1,0:T(8,128)(2,1)S(1)} %collective-permute-done.1.refs_2_, ...), custom_call_target="tpu_custom_call" | custom-call | tf_op jit(solution)/shard_map/lagged/pallas_call | solution.py:702
  58.3 5.0 %convolutions.2.conv_ref = bf16[6,128,3072]{2,1,0:T(8,128)(2,1)S(1)} custom-call(f32[24,768]{1,0:T(8,128)S(1)} %get-tuple-element.136.filt_ref, bf16[512,768]{1,0:T(8,128)(2,1)S(1)} %get-tuple-element.147.refs_0_, bf16[512,768]{1,0:T(8,128)(2,1)S(1)} %collective-permute-done.refs_1_, bf16[528,768]{1,0:T(8,128)(2,1)S(1)} %collective-permute-done.1.refs_2_, ...), custom_call_target="tpu_custom_call" | custom-call | tf_op jit(solution)/shard_map/convolutions/pallas_call | solution.py:668
  66.2 4.9 %collective-permute-done.8.refs_2_ = bf16[192,512]{1,0:T(8,128)(2,1)S(1)} collective-permute-done((bf16[192,512]{1,0:T(8,128)(2,1)S(1)}, bf16[192,512]{1,0:T(8,128)(2,1)S(1)}, u32[]{:S(2)}, u32[]{:S(2)}) %collective-permute-start.8) | collective-permute-done | bytes 196640 | tf_op jit(solution)/shard_map/ppermute | solution.py:1055
  74.4 3.5 %collective-permute-start.10 = (bf16[192,512]{1,0:T(8,128)(2,1)S(1)}, bf16[192,512]{1,0:T(8,128)(2,1)S(1)}, u32[]{:S(2)}, u32[]{:S(2)}) collective-permute-start(bf16[192,512]{1,0:T(8,128)(2,1)S(1)} %get-tuple-element.146), channel_id=1, source_target_pairs={{0,2},{1,3},{2,0},{3,1},{4,6},{5,7},{6,4},{7,5},{8,10},{9,11},{10,... | collective-permute-start | bytes 589832 | tf_op jit(solution)/shard_map/ppermute | solution.py:1062
  77.9 16.5 %spectral_unmix.1 = (bf16[192,512]{1,0:T(8,128)(2,1)S(1)}, f32[16,512]{1,0:T(8,128)S(1)}) custom-call(s32[1]{0:T(128)S(6)} %copy.20.len_ref, f32[4,24,384]{2,1,0:T(8,128)S(1)} %get-tuple-element.108.taps_ref, f32[192,512]{1,0:T(8,128)S(1)} %get-tuple-element.109.x_ref, f32[192,512]{1,0:T(8,128)S(1)} %get-tuple-element.126.bh_ref, ...), custom_call_target="tpu_custom_call" | custom-call | flops 8455716864 | bytes 25165824 | tf_op jit(solution)/shard_map/spectral_unmix/pallas_call | solution.py:609
  97.0 2.0 %collective-permute-start.13 = (bf16[384,512]{1,0:T(8,128)(2,1)S(1)}, bf16[384,512]{1,0:T(8,128)(2,1)S(1)}, u32[]{:S(2)}, u32[]{:S(2)}) collective-permute-start(bf16[384,512]{1,0:T(8,128)(2,1)S(1)} %rows_message.1.refs_0_), channel_id=1, source_target_pairs={{0,1},{1,2},{2,3},{3,0},{4,5},{5,6},{6,7},{7,4},{8,9},{9,10},{10,1... | collective-permute-start | bytes 1179656 | tf_op jit(solution)/shard_map/ppermute | solution.py:1055
  99.0 5.0 %convolutions.3.conv_two_ref = bf16[6,128,3072]{2,1,0:T(8,128)(2,1)S(1)} custom-call(f32[24,768]{1,0:T(8,128)S(1)} %get-tuple-element.136.filt_ref, bf16[512,768]{1,0:T(8,128)(2,1)S(1)} %get-tuple-element.147.refs_0_, bf16[512,768]{1,0:T(8,128)(2,1)S(1)} %collective-permute-done.refs_1_, bf16[528,768]{1,0:T(8,128)(2,1)S(1)} %collective-permute-done.1.refs_2_, ...), custom_call_target="tpu_custom_call" | custom-call | tf_op jit(solution)/shard_map/convolutions/pallas_call | solution.py:668
  104.0 11.6 %collective-permute-done.19.from_y.refs_6_ = bf16[800,512]{1,0:T(8,128)(2,1)S(1)} collective-permute-done((bf16[800,512]{1,0:T(8,128)(2,1)S(1)}, bf16[800,512]{1,0:T(8,128)(2,1)S(1)}, u32[]{:S(2)}, u32[]{:S(2)}) %collective-permute-start.19) | collective-permute-done | bytes 819232 | tf_op jit(solution)/shard_map/ppermute | solution.py:1067
  118.1 11.9 %matrix_grads.1 = (f32[12,64,512]{2,1,0:T(8,128)S(1)}, bf16[2304,512]{1,0:T(8,128)(2,1)S(1)}) custom-call(bf16[6,128,3072]{2,1,0:T(8,128)(2,1)S(1)} %convolutions.2.conv_ref, bf16[6,128,3072]{2,1,0:T(8,128)(2,1)S(1)} %convolutions.3.conv_two_ref, bf16[512,3072]{1,0:T(8,128)(2,1)S(1)} %get-tuple-element.133.refs_0_, ...), custom_call_target="tpu_custom_call" | custom-call | tf_op jit(solution)/shard_map/matrix_grads/pallas_call | solution.py:761
  134.2 3.1 %collective-permute-start.26 = (f32[16,512]{1,0:T(8,128)S(1)}, f32[16,512]{1,0:T(8,128)S(1)}, u32[]{:S(2)}, u32[]{:S(2)}) collective-permute-start(f32[16,512]{1,0:T(8,128)S(1)} %ordered_sum.2.refs_0_), channel_id=1, source_target_pairs={{0,2},{1,3},{2,0},{3,1},{4,6},{5,7},{6,4},{7,5},{8,10},{9,11},{10,... | collective-permute-start | bytes 98312 | tf_op jit(solution)/shard_map/ppermute | solution.py:1055
  137.4 2.0 %collective-permute-start.27 = (f32[16,512]{1,0:T(8,128)S(1)}, f32[16,512]{1,0:T(8,128)S(1)}, u32[]{:S(2)}, u32[]{:S(2)}) collective-permute-start(f32[16,512]{1,0:T(8,128)S(1)} %ordered_sum.2.refs_0_), channel_id=1, source_target_pairs={{0,1},{1,2},{2,3},{3,0},{4,5},{5,6},{6,7},{7,4},{8,9},{9,10},{10,1... | collective-permute-start | bytes 98312 | tf_op jit(solution)/shard_map/ppermute | solution.py:1055
  139.5 3.7 %finish.1 = (f32[12,64,512]{2,1,0:T(8,128)}, f32[3,512,512]{2,1,0:T(8,128)}, f32[512,512]{1,0:T(8,128)}, f32[512,512]{1,0:T(8,128)}, f32[512,512]{1,0:T(8,128)}) custom-call(f32[12,64,512]{2,1,0:T(8,128)S(1)} %get-tuple-element.189.keep_ref, bf16[3072,512]{1,0:T(8,128)(2,1)S(1)} %whole_chunks.1.send_ref, bf16[3072,512]{1,0:T(8,128)(2,1)S(1)} %collective-permute-done.24.recv_ref), custom_call_target="tpu_custom_call" | custom-call | flops 393216 | bytes 3932160 | tf_op jit(solution)/shard_map/finish/pallas_call | solution.py:1037
  (76 shorter events, 25.5 us)
Async XLA Ops:
  2.7 23.9 %collective-permute-start.2 = (bf16[3,256,512]{2,1,0:T(8,128)(2,1)}, bf16[3,256,512]{2,1,0:T(8,128)(2,1)S(1)}, u32[]{:S(2)}, u32[]{:S(2)}) collective-permute-start(bf16[3,256,512]{2,1,0:T(8,128)(2,1)} %half_weights.1), channel_id=1, source_target_pairs={{0,1},{1,0},{2,3},{3,2},{4,5},{5,4},{6,7},{7,6},{8,9},{9,8},{10,11... | collective-permute-start | bytes 2359304 | tf_op jit(solution)/shard_map/ppermute | solution.py:1067
  10.7 21.4 %collective-permute-start.1 = (bf16[528,768]{1,0:T(8,128)(2,1)S(1)}, bf16[528,768]{1,0:T(8,128)(2,1)S(1)}, u32[]{:S(2)}, u32[]{:S(2)}) collective-permute-start(bf16[528,768]{1,0:T(8,128)(2,1)S(1)} %get-tuple-element.115), channel_id=1, source_target_pairs={{0,16},{4,20},{8,24},{12,28},{16,0},{20,4},{24,8},{28,12},{1,17},{... | collective-permute-start | bytes 2433032 | tf_op jit(solution)/shard_map/ppermute | solution.py:1067
  12.2 19.9 %collective-permute-start = (bf16[512,768]{1,0:T(8,128)(2,1)S(1)}, bf16[512,768]{1,0:T(8,128)(2,1)S(1)}, u32[]{:S(2)}, u32[]{:S(2)}) collective-permute-start(bf16[512,768]{1,0:T(8,128)(2,1)S(1)} %get-tuple-element.147.refs_0_), channel_id=1, source_target_pairs={{0,8},{4,12},{8,0},{12,4},{16,24},{20,28},{24,16},{28,20},{1,9},{5... | collective-permute-start | bytes 2359304 | tf_op jit(solution)/shard_map/ppermute | solution.py:1067
  26.7 21.0 %collective-permute-start.6 = (bf16[512,768]{1,0:T(8,128)(2,1)S(1)}, bf16[512,768]{1,0:T(8,128)(2,1)S(1)}, u32[]{:S(2)}, u32[]{:S(2)}) collective-permute-start(bf16[512,768]{1,0:T(8,128)(2,1)S(1)} %get-tuple-element.147.refs_0_), channel_id=1, source_target_pairs={{0,24},{4,28},{8,16},{12,20},{16,8},{20,12},{24,0},{28,4},{1,25},{... | collective-permute-start | bytes 2359304 | tf_op jit(solution)/shard_map/ppermute | solution.py:1067
  27.3 12.0 %collective-permute-start.4 = (bf16[192,512]{1,0:T(8,128)(2,1)S(1)}, bf16[192,512]{1,0:T(8,128)(2,1)S(1)}, u32[]{:S(2)}, u32[]{:S(2)}) collective-permute-start(bf16[192,512]{1,0:T(8,128)(2,1)S(1)} %get-tuple-element.116.nt_ref.refs_0_), channel_id=1, source_target_pairs={{0,2},{1,3},{2,0},{3,1},{4,6},{5,7},{6,4},{7,5},{8,10},{9,11},{10,... | collective-permute-start | bytes 589832 | tf_op jit(solution)/shard_map/ppermute | solution.py:1055
  41.4 11.4 %collective-permute-start.5 = (bf16[192,512]{1,0:T(8,128)(2,1)S(1)}, bf16[192,512]{1,0:T(8,128)(2,1)S(1)}, u32[]{:S(2)}, u32[]{:S(2)}) collective-permute-start(bf16[192,512]{1,0:T(8,128)(2,1)S(1)} %get-tuple-element.123), channel_id=1, source_target_pairs={{0,2},{1,3},{2,0},{3,1},{4,6},{5,7},{6,4},{7,5},{8,10},{9,11},{10,... | collective-permute-start | bytes 589832 | tf_op jit(solution)/shard_map/ppermute | solution.py:1062
  41.5 21.8 %collective-permute-start.15 = (bf16[192,512]{1,0:T(8,128)(2,1)S(1)}, bf16[192,512]{1,0:T(8,128)(2,1)S(1)}, u32[]{:S(2)}, u32[]{:S(2)}) collective-permute-start(bf16[192,512]{1,0:T(8,128)(2,1)S(1)} %collective-permute-done.4.nt_ref.refs_1_), channel_id=1, source_target_pairs={{0,1},{1,0},{2,3},{3,2},{4,5},{5,4},{6,7},{7,6},{8,9},{9,8},{10,11... | collective-permute-start | bytes 589832 | tf_op jit(solution)/shard_map/ppermute | solution.py:1067
  44.6 18.7 %collective-permute-start.14 = (bf16[192,512]{1,0:T(8,128)(2,1)S(1)}, bf16[192,512]{1,0:T(8,128)(2,1)S(1)}, u32[]{:S(2)}, u32[]{:S(2)}) collective-permute-start(bf16[192,512]{1,0:T(8,128)(2,1)S(1)} %get-tuple-element.116.nt_ref.refs_0_), channel_id=1, source_target_pairs={{0,1},{1,0},{2,3},{3,2},{4,5},{5,4},{6,7},{7,6},{8,9},{9,8},{10,11... | collective-permute-start | bytes 589832 | tf_op jit(solution)/shard_map/ppermute | solution.py:1067
  53.1 13.1 %collective-permute-start.7 = (bf16[192,512]{1,0:T(8,128)(2,1)S(1)}, bf16[192,512]{1,0:T(8,128)(2,1)S(1)}, u32[]{:S(2)}, u32[]{:S(2)}) collective-permute-start(bf16[192,512]{1,0:T(8,128)(2,1)S(1)} %get-tuple-element.137.refs_0_), channel_id=1, source_target_pairs={{0,3},{1,0},{2,1},{3,2},{4,7},{5,4},{6,5},{7,6},{8,11},{9,8},{10,9... | collective-permute-start | bytes 589832 | tf_op jit(solution)/shard_map/ppermute | solution.py:1055
  55.1 16.1 %collective-permute-start.8 = (bf16[192,512]{1,0:T(8,128)(2,1)S(1)}, bf16[192,512]{1,0:T(8,128)(2,1)S(1)}, u32[]{:S(2)}, u32[]{:S(2)}) collective-permute-start(bf16[192,512]{1,0:T(8,128)(2,1)S(1)} %get-tuple-element.137.refs_0_), channel_id=1, source_target_pairs={{0,2},{1,3},{2,0},{3,1},{4,6},{5,7},{6,4},{7,5},{8,10},{9,11},{10,... | collective-permute-start | bytes 589832 | tf_op jit(solution)/shard_map/ppermute | solution.py:1055
  55.1 16.1 %collective-permute-start.9 = (bf16[192,512]{1,0:T(8,128)(2,1)S(1)}, bf16[192,512]{1,0:T(8,128)(2,1)S(1)}, u32[]{:S(2)}, u32[]{:S(2)}) collective-permute-start(bf16[192,512]{1,0:T(8,128)(2,1)S(1)} %get-tuple-element.137.refs_0_), channel_id=1, source_target_pairs={{0,1},{1,2},{2,3},{3,0},{4,5},{5,6},{6,7},{7,4},{8,9},{9,10},{10,1... | collective-permute-start | bytes 589832 | tf_op jit(solution)/shard_map/ppermute | solution.py:1055
  71.4 23.3 %collective-permute-start.17 = (bf16[768,512]{1,0:T(8,128)(2,1)S(1)}, bf16[768,512]{1,0:T(8,128)(2,1)S(1)}, u32[]{:S(2)}, u32[]{:S(2)}) collective-permute-start(bf16[768,512]{1,0:T(8,128)(2,1)S(1)} %pack_rows.1.refs_3_), channel_id=1, source_target_pairs={{0,8},{4,12},{8,0},{12,4},{16,24},{20,28},{24,16},{28,20},{1,9},{5... | collective-permute-start | bytes 2359304 | tf_op jit(solution)/shard_map/ppermute | solution.py:1067
  72.9 21.8 %collective-permute-start.18 = (bf16[768,512]{1,0:T(8,128)(2,1)S(1)}, bf16[768,512]{1,0:T(8,128)(2,1)S(1)}, u32[]{:S(2)}, u32[]{:S(2)}) collective-permute-start(bf16[768,512]{1,0:T(8,128)(2,1)S(1)} %pack_rows.1.refs_3_), channel_id=1, source_target_pairs={{0,16},{4,20},{8,24},{12,28},{16,0},{20,4},{24,8},{28,12},{1,17},{... | collective-permute-start | bytes 2359304 | tf_op jit(solution)/shard_map/ppermute | solution.py:1067
  74.4 20.0 %collective-permute-start.10 = (bf16[192,512]{1,0:T(8,128)(2,1)S(1)}, bf16[192,512]{1,0:T(8,128)(2,1)S(1)}, u32[]{:S(2)}, u32[]{:S(2)}) collective-permute-start(bf16[192,512]{1,0:T(8,128)(2,1)S(1)} %get-tuple-element.146), channel_id=1, source_target_pairs={{0,2},{1,3},{2,0},{3,1},{4,6},{5,7},{6,4},{7,5},{8,10},{9,11},{10,... | collective-permute-start | bytes 589832 | tf_op jit(solution)/shard_map/ppermute | solution.py:1062
  77.9 16.6 %collective-permute-start.16 = (bf16[768,512]{1,0:T(8,128)(2,1)S(1)}, bf16[768,512]{1,0:T(8,128)(2,1)S(1)}, u32[]{:S(2)}, u32[]{:S(2)}) collective-permute-start(bf16[768,512]{1,0:T(8,128)(2,1)S(1)} %get-tuple-element.167), channel_id=1, source_target_pairs={{0,4},{4,0},{8,12},{12,8},{16,20},{20,16},{24,28},{28,24},{1,5},{5... | collective-permute-start | bytes 2359304 | tf_op jit(solution)/shard_map/ppermute | solution.py:1067
  94.8 20.8 %collective-permute-start.19 = (bf16[800,512]{1,0:T(8,128)(2,1)S(1)}, bf16[800,512]{1,0:T(8,128)(2,1)S(1)}, u32[]{:S(2)}, u32[]{:S(2)}) collective-permute-start(bf16[800,512]{1,0:T(8,128)(2,1)S(1)} %get-tuple-element.174), channel_id=1, source_target_pairs={{0,16},{4,20},{8,24},{12,28},{16,0},{20,4},{24,8},{28,12},{1,17},{... | collective-permute-start | bytes 2457608 | tf_op jit(solution)/shard_map/ppermute | solution.py:1067
  95.4 20.4 %collective-permute-start.20 = (bf16[800,512]{1,0:T(8,128)(2,1)S(1)}, bf16[800,512]{1,0:T(8,128)(2,1)S(1)}, u32[]{:S(2)}, u32[]{:S(2)}) collective-permute-start(bf16[800,512]{1,0:T(8,128)(2,1)S(1)} %get-tuple-element.175), channel_id=1, source_target_pairs={{0,8},{4,12},{8,0},{12,4},{16,24},{20,28},{24,16},{28,20},{1,9},{5... | collective-permute-start | bytes 2457608 | tf_op jit(solution)/shard_map/ppermute | solution.py:1067
  96.0 34.0 %collective-permute-start.11 = (bf16[384,512]{1,0:T(8,128)(2,1)S(1)}, bf16[384,512]{1,0:T(8,128)(2,1)S(1)}, u32[]{:S(2)}, u32[]{:S(2)}) collective-permute-start(bf16[384,512]{1,0:T(8,128)(2,1)S(1)} %rows_message.1.refs_0_), channel_id=1, source_target_pairs={{0,3},{1,0},{2,1},{3,2},{4,7},{5,4},{6,5},{7,6},{8,11},{9,8},{10,9... | collective-permute-start | bytes 1179656 | tf_op jit(solution)/shard_map/ppermute | solution.py:1055
  96.5 34.0 %collective-permute-start.12 = (bf16[384,512]{1,0:T(8,128)(2,1)S(1)}, bf16[384,512]{1,0:T(8,128)(2,1)S(1)}, u32[]{:S(2)}, u32[]{:S(2)}) collective-permute-start(bf16[384,512]{1,0:T(8,128)(2,1)S(1)} %rows_message.1.refs_0_), channel_id=1, source_target_pairs={{0,2},{1,3},{2,0},{3,1},{4,6},{5,7},{6,4},{7,5},{8,10},{9,11},{10,... | collective-permute-start | bytes 1179656 | tf_op jit(solution)/shard_map/ppermute | solution.py:1055
  97.0 33.5 %collective-permute-start.13 = (bf16[384,512]{1,0:T(8,128)(2,1)S(1)}, bf16[384,512]{1,0:T(8,128)(2,1)S(1)}, u32[]{:S(2)}, u32[]{:S(2)}) collective-permute-start(bf16[384,512]{1,0:T(8,128)(2,1)S(1)} %rows_message.1.refs_0_), channel_id=1, source_target_pairs={{0,1},{1,2},{2,3},{3,0},{4,5},{5,6},{6,7},{7,4},{8,9},{9,10},{10,1... | collective-permute-start | bytes 1179656 | tf_op jit(solution)/shard_map/ppermute | solution.py:1055
  116.0 15.7 %collective-permute-start.22 = (bf16[416,512]{1,0:T(8,128)(2,1)S(1)}, bf16[416,512]{1,0:T(8,128)(2,1)S(1)}, u32[]{:S(2)}, u32[]{:S(2)}) collective-permute-start(bf16[416,512]{1,0:T(8,128)(2,1)S(1)} %get-tuple-element.190.lower_ref), channel_id=1, source_target_pairs={{0,8},{4,12},{8,0},{12,4},{16,24},{20,28},{24,16},{28,20},{1,9},{5... | collective-permute-start | bytes 1277960 | tf_op jit(solution)/shard_map/ppermute | solution.py:1067
  116.6 15.0 %collective-permute-start.21 = (bf16[384,512]{1,0:T(8,128)(2,1)S(1)}, bf16[384,512]{1,0:T(8,128)(2,1)S(1)}, u32[]{:S(2)}, u32[]{:S(2)}) collective-permute-start(bf16[384,512]{1,0:T(8,128)(2,1)S(1)} %get-tuple-element.176.upper_ref), channel_id=1, source_target_pairs={{0,16},{4,20},{8,24},{12,28},{16,0},{20,4},{24,8},{28,12},{1,17},{... | collective-permute-start | bytes 1179656 | tf_op jit(solution)/shard_map/ppermute | solution.py:1067
  134.2 9.0 %collective-permute-start.25 = (f32[16,512]{1,0:T(8,128)S(1)}, f32[16,512]{1,0:T(8,128)S(1)}, u32[]{:S(2)}, u32[]{:S(2)}) collective-permute-start(f32[16,512]{1,0:T(8,128)S(1)} %ordered_sum.2.refs_0_), channel_id=1, source_target_pairs={{0,3},{1,0},{2,1},{3,2},{4,7},{5,4},{6,5},{7,6},{8,11},{9,8},{10,9... | collective-permute-start | bytes 98312 | tf_op jit(solution)/shard_map/ppermute | solution.py:1055
  134.2 9.0 %collective-permute-start.26 = (f32[16,512]{1,0:T(8,128)S(1)}, f32[16,512]{1,0:T(8,128)S(1)}, u32[]{:S(2)}, u32[]{:S(2)}) collective-permute-start(f32[16,512]{1,0:T(8,128)S(1)} %ordered_sum.2.refs_0_), channel_id=1, source_target_pairs={{0,2},{1,3},{2,0},{3,1},{4,6},{5,7},{6,4},{7,5},{8,10},{9,11},{10,... | collective-permute-start | bytes 98312 | tf_op jit(solution)/shard_map/ppermute | solution.py:1055
  (11 other events, 67.1 us)

commit v7 on v6

--- a/solution.py
+++ b/solution.py
@@ -853,6 +853,33 @@
         compiler_params=params(),
         cost_estimate=cost(n * pieces[0].size, 4 * n * pieces[0].size),
         name="ordered_sum",
+    )(*pieces)
+
+
+def gains_sum_kernel(n, *refs):
+    pieces, (first_ref, second_ref, scr) = refs[:n], refs[n:]
+    me = lax.axis_index("mp")
+    for r in range(n):
+        scr[lax.rem(me + r, n)] = pieces[r][...]
+    total = scr[0]
+    for r in range(1, n):
+        total = total + scr[r]
+    first_ref[...] = total[0]
+    second_ref[...] = total[8]
+
+
+def gains_sum(pieces):
+    n = len(pieces)
+    shape = pieces[0].shape
+    return pl.pallas_call(
+        functools.partial(gains_sum_kernel, n),
+        in_specs=[whole()] * n,
+        out_specs=[whole()] * 2,
+        out_shape=[jax.ShapeDtypeStruct(shape[1:], F32)] * 2,
+        scratch_shapes=[pltpu.VMEM((n,) + shape, F32)],
+        compiler_params=params(),
+        cost_estimate=cost(n * pieces[0].size, 4 * n * pieces[0].size),
+        name="gains_sum",
     )(*pieces)
 
 
@@ -1182,13 +1209,13 @@
     gains = fetch_shifted(gains, "mp", n)
     recv = swap(send, "dp", n_dp, 1)
     stu_grad, ar_grad, *w_grads = finish(keep, send, recv, order, custom)
-    gains = ordered_sum(after(gains, stu_grad), "mp", 0)
+    first_grad, second_grad = gains_sum(after(gains, stu_grad))
     if custom:
         gate_grad, up_grad, down_grad = w_grads
     else:
         gate_grad, up_grad, down_grad = (g.astype(F32) for g in lax.psum(tuple(grads), "dp"))
     return (
-        output, input_grad, stu_grad, ar_grad, gains[0], gains[8], gate_grad, up_grad, down_grad,
+        output, input_grad, stu_grad, ar_grad, first_grad, second_grad, gate_grad, up_grad, down_grad,
     )
 
 

time: 144 us -> 144 us (level)
  no operation moved by 1% of the time
where the time goes in v7:
time: 144 us
  Pallas kernels  73.3 us (51%)
  starting transfers between devices  33.8 us (23%)
  waiting for transfers between devices  32.5 us (23%)
  local copies, waits for them, and re-layouts  1.92 us (1%)
  between operations  1.65 us (1%)
    ppermute x16, waiting for transfers between devices, swap(): return lax.ppermute(value, axis, [(i, i ^ bits) for i in range(n)])  17.1 us
    ppermute x16, starting transfers between devices, swap(): return lax.ppermute(value, axis, [(i, i ^ bits) for i in range(n)])  16.9 us
    pallas_call x1, Pallas kernels, spectral_unmix(): pl.pallas_call(functools.partial(unmix_kernel, kb, n), grid=(count // kb,...  16.5 us
    ppermute x10, starting transfers between devices, fetch_shifted(): pieces[r] = lax.ppermute(value, axis, [(i, (i - r) % n) for i in range(n)])  13.3 us
    pallas_call x1, Pallas kernels, spectral_mix(): pl.pallas_call(functools.partial(mix_kernel, kb, n), grid=(filt // kb,),...  12.8 us
    pallas_call x1, Pallas kernels, matrix_grads(): pl.pallas_call(functools.partial(grads_kernel, steps, order, groups, rows...  11.9 us
    ppermute x10, waiting for transfers between devices, fetch_shifted(): pieces[r] = lax.ppermute(value, axis, [(i, (i - r) % n) for i in range(n)])  10.4 us
    pallas_call x2, Pallas kernels, convolutions(): pl.pallas_call(functools.partial(conv_kernel, groups, tile, own, first),...  9.97 us
  transfers between devices with their start and end apart: 28, of which 9 were waited for; matrix products, arithmetic and copies ran while one was open for 0% of the time, Pallas kernels for 49%

profile of v7, /device:TPU:0, one launch (start us, length us, event | category | flops | bytes accessed | tf_op | source)
XLA Modules:
  0.0 143.9 jit_solution(14978611958286493869)
XLA Ops:
  0.6 2.0 %half_weights.1 = bf16[3,256,512]{2,1,0:T(8,128)(2,1)} custom-call(bf16[512,512]{1,0:T(8,128)(2,1)} %gw_ref.3, bf16[512,512]{1,0:T(8,128)(2,1)} %uw_ref.3, bf16[512,512]{1,0:T(8,128)(2,1)} %dw_ref.3), custom_call_target="tpu_custom_call" | custom-call | bytes 1572864 | tf_op jit(solution)/shard_map/half_weights/pallas_call | solution.py:316
  2.7 3.1 %collective-permute-start.2 = (bf16[3,256,512]{2,1,0:T(8,128)(2,1)}, bf16[3,256,512]{2,1,0:T(8,128)(2,1)S(1)}, u32[]{:S(2)}, u32[]{:S(2)}) collective-permute-start(bf16[3,256,512]{2,1,0:T(8,128)(2,1)} %half_weights.1), channel_id=1, source_target_pairs={{0,1},{1,0},{2,3},{3,2},{4,5},{5,4},{6,7},{7,6},{8,9},{9,8},{10,11... | collective-permute-start | bytes 2359304 | tf_op jit(solution)/shard_map/ppermute | solution.py:1094
  13.7 12.8 %spectral_mix.1 = (f32[192,512]{1,0:T(8,128)S(1)}, bf16[192,512]{1,0:T(8,128)(2,1)S(1)}) custom-call(s32[1]{0:T(128)S(6)} %copy.20.len_ref, f32[4,24,384]{2,1,0:T(8,128)S(1)} %get-tuple-element.110.taps_ref, f32[192,512]{1,0:T(8,128)S(1)} %get-tuple-element.111.x_ref, bf16[2,384,512]{2,1,0:T(8,128)(2,1)S(1)} %get-tuple-element.112.u_ref, ...), custom_call_target="tpu_custom_call" | custom-call | tf_op jit(solution)/shard_map/spectral_mix/pallas_call | solution.py:261
  27.3 2.6 %collective-permute-start.4 = (bf16[192,512]{1,0:T(8,128)(2,1)S(1)}, bf16[192,512]{1,0:T(8,128)(2,1)S(1)}, u32[]{:S(2)}, u32[]{:S(2)}) collective-permute-start(bf16[192,512]{1,0:T(8,128)(2,1)S(1)} %get-tuple-element.118.nt_ref.refs_0_), channel_id=1, source_target_pairs={{0,2},{1,3},{2,0},{3,1},{4,6},{5,7},{6,4},{7,5},{8,10},{9,11},{10,... | collective-permute-start | bytes 589832 | tf_op jit(solution)/shard_map/ppermute | solution.py:1082
  30.1 2.0 %collective-permute-done.refs_1_ = bf16[512,768]{1,0:T(8,128)(2,1)S(1)} collective-permute-done((bf16[512,768]{1,0:T(8,128)(2,1)S(1)}, bf16[512,768]{1,0:T(8,128)(2,1)S(1)}, u32[]{:S(2)}, u32[]{:S(2)}) %collective-permute-start) | collective-permute-done | bytes 786464 | tf_op jit(solution)/shard_map/ppermute | solution.py:1094
  32.3 2.1 %feed_forward.2 = (bf16[192,512]{1,0:T(8,128)(2,1)S(1)}, bf16[192,512]{1,0:T(8,128)(2,1)S(1)}, bf16[192,512]{1,0:T(8,128)(2,1)S(1)}, bf16[192,512]{1,0:T(8,128)(2,1)S(1)}, bf16[192,512]{1,0:T(8,128)(2,1)S(1)}) custom-call(bf16[192,512]{1,0:T(8,128)(2,1)S(1)} %get-tuple-element.118.nt_ref.refs_0_, bf16[768,512]{1,0:T(8,128)(2,1)S(1)} %dealt_rows.1.cot_ref, ...), custom_call_target="tpu_custom_call" | custom-call | flops 1207959552 | bytes 4325376 | tf_op jit(solution)/shard_map/feed_forward/pallas_call | solution.py:388
  34.4 4.9 %collective-permute-done.4.nt_ref.refs_1_ = bf16[192,512]{1,0:T(8,128)(2,1)S(1)} collective-permute-done((bf16[192,512]{1,0:T(8,128)(2,1)S(1)}, bf16[192,512]{1,0:T(8,128)(2,1)S(1)}, u32[]{:S(2)}, u32[]{:S(2)}) %collective-permute-start.4) | collective-permute-done | bytes 196640 | tf_op jit(solution)/shard_map/ppermute | solution.py:1082
  39.3 2.1 %feed_forward.3 = (bf16[192,512]{1,0:T(8,128)(2,1)S(1)}, bf16[192,512]{1,0:T(8,128)(2,1)S(1)}, bf16[192,512]{1,0:T(8,128)(2,1)S(1)}, bf16[192,512]{1,0:T(8,128)(2,1)S(1)}, bf16[192,512]{1,0:T(8,128)(2,1)S(1)}) custom-call(bf16[192,512]{1,0:T(8,128)(2,1)S(1)} %collective-permute-done.4.nt_ref.refs_1_, bf16[768,512]{1,0:T(8,128)(2,1)S(1)} %dealt_rows.1.cot_ref, ...), custom_call_target="tpu_custom_call" | custom-call | flops 1207959552 | bytes 4325376 | tf_op jit(solution)/shard_map/feed_forward/pallas_call | solution.py:388
  41.5 3.1 %collective-permute-start.15 = (bf16[192,512]{1,0:T(8,128)(2,1)S(1)}, bf16[192,512]{1,0:T(8,128)(2,1)S(1)}, u32[]{:S(2)}, u32[]{:S(2)}) collective-permute-start(bf16[192,512]{1,0:T(8,128)(2,1)S(1)} %collective-permute-done.4.nt_ref.refs_1_), channel_id=1, source_target_pairs={{0,1},{1,0},{2,3},{3,2},{4,5},{5,4},{6,7},{7,6},{8,9},{9,8},{10,11... | collective-permute-start | bytes 589832 | tf_op jit(solution)/shard_map/ppermute | solution.py:1094
  44.7 3.1 %collective-permute-done.6.refs_3_ = bf16[512,768]{1,0:T(8,128)(2,1)S(1)} collective-permute-done((bf16[512,768]{1,0:T(8,128)(2,1)S(1)}, bf16[512,768]{1,0:T(8,128)(2,1)S(1)}, u32[]{:S(2)}, u32[]{:S(2)}) %collective-permute-start.6) | collective-permute-done | bytes 786464 | tf_op jit(solution)/shard_map/ppermute | solution.py:1094
  47.8 5.1 %collective-permute-done.5.refs_1_ = bf16[192,512]{1,0:T(8,128)(2,1)S(1)} collective-permute-done((bf16[192,512]{1,0:T(8,128)(2,1)S(1)}, bf16[192,512]{1,0:T(8,128)(2,1)S(1)}, u32[]{:S(2)}, u32[]{:S(2)}) %collective-permute-start.5) | collective-permute-done | bytes 196640 | tf_op jit(solution)/shard_map/ppermute | solution.py:1089
  53.1 1.9 %collective-permute-start.7 = (bf16[192,512]{1,0:T(8,128)(2,1)S(1)}, bf16[192,512]{1,0:T(8,128)(2,1)S(1)}, u32[]{:S(2)}, u32[]{:S(2)}) collective-permute-start(bf16[192,512]{1,0:T(8,128)(2,1)S(1)} %get-tuple-element.139.refs_0_), channel_id=1, source_target_pairs={{0,3},{1,0},{2,1},{3,2},{4,7},{5,4},{6,5},{7,6},{8,11},{9,8},{10,9... | collective-permute-start | bytes 589832 | tf_op jit(solution)/shard_map/ppermute | solution.py:1082
  55.7 2.6 %lagged.1 = (bf16[512,3072]{1,0:T(8,128)(2,1)S(1)}, bf16[512,3072]{1,0:T(8,128)(2,1)S(1)}, bf16[512,3072]{1,0:T(8,128)(2,1)S(1)}) custom-call(bf16[512,768]{1,0:T(8,128)(2,1)S(1)} %get-tuple-element.149.refs_0_, bf16[512,768]{1,0:T(8,128)(2,1)S(1)} %collective-permute-done.refs_1_, bf16[528,768]{1,0:T(8,128)(2,1)S(1)} %collective-permute-done.1.refs_2_, ...), custom_call_target="tpu_custom_call" | custom-call | tf_op jit(solution)/shard_map/lagged/pallas_call | solution.py:702
  58.3 5.0 %convolutions.2.conv_ref = bf16[6,128,3072]{2,1,0:T(8,128)(2,1)S(1)} custom-call(f32[24,768]{1,0:T(8,128)S(1)} %get-tuple-element.138.filt_ref, bf16[512,768]{1,0:T(8,128)(2,1)S(1)} %get-tuple-element.149.refs_0_, bf16[512,768]{1,0:T(8,128)(2,1)S(1)} %collective-permute-done.refs_1_, bf16[528,768]{1,0:T(8,128)(2,1)S(1)} %collective-permute-done.1.refs_2_, ...), custom_call_target="tpu_custom_call" | custom-call | tf_op jit(solution)/shard_map/convolutions/pallas_call | solution.py:668
  66.2 4.9 %collective-permute-done.8.refs_2_ = bf16[192,512]{1,0:T(8,128)(2,1)S(1)} collective-permute-done((bf16[192,512]{1,0:T(8,128)(2,1)S(1)}, bf16[192,512]{1,0:T(8,128)(2,1)S(1)}, u32[]{:S(2)}, u32[]{:S(2)}) %collective-permute-start.8) | collective-permute-done | bytes 196640 | tf_op jit(solution)/shard_map/ppermute | solution.py:1082
  74.4 3.5 %collective-permute-start.10 = (bf16[192,512]{1,0:T(8,128)(2,1)S(1)}, bf16[192,512]{1,0:T(8,128)(2,1)S(1)}, u32[]{:S(2)}, u32[]{:S(2)}) collective-permute-start(bf16[192,512]{1,0:T(8,128)(2,1)S(1)} %get-tuple-element.148), channel_id=1, source_target_pairs={{0,2},{1,3},{2,0},{3,1},{4,6},{5,7},{6,4},{7,5},{8,10},{9,11},{10,... | collective-permute-start | bytes 589832 | tf_op jit(solution)/shard_map/ppermute | solution.py:1089
  77.9 16.5 %spectral_unmix.1 = (bf16[192,512]{1,0:T(8,128)(2,1)S(1)}, f32[16,512]{1,0:T(8,128)S(1)}) custom-call(s32[1]{0:T(128)S(6)} %copy.20.len_ref, f32[4,24,384]{2,1,0:T(8,128)S(1)} %get-tuple-element.110.taps_ref, f32[192,512]{1,0:T(8,128)S(1)} %get-tuple-element.111.x_ref, f32[192,512]{1,0:T(8,128)S(1)} %get-tuple-element.128.bh_ref, ...), custom_call_target="tpu_custom_call" | custom-call | flops 8455716864 | bytes 25165824 | tf_op jit(solution)/shard_map/spectral_unmix/pallas_call | solution.py:609
  97.0 2.0 %collective-permute-start.13 = (bf16[384,512]{1,0:T(8,128)(2,1)S(1)}, bf16[384,512]{1,0:T(8,128)(2,1)S(1)}, u32[]{:S(2)}, u32[]{:S(2)}) collective-permute-start(bf16[384,512]{1,0:T(8,128)(2,1)S(1)} %rows_message.1.refs_0_), channel_id=1, source_target_pairs={{0,1},{1,2},{2,3},{3,0},{4,5},{5,6},{6,7},{7,4},{8,9},{9,10},{10,1... | collective-permute-start | bytes 1179656 | tf_op jit(solution)/shard_map/ppermute | solution.py:1082
  99.0 5.0 %convolutions.3.conv_two_ref = bf16[6,128,3072]{2,1,0:T(8,128)(2,1)S(1)} custom-call(f32[24,768]{1,0:T(8,128)S(1)} %get-tuple-element.138.filt_ref, bf16[512,768]{1,0:T(8,128)(2,1)S(1)} %get-tuple-element.149.refs_0_, bf16[512,768]{1,0:T(8,128)(2,1)S(1)} %collective-permute-done.refs_1_, bf16[528,768]{1,0:T(8,128)(2,1)S(1)} %collective-permute-done.1.refs_2_, ...), custom_call_target="tpu_custom_call" | custom-call | tf_op jit(solution)/shard_map/convolutions/pallas_call | solution.py:668
  104.0 11.6 %collective-permute-done.19.from_y.refs_6_ = bf16[800,512]{1,0:T(8,128)(2,1)S(1)} collective-permute-done((bf16[800,512]{1,0:T(8,128)(2,1)S(1)}, bf16[800,512]{1,0:T(8,128)(2,1)S(1)}, u32[]{:S(2)}, u32[]{:S(2)}) %collective-permute-start.19) | collective-permute-done | bytes 819232 | tf_op jit(solution)/shard_map/ppermute | solution.py:1094
  118.1 11.9 %matrix_grads.1 = (f32[12,64,512]{2,1,0:T(8,128)S(1)}, bf16[2304,512]{1,0:T(8,128)(2,1)S(1)}) custom-call(bf16[6,128,3072]{2,1,0:T(8,128)(2,1)S(1)} %convolutions.2.conv_ref, bf16[6,128,3072]{2,1,0:T(8,128)(2,1)S(1)} %convolutions.3.conv_two_ref, bf16[512,3072]{1,0:T(8,128)(2,1)S(1)} %get-tuple-element.135.refs_0_, ...), custom_call_target="tpu_custom_call" | custom-call | tf_op jit(solution)/shard_map/matrix_grads/pallas_call | solution.py:761
  134.2 3.1 %collective-permute-start.26 = (f32[16,512]{1,0:T(8,128)S(1)}, f32[16,512]{1,0:T(8,128)S(1)}, u32[]{:S(2)}, u32[]{:S(2)}) collective-permute-start(f32[16,512]{1,0:T(8,128)S(1)} %ordered_sum.1.refs_0_), channel_id=1, source_target_pairs={{0,2},{1,3},{2,0},{3,1},{4,6},{5,7},{6,4},{7,5},{8,10},{9,11},{10,... | collective-permute-start | bytes 98312 | tf_op jit(solution)/shard_map/ppermute | solution.py:1082
  137.4 2.0 %collective-permute-start.27 = (f32[16,512]{1,0:T(8,128)S(1)}, f32[16,512]{1,0:T(8,128)S(1)}, u32[]{:S(2)}, u32[]{:S(2)}) collective-permute-start(f32[16,512]{1,0:T(8,128)S(1)} %ordered_sum.1.refs_0_), channel_id=1, source_target_pairs={{0,1},{1,2},{2,3},{3,0},{4,5},{5,6},{6,7},{7,4},{8,9},{9,10},{10,1... | collective-permute-start | bytes 98312 | tf_op jit(solution)/shard_map/ppermute | solution.py:1082
  139.5 3.7 %finish.1 = (f32[12,64,512]{2,1,0:T(8,128)}, f32[3,512,512]{2,1,0:T(8,128)}, f32[512,512]{1,0:T(8,128)}, f32[512,512]{1,0:T(8,128)}, f32[512,512]{1,0:T(8,128)}) custom-call(f32[12,64,512]{2,1,0:T(8,128)S(1)} %get-tuple-element.191.keep_ref, bf16[3072,512]{1,0:T(8,128)(2,1)S(1)} %whole_chunks.1.send_ref, bf16[3072,512]{1,0:T(8,128)(2,1)S(1)} %collective-permute-done.24.recv_ref), custom_call_target="tpu_custom_call" | custom-call | flops 393216 | bytes 3932160 | tf_op jit(solution)/shard_map/finish/pallas_call | solution.py:1064
  (75 shorter events, 25.5 us)
Async XLA Ops:
  2.7 23.9 %collective-permute-start.2 = (bf16[3,256,512]{2,1,0:T(8,128)(2,1)}, bf16[3,256,512]{2,1,0:T(8,128)(2,1)S(1)}, u32[]{:S(2)}, u32[]{:S(2)}) collective-permute-start(bf16[3,256,512]{2,1,0:T(8,128)(2,1)} %half_weights.1), channel_id=1, source_target_pairs={{0,1},{1,0},{2,3},{3,2},{4,5},{5,4},{6,7},{7,6},{8,9},{9,8},{10,11... | collective-permute-start | bytes 2359304 | tf_op jit(solution)/shard_map/ppermute | solution.py:1094
  10.7 21.4 %collective-permute-start.1 = (bf16[528,768]{1,0:T(8,128)(2,1)S(1)}, bf16[528,768]{1,0:T(8,128)(2,1)S(1)}, u32[]{:S(2)}, u32[]{:S(2)}) collective-permute-start(bf16[528,768]{1,0:T(8,128)(2,1)S(1)} %get-tuple-element.117), channel_id=1, source_target_pairs={{0,16},{4,20},{8,24},{12,28},{16,0},{20,4},{24,8},{28,12},{1,17},{... | collective-permute-start | bytes 2433032 | tf_op jit(solution)/shard_map/ppermute | solution.py:1094
  12.2 19.9 %collective-permute-start = (bf16[512,768]{1,0:T(8,128)(2,1)S(1)}, bf16[512,768]{1,0:T(8,128)(2,1)S(1)}, u32[]{:S(2)}, u32[]{:S(2)}) collective-permute-start(bf16[512,768]{1,0:T(8,128)(2,1)S(1)} %get-tuple-element.149.refs_0_), channel_id=1, source_target_pairs={{0,8},{4,12},{8,0},{12,4},{16,24},{20,28},{24,16},{28,20},{1,9},{5... | collective-permute-start | bytes 2359304 | tf_op jit(solution)/shard_map/ppermute | solution.py:1094
  26.7 21.0 %collective-permute-start.6 = (bf16[512,768]{1,0:T(8,128)(2,1)S(1)}, bf16[512,768]{1,0:T(8,128)(2,1)S(1)}, u32[]{:S(2)}, u32[]{:S(2)}) collective-permute-start(bf16[512,768]{1,0:T(8,128)(2,1)S(1)} %get-tuple-element.149.refs_0_), channel_id=1, source_target_pairs={{0,24},{4,28},{8,16},{12,20},{16,8},{20,12},{24,0},{28,4},{1,25},{... | collective-permute-start | bytes 2359304 | tf_op jit(solution)/shard_map/ppermute | solution.py:1094
  27.3 12.0 %collective-permute-start.4 = (bf16[192,512]{1,0:T(8,128)(2,1)S(1)}, bf16[192,512]{1,0:T(8,128)(2,1)S(1)}, u32[]{:S(2)}, u32[]{:S(2)}) collective-permute-start(bf16[192,512]{1,0:T(8,128)(2,1)S(1)} %get-tuple-element.118.nt_ref.refs_0_), channel_id=1, source_target_pairs={{0,2},{1,3},{2,0},{3,1},{4,6},{5,7},{6,4},{7,5},{8,10},{9,11},{10,... | collective-permute-start | bytes 589832 | tf_op jit(solution)/shard_map/ppermute | solution.py:1082
  41.4 11.4 %collective-permute-start.5 = (bf16[192,512]{1,0:T(8,128)(2,1)S(1)}, bf16[192,512]{1,0:T(8,128)(2,1)S(1)}, u32[]{:S(2)}, u32[]{:S(2)}) collective-permute-start(bf16[192,512]{1,0:T(8,128)(2,1)S(1)} %get-tuple-element.125), channel_id=1, source_target_pairs={{0,2},{1,3},{2,0},{3,1},{4,6},{5,7},{6,4},{7,5},{8,10},{9,11},{10,... | collective-permute-start | bytes 589832 | tf_op jit(solution)/shard_map/ppermute | solution.py:1089
  41.5 21.8 %collective-permute-start.15 = (bf16[192,512]{1,0:T(8,128)(2,1)S(1)}, bf16[192,512]{1,0:T(8,128)(2,1)S(1)}, u32[]{:S(2)}, u32[]{:S(2)}) collective-permute-start(bf16[192,512]{1,0:T(8,128)(2,1)S(1)} %collective-permute-done.4.nt_ref.refs_1_), channel_id=1, source_target_pairs={{0,1},{1,0},{2,3},{3,2},{4,5},{5,4},{6,7},{7,6},{8,9},{9,8},{10,11... | collective-permute-start | bytes 589832 | tf_op jit(solution)/shard_map/ppermute | solution.py:1094
  44.6 18.7 %collective-permute-start.14 = (bf16[192,512]{1,0:T(8,128)(2,1)S(1)}, bf16[192,512]{1,0:T(8,128)(2,1)S(1)}, u32[]{:S(2)}, u32[]{:S(2)}) collective-permute-start(bf16[192,512]{1,0:T(8,128)(2,1)S(1)} %get-tuple-element.118.nt_ref.refs_0_), channel_id=1, source_target_pairs={{0,1},{1,0},{2,3},{3,2},{4,5},{5,4},{6,7},{7,6},{8,9},{9,8},{10,11... | collective-permute-start | bytes 589832 | tf_op jit(solution)/shard_map/ppermute | solution.py:1094
  53.1 13.1 %collective-permute-start.7 = (bf16[192,512]{1,0:T(8,128)(2,1)S(1)}, bf16[192,512]{1,0:T(8,128)(2,1)S(1)}, u32[]{:S(2)}, u32[]{:S(2)}) collective-permute-start(bf16[192,512]{1,0:T(8,128)(2,1)S(1)} %get-tuple-element.139.refs_0_), channel_id=1, source_target_pairs={{0,3},{1,0},{2,1},{3,2},{4,7},{5,4},{6,5},{7,6},{8,11},{9,8},{10,9... | collective-permute-start | bytes 589832 | tf_op jit(solution)/shard_map/ppermute | solution.py:1082
  55.1 16.1 %collective-permute-start.8 = (bf16[192,512]{1,0:T(8,128)(2,1)S(1)}, bf16[192,512]{1,0:T(8,128)(2,1)S(1)}, u32[]{:S(2)}, u32[]{:S(2)}) collective-permute-start(bf16[192,512]{1,0:T(8,128)(2,1)S(1)} %get-tuple-element.139.refs_0_), channel_id=1, source_target_pairs={{0,2},{1,3},{2,0},{3,1},{4,6},{5,7},{6,4},{7,5},{8,10},{9,11},{10,... | collective-permute-start | bytes 589832 | tf_op jit(solution)/shard_map/ppermute | solution.py:1082
  55.1 16.1 %collective-permute-start.9 = (bf16[192,512]{1,0:T(8,128)(2,1)S(1)}, bf16[192,512]{1,0:T(8,128)(2,1)S(1)}, u32[]{:S(2)}, u32[]{:S(2)}) collective-permute-start(bf16[192,512]{1,0:T(8,128)(2,1)S(1)} %get-tuple-element.139.refs_0_), channel_id=1, source_target_pairs={{0,1},{1,2},{2,3},{3,0},{4,5},{5,6},{6,7},{7,4},{8,9},{9,10},{10,1... | collective-permute-start | bytes 589832 | tf_op jit(solution)/shard_map/ppermute | solution.py:1082
  71.4 23.3 %collective-permute-start.17 = (bf16[768,512]{1,0:T(8,128)(2,1)S(1)}, bf16[768,512]{1,0:T(8,128)(2,1)S(1)}, u32[]{:S(2)}, u32[]{:S(2)}) collective-permute-start(bf16[768,512]{1,0:T(8,128)(2,1)S(1)} %pack_rows.1.refs_3_), channel_id=1, source_target_pairs={{0,8},{4,12},{8,0},{12,4},{16,24},{20,28},{24,16},{28,20},{1,9},{5... | collective-permute-start | bytes 2359304 | tf_op jit(solution)/shard_map/ppermute | solution.py:1094
  72.9 21.8 %collective-permute-start.18 = (bf16[768,512]{1,0:T(8,128)(2,1)S(1)}, bf16[768,512]{1,0:T(8,128)(2,1)S(1)}, u32[]{:S(2)}, u32[]{:S(2)}) collective-permute-start(bf16[768,512]{1,0:T(8,128)(2,1)S(1)} %pack_rows.1.refs_3_), channel_id=1, source_target_pairs={{0,16},{4,20},{8,24},{12,28},{16,0},{20,4},{24,8},{28,12},{1,17},{... | collective-permute-start | bytes 2359304 | tf_op jit(solution)/shard_map/ppermute | solution.py:1094
  74.4 20.0 %collective-permute-start.10 = (bf16[192,512]{1,0:T(8,128)(2,1)S(1)}, bf16[192,512]{1,0:T(8,128)(2,1)S(1)}, u32[]{:S(2)}, u32[]{:S(2)}) collective-permute-start(bf16[192,512]{1,0:T(8,128)(2,1)S(1)} %get-tuple-element.148), channel_id=1, source_target_pairs={{0,2},{1,3},{2,0},{3,1},{4,6},{5,7},{6,4},{7,5},{8,10},{9,11},{10,... | collective-permute-start | bytes 589832 | tf_op jit(solution)/shard_map/ppermute | solution.py:1089
  77.9 16.6 %collective-permute-start.16 = (bf16[768,512]{1,0:T(8,128)(2,1)S(1)}, bf16[768,512]{1,0:T(8,128)(2,1)S(1)}, u32[]{:S(2)}, u32[]{:S(2)}) collective-permute-start(bf16[768,512]{1,0:T(8,128)(2,1)S(1)} %get-tuple-element.169), channel_id=1, source_target_pairs={{0,4},{4,0},{8,12},{12,8},{16,20},{20,16},{24,28},{28,24},{1,5},{5... | collective-permute-start | bytes 2359304 | tf_op jit(solution)/shard_map/ppermute | solution.py:1094
  94.8 20.8 %collective-permute-start.19 = (bf16[800,512]{1,0:T(8,128)(2,1)S(1)}, bf16[800,512]{1,0:T(8,128)(2,1)S(1)}, u32[]{:S(2)}, u32[]{:S(2)}) collective-permute-start(bf16[800,512]{1,0:T(8,128)(2,1)S(1)} %get-tuple-element.176), channel_id=1, source_target_pairs={{0,16},{4,20},{8,24},{12,28},{16,0},{20,4},{24,8},{28,12},{1,17},{... | collective-permute-start | bytes 2457608 | tf_op jit(solution)/shard_map/ppermute | solution.py:1094
  95.4 20.4 %collective-permute-start.20 = (bf16[800,512]{1,0:T(8,128)(2,1)S(1)}, bf16[800,512]{1,0:T(8,128)(2,1)S(1)}, u32[]{:S(2)}, u32[]{:S(2)}) collective-permute-start(bf16[800,512]{1,0:T(8,128)(2,1)S(1)} %get-tuple-element.177), channel_id=1, source_target_pairs={{0,8},{4,12},{8,0},{12,4},{16,24},{20,28},{24,16},{28,20},{1,9},{5... | collective-permute-start | bytes 2457608 | tf_op jit(solution)/shard_map/ppermute | solution.py:1094
  96.0 34.0 %collective-permute-start.11 = (bf16[384,512]{1,0:T(8,128)(2,1)S(1)}, bf16[384,512]{1,0:T(8,128)(2,1)S(1)}, u32[]{:S(2)}, u32[]{:S(2)}) collective-permute-start(bf16[384,512]{1,0:T(8,128)(2,1)S(1)} %rows_message.1.refs_0_), channel_id=1, source_target_pairs={{0,3},{1,0},{2,1},{3,2},{4,7},{5,4},{6,5},{7,6},{8,11},{9,8},{10,9... | collective-permute-start | bytes 1179656 | tf_op jit(solution)/shard_map/ppermute | solution.py:1082
  96.5 34.0 %collective-permute-start.12 = (bf16[384,512]{1,0:T(8,128)(2,1)S(1)}, bf16[384,512]{1,0:T(8,128)(2,1)S(1)}, u32[]{:S(2)}, u32[]{:S(2)}) collective-permute-start(bf16[384,512]{1,0:T(8,128)(2,1)S(1)} %rows_message.1.refs_0_), channel_id=1, source_target_pairs={{0,2},{1,3},{2,0},{3,1},{4,6},{5,7},{6,4},{7,5},{8,10},{9,11},{10,... | collective-permute-start | bytes 1179656 | tf_op jit(solution)/shard_map/ppermute | solution.py:1082
  97.0 33.5 %collective-permute-start.13 = (bf16[384,512]{1,0:T(8,128)(2,1)S(1)}, bf16[384,512]{1,0:T(8,128)(2,1)S(1)}, u32[]{:S(2)}, u32[]{:S(2)}) collective-permute-start(bf16[384,512]{1,0:T(8,128)(2,1)S(1)} %rows_message.1.refs_0_), channel_id=1, source_target_pairs={{0,1},{1,2},{2,3},{3,0},{4,5},{5,6},{6,7},{7,4},{8,9},{9,10},{10,1... | collective-permute-start | bytes 1179656 | tf_op jit(solution)/shard_map/ppermute | solution.py:1082
  116.0 15.7 %collective-permute-start.22 = (bf16[416,512]{1,0:T(8,128)(2,1)S(1)}, bf16[416,512]{1,0:T(8,128)(2,1)S(1)}, u32[]{:S(2)}, u32[]{:S(2)}) collective-permute-start(bf16[416,512]{1,0:T(8,128)(2,1)S(1)} %get-tuple-element.192.lower_ref), channel_id=1, source_target_pairs={{0,8},{4,12},{8,0},{12,4},{16,24},{20,28},{24,16},{28,20},{1,9},{5... | collective-permute-start | bytes 1277960 | tf_op jit(solution)/shard_map/ppermute | solution.py:1094
  116.6 15.0 %collective-permute-start.21 = (bf16[384,512]{1,0:T(8,128)(2,1)S(1)}, bf16[384,512]{1,0:T(8,128)(2,1)S(1)}, u32[]{:S(2)}, u32[]{:S(2)}) collective-permute-start(bf16[384,512]{1,0:T(8,128)(2,1)S(1)} %get-tuple-element.178.upper_ref), channel_id=1, source_target_pairs={{0,16},{4,20},{8,24},{12,28},{16,0},{20,4},{24,8},{28,12},{1,17},{... | collective-permute-start | bytes 1179656 | tf_op jit(solution)/shard_map/ppermute | solution.py:1094
  134.2 9.0 %collective-permute-start.25 = (f32[16,512]{1,0:T(8,128)S(1)}, f32[16,512]{1,0:T(8,128)S(1)}, u32[]{:S(2)}, u32[]{:S(2)}) collective-permute-start(f32[16,512]{1,0:T(8,128)S(1)} %ordered_sum.1.refs_0_), channel_id=1, source_target_pairs={{0,3},{1,0},{2,1},{3,2},{4,7},{5,4},{6,5},{7,6},{8,11},{9,8},{10,9... | collective-permute-start | bytes 98312 | tf_op jit(solution)/shard_map/ppermute | solution.py:1082
  134.2 9.0 %collective-permute-start.26 = (f32[16,512]{1,0:T(8,128)S(1)}, f32[16,512]{1,0:T(8,128)S(1)}, u32[]{:S(2)}, u32[]{:S(2)}) collective-permute-start(f32[16,512]{1,0:T(8,128)S(1)} %ordered_sum.1.refs_0_), channel_id=1, source_target_pairs={{0,2},{1,3},{2,0},{3,1},{4,6},{5,7},{6,4},{7,5},{8,10},{9,11},{10,... | collective-permute-start | bytes 98312 | tf_op jit(solution)/shard_map/ppermute | solution.py:1082
  (11 other events, 67.1 us)
